TPU v7x, 32 devices: a whole 2x2x4 slice. The times are simulated.
32 devices in a mesh: rx: 2 (over core), space: 16 (over z, y, x).
Axes of the slice: x: 2, y: 2, z: 4, core: 2. Of those that a mesh axis runs over, the one named last changes fastest.
Arguments:
- conductivity: float32 [48, 32, 128], P('space'), may hold values from 0.1 to 1
- background: float32 [4, 2, 3, 48, 32, 128], P(None, None, None, 'space'), may hold values from -6 to 6
- warm_start: float32 [4, 2, 3, 48, 32, 128], P('rx', None, None, 'space'), may hold values from -8 to 8
- data_weight: float32 [4, 2, 3], P('rx'), may hold values from -640 to 640
- recv_cell: int32 [4], P('rx'), may hold values from 0 to 196607
- src_group: int32 [4], P('rx'), may hold values from 0 to 3
- group_freq: int32 [4], replicated, may hold values from 0 to 7
Outputs:
- block: float32 [8, 8], P('rx')
- smoothed: bfloat16 [4, 2, 48, 32, 128], P('rx', None, 'space')
All inputs are finite; a program needn't handle non-finite values.
Results may differ from a plain program's by a relative error of at most 0.01.
Values may be sent and summed in bfloat16 or wider, within the bound.
No kernel may reach another device: no remote copies, remote signals or barrier semaphores. Data moves between devices by JAX's collectives and lax.ppermute only.
A program may use at most 64 MiB of HBM per device.

v0:
```python
import jax
import jax.numpy as jnp
from jax import lax
from jax.sharding import PartitionSpec as P

ITERS = 3


RELAX = 0.2
KAPPA = 0.1


def with_halo(x, sides, width):
    for axis, dim in sides:
        peers, length = (lax.axis_size(axis), x.shape[dim])
        up = [(i, (i + 1) % peers) for i in range(peers - 1)]
        down = [(j, i) for i, j in up]
        last = lax.slice_in_dim(x, length - width, length, axis=dim)
        leading = lax.slice_in_dim(x, 0, width, axis=dim)
        before = lax.ppermute(last, axis, up)
        after = lax.ppermute(leading, axis, down)
        x = jnp.concatenate([before, x, after], axis=dim)
    return x


def forward_y(f):
    return jnp.concatenate([f[..., 1:, :] - f[..., :-1, :], -f[..., -1:, :]], axis=-2)


def forward_z(f):
    return jnp.concatenate([f[..., 1:] - f[..., :-1], -f[..., -1:]], axis=-1)


def backward_y(f):
    return jnp.concatenate([f[..., :1, :], f[..., 1:, :] - f[..., :-1, :]], axis=-2)


def backward_z(f):
    return jnp.concatenate([f[..., :1], f[..., 1:] - f[..., :-1]], axis=-1)


def curl_curl(padded):
    comp_x = padded[..., 0, :, :, :]
    comp_y = padded[..., 1, :, :, :]
    comp_z = padded[..., 2, :, :, :]
    low_x = comp_x[..., :-1, :, :]
    low_y = comp_y[..., :-1, :, :]
    low_z = comp_z[..., :-1, :, :]
    mag_x = forward_y(low_z) - forward_z(low_y)
    mag_y = forward_z(low_x) - (comp_z[..., 1:, :, :] - comp_z[..., :-1, :, :])
    mag_z = comp_y[..., 1:, :, :] - comp_y[..., :-1, :, :] - forward_y(low_x)
    curl_x = backward_y(mag_z[..., 1:, :, :]) - backward_z(mag_y[..., 1:, :, :])
    curl_y = backward_z(mag_x[..., 1:, :, :]) - (mag_z[..., 1:, :, :] - mag_z[..., :-1, :, :])
    curl_z = mag_y[..., 1:, :, :] - mag_y[..., :-1, :, :] - backward_y(mag_x[..., 1:, :, :])
    return jnp.stack([curl_x, curl_y, curl_z], axis=-4)


def operate(adjoint, padded, coef):
    curl = curl_curl(padded)
    real_part = curl[..., 0, :, :, :, :] - coef * adjoint[..., 1, :, :, :, :]
    imag_part = curl[..., 1, :, :, :, :] + coef * adjoint[..., 0, :, :, :, :]
    return jnp.stack([real_part, imag_part], axis=-5)


def sensitivity(adjoint, field, coef):
    field_re = field[..., 0, :, :, :, :]
    field_im = field[..., 1, :, :, :, :]
    adj_re = adjoint[..., 0, :, :, :, :]
    adj_im = adjoint[..., 1, :, :, :, :]
    prod_re = jnp.sum(field_re * adj_re - field_im * adj_im, axis=-4)
    prod_im = jnp.sum(field_re * adj_im + field_im * adj_re, axis=-4)
    return (coef * jnp.stack([prod_re, prod_im], axis=-4)).astype(jnp.bfloat16)


def neighbours_y(f):
    zeros = jnp.zeros_like(f[..., :1, :])
    return jnp.concatenate([f[..., 1:, :], zeros], axis=-2) + jnp.concatenate(
        [zeros, f[..., :-1, :]], axis=-2
    )


def neighbours_z(f):
    zeros = jnp.zeros_like(f[..., :1])
    return jnp.concatenate([f[..., 1:], zeros], axis=-1) + jnp.concatenate(
        [zeros, f[..., :-1]], axis=-1
    )


def smooth_step(padded):
    centre = padded[..., 1:-1, :, :]
    near = (
        padded[..., 2:, :, :] + padded[..., :-2, :, :] + neighbours_y(centre) + neighbours_z(centre)
    )
    return centre + KAPPA * (near - 6.0 * centre)


def point_terms(data_weight, recv_cell, first_plane, planes, height, breadth):
    plane_ids = first_plane + jnp.arange(planes, dtype=jnp.int32)
    inner = jnp.arange(height * breadth, dtype=jnp.int32).reshape(height, breadth)
    flat = plane_ids[:, None, None] * (height * breadth) + inner[None]
    point = (flat[None] == recv_cell[:, None, None, None]).astype(jnp.float32)
    return data_weight[:, :, :, None, None, None] * point[:, None, None]


def shards(conductivity, background, warm_start, data_weight, recv_cell, src_group, group_freq):
    count = warm_start.shape[0]
    groups = background.shape[0]
    depth, height, breadth = conductivity.shape
    cells = depth * height * breadth
    selector = (src_group[:, None] == jnp.arange(groups, dtype=jnp.int32)[None, :]).astype(
        jnp.float32
    )
    freq_value = jnp.sum(selector * group_freq.astype(jnp.float32)[None, :], axis=1)
    angular = 0.25 * jnp.power(jnp.float32(1.25), freq_value)
    coef = angular[:, None, None, None, None] * conductivity[None, None]
    field = jnp.sum(selector[:, :, None, None, None, None, None] * background[None], axis=1)
    adjoint = warm_start
    source_term = point_terms(
        data_weight, recv_cell, lax.axis_index("space") * depth, depth, height, breadth
    )
    for sweep in range(ITERS):
        padded = with_halo(adjoint, (("space", 3),), 1)
        adjoint = adjoint + RELAX * (source_term - operate(adjoint, padded, coef))
    rows = sensitivity(adjoint, field, coef)
    value = rows.astype(jnp.float32)
    for sweep in range(2):
        value = smooth_step(with_halo(value, (("space", 2),), 1))
    smoothed = value.astype(jnp.bfloat16)
    flat_rows = rows.reshape(2 * count, cells)
    flat_smooth = smoothed.reshape(2 * count, cells)
    partial_block = jnp.einsum(
        "rc,kc->rk",
        flat_rows,
        lax.all_gather(flat_smooth, "rx", axis=0, tiled=True),
        preferred_element_type=jnp.float32,
    )
    total = lax.psum(partial_block, "space")
    block = total / (cells * lax.axis_size("space"))
    return (block, smoothed)


def solution(mesh):
    in_specs = (
        P("space", None, None),
        P(None, None, None, "space", None, None),
        P("rx", None, None, "space", None, None),
        P("rx", None, None),
        P("rx"),
        P("rx"),
        P(),
    )
    out_specs = (P("rx", None), P("rx", None, "space", None, None))
    return jax.shard_map(shards, mesh=mesh, in_specs=in_specs, out_specs=out_specs, check_vma=False)
```

profile of v0, /device:TPU:0, one launch (start us, length us, event | category | flops | bytes accessed | tf_op | source)
XLA Modules:
  0.0 123.5 jit_solution(16449622634678132276)
XLA Ops:
  0.7 1.1 fusion.56
  1.8 4.9 %collective-permute-start = (f32[2,2,3,1,32,128]{5,4,3,1,0,2:T(8,128)S(1)}, f32[2,2,3,1,32,128]{5,4,3,1,0,2:T(8,128)S(1)}, u32[]{:S(2)}, u32[]{:S(2)}) collective-permute-start(f32[2,2,3,1,32,128]{5,4,3,1,0,2:T(8,128)S(1)} %copy.93), channel_id=1, source_target_pairs={{0,1},{1,2},{2,3},{3,4},{4,5},{5,6},{6,7},{7,8},{8,9},{9,10},{10,1... | collective-permute-start | bytes 589832 | tf_op jit(solution)/shard_map/ppermute | solution.py:20
  6.7 1.3 %collective-permute-start.1 = (f32[2,2,3,1,32,128]{5,4,3,1,0,2:T(8,128)S(1)}, f32[2,2,3,1,32,128]{5,4,3,1,0,2:T(8,128)S(1)}, u32[]{:S(2)}, u32[]{:S(2)}) collective-permute-start(f32[2,2,3,1,32,128]{5,4,3,1,0,2:T(8,128)S(1)} %copy.94), channel_id=1, source_target_pairs={{1,0},{2,1},{3,2},{4,3},{5,4},{6,5},{7,6},{8,7},{9,8},{10,9},{11,1... | collective-permute-start | bytes 589832 | tf_op jit(solution)/shard_map/ppermute | solution.py:21
  8.0 0.2 select_reduce_fusion
  8.5 2.3 %collective-permute-done = f32[2,2,3,1,32,128]{5,4,3,1,0,2:T(8,128)S(1)} collective-permute-done((f32[2,2,3,1,32,128]{5,4,3,1,0,2:T(8,128)S(1)}, f32[2,2,3,1,32,128]{5,4,3,1,0,2:T(8,128)S(1)}, u32[]{:S(2)}, u32[]{:S(2)}) %collective-permute-start) | collective-permute-done | bytes 196640 | tf_op jit(solution)/shard_map/ppermute | solution.py:20
  10.9 6.1 %collective-permute-done.1 = f32[2,2,3,1,32,128]{5,4,3,1,0,2:T(8,128)S(1)} collective-permute-done((f32[2,2,3,1,32,128]{5,4,3,1,0,2:T(8,128)S(1)}, f32[2,2,3,1,32,128]{5,4,3,1,0,2:T(8,128)S(1)}, u32[]{:S(2)}, u32[]{:S(2)}) %collective-permute-start.1) | collective-permute-done | bytes 196640 | tf_op jit(solution)/shard_map/ppermute | solution.py:21
  17.1 0.2 slice_negate_fusion.4
  17.3 0.2 slice_subtract_fusion.13
  18.5 0.2 copy.73
  19.2 0.5 copy-done.7
  19.9 3.4 %collective-permute-start.2 = (f32[2,2,3,1,32,128]{5,4,3,1,0,2:T(8,128)S(1)}, f32[2,2,3,1,32,128]{5,4,3,1,0,2:T(8,128)S(1)}, u32[]{:S(2)}, u32[]{:S(2)}) collective-permute-start(f32[2,2,3,1,32,128]{5,4,3,1,0,2:T(8,128)S(1)} %copy.95), channel_id=1, source_target_pairs={{0,1},{1,2},{2,3},{3,4},{4,5},{5,6},{6,7},{7,8},{8,9},{9,10},{10,1... | collective-permute-start | bytes 589832 | tf_op jit(solution)/shard_map/ppermute | solution.py:20
  23.4 1.3 %collective-permute-start.3 = (f32[2,2,3,1,32,128]{5,4,3,1,0,2:T(8,128)S(1)}, f32[2,2,3,1,32,128]{5,4,3,1,0,2:T(8,128)S(1)}, u32[]{:S(2)}, u32[]{:S(2)}) collective-permute-start(f32[2,2,3,1,32,128]{5,4,3,1,0,2:T(8,128)S(1)} %copy.96), channel_id=1, source_target_pairs={{1,0},{2,1},{3,2},{4,3},{5,4},{6,5},{7,6},{8,7},{9,8},{10,9},{11,1... | collective-permute-start | bytes 589832 | tf_op jit(solution)/shard_map/ppermute | solution.py:21
  24.7 2.0 %collective-permute-done.2 = f32[2,2,3,1,32,128]{5,4,3,1,0,2:T(8,128)S(1)} collective-permute-done((f32[2,2,3,1,32,128]{5,4,3,1,0,2:T(8,128)S(1)}, f32[2,2,3,1,32,128]{5,4,3,1,0,2:T(8,128)S(1)}, u32[]{:S(2)}, u32[]{:S(2)}) %collective-permute-start.2) | collective-permute-done | bytes 196640 | tf_op jit(solution)/shard_map/ppermute | solution.py:20
  26.7 0.1 constant_dynamic-update-slice_fusion.4
  26.9 4.8 %collective-permute-done.3 = f32[2,2,3,1,32,128]{5,4,3,1,0,2:T(8,128)S(1)} collective-permute-done((f32[2,2,3,1,32,128]{5,4,3,1,0,2:T(8,128)S(1)}, f32[2,2,3,1,32,128]{5,4,3,1,0,2:T(8,128)S(1)}, u32[]{:S(2)}, u32[]{:S(2)}) %collective-permute-start.3) | collective-permute-done | bytes 196640 | tf_op jit(solution)/shard_map/ppermute | solution.py:21
  32.7 0.8 slice_subtract_fusion.28
  33.5 0.7 slice.735
  34.5 0.8 fusion.39
  35.4 0.2 copy.80
  35.7 1.0 fusion.38
  36.7 1.0 fusion.48
  37.9 0.3 fusion.3
  38.3 4.3 %collective-permute-start.4 = (f32[2,2,3,1,32,128]{5,4,3,1,0,2:T(8,128)S(1)}, f32[2,2,3,1,32,128]{5,4,3,1,0,2:T(8,128)S(1)}, u32[]{:S(2)}, u32[]{:S(2)}) collective-permute-start(f32[2,2,3,1,32,128]{5,4,3,1,0,2:T(8,128)S(1)} %copy.97), channel_id=1, source_target_pairs={{0,1},{1,2},{2,3},{3,4},{4,5},{5,6},{6,7},{7,8},{8,9},{9,10},{10,1... | collective-permute-start | bytes 589832 | tf_op jit(solution)/shard_map/ppermute | solution.py:20
  42.7 1.1 multiply_reduce_fusion
  43.8 1.3 %collective-permute-start.5 = (f32[2,2,3,1,32,128]{5,4,3,1,0,2:T(8,128)S(1)}, f32[2,2,3,1,32,128]{5,4,3,1,0,2:T(8,128)S(1)}, u32[]{:S(2)}, u32[]{:S(2)}) collective-permute-start(f32[2,2,3,1,32,128]{5,4,3,1,0,2:T(8,128)S(1)} %copy.98), channel_id=1, source_target_pairs={{1,0},{2,1},{3,2},{4,3},{5,4},{6,5},{7,6},{8,7},{9,8},{10,9},{11,1... | collective-permute-start | bytes 589832 | tf_op jit(solution)/shard_map/ppermute | solution.py:21
  45.1 0.7 collective-permute-done.4
  45.8 0.3 constant_dynamic-update-slice_fusion.7
  46.1 5.3 %collective-permute-done.5 = f32[2,2,3,1,32,128]{5,4,3,1,0,2:T(8,128)S(1)} collective-permute-done((f32[2,2,3,1,32,128]{5,4,3,1,0,2:T(8,128)S(1)}, f32[2,2,3,1,32,128]{5,4,3,1,0,2:T(8,128)S(1)}, u32[]{:S(2)}, u32[]{:S(2)}) %collective-permute-start.5) | collective-permute-done | bytes 196640 | tf_op jit(solution)/shard_map/ppermute | solution.py:21
  52.5 0.8 slice_subtract_fusion.22
  53.3 0.7 slice.775
  54.0 0.7 fusion.34
  54.9 0.8 fusion.33
  55.8 0.2 copy.87
  56.1 1.2 fusion.32
  57.6 0.4 fusion.5
  58.0 0.7 copy-done.1
  59.0 4.2 %collective-permute-start.7 = (f32[2,2,1,32,128]{4,3,2,1,0:T(8,128)S(1)}, f32[2,2,1,32,128]{4,3,2,1,0:T(8,128)S(1)}, u32[]{:S(2)}, u32[]{:S(2)}) collective-permute-start(f32[2,2,1,32,128]{4,3,2,1,0:T(8,128)S(1)} %get-tuple-element.38), channel_id=1, source_target_pairs={{0,1},{1,2},{2,3},{3,4},{4,5},{5,6},{6,7},{7,8},{8,9},{9,10},{10,1... | collective-permute-start | bytes 196616 | tf_op jit(solution)/shard_map/ppermute | solution.py:20
  63.2 1.3 %collective-permute-start.6 = (f32[2,2,1,32,128]{4,3,2,1,0:T(8,128)S(1)}, f32[2,2,1,32,128]{4,3,2,1,0:T(8,128)S(1)}, u32[]{:S(2)}, u32[]{:S(2)}) collective-permute-start(f32[2,2,1,32,128]{4,3,2,1,0:T(8,128)S(1)} %get-tuple-element.37), channel_id=1, source_target_pairs={{1,0},{2,1},{3,2},{4,3},{5,4},{6,5},{7,6},{8,7},{9,8},{10,9},{11,1... | collective-permute-start | bytes 196616 | tf_op jit(solution)/shard_map/ppermute | solution.py:21
  64.6 0.5 collective-permute-done.7
  65.1 4.3 %collective-permute-done.6 = f32[2,2,1,32,128]{4,3,2,1,0:T(8,128)S(1)} collective-permute-done((f32[2,2,1,32,128]{4,3,2,1,0:T(8,128)S(1)}, f32[2,2,1,32,128]{4,3,2,1,0:T(8,128)S(1)}, u32[]{:S(2)}, u32[]{:S(2)}) %collective-permute-start.6) | collective-permute-done | bytes 65568 | tf_op jit(solution)/shard_map/ppermute | solution.py:21
  69.7 5.1 %collective-permute-start.9 = (f32[2,2,1,32,128]{4,3,2,1,0:T(8,128)S(1)}, f32[2,2,1,32,128]{4,3,2,1,0:T(8,128)S(1)}, u32[]{:S(2)}, u32[]{:S(2)}) collective-permute-start(f32[2,2,1,32,128]{4,3,2,1,0:T(8,128)S(1)} %get-tuple-element.32), channel_id=1, source_target_pairs={{0,1},{1,2},{2,3},{3,4},{4,5},{5,6},{6,7},{7,8},{8,9},{9,10},{10,1... | collective-permute-start | bytes 196616 | tf_op jit(solution)/shard_map/ppermute | solution.py:20
  74.8 1.3 %collective-permute-start.8 = (f32[2,2,1,32,128]{4,3,2,1,0:T(8,128)S(1)}, f32[2,2,1,32,128]{4,3,2,1,0:T(8,128)S(1)}, u32[]{:S(2)}, u32[]{:S(2)}) collective-permute-start(f32[2,2,1,32,128]{4,3,2,1,0:T(8,128)S(1)} %get-tuple-element.31), channel_id=1, source_target_pairs={{1,0},{2,1},{3,2},{4,3},{5,4},{6,5},{7,6},{8,7},{9,8},{10,9},{11,1... | collective-permute-start | bytes 196616 | tf_op jit(solution)/shard_map/ppermute | solution.py:21
  76.1 0.5 collective-permute-done.9
  76.7 4.3 %collective-permute-done.8 = f32[2,2,1,32,128]{4,3,2,1,0:T(8,128)S(1)} collective-permute-done((f32[2,2,1,32,128]{4,3,2,1,0:T(8,128)S(1)}, f32[2,2,1,32,128]{4,3,2,1,0:T(8,128)S(1)}, u32[]{:S(2)}, u32[]{:S(2)}) %collective-permute-start.8) | collective-permute-done | bytes 65568 | tf_op jit(solution)/shard_map/ppermute | solution.py:21
  81.2 1.9 %all-gather = bf16[2,4,12288]{2,1,0:T(4,128)(2,1)S(1)} all-gather(bf16[1,4,12288]{2,1,0:T(4,128)(2,1)S(1)} %reshape.239), channel_id=1, replica_groups=mesh['rx'=2,'space'=16] {'rx'}, dimensions={0}, use_global_device_ids=true | all-gather | bytes 294912 | tf_op jit(solution)/shard_map/all_gather | solution.py:134
  83.2 0.2 fusion.63
  83.4 39.5 %psum.7 = f32[4,8]{1,0:T(4,128)S(1)} all-reduce(f32[4,8]{1,0:T(4,128)S(1)} %fusion.63), channel_id=1, replica_groups=mesh['rx'=2,'space'=16] {'space'}, use_global_device_ids=true, to_apply=%region_4.0 | all-reduce | flops 32 | bytes 256 | tf_op jit(solution)/shard_map/psum | solution.py:137
  122.9 0.6 broadcast_multiply_fusion.1
  (121 shorter events, 6.3 us)
Async XLA Ops:
  0.6 10.2 %copy-start = (f32[2,2,3,3,32,128]{5,4,3,2,1,0:T(8,128)S(1)}, f32[2,2,3,3,32,128]{5,4,3,2,1,0:T(8,128)}, u32[]{:S(2)}) copy-start(f32[2,2,3,3,32,128]{5,4,3,2,1,0:T(8,128)} %param.9) | copy-start | bytes 1769476
  0.6 7.4 %copy-start.10 = (s32[4]{0:T(128)S(1)}, s32[4]{0:T(128)}, u32[]{:S(2)}) copy-start(s32[4]{0:T(128)} %param.13) | copy-start | bytes 52
  0.7 7.4 %copy-start.11 = (s32[2]{0:T(128)S(1)}, s32[2]{0:T(128)}, u32[]{:S(2)}) copy-start(s32[2]{0:T(128)} %param.12) | copy-start | bytes 28
  0.7 7.6 %copy-start.8 = (f32[3,32,128]{2,1,0:T(8,128)S(1)}, f32[3,32,128]{2,1,0:T(8,128)}, u32[]{:S(2)}) copy-start(f32[3,32,128]{2,1,0:T(8,128)} %param.7) | copy-start | bytes 147460
  0.7 7.7 %copy-start.9 = (s32[2]{0:T(128)S(1)}, s32[2]{0:T(128)}, u32[]{:S(2)}) copy-start(s32[2]{0:T(128)} %param.11) | copy-start | bytes 28
  1.8 9.0 %collective-permute-start = (f32[2,2,3,1,32,128]{5,4,3,1,0,2:T(8,128)S(1)}, f32[2,2,3,1,32,128]{5,4,3,1,0,2:T(8,128)S(1)}, u32[]{:S(2)}, u32[]{:S(2)}) collective-permute-start(f32[2,2,3,1,32,128]{5,4,3,1,0,2:T(8,128)S(1)} %copy.93), channel_id=1, source_target_pairs={{0,1},{1,2},{2,3},{3,4},{4,5},{5,6},{6,7},{7,8},{8,9},{9,10},{10,1... | collective-permute-start | bytes 589832 | tf_op jit(solution)/shard_map/ppermute | solution.py:20
  6.7 10.3 %collective-permute-start.1 = (f32[2,2,3,1,32,128]{5,4,3,1,0,2:T(8,128)S(1)}, f32[2,2,3,1,32,128]{5,4,3,1,0,2:T(8,128)S(1)}, u32[]{:S(2)}, u32[]{:S(2)}) collective-permute-start(f32[2,2,3,1,32,128]{5,4,3,1,0,2:T(8,128)S(1)} %copy.94), channel_id=1, source_target_pairs={{1,0},{2,1},{3,2},{4,3},{5,4},{6,5},{7,6},{8,7},{9,8},{10,9},{11,1... | collective-permute-start | bytes 589832 | tf_op jit(solution)/shard_map/ppermute | solution.py:21
  19.0 0.7 copy-start.7
  19.9 6.8 %collective-permute-start.2 = (f32[2,2,3,1,32,128]{5,4,3,1,0,2:T(8,128)S(1)}, f32[2,2,3,1,32,128]{5,4,3,1,0,2:T(8,128)S(1)}, u32[]{:S(2)}, u32[]{:S(2)}) collective-permute-start(f32[2,2,3,1,32,128]{5,4,3,1,0,2:T(8,128)S(1)} %copy.95), channel_id=1, source_target_pairs={{0,1},{1,2},{2,3},{3,4},{4,5},{5,6},{6,7},{7,8},{8,9},{9,10},{10,1... | collective-permute-start | bytes 589832 | tf_op jit(solution)/shard_map/ppermute | solution.py:20
  23.4 8.3 %collective-permute-start.3 = (f32[2,2,3,1,32,128]{5,4,3,1,0,2:T(8,128)S(1)}, f32[2,2,3,1,32,128]{5,4,3,1,0,2:T(8,128)S(1)}, u32[]{:S(2)}, u32[]{:S(2)}) collective-permute-start(f32[2,2,3,1,32,128]{5,4,3,1,0,2:T(8,128)S(1)} %copy.96), channel_id=1, source_target_pairs={{1,0},{2,1},{3,2},{4,3},{5,4},{6,5},{7,6},{8,7},{9,8},{10,9},{11,1... | collective-permute-start | bytes 589832 | tf_op jit(solution)/shard_map/ppermute | solution.py:21
  34.5 1.2 copy-start.5
  38.2 4.5 %copy-start.2 = (f32[4,2,3,3,32,128]{5,4,3,2,1,0:T(8,128)S(1)}, f32[4,2,3,3,32,128]{5,4,3,2,1,0:T(8,128)}, u32[]{:S(2)}) copy-start(f32[4,2,3,3,32,128]{5,4,3,2,1,0:T(8,128)} %param.8) | copy-start | bytes 3538948
  38.3 7.5 %collective-permute-start.4 = (f32[2,2,3,1,32,128]{5,4,3,1,0,2:T(8,128)S(1)}, f32[2,2,3,1,32,128]{5,4,3,1,0,2:T(8,128)S(1)}, u32[]{:S(2)}, u32[]{:S(2)}) collective-permute-start(f32[2,2,3,1,32,128]{5,4,3,1,0,2:T(8,128)S(1)} %copy.97), channel_id=1, source_target_pairs={{0,1},{1,2},{2,3},{3,4},{4,5},{5,6},{6,7},{7,8},{8,9},{9,10},{10,1... | collective-permute-start | bytes 589832 | tf_op jit(solution)/shard_map/ppermute | solution.py:20
  43.8 7.6 %collective-permute-start.5 = (f32[2,2,3,1,32,128]{5,4,3,1,0,2:T(8,128)S(1)}, f32[2,2,3,1,32,128]{5,4,3,1,0,2:T(8,128)S(1)}, u32[]{:S(2)}, u32[]{:S(2)}) collective-permute-start(f32[2,2,3,1,32,128]{5,4,3,1,0,2:T(8,128)S(1)} %copy.98), channel_id=1, source_target_pairs={{1,0},{2,1},{3,2},{4,3},{5,4},{6,5},{7,6},{8,7},{9,8},{10,9},{11,1... | collective-permute-start | bytes 589832 | tf_op jit(solution)/shard_map/ppermute | solution.py:21
  56.0 1.3 %copy-start.3 = (f32[2,2,1,3,31,128]{5,4,3,1,0,2:T(8,128)S(1)}, f32[2,2,1,3,31,128]{5,4,3,1,0,2:T(8,128)}, u32[]{:S(2)}) copy-start(f32[2,2,1,3,31,128]{5,4,3,1,0,2:T(8,128)} %fusion.34) | copy-start | bytes 571396
  56.0 1.3 %copy-start.4 = (f32[2,2,1,3,32,127]{5,4,3,1,0,2:T(8,128)S(1)}, f32[2,2,1,3,32,127]{5,4,3,1,0,2:T(8,128)}, u32[]{:S(2)}) copy-start(f32[2,2,1,3,32,127]{5,4,3,1,0,2:T(8,128)} %fusion.33) | copy-start | bytes 585220
  57.6 1.1 copy-start.1
  59.0 6.1 %collective-permute-start.7 = (f32[2,2,1,32,128]{4,3,2,1,0:T(8,128)S(1)}, f32[2,2,1,32,128]{4,3,2,1,0:T(8,128)S(1)}, u32[]{:S(2)}, u32[]{:S(2)}) collective-permute-start(f32[2,2,1,32,128]{4,3,2,1,0:T(8,128)S(1)} %get-tuple-element.38), channel_id=1, source_target_pairs={{0,1},{1,2},{2,3},{3,4},{4,5},{5,6},{6,7},{7,8},{8,9},{9,10},{10,1... | collective-permute-start | bytes 196616 | tf_op jit(solution)/shard_map/ppermute | solution.py:20
  63.2 6.2 %collective-permute-start.6 = (f32[2,2,1,32,128]{4,3,2,1,0:T(8,128)S(1)}, f32[2,2,1,32,128]{4,3,2,1,0:T(8,128)S(1)}, u32[]{:S(2)}, u32[]{:S(2)}) collective-permute-start(f32[2,2,1,32,128]{4,3,2,1,0:T(8,128)S(1)} %get-tuple-element.37), channel_id=1, source_target_pairs={{1,0},{2,1},{3,2},{4,3},{5,4},{6,5},{7,6},{8,7},{9,8},{10,9},{11,1... | collective-permute-start | bytes 196616 | tf_op jit(solution)/shard_map/ppermute | solution.py:21
  69.7 7.0 %collective-permute-start.9 = (f32[2,2,1,32,128]{4,3,2,1,0:T(8,128)S(1)}, f32[2,2,1,32,128]{4,3,2,1,0:T(8,128)S(1)}, u32[]{:S(2)}, u32[]{:S(2)}) collective-permute-start(f32[2,2,1,32,128]{4,3,2,1,0:T(8,128)S(1)} %get-tuple-element.32), channel_id=1, source_target_pairs={{0,1},{1,2},{2,3},{3,4},{4,5},{5,6},{6,7},{7,8},{8,9},{9,10},{10,1... | collective-permute-start | bytes 196616 | tf_op jit(solution)/shard_map/ppermute | solution.py:20
  74.8 6.2 %collective-permute-start.8 = (f32[2,2,1,32,128]{4,3,2,1,0:T(8,128)S(1)}, f32[2,2,1,32,128]{4,3,2,1,0:T(8,128)S(1)}, u32[]{:S(2)}, u32[]{:S(2)}) collective-permute-start(f32[2,2,1,32,128]{4,3,2,1,0:T(8,128)S(1)} %get-tuple-element.31), channel_id=1, source_target_pairs={{1,0},{2,1},{3,2},{4,3},{5,4},{6,5},{7,6},{8,7},{9,8},{10,9},{11,1... | collective-permute-start | bytes 196616 | tf_op jit(solution)/shard_map/ppermute | solution.py:21
  81.1 42.4 %copy-start.6 = (bf16[2,2,3,32,128]{4,3,2,1,0:T(8,128)(2,1)}, bf16[2,2,3,32,128]{4,3,2,1,0:T(8,128)(2,1)S(1)}, u32[]{:S(2)}) copy-start(bf16[2,2,3,32,128]{4,3,2,1,0:T(8,128)(2,1)S(1)} %fusion.22) | copy-start | bytes 294916
where the time goes:
time: 124 us; the launch traced here: 123 us
  blocking collectives  41.4 us (33%)
  waiting for transfers between devices  30.8 us (25%)
  starting transfers between devices  28.4 us (23%)
  other arithmetic  15.5 us (12%)
  local copies, waits for them, and re-layouts  5.66 us (5%)
  between operations  1.52 us (1%)
    psum x1, blocking collectives, shards(): total = lax.psum(partial_block, 'space')  39.5 us
    ppermute x5, waiting for transfers between devices, with_halo(): after = lax.ppermute(leading, axis, down)  24.7 us
    ppermute x5, starting transfers between devices, with_halo(): before = lax.ppermute(last, axis, up)  21.9 us
    ppermute x5, starting transfers between devices, with_halo(): after = lax.ppermute(leading, axis, down)  6.46 us
    ppermute x5, waiting for transfers between devices, with_halo(): before = lax.ppermute(last, axis, up)  6.06 us
    another operation x9, other arithmetic, curl_curl(): return jnp.stack([curl_x, curl_y, curl_z], axis=-4)  2.67 us
  transfers between devices with their start and end apart: 10, of which 10 were waited for; matrix products, arithmetic and copies ran while one was open for 2% of the time, Pallas kernels for 0%

commit v1 on v0

v1 whole, which is shorter than its diff:
```python
import functools

import jax
import jax.numpy as jnp
from jax import lax
from jax.experimental import pallas as pl
from jax.experimental.pallas import tpu as pltpu
from jax.sharding import PartitionSpec as P

RELAX = 0.2
KAPPA = 0.1
UP = 7
DOWN = 6
REACH = 2
FULL = pl.BlockSpec(memory_space=pltpu.VMEM)
HBM = pl.BlockSpec(memory_space=pltpu.HBM)
SCALARS = pl.BlockSpec(memory_space=pltpu.SMEM)
KERNEL = pltpu.CompilerParams(vmem_limit_bytes=8 * 2**20)
F32 = jnp.float32


class Steps:
    def __init__(self, breadth):
        sub = lax.broadcasted_iota(jnp.int32, (8, breadth), 0)
        lane = lax.broadcasted_iota(jnp.int32, (8, breadth), 1)
        self.breadth = breadth
        self.sub, self.lane = sub, lane
        self.not_last_row, self.not_first_row = sub < 7, sub > 0
        self.not_last, self.not_first = lane < breadth - 1, lane > 0

    def after_y(self, f):
        return f[1:] + [jnp.where(self.not_last_row, pltpu.roll(f[0], 7, 0), 0.0)]

    def before_y(self, f):
        return [jnp.where(self.not_first_row, pltpu.roll(f[-1], 1, 0), 0.0)] + f[:-1]

    def after_z(self, f):
        return [jnp.where(self.not_last, pltpu.roll(v, self.breadth - 1, 1), 0.0) for v in f]

    def before_z(self, f):
        return [jnp.where(self.not_first, pltpu.roll(v, 1, 1), 0.0) for v in f]

    def up_y(self, f):
        return sub_(self.after_y(f), f)

    def up_z(self, f):
        return sub_(self.after_z(f), f)

    def down_y(self, f):
        return sub_(f, self.before_y(f))

    def down_z(self, f):
        return sub_(f, self.before_z(f))


def sub_(a, b):
    return [x - y for x, y in zip(a, b)]


def add_(a, b):
    return [x + y for x, y in zip(a, b)]


def mul_(a, b):
    return [x * y for x, y in zip(a, b)]


def turned(ref, at, turns):
    return [ref[at + (pl.ds(r, 8, stride=turns), slice(None))] for r in range(turns)]


def joined(f, dtype):
    return jnp.concatenate(f, axis=0).astype(dtype)


def parted(value, turns):
    value = value.astype(F32)
    return [value[8 * r : 8 * r + 8] for r in range(turns)]


def angular_of(freq):
    angular = F32(0.25)
    for bit, factor in ((1, 1.25), (2, 1.25**2), (4, 1.25**4)):
        angular = angular * jnp.where((freq & bit) != 0, F32(factor), F32(1.0))
    return angular


def signed(part):
    return jnp.where(part == 0, F32(1.0), F32(-1.0))


class Point:
    def __init__(self, cell, first, turns, steps):
        height, breadth = 8 * turns, steps.breadth
        row = (cell // breadth) % height
        self.plane = cell // (height * breadth) - first
        self.turn = row % turns
        self.here = (steps.sub == row // turns) & (steps.lane == cell % breadth)

    def amount(self, low, high):
        reached = (self.plane >= low) & (self.plane < high)
        return jnp.where(reached, F32(RELAX), F32(0.0)), jnp.clip(self.plane, low, high - 1)


def magnetic_yz(steps, e, e_next):
    ex, ey, ez = e
    if e_next is None:
        hy = add_(steps.up_z(ex), ez)
        hz = [-v - w for v, w in zip(ey, steps.up_y(ex))]
    else:
        hy = sub_(steps.up_z(ex), sub_(e_next[2], ez))
        hz = sub_(sub_(e_next[1], ey), steps.up_y(ex))
    return hy, hz


def curl_back(steps, hx, hy, hz, before):
    hy_before, hz_before = before
    cx = sub_(steps.down_y(hz), steps.down_z(hy))
    cy = sub_(steps.down_z(hx), sub_(hz, hz_before))
    cz = sub_(sub_(hy, hy_before), steps.down_y(hx))
    return cx, cy, cz


def first_kernel(
    start_ref, cond_ref, weight_ref, cell_ref, group_ref, freq_ref, up_ref, down_ref, own_ref, edge_ref, held_ref,
    raw, raw_cond, weight, cell, group, freq, sems,
):
    count, _, _, depth, height, breadth = start_ref.shape
    turns = height // 8
    steps = Steps(breadth)
    pairs = ((start_ref, raw), (cond_ref, raw_cond), (weight_ref, weight), (cell_ref, cell), (group_ref, group), (freq_ref, freq))
    copies = [pltpu.make_async_copy(a, b, sems.at[k]) for k, (a, b) in enumerate(pairs)]
    for copy in copies:
        copy.start()
    for copy in copies:
        copy.wait()
    half = up_ref.dtype
    first = lax.axis_index("space") * depth
    for p in range(depth):
        plane = turned(raw_cond, (p,), turns)
        for r in range(turns):
            held_ref[p, r] = plane[r]
    up_ref[2 * count * UP] = joined([held_ref[depth - 1, r] for r in range(turns)], half)
    down_ref[2 * count * DOWN] = joined([held_ref[0, r] for r in range(turns)], half)

    def one(i, _):
        s, part = i // 2, i % 2
        scale = RELAX * signed(part) * angular_of(freq[group[s]])

        def electric(p):
            return [turned(raw, (s, part, comp, p), turns) for comp in range(3)]

        e = electric(0)
        for k, f in enumerate(e[1:]):
            down_ref[i * DOWN + k] = joined(f, half)
            for r in range(turns):
                edge_ref[i, k, r] = f[r]
        before = [-v for v in e[2]], e[1]
        for p in range(depth):
            e_next = electric(p + 1) if p < depth - 1 else None
            hy, hz = magnetic_yz(steps, e, e_next)
            if e_next is None:
                for k, f in enumerate((hy, hz)):
                    up_ref[i * UP + k] = joined(f, half)
                    for r in range(turns):
                        edge_ref[i, 2 + k, r] = f[r]
            hx = sub_(steps.up_y(e[2]), steps.up_z(e[1]))
            curl = curl_back(steps, hx, hy, hz, before)
            before = hy, hz
            coef = [scale * held_ref[p, r] for r in range(turns)]
            for comp in range(3):
                other = turned(raw, (s, 1 - part, comp, p), turns)
                for r in range(turns):
                    own_ref[i, comp, p, r] = e[comp][r] - RELAX * curl[comp][r] + coef[r] * other[r]
            e = e_next
        point = Point(cell[s], first, turns, steps)
        amount, at = point.amount(0, depth)
        for comp in range(3):
            add = jnp.where(point.here, amount * weight[s, part, comp], 0.0)
            own_ref[i, comp, at, point.turn] = own_ref[i, comp, at, point.turn] + add

        def swept(comp, p):
            return [own_ref[i, comp, p, r] for r in range(turns)]

        for comp in range(3):
            up_ref[i * UP + 2 + comp] = joined(swept(comp, depth - 1), half)
        ex, ey, ez = [swept(comp, depth - 2) for comp in range(3)]
        up_ref[i * UP + 5] = joined(add_(steps.up_z(ex), ez), half)
        up_ref[i * UP + 6] = joined([-v - w for v, w in zip(ey, steps.up_y(ex))], half)
        ex, ey, ez = [swept(comp, 0) for comp in range(3)]
        down_ref[i * DOWN + 2] = joined(ey, half)
        down_ref[i * DOWN + 3] = joined(ez, half)
        down_ref[i * DOWN + 4] = joined(sub_(steps.up_z(ex), swept(2, 1)), half)
        down_ref[i * DOWN + 5] = joined(sub_(swept(1, 1), steps.up_y(ex)), half)
        return 0

    lax.fori_loop(0, 2 * count, one, 0)


def stage_kernel(count, groups_at, scalar_ref, field_ref, out_ref, raw, sems):
    _, _, _, depth, height, _ = field_ref.shape
    turns = height // 8
    copies = []
    for s in range(count):
        group = scalar_ref[groups_at + s].astype(jnp.int32)
        copies.append(pltpu.make_async_copy(field_ref.at[group], raw.at[s], sems.at[s]))
        copies[-1].start()
    for copy in copies:
        copy.wait()

    def one(i, _):
        s, part = i // 2, i % 2
        for comp in range(3):
            for p in range(depth):
                plane = turned(raw, (s, part, comp, p), turns)
                for r in range(turns):
                    out_ref[i, comp, p, r] = plane[r]
        return 0

    lax.fori_loop(0, 2 * count, one, 0)


def sweep_kernel(
    scalar_ref, own_ref, edge_ref, held_ref, field_ref, low_ref, high_ref, rows_ref, up_ref, down_ref, one_, two_,
):
    parts, _, depth, turns, _, breadth = own_ref.shape
    count = parts // 2
    height = 8 * turns
    steps = Steps(breadth)
    first = scalar_ref[0].astype(jnp.int32)
    planes = scalar_ref[1].astype(jnp.int32)
    relax_low = jnp.where(first > 0, F32(RELAX), F32(0.0))
    relax_high = jnp.where(first + depth < planes, F32(RELAX), F32(0.0))
    weights_at = scalar_ref.shape[0] - 6 * count

    def angular_at(s):
        group = scalar_ref[2 + count + s].astype(jnp.int32)
        return angular_of(scalar_ref[2 + 2 * count + group].astype(jnp.int32))

    def load(ref, i, comp, p):
        return [ref[i, comp, p + 1, r] for r in range(turns)]

    def store(ref, i, comp, p, f):
        for r in range(turns):
            ref[i, comp, p + 1, r] = f[r]

    def scaled(a, f, factor):
        return [x + factor * y for x, y in zip(a, f)]

    def conductivity(p):
        if p < 0:
            return parted(low_ref[parts * UP], turns)
        if p >= depth:
            return parted(high_ref[parts * DOWN], turns)
        return [held_ref[p, r] for r in range(turns)]

    def add_point(ref, i, low, high):
        s, part = i // 2, i % 2
        point = Point(scalar_ref[2 + s].astype(jnp.int32), first, turns, steps)
        amount, at = point.amount(low, high)
        for comp in range(3):
            add = jnp.where(point.here, amount * scalar_ref[weights_at + i * 3 + comp], 0.0)
            ref[i, comp, at + 1, point.turn] = ref[i, comp, at + 1, point.turn] + add

    def received(ref, at):
        return parted(ref[at], turns)

    def join_slabs(i, _):
        ey, ez, ly, lz = [[edge_ref[i, k, r] for r in range(turns)] for k in range(4)]
        cross = add_(steps.down_y(ey), steps.down_z(ez))
        below = [received(low_ref, i * UP + 2 + comp) for comp in range(3)]
        store(one_, i, 0, -1, scaled(below[0], cross, -relax_low))
        store(one_, i, 1, -1, scaled(below[1], ey, relax_low))
        store(one_, i, 2, -1, scaled(below[2], ez, relax_low))
        low_y, low_z = received(low_ref, i * UP), received(low_ref, i * UP + 1)
        high_y, high_z = received(high_ref, i * DOWN), received(high_ref, i * DOWN + 1)
        cross = add_(steps.down_y(high_y), steps.down_z(high_z))
        for p in range(depth):
            e = [[own_ref[i, comp, p, r] for r in range(turns)] for comp in range(3)]
            if p == 0:
                e[1] = scaled(e[1], low_z, -RELAX)
                e[2] = scaled(e[2], low_y, RELAX)
            if p == depth - 1:
                e = [scaled(e[0], cross, -RELAX), scaled(e[1], high_y, RELAX), scaled(e[2], high_z, RELAX)]
            for comp in range(3):
                store(one_, i, comp, p, e[comp])
        store(one_, i, 1, depth, scaled(received(high_ref, i * DOWN + 2), lz, -relax_high))
        store(one_, i, 2, depth, scaled(received(high_ref, i * DOWN + 3), ly, relax_high))
        return 0

    def second_sweep(i, _):
        s, part = i // 2, i % 2
        other = i + 1 - 2 * part
        scale = RELAX * signed(part) * angular_at(s)
        e = [load(one_, i, comp, -1) for comp in range(3)]
        before = sub_(received(low_ref, i * UP + 5), e[2]), add_(received(low_ref, i * UP + 6), e[1])
        for p in range(-1, depth + 1):
            relax = relax_low if p < 0 else relax_high if p == depth else F32(RELAX)
            if p < depth:
                e_next = [load(one_, i, comp, p + 1) if comp or p < depth - 1 else None for comp in range(3)]
                hy, hz = magnetic_yz(steps, e, e_next)
            else:
                hy = add_(received(high_ref, i * DOWN + 4), e[2])
                hz = sub_(received(high_ref, i * DOWN + 5), e[1])
            hx = sub_(steps.up_y(e[2]), steps.up_z(e[1]))
            if p < depth:
                curl = curl_back(steps, hx, hy, hz, before)
            else:
                curl = None, sub_(steps.down_z(hx), sub_(hz, before[1])), sub_(sub_(hy, before[0]), steps.down_y(hx))
            before = hy, hz
            coef = [scale * v for v in conductivity(p)]
            for comp in range(1 if p == depth else 0, 3):
                beside = load(one_, other, comp, p)
                store(
                    two_, i, comp, p,
                    [e[comp][r] - relax * curl[comp][r] + coef[r] * beside[r] for r in range(turns)],
                )
            e = e_next
        add_point(two_, i, -1, depth + 1)
        return 0

    def third_sweep(i, _):
        s, part = i // 2, i % 2
        other = i + 1 - 2 * part
        scale = RELAX * signed(part) * angular_at(s)
        e = [load(two_, i, comp, 0) for comp in range(3)]
        before = magnetic_yz(steps, [load(two_, i, comp, -1) for comp in range(3)], e)
        for p in range(depth):
            e_next = [load(two_, i, comp, p + 1) if comp or p < depth - 1 else None for comp in range(3)]
            hy, hz = magnetic_yz(steps, e, e_next)
            hx = sub_(steps.up_y(e[2]), steps.up_z(e[1]))
            curl = curl_back(steps, hx, hy, hz, before)
            before = hy, hz
            coef = [scale * v for v in conductivity(p)]
            for comp in range(3):
                beside = load(two_, other, comp, p)
                store(
                    one_, i, comp, p,
                    [e[comp][r] - RELAX * curl[comp][r] + coef[r] * beside[r] for r in range(turns)],
                )
            e = e_next
        add_point(one_, i, 0, depth)
        return 0

    def sensitivity(s, _):
        angular = angular_at(s)
        for p in range(depth):
            total = [[None] * turns, [None] * turns]
            for r in range(turns):
                row_re = row_im = jnp.zeros((8, breadth), F32)
                for comp in range(3):
                    re, im = one_[2 * s, comp, p + 1, r], one_[2 * s + 1, comp, p + 1, r]
                    field_re, field_im = field_ref[2 * s, comp, p, r], field_ref[2 * s + 1, comp, p, r]
                    row_re += field_re * re - field_im * im
                    row_im += field_re * im + field_im * re
                coef = angular * held_ref[p, r]
                total[0][r] = coef * row_re
                total[1][r] = coef * row_im
            for part in range(2):
                value = joined(total[part], rows_ref.dtype)
                rows_ref[s, part, p] = value
                if p >= depth - REACH:
                    up_ref[s, part, p - depth + REACH] = value
                if p < REACH:
                    down_ref[s, part, p] = value
        return 0

    lax.fori_loop(0, parts, join_slabs, 0)
    lax.fori_loop(0, parts, second_sweep, 0)
    lax.fori_loop(0, parts, third_sweep, 0)
    lax.fori_loop(0, count, sensitivity, 0)


def smooth_kernel(scale, scalar_ref, rows_ref, low_ref, high_ref, all_ref, smooth_ref, block_ref, lines):
    count, _, depth, height, breadth = rows_ref.shape
    ranks = all_ref.shape[0]
    turns = height // 8
    steps = Steps(breadth)
    first = scalar_ref[0].astype(jnp.int32)
    planes = scalar_ref[1].astype(jnp.int32)
    below = jnp.where(first > 0, F32(1.0), F32(0.0))
    above = jnp.where(first + depth < planes, F32(1.0), F32(0.0))
    many = ranks * count * 2

    def near(before, centre, after):
        total = add_(add_(before, after), add_(steps.after_y(centre), steps.before_y(centre)))
        total = add_(total, add_(steps.after_z(centre), steps.before_z(centre)))
        return [c + KAPPA * (t - 6.0 * c) for c, t in zip(centre, total)]

    sums = []
    for s in range(count):
        for part in range(2):
            value = [parted(low_ref[s, part, p], turns) for p in range(REACH)]
            value += [parted(rows_ref[s, part, p], turns) for p in range(depth)]
            value += [parted(high_ref[s, part, p], turns) for p in range(REACH)]
            once = [near(*value[i - 1 : i + 2]) for i in range(1, depth + 3)]
            once[0] = [v * below for v in once[0]]
            once[-1] = [v * above for v in once[-1]]
            twice = [near(*once[i - 1 : i + 2]) for i in range(1, depth + 1)]
            slot = 2 * s + part
            for p in range(depth):
                for r in range(turns):
                    lines[slot, p, pl.ds(r, 8, stride=turns), :] = twice[p][r]
                smooth_ref[s, part, p] = lines[slot, p].astype(smooth_ref.dtype)
            twice = [[v.astype(smooth_ref.dtype).astype(F32) for v in f] for f in twice]
            for r in range(ranks):
                for t in range(count):
                    for q in range(2):
                        total = None
                        for p in range(depth):
                            for prod in mul_(twice[p], parted(all_ref[r, t, q, p], turns)):
                                total = prod if total is None else total + prod
                        sums.append(total)
    ones = jnp.ones((breadth, breadth), F32)
    table = jnp.concatenate(sums, axis=0)
    table = jnp.dot(table, ones, precision=lax.Precision.HIGHEST, preferred_element_type=F32)
    for a in range(2 * count):
        line = jnp.zeros((8, breadth), F32)
        for b in range(many):
            at = (a * many + b) * 8
            line = line + jnp.where(steps.lane == b, table[at : at + 8], 0.0)
        line = jnp.sum(line, axis=0, keepdims=True) * scale
        for peer in range(block_ref.shape[0]):
            block_ref[peer, a : a + 1, :] = line[:, :many]


def shards(conductivity, background, warm_start, data_weight, recv_cell, src_group, group_freq):
    count = warm_start.shape[0]
    depth, height, breadth = conductivity.shape
    turns = height // 8
    peers = lax.axis_size("space")
    ranks = lax.axis_size("rx")
    cells = depth * height * breadth * peers
    half = jnp.bfloat16
    first = lax.axis_index("space") * depth
    place = jnp.stack([first, jnp.int32(peers * depth)])
    integers = jnp.concatenate([place, recv_cell, src_group, group_freq]).astype(F32)
    scalars = jnp.concatenate([integers, data_weight.reshape(-1)])
    rising = [(i, i + 1) for i in range(peers - 1)]
    falling = [(i + 1, i) for i in range(peers - 1)]
    shape = jax.ShapeDtypeStruct

    plane = (turns, 8, breadth)
    up, down, own, edge, held = pl.pallas_call(
        first_kernel,
        out_shape=(
            shape((2 * count * UP + 1, height, breadth), half),
            shape((2 * count * DOWN + 1, height, breadth), half),
            shape((2 * count, 3, depth) + plane, F32),
            shape((2 * count, 4) + plane, F32),
            shape((depth,) + plane, F32),
        ),
        in_specs=[HBM] * 6,
        out_specs=(FULL,) * 5,
        scratch_shapes=[
            pltpu.VMEM(warm_start.shape, F32),
            pltpu.VMEM(conductivity.shape, F32),
            pltpu.SMEM(data_weight.shape, F32),
            pltpu.SMEM(recv_cell.shape, jnp.int32),
            pltpu.SMEM(src_group.shape, jnp.int32),
            pltpu.SMEM(group_freq.shape, jnp.int32),
            pltpu.SemaphoreType.DMA((6,)),
        ],
        compiler_params=KERNEL,
        name="first_sweep",
    )(warm_start, conductivity, data_weight, recv_cell, src_group, group_freq)
    low = lax.ppermute(up, "space", rising)
    high = lax.ppermute(down, "space", falling)

    field = pl.pallas_call(
        functools.partial(stage_kernel, count, 2 + count),
        out_shape=shape((2 * count, 3, depth) + plane, F32),
        in_specs=[SCALARS, HBM],
        out_specs=FULL,
        scratch_shapes=[
            pltpu.VMEM((count,) + background.shape[1:], F32),
            pltpu.SemaphoreType.DMA((count,)),
        ],
        compiler_params=KERNEL,
        name="stage_field",
    )(scalars, background)

    rows_of = shape((count, 2, depth, height, breadth), half)
    ends_of = shape((count, 2, REACH, height, breadth), half)
    adjoint_scratch = pltpu.VMEM((2 * count, 3, depth + 2) + plane, F32)
    rows, up, down = pl.pallas_call(
        sweep_kernel,
        out_shape=(rows_of, ends_of, ends_of),
        in_specs=[SCALARS] + [FULL] * 6,
        out_specs=(FULL,) * 3,
        scratch_shapes=[adjoint_scratch, adjoint_scratch],
        compiler_params=KERNEL,
        name="sweeps",
    )(scalars, own, edge, held, field, low, high)
    low = lax.ppermute(up, "space", rising)
    high = lax.ppermute(down, "space", falling)
    every = lax.all_gather(rows, "rx", axis=0)

    many = 2 * count * ranks
    smoothed, partial_block = pl.pallas_call(
        functools.partial(smooth_kernel, 1.0 / cells),
        out_shape=(rows_of, shape((peers, 2 * count, many), F32)),
        in_specs=[SCALARS] + [FULL] * 4,
        out_specs=(FULL, FULL),
        scratch_shapes=[pltpu.VMEM((2 * count, depth, height, breadth), F32)],
        compiler_params=KERNEL,
        name="smooth",
    )(scalars, rows, low, high, every)
    pieces = lax.all_to_all(partial_block, "space", 0, 0)
    return (jnp.sum(pieces, axis=0), smoothed)


def solution(mesh):
    in_specs = (
        P("space", None, None),
        P(None, None, None, "space", None, None),
        P("rx", None, None, "space", None, None),
        P("rx", None, None),
        P("rx"),
        P("rx"),
        P(),
    )
    out_specs = (P("rx", None), P("rx", None, "space", None, None))
    return jax.shard_map(shards, mesh=mesh, in_specs=in_specs, out_specs=out_specs, check_vma=False)
```

time: 124 us -> 52.8 us (0.43)
  blocking collectives: 41.4 us -> 16.8 us
  waiting for transfers between devices: 30.8 us -> 9.29 us
  starting transfers between devices: 28.4 us -> 10.8 us
  other arithmetic: 15.5 us -> 0.69 us
  Pallas kernels: 0 us -> 6.78 us
  local copies, waits for them, and re-layouts: 5.66 us -> 7.3 us
    psum x1 -> x0, blocking collectives: 39.5 us -> none  [shards(): total = lax.psum(partial_block, 'space')]
    ppermute x10 -> x4, waiting for transfers between devices: 30.8 us -> 9.29 us  [the longest x2 9.28 us: shards(): high = lax.ppermute(down, 'space', falling)]
    ppermute x10 -> x4, starting transfers between devices: 28.4 us -> 10.8 us  [the longest x2 8.26 us: shards(): low = lax.ppermute(up, 'space', rising)]
    all_to_all x0 -> x1, blocking collectives: none -> 14.8 us  [shards(): pieces = lax.all_to_all(partial_block, 'space', 0, 0)]
    pallas_call x0 -> x4, Pallas kernels: none -> 6.78 us  [the longest x1 2.48 us: shards(): pl.pallas_call(sweep_kernel, out_shape=(rows_of, ends_of, ends_of), in_sp...]
    sub x31 -> x0, other arithmetic: 5.4 us -> none  [the longest x3 1.74 us: backward_z(): return jnp.concatenate([f[..., :1], f[..., 1:] - f[..., :-1]], axis=-1)]
    unnamed x36 -> x14, local copies, waits for them, and re-layouts: 1.55 us -> 5.77 us
    slice x18 -> x0, local copies, waits for them, and re-layouts: 3.3 us -> none  [the longest x9 1.85 us: backward_z(): return jnp.concatenate([f[..., :1], f[..., 1:] - f[..., :-1]], axis=-1)]
  transfers between devices with their start and end apart: 10 -> 4, of which waited for: 10 -> 2; matrix products, arithmetic and copies ran while one was open for 2% -> 3% of each run, Pallas kernels for 0% -> 1%
where the time goes in v1:
time: 52.8 us; the launch traced here: 52.4 us
  blocking collectives  16.8 us (32%)
  starting transfers between devices  10.8 us (20%)
  waiting for transfers between devices  9.29 us (18%)
  local copies, waits for them, and re-layouts  7.3 us (14%)
  Pallas kernels  6.78 us (13%)
  between operations  0.71 us (1%)
  other arithmetic  0.69 us (1%)
    all_to_all x1, blocking collectives, shards(): pieces = lax.all_to_all(partial_block, 'space', 0, 0)  14.8 us
    ppermute x2, waiting for transfers between devices, shards(): high = lax.ppermute(down, 'space', falling)  9.28 us
    ppermute x2, starting transfers between devices, shards(): low = lax.ppermute(up, 'space', rising)  8.26 us
    unnamed x14, local copies, waits for them, and re-layouts  5.77 us
    ppermute x2, starting transfers between devices, shards(): high = lax.ppermute(down, 'space', falling)  2.58 us
    pallas_call x1, Pallas kernels, shards(): pl.pallas_call(sweep_kernel, out_shape=(rows_of, ends_of, ends_of), in_sp...  2.48 us
    all_gather x1, blocking collectives, shards(): every = lax.all_gather(rows, 'rx', axis=0)  1.95 us
    pallas_call x1, Pallas kernels, shards(): pl.pallas_call(first_kernel, out_shape=(shape((2 * count * UP + 1, height...  1.89 us
  transfers between devices with their start and end apart: 4, of which 2 were waited for; matrix products, arithmetic and copies ran while one was open for 3% of the time, Pallas kernels for 1%

profile of v1, /device:TPU:0, one launch (start us, length us, event | category | flops | bytes accessed | tf_op | source)
XLA Modules:
  0.0 52.4 jit_solution(7625862845794460963)
XLA Ops:
  0.6 0.0 copy-start.1
  0.6 1.1 %copy-done.1 = f32[2,2,3,3,32,128]{5,4,3,2,1,0:T(8,128)S(1)} copy-done((f32[2,2,3,3,32,128]{5,4,3,2,1,0:T(8,128)S(1)}, f32[2,2,3,3,32,128]{5,4,3,2,1,0:T(8,128)}, u32[]{:S(2)}) %copy-start.1) | copy-done | bytes 589848
  1.7 0.0 copy-start.2
  1.7 0.8 %copy-done.2 = f32[3,32,128]{2,1,0:T(8,128)S(1)} copy-done((f32[3,32,128]{2,1,0:T(8,128)S(1)}, f32[3,32,128]{2,1,0:T(8,128)}, u32[]{:S(2)}) %copy-start.2) | copy-done | bytes 49176
  2.5 0.0 copy-start.3
  2.5 0.7 %copy-done.3 = f32[2,2,3]{2,1,0:T(2,128)S(1)} copy-done((f32[2,2,3]{2,1,0:T(2,128)S(1)}, f32[2,2,3]{2,1,0:T(2,128)}, u32[]{:S(2)}) %copy-start.3) | copy-done | bytes 72
  3.2 0.0 copy-start.4
  3.2 0.7 %copy-done.4 = s32[2]{0:T(128)S(1)} copy-done((s32[2]{0:T(128)S(1)}, s32[2]{0:T(128)}, u32[]{:S(2)}) %copy-start.4) | copy-done | bytes 32
  3.8 0.0 copy-start.5
  3.8 0.7 %copy-done.5 = s32[2]{0:T(128)S(1)} copy-done((s32[2]{0:T(128)S(1)}, s32[2]{0:T(128)}, u32[]{:S(2)}) %copy-start.5) | copy-done | bytes 32
  4.5 0.0 copy-start.6
  4.5 0.7 %copy-done.6 = s32[4]{0:T(128)S(1)} copy-done((s32[4]{0:T(128)S(1)}, s32[4]{0:T(128)}, u32[]{:S(2)}) %copy-start.6) | copy-done | bytes 40
  5.1 1.9 %first_sweep.1 = (bf16[29,32,128]{2,1,0:T(8,128)(2,1)S(1)}, bf16[25,32,128]{2,1,0:T(8,128)(2,1)S(1)}, f32[4,3,3,4,8,128]{5,4,3,2,1,0:T(8,128)S(1)}, f32[4,4,4,8,128]{4,3,2,1,0:T(8,128)S(1)}, f32[3,4,8,128]{3,2,1,0:T(8,128)S(1)}) custom-call(f32[2,2,3,3,32,128]{5,4,3,2,1,0:T(8,128)S(1)} %copy-done.1, f32[3,32,128]{2,1,0:T(8,128)S(1)} %copy-done.2, ...), custom_call_target="tpu_custom_call" | custom-call | tf_op jit(solution)/shard_map/first_sweep/pallas_call | solution.py:444
  7.0 4.9 %collective-permute-start = (bf16[29,32,128]{2,1,0:T(8,128)(2,1)S(1)}, bf16[29,32,128]{2,1,0:T(8,128)(2,1)S(1)}, u32[]{:S(2)}, u32[]{:S(2)}) collective-permute-start(bf16[29,32,128]{2,1,0:T(8,128)(2,1)S(1)} %get-tuple-element.15), channel_id=1, source_target_pairs={{0,1},{1,2},{2,3},{3,4},{4,5},{5,6},{6,7},{7,8},{8,9},{9,10},{10,1... | collective-permute-start | bytes 712712 | tf_op jit(solution)/shard_map/ppermute | solution.py:467
  11.9 1.3 %collective-permute-start.1 = (bf16[25,32,128]{2,1,0:T(8,128)(2,1)S(1)}, bf16[25,32,128]{2,1,0:T(8,128)(2,1)S(1)}, u32[]{:S(2)}, u32[]{:S(2)}) collective-permute-start(bf16[25,32,128]{2,1,0:T(8,128)(2,1)S(1)} %get-tuple-element.16), channel_id=1, source_target_pairs={{1,0},{2,1},{3,2},{4,3},{5,4},{6,5},{7,6},{8,7},{9,8},{10,9},{11,1... | collective-permute-start | bytes 614408 | tf_op jit(solution)/shard_map/ppermute | solution.py:468
  13.2 0.8 %reshape.7 = f32[12]{0:T(128)S(1)} reshape(f32[2,2,3]{2,1,0:T(2,128)} %weight_ref.1) | data formatting | bytes 96 | tf_op jit(solution)/shard_map/reshape | solution.py:438
  14.0 0.8 %concatenate.6 = s32[10]{0:T(128)S(1)} concatenate(s32[1]{0:T(128)} %bitcast, s32[1]{0:T(128)} %constant.2.clone.1, s32[2]{0:T(128)} %cell_ref.1, s32[2]{0:T(128)} %group_ref.1, s32[4]{0:T(128)} %freq_ref.1), dimensions={0} | concatenate | bytes 80 | tf_op jit(solution)/shard_map/concatenate | solution.py:437
  14.8 0.1 pad_maximum_fusion.scalar_ref
  14.8 0.0 copy-start
  14.8 1.3 %copy-done = f32[4,2,3,3,32,128]{5,4,3,2,1,0:T(8,128)S(1)} copy-done((f32[4,2,3,3,32,128]{5,4,3,2,1,0:T(8,128)S(1)}, f32[4,2,3,3,32,128]{5,4,3,2,1,0:T(8,128)}, u32[]{:S(2)}) %copy-start) | copy-done | bytes 1179672
  16.1 0.8 %stage_field.1.field_ref = f32[4,3,3,4,8,128]{5,4,3,2,1,0:T(8,128)S(1)} custom-call(f32[22]{0:T(128)S(1)} %pad_maximum_fusion.scalar_ref, f32[4,2,3,3,32,128]{5,4,3,2,1,0:T(8,128)S(1)} %copy-done), custom_call_target="tpu_custom_call" | custom-call | tf_op jit(solution)/shard_map/stage_field/pallas_call | solution.py:470
  16.9 6.4 %collective-permute-done.1.high_ref = bf16[25,32,128]{2,1,0:T(8,128)(2,1)S(1)} collective-permute-done((bf16[25,32,128]{2,1,0:T(8,128)(2,1)S(1)}, bf16[25,32,128]{2,1,0:T(8,128)(2,1)S(1)}, u32[]{:S(2)}, u32[]{:S(2)}) %collective-permute-start.1) | collective-permute-done | bytes 204832 | tf_op jit(solution)/shard_map/ppermute | solution.py:468
  23.3 0.0 collective-permute-done.low_ref
  23.3 2.5 %sweeps.1 = (bf16[2,2,3,32,128]{4,3,2,1,0:T(8,128)(2,1)S(1)}, bf16[2,2,2,32,128]{4,3,2,1,0:T(8,128)(2,1)S(1)}, bf16[2,2,2,32,128]{4,3,2,1,0:T(8,128)(2,1)S(1)}) custom-call(f32[22]{0:T(128)S(1)} %pad_maximum_fusion.scalar_ref, f32[4,3,3,4,8,128]{5,4,3,2,1,0:T(8,128)S(1)} %get-tuple-element.12.own_ref, f32[4,4,4,8,128]{4,3,2,1,0:T(8,128)S(1)} %get-tuple-element.13.edge_ref, ...), custom_call_target="tpu_custom_call" | custom-call | tf_op jit(solution)/shard_map/sweeps/pallas_call | solution.py:486
  25.7 3.4 %collective-permute-start.2 = (bf16[2,2,2,32,128]{4,3,2,1,0:T(8,128)(2,1)S(1)}, bf16[2,2,2,32,128]{4,3,2,1,0:T(8,128)(2,1)S(1)}, u32[]{:S(2)}, u32[]{:S(2)}) collective-permute-start(bf16[2,2,2,32,128]{4,3,2,1,0:T(8,128)(2,1)S(1)} %get-tuple-element.18), channel_id=1, source_target_pairs={{0,1},{1,2},{2,3},{3,4},{4,5},{5,6},{6,7},{7,8},{8,9},{9,10},{10,1... | collective-permute-start | bytes 196616 | tf_op jit(solution)/shard_map/ppermute | solution.py:495
  29.2 1.3 %collective-permute-start.3 = (bf16[2,2,2,32,128]{4,3,2,1,0:T(8,128)(2,1)S(1)}, bf16[2,2,2,32,128]{4,3,2,1,0:T(8,128)(2,1)S(1)}, u32[]{:S(2)}, u32[]{:S(2)}) collective-permute-start(bf16[2,2,2,32,128]{4,3,2,1,0:T(8,128)(2,1)S(1)} %get-tuple-element.19), channel_id=1, source_target_pairs={{1,0},{2,1},{3,2},{4,3},{5,4},{6,5},{7,6},{8,7},{9,8},{10,9},{11,1... | collective-permute-start | bytes 196616 | tf_op jit(solution)/shard_map/ppermute | solution.py:496
  30.5 1.9 %all-gather = bf16[4,2,3,32,128]{4,3,2,1,0:T(8,128)(2,1)S(1)} all-gather(bf16[2,2,3,32,128]{4,3,2,1,0:T(8,128)(2,1)S(1)} %get-tuple-element.17.rows_ref), channel_id=2, replica_groups=mesh['rx'=2,'space'=16] {'rx'}, dimensions={0}, use_global_device_ids=true | all-gather | bytes 294912 | tf_op jit(solution)/shard_map/all_gather | solution.py:497
  32.4 0.0 collective-permute-done.2.low_ref
  32.4 2.9 %collective-permute-done.3.high_ref = bf16[2,2,2,32,128]{4,3,2,1,0:T(8,128)(2,1)S(1)} collective-permute-done((bf16[2,2,2,32,128]{4,3,2,1,0:T(8,128)(2,1)S(1)}, bf16[2,2,2,32,128]{4,3,2,1,0:T(8,128)(2,1)S(1)}, u32[]{:S(2)}, u32[]{:S(2)}) %collective-permute-start.3) | collective-permute-done | bytes 65568 | tf_op jit(solution)/shard_map/ppermute | solution.py:496
  35.3 1.6 %smooth.1 = (bf16[2,2,3,32,128]{4,3,2,1,0:T(8,128)(2,1)}, f32[16,4,8]{2,1,0:T(4,128)S(1)}) custom-call(f32[22]{0:T(128)S(1)} %pad_maximum_fusion.scalar_ref, bf16[2,2,3,32,128]{4,3,2,1,0:T(8,128)(2,1)S(1)} %get-tuple-element.17.rows_ref, bf16[2,2,2,32,128]{4,3,2,1,0:T(8,128)(2,1)S(1)} %collective-permute-done.2.low_ref, ...), custom_call_target="tpu_custom_call" | custom-call | tf_op jit(solution)/shard_map/smooth/pallas_call | solution.py:500
  36.9 14.8 %all_to_all.5 = f32[16,4,8]{2,1,0:T(4,128)S(1)} all-to-all(f32[16,4,8]{2,1,0:T(4,128)S(1)} %get-tuple-element.20), channel_id=1, replica_groups=mesh['rx'=2,'space'=16] {'space'}, dimensions={0} | all-to-all | bytes 4096 | tf_op jit(solution)/shard_map/all_to_all | solution.py:509
  51.8 0.6 %reduce_sum.9 = f32[4,8]{1,0:T(4,128)} reduce(f32[16,4,8]{2,1,0:T(4,128)S(1)} %all_to_all.5, f32[]{:T(128)} %constant.3.clone.1), dimensions={0}, to_apply=%region_0.0 | reduce | flops 480 | bytes 2180 | tf_op jit(solution)/shard_map/reduce_sum | solution.py:510
  (1 shorter events, 0.0 us)
Async XLA Ops:
  0.6 1.1 %copy-start.1 = (f32[2,2,3,3,32,128]{5,4,3,2,1,0:T(8,128)S(1)}, f32[2,2,3,3,32,128]{5,4,3,2,1,0:T(8,128)}, u32[]{:S(2)}) copy-start(f32[2,2,3,3,32,128]{5,4,3,2,1,0:T(8,128)} %start_ref.1) | copy-start | bytes 1769476
  1.7 0.8 %copy-start.2 = (f32[3,32,128]{2,1,0:T(8,128)S(1)}, f32[3,32,128]{2,1,0:T(8,128)}, u32[]{:S(2)}) copy-start(f32[3,32,128]{2,1,0:T(8,128)} %cond_ref.1) | copy-start | bytes 147460
  2.5 0.7 %copy-start.3 = (f32[2,2,3]{2,1,0:T(2,128)S(1)}, f32[2,2,3]{2,1,0:T(2,128)}, u32[]{:S(2)}) copy-start(f32[2,2,3]{2,1,0:T(2,128)} %weight_ref.1) | copy-start | bytes 148
  3.2 0.7 %copy-start.4 = (s32[2]{0:T(128)S(1)}, s32[2]{0:T(128)}, u32[]{:S(2)}) copy-start(s32[2]{0:T(128)} %cell_ref.1) | copy-start | bytes 28
  3.8 0.7 %copy-start.5 = (s32[2]{0:T(128)S(1)}, s32[2]{0:T(128)}, u32[]{:S(2)}) copy-start(s32[2]{0:T(128)} %group_ref.1) | copy-start | bytes 28
  4.5 0.7 %copy-start.6 = (s32[4]{0:T(128)S(1)}, s32[4]{0:T(128)}, u32[]{:S(2)}) copy-start(s32[4]{0:T(128)} %freq_ref.1) | copy-start | bytes 52
  7.0 16.2 %collective-permute-start = (bf16[29,32,128]{2,1,0:T(8,128)(2,1)S(1)}, bf16[29,32,128]{2,1,0:T(8,128)(2,1)S(1)}, u32[]{:S(2)}, u32[]{:S(2)}) collective-permute-start(bf16[29,32,128]{2,1,0:T(8,128)(2,1)S(1)} %get-tuple-element.15), channel_id=1, source_target_pairs={{0,1},{1,2},{2,3},{3,4},{4,5},{5,6},{6,7},{7,8},{8,9},{9,10},{10,1... | collective-permute-start | bytes 712712 | tf_op jit(solution)/shard_map/ppermute | solution.py:467
  11.9 11.3 %collective-permute-start.1 = (bf16[25,32,128]{2,1,0:T(8,128)(2,1)S(1)}, bf16[25,32,128]{2,1,0:T(8,128)(2,1)S(1)}, u32[]{:S(2)}, u32[]{:S(2)}) collective-permute-start(bf16[25,32,128]{2,1,0:T(8,128)(2,1)S(1)} %get-tuple-element.16), channel_id=1, source_target_pairs={{1,0},{2,1},{3,2},{4,3},{5,4},{6,5},{7,6},{8,7},{9,8},{10,9},{11,1... | collective-permute-start | bytes 614408 | tf_op jit(solution)/shard_map/ppermute | solution.py:468
  14.8 1.3 %copy-start = (f32[4,2,3,3,32,128]{5,4,3,2,1,0:T(8,128)S(1)}, f32[4,2,3,3,32,128]{5,4,3,2,1,0:T(8,128)}, u32[]{:S(2)}) copy-start(f32[4,2,3,3,32,128]{5,4,3,2,1,0:T(8,128)} %field_ref.1) | copy-start | bytes 3538948
  25.7 6.7 %collective-permute-start.2 = (bf16[2,2,2,32,128]{4,3,2,1,0:T(8,128)(2,1)S(1)}, bf16[2,2,2,32,128]{4,3,2,1,0:T(8,128)(2,1)S(1)}, u32[]{:S(2)}, u32[]{:S(2)}) collective-permute-start(bf16[2,2,2,32,128]{4,3,2,1,0:T(8,128)(2,1)S(1)} %get-tuple-element.18), channel_id=1, source_target_pairs={{0,1},{1,2},{2,3},{3,4},{4,5},{5,6},{6,7},{7,8},{8,9},{9,10},{10,1... | collective-permute-start | bytes 196616 | tf_op jit(solution)/shard_map/ppermute | solution.py:495
  29.2 6.2 %collective-permute-start.3 = (bf16[2,2,2,32,128]{4,3,2,1,0:T(8,128)(2,1)S(1)}, bf16[2,2,2,32,128]{4,3,2,1,0:T(8,128)(2,1)S(1)}, u32[]{:S(2)}, u32[]{:S(2)}) collective-permute-start(bf16[2,2,2,32,128]{4,3,2,1,0:T(8,128)(2,1)S(1)} %get-tuple-element.19), channel_id=1, source_target_pairs={{1,0},{2,1},{3,2},{4,3},{5,4},{6,5},{7,6},{8,7},{9,8},{10,9},{11,1... | collective-permute-start | bytes 196616 | tf_op jit(solution)/shard_map/ppermute | solution.py:496

commit v2 on v0

v2 whole, which is shorter than its diff:
```python
import functools

import jax
import jax.numpy as jnp
from jax import lax
from jax.experimental import pallas as pl
from jax.experimental.pallas import tpu as pltpu
from jax.sharding import PartitionSpec as P

SENT = 6
RELAX = 0.2
KAPPA = 0.1
REACH = 2
FULL = pl.BlockSpec(memory_space=pltpu.VMEM)
HBM = pl.BlockSpec(memory_space=pltpu.HBM)
SCALARS = pl.BlockSpec(memory_space=pltpu.SMEM)
KERNEL = pltpu.CompilerParams(vmem_limit_bytes=8 * 2**20)
F32 = jnp.float32


class Steps:
    def __init__(self, height, breadth):
        self.height, self.breadth = height, breadth
        self.sub = lax.broadcasted_iota(jnp.int32, (8, breadth), 0)
        self.lane = lax.broadcasted_iota(jnp.int32, (height, breadth), 1)

    def after_y(self, f):
        f = pltpu.roll(f, self.height - 1, 0)
        return jnp.concatenate([f[:-8], jnp.where(self.sub < 7, f[-8:], 0.0)], axis=0)

    def before_y(self, f):
        f = pltpu.roll(f, 1, 0)
        return jnp.concatenate([jnp.where(self.sub > 0, f[:8], 0.0), f[8:]], axis=0)

    def after_z(self, f):
        return jnp.where(self.lane < self.breadth - 1, pltpu.roll(f, self.breadth - 1, 1), 0.0)

    def before_z(self, f):
        return jnp.where(self.lane > 0, pltpu.roll(f, 1, 1), 0.0)

    def up_y(self, f):
        return self.after_y(f) - f

    def up_z(self, f):
        return self.after_z(f) - f

    def down_y(self, f):
        return f - self.before_y(f)

    def down_z(self, f):
        return f - self.before_z(f)

    def magnetic_yz(self, e, e_next):
        ex, ey, ez = e
        if e_next is None:
            return self.up_z(ex) + ez, -ey - self.up_y(ex)
        return self.up_z(ex) - (e_next[2] - ez), (e_next[1] - ey) - self.up_y(ex)

    def magnetic_x(self, e):
        return self.up_y(e[2]) - self.up_z(e[1])

    def curl_back(self, comp, hx, hy, hz, before):
        if comp == 0:
            return self.down_y(hz) - self.down_z(hy)
        if comp == 1:
            return self.down_z(hx) - (hz - before[1])
        return (hy - before[0]) - self.down_y(hx)


def angular_of(freq):
    angular = F32(0.25)
    for bit, factor in ((1, 1.25), (2, 1.25**2), (4, 1.25**4)):
        angular = angular * jnp.where((freq & bit) != 0, F32(factor), F32(1.0))
    return angular


def split(number, size):
    if size & (size - 1):
        return number // size, number % size
    return number >> (size.bit_length() - 1), number & (size - 1)


class Point:
    def __init__(self, cell, first, steps):
        plane, inner = split(cell, steps.height * steps.breadth)
        row, lane = split(inner, steps.breadth)
        block, sub = split(row, 8)
        self.plane = plane - first
        self.rows = pl.ds(pl.multiple_of(block * 8, 8), 8)
        self.row, self.sub, self.lane, self.steps = row, sub, lane, steps

    def spread(self, value):
        here = (self.steps.sub == self.sub) & (self.steps.lane[:8] == self.lane)
        return jnp.where(here, RELAX * value, 0.0)

    def add_to(self, ref, low, high, shift, weight):
        @pl.when((self.plane >= low) & (self.plane < high))
        def _():
            for part in range(2):
                for comp in range(3):
                    at = (part, comp, self.plane + shift, self.rows)
                    ref[at] = ref[at] + self.spread(weight(part, comp))


def first_kernel(s, *refs):
    if s == 0:
        start_ref, cond_ref, weight_ref, cell_ref, group_ref, freq_ref = refs[:6]
        far_ref, near_ref, own_ref, edge_ref, held_ref, later_ref = refs[6:12]
        raw, weight, cell, group, freq, sent, sems = refs[12:]
        pairs = [
            (cell_ref, cell), (group_ref, group), (freq_ref, freq), (weight_ref, weight),
            (start_ref.at[0], raw), (cond_ref, held_ref), (start_ref.at[pl.ds(1, later_ref.shape[0])], later_ref),
        ]
    else:
        later_ref, held_ref, weight_ref, cell_ref, group_ref, freq_ref = refs[:6]
        far_ref, near_ref, own_ref, edge_ref = refs[6:10]
        weight, cell, group, freq, sent, sems = refs[10:]
        raw = later_ref.at[s - 1]
        pairs = [(cell_ref, cell), (group_ref, group), (freq_ref, freq), (weight_ref, weight)]
    depth, height, breadth = held_ref.shape
    copies = [pltpu.make_async_copy(a, b, sems.at[k]) for k, (a, b) in enumerate(pairs)]
    for copy in copies:
        copy.start()
    for copy in copies[:6]:
        copy.wait()
    steps = Steps(height, breadth)
    half = far_ref.dtype
    index = lax.axis_index("space")
    first = index * depth
    down = index & 1
    up = 1 - down
    scale = RELAX * angular_of(freq[group[s]])
    scales = scale, -scale
    point = Point(cell[s], first, steps)
    if s == 0:
        sent[up, 2 * SENT] = held_ref[depth - 1].astype(half)
        sent[down, 2 * SENT] = held_ref[0].astype(half)

    before = []
    for part in range(2):
        ey, ez = raw[part, 1, 0], raw[part, 2, 0]
        for k, f in enumerate((ey, ez)):
            sent[down, part * SENT + k] = f.astype(half)
            edge_ref[part, k] = f
        before.append((-ez, ey))
    for p in range(depth):
        for part in range(2):
            e = [raw[part, comp, p] for comp in range(3)]
            e_next = [None if comp == 0 else raw[part, comp, p + 1] for comp in range(3)] if p < depth - 1 else None
            hy, hz = steps.magnetic_yz(e, e_next)
            if e_next is None:
                for k, f in enumerate((hy, hz)):
                    sent[up, part * SENT + k] = f.astype(half)
                    edge_ref[part, 2 + k] = f
            hx = steps.magnetic_x(e)
            coef = scales[part] * held_ref[p]
            for comp in range(3):
                curl = steps.curl_back(comp, hx, hy, hz, before[part])
                own_ref[part, comp, p] = e[comp] - RELAX * curl + coef * raw[1 - part, comp, p]
            before[part] = hy, hz
    point.add_to(own_ref, 0, depth, 0, lambda part, comp: weight[s, part, comp])

    last = depth - 1
    at_last = jnp.where(point.plane == last, F32(1.0), F32(0.0))
    row = lax.broadcasted_iota(jnp.int32, (height, breadth), 0)
    here = jnp.where((row == point.row) & (steps.lane == point.lane), RELAX * at_last, 0.0)
    for part in range(2):
        ex, ey, ez = [own_ref[part, comp, 0] for comp in range(3)]
        hy, hz = steps.up_z(ex) - own_ref[part, 2, 1], own_ref[part, 1, 1] - steps.up_y(ex)
        for k, f in enumerate((ey, ez, hy, hz)):
            sent[down, part * SENT + 2 + k] = f.astype(half)
        e = [own_ref[part, comp, last] for comp in range(3)]
        behind = steps.magnetic_yz([own_ref[part, comp, last - 1] for comp in range(3)], e)
        hy, hz = steps.magnetic_yz(e, None)
        hx = steps.magnetic_x(e)
        coef = scales[part] * held_ref[last]
        after = []
        for comp in range(3):
            curl = steps.curl_back(comp, hx, hy, hz, behind)
            value = e[comp] - RELAX * curl + coef * own_ref[1 - part, comp, last]
            after.append(value + here * weight[s, part, comp])
        for k, f in enumerate((hy, hz) + steps.magnetic_yz(after, None)):
            sent[up, part * SENT + 2 + k] = f.astype(half)
    far_ref[...] = sent[0]
    near_ref[...] = sent[1]
    for copy in copies[6:]:
        copy.wait()


def stage_kernel(count, groups_at, scalar_ref, field_ref, out_ref, sems):
    copies = []
    for s in range(count):
        group = scalar_ref[groups_at + s].astype(jnp.int32)
        copies.append(pltpu.make_async_copy(field_ref.at[group], out_ref.at[s], sems.at[s]))
        copies[-1].start()
    for copy in copies:
        copy.wait()


def sweep_kernel(s, count, *refs):
    last = s == count - 1
    if last:
        scalar_ref, own_ref, edge_ref, held_ref, field_ref, far_in, near_in, far_cond, near_cond = refs[:9]
        earlier = refs[9 : 9 + s]
        rows_ref, far_ref, near_ref, one_, two_, got, conds, sent = refs[9 + s :]
    else:
        scalar_ref, own_ref, edge_ref, held_ref, field_ref, far_in, near_in, far_cond, near_cond = refs[:9]
        rows_ref, one_, two_, got, conds = refs[9:]
    depth, height, breadth = held_ref.shape
    steps = Steps(height, breadth)
    first = scalar_ref[0].astype(jnp.int32)
    planes = scalar_ref[1].astype(jnp.int32)
    relax_low = jnp.where(first > 0, F32(RELAX), F32(0.0))
    relax_high = jnp.where(first + depth < planes, F32(RELAX), F32(0.0))
    group = scalar_ref[2 + count + s].astype(jnp.int32)
    angular = angular_of(scalar_ref[2 + 2 * count + group].astype(jnp.int32))
    scales = RELAX * angular, -RELAX * angular
    point = Point(scalar_ref[2 + s].astype(jnp.int32), first, steps)
    weights_at = scalar_ref.shape[0] - 6 * count + 6 * s
    odd = lax.axis_index("space") & 1
    low, high = odd, 1 - odd
    got[0] = far_in[...]
    got[1] = near_in[...]
    conds[0] = far_cond[2 * SENT]
    conds[1] = near_cond[2 * SENT]

    def received(side, part, k):
        return got[side, part * SENT + k].astype(F32)

    def conductivity(p):
        if p < 0:
            return conds[low].astype(F32)
        if p >= depth:
            return conds[high].astype(F32)
        return held_ref[p]

    def weight(part, comp):
        return scalar_ref[weights_at + part * 3 + comp]

    for part in range(2):
        ey, ez, ly, lz = [edge_ref[part, k] for k in range(4)]
        one_[part, 0, 0] = -relax_low * (steps.down_y(ey) + steps.down_z(ez))
        one_[part, 1, 0] = relax_low * ey
        one_[part, 2, 0] = relax_low * ez
        e = [own_ref[part, comp, 0] for comp in range(3)]
        one_[part, 0, 1] = e[0]
        one_[part, 1, 1] = e[1] - RELAX * received(low, part, 1)
        one_[part, 2, 1] = e[2] + RELAX * received(low, part, 0)
        for p in range(1, depth - 1):
            for comp in range(3):
                one_[part, comp, p + 1] = own_ref[part, comp, p]
        e = [own_ref[part, comp, depth - 1] for comp in range(3)]
        high_y, high_z = received(high, part, 0), received(high, part, 1)
        one_[part, 0, depth] = e[0] - RELAX * (steps.down_y(high_y) + steps.down_z(high_z))
        one_[part, 1, depth] = e[1] + RELAX * high_y
        one_[part, 2, depth] = e[2] + RELAX * high_z
        one_[part, 1, depth + 1] = received(high, part, 2) - relax_high * lz
        one_[part, 2, depth + 1] = received(high, part, 3) + relax_high * ly

    before = [(-one_[part, 2, 0], one_[part, 1, 0]) for part in range(2)]
    for p in range(-1, depth + 1):
        relax = relax_low if p < 0 else relax_high if p == depth else F32(RELAX)
        for part in range(2):
            e = [one_[part, comp, p + 1] if comp or p < depth else None for comp in range(3)]
            if p < depth:
                e_next = [None if comp == 0 else one_[part, comp, p + 2] for comp in range(3)]
                hy, hz = steps.magnetic_yz(e, e_next)
            else:
                hy, hz = received(high, part, 4) + e[2], received(high, part, 5) - e[1]
            hx = steps.magnetic_x(e)
            coef = scales[part] * conductivity(p)
            for comp in range(1 if p == depth else 0, 3):
                curl = steps.curl_back(comp, hx, hy, hz, before[part])
                two_[part, comp, p + 1] = e[comp] - relax * curl + coef * one_[1 - part, comp, p + 1]
            if p < 0:
                hy, hz = hy + received(low, part, 2), hz + received(low, part, 3)
            before[part] = hy, hz
    point.add_to(two_, 0, depth + 1, 1, weight)

    before = []
    for part in range(2):
        e = [two_[part, comp, 0] for comp in range(3)]
        hy, hz = steps.magnetic_yz(e, [None, two_[part, 1, 1], two_[part, 2, 1]])
        before.append((hy + received(low, part, 4), hz + received(low, part, 5)))
    for p in range(depth):
        for part in range(2):
            e = [two_[part, comp, p + 1] for comp in range(3)]
            hy, hz = steps.magnetic_yz(e, [None, two_[part, 1, p + 2], two_[part, 2, p + 2]])
            hx = steps.magnetic_x(e)
            coef = scales[part] * conductivity(p)
            for comp in range(3):
                curl = steps.curl_back(comp, hx, hy, hz, before[part])
                one_[part, comp, p + 1] = e[comp] - RELAX * curl + coef * two_[1 - part, comp, p + 1]
            before[part] = hy, hz
    point.add_to(one_, 0, depth, 1, weight)

    for p in range(depth):
        row_re = row_im = None
        for comp in range(3):
            re, im = one_[0, comp, p + 1], one_[1, comp, p + 1]
            field_re, field_im = field_ref[s, 0, comp, p], field_ref[s, 1, comp, p]
            add_re, add_im = field_re * re - field_im * im, field_re * im + field_im * re
            row_re, row_im = (add_re, add_im) if comp == 0 else (row_re + add_re, row_im + add_im)
        coef = angular * held_ref[p]
        for part, value in enumerate((row_re, row_im)):
            value = (coef * value).astype(rows_ref.dtype)
            if not last:
                rows_ref[part, p] = value
                continue
            rows_ref[s, part, p] = value
            if p >= depth - REACH:
                sent[high, s, part, p - depth + REACH] = value
            if p < REACH:
                sent[low, s, part, p] = value
    if last:
        for t, ref in enumerate(earlier):
            rows_ref[t] = ref[...]
            sent[high, t] = ref[:, depth - REACH :]
            sent[low, t] = ref[:, :REACH]
        far_ref[...] = sent[0]
        near_ref[...] = sent[1]


def smooth_kernel(scale, scalar_ref, rows_ref, far_in, near_in, all_ref, smooth_ref, block_ref, got):
    count, _, depth, height, breadth = rows_ref.shape
    ranks = all_ref.shape[0]
    steps = Steps(height, breadth)
    first = scalar_ref[0].astype(jnp.int32)
    planes = scalar_ref[1].astype(jnp.int32)
    below = jnp.where(first > 0, F32(1.0), F32(0.0))
    above = jnp.where(first + depth < planes, F32(1.0), F32(0.0))
    many = ranks * count * 2
    got[0] = far_in[...]
    got[1] = near_in[...]
    odd = lax.axis_index("space") & 1
    low, high = odd, 1 - odd

    def near(before, centre, after):
        total = (before + after) + (steps.after_y(centre) + steps.before_y(centre))
        total = total + (steps.after_z(centre) + steps.before_z(centre))
        return (1.0 - 6.0 * KAPPA) * centre + KAPPA * total

    for s in range(count):
        for part in range(2):
            value = [got[low, s, part, p].astype(F32) for p in range(REACH)]
            value += [rows_ref[s, part, p].astype(F32) for p in range(depth)]
            value += [got[high, s, part, p].astype(F32) for p in range(REACH)]
            once = [near(*value[i - 1 : i + 2]) for i in range(1, depth + 3)]
            once[0] = once[0] * below
            once[-1] = once[-1] * above
            for p in range(depth):
                smooth_ref[s, part, p] = near(*once[p : p + 3]).astype(smooth_ref.dtype)

    sums = [[None] * many for _ in range(2 * count)]
    for p in range(depth):
        for k in range(0, height, 16):
            mine = [smooth_ref[a // 2, a % 2, p, k : k + 16].astype(F32) for a in range(2 * count)]
            for b in range(many):
                r, t = divmod(b // 2, count)
                other = all_ref[r, t, b % 2, p, k : k + 16].astype(F32)
                for a in range(2 * count):
                    prod = mine[a] * other
                    prod = prod[:8] + prod[8:]
                    sums[a][b] = prod if sums[a][b] is None else sums[a][b] + prod
    ones = jnp.ones((breadth, breadth), F32)
    table = jnp.concatenate([v for line in sums for v in line], axis=0)
    table = jnp.dot(table, ones, precision=lax.Precision.HIGHEST, preferred_element_type=F32)
    for a in range(2 * count):
        line = None
        for b in range(many):
            at = (a * many + b) * 8
            add = jnp.where(steps.lane[:8] == b, table[at : at + 8], 0.0)
            line = add if line is None else line + add
        line = jnp.sum(line, axis=0, keepdims=True) * scale
        for peer in range(block_ref.shape[0]):
            block_ref[peer, a : a + 1, :] = line[:, :many]


def in_hbm(x):
    return pltpu.with_memory_space_constraint(x, pltpu.HBM)


def shards(conductivity, background, warm_start, data_weight, recv_cell, src_group, group_freq):
    count = warm_start.shape[0]
    depth, height, breadth = conductivity.shape
    plane = (height, breadth)
    peers = lax.axis_size("space")
    ranks = lax.axis_size("rx")
    cells = depth * height * breadth * peers
    half = jnp.bfloat16
    first = lax.axis_index("space") * depth
    place = jnp.stack([first, jnp.int32(peers * depth)])
    integers = jnp.concatenate([place, recv_cell, src_group, group_freq]).astype(F32)
    scalars = jnp.concatenate([integers, data_weight.reshape(-1)])
    far = [(i, i + 1) for i in range(1, peers - 1, 2)]
    near = [(i, i + 1) for i in range(0, peers - 1, 2)]
    far, near = [pairs + [(j, i) for i, j in pairs] for pairs in (far, near)]
    shape = jax.ShapeDtypeStruct
    small = [in_hbm(x) for x in (data_weight, recv_cell, src_group, group_freq)]
    small_scratch = [
        pltpu.SMEM(data_weight.shape, F32),
        pltpu.SMEM(recv_cell.shape, jnp.int32),
        pltpu.SMEM(src_group.shape, jnp.int32),
        pltpu.SMEM(group_freq.shape, jnp.int32),
    ]

    own, edges, fars, nears = [], [], [], []
    for s in range(count):
        message = shape((2 * SENT + (s == 0),) + plane, half)
        outs = [message, message, shape((2, 3, depth) + plane, F32), shape((2, 4) + plane, F32)]
        scratch = small_scratch + [pltpu.VMEM((2,) + message.shape, half), pltpu.SemaphoreType.DMA((7,))]
        if s == 0:
            operands = [in_hbm(warm_start), in_hbm(conductivity)] + small
            specs = [HBM] * 6
            outs += [shape(conductivity.shape, F32), shape((count - 1,) + warm_start.shape[1:], F32)]
            scratch = [pltpu.VMEM(warm_start.shape[1:], F32)] + scratch
        else:
            operands = [later, held] + small
            specs = [FULL] * 2 + [HBM] * 4
        result = pl.pallas_call(
            functools.partial(first_kernel, s),
            out_shape=tuple(outs),
            in_specs=specs,
            out_specs=(FULL,) * len(outs),
            scratch_shapes=scratch,
            compiler_params=KERNEL,
            name="first_sweep",
        )(*operands)
        if s == 0:
            held, later = result[4:]
        own.append(result[2])
        edges.append(result[3])
        fars.append(lax.ppermute(result[0], "space", far))
        nears.append(lax.ppermute(result[1], "space", near))

    field = pl.pallas_call(
        functools.partial(stage_kernel, count, 2 + count),
        out_shape=shape((count,) + background.shape[1:], F32),
        in_specs=[SCALARS, HBM],
        out_specs=FULL,
        scratch_shapes=[pltpu.SemaphoreType.DMA((count,))],
        compiler_params=KERNEL,
        name="stage_field",
    )(scalars, in_hbm(background))

    rows_of = shape((count, 2, depth) + plane, half)
    ends_of = shape((count, 2, REACH) + plane, half)
    adjoint_scratch = pltpu.VMEM((2, 3, depth + 2) + plane, F32)
    earlier = []
    for s in range(count):
        last = s == count - 1
        operands = [scalars, own[s], edges[s], held, field, fars[s], nears[s], fars[0], nears[0]]
        scratch = [
            adjoint_scratch,
            adjoint_scratch,
            pltpu.VMEM((2,) + fars[s].shape, half),
            pltpu.VMEM((2,) + plane, half),
        ]
        if last:
            operands += earlier
            outs = (rows_of, ends_of, ends_of)
            scratch.append(pltpu.VMEM((2,) + ends_of.shape, half))
        else:
            outs = (shape((2, depth) + plane, half),)
        result = pl.pallas_call(
            functools.partial(sweep_kernel, s, count),
            out_shape=outs,
            in_specs=[SCALARS] + [FULL] * (len(operands) - 1),
            out_specs=(FULL,) * len(outs),
            scratch_shapes=scratch,
            compiler_params=KERNEL,
            name="sweeps",
        )(*operands)
        earlier.append(result[0])
    rows, to_far, to_near = result
    from_far = lax.ppermute(to_far, "space", far)
    from_near = lax.ppermute(to_near, "space", near)
    every = lax.all_gather(rows, "rx", axis=0)

    many = 2 * count * ranks
    smoothed, partial_block = pl.pallas_call(
        functools.partial(smooth_kernel, 1.0 / cells),
        out_shape=(rows_of, shape((peers, 2 * count, many), F32)),
        in_specs=[SCALARS] + [FULL] * 4,
        out_specs=(FULL, FULL),
        scratch_shapes=[pltpu.VMEM((2,) + ends_of.shape, half)],
        compiler_params=KERNEL,
        name="smooth",
    )(scalars, rows, from_far, from_near, every)
    pieces = lax.all_to_all(partial_block, "space", 0, 0)
    return (jnp.sum(pieces, axis=0), smoothed)


def solution(mesh):
    in_specs = (
        P("space", None, None),
        P(None, None, None, "space", None, None),
        P("rx", None, None, "space", None, None),
        P("rx", None, None),
        P("rx"),
        P("rx"),
        P(),
    )
    out_specs = (P("rx", None), P("rx", None, "space", None, None))
    return jax.shard_map(shards, mesh=mesh, in_specs=in_specs, out_specs=out_specs, check_vma=False)
```

time: 124 us -> 43.1 us (0.35)
  waiting for transfers between devices: 30.8 us -> 0.93 us
  blocking collectives: 41.4 us -> 14.3 us
  other arithmetic: 15.5 us -> 0.69 us
  starting transfers between devices: 28.4 us -> 16.3 us
  Pallas kernels: 0 us -> 8.29 us
  local copies, waits for them, and re-layouts: 5.66 us -> 1.53 us
    psum x1 -> x0, blocking collectives: 39.5 us -> none  [shards(): total = lax.psum(partial_block, 'space')]
    ppermute x10 -> x6, waiting for transfers between devices: 30.8 us -> 0.93 us  [the longest x1 0.92 us: shards(): from_near = lax.ppermute(to_near, 'space', near)]
    all_to_all x0 -> x1, blocking collectives: none -> 12.4 us  [shards(): pieces = lax.all_to_all(partial_block, 'space', 0, 0)]
    ppermute x10 -> x6, starting transfers between devices: 28.4 us -> 16.3 us  [the longest x2 10 us: shards(): nears.append(lax.ppermute(result[1], 'space', near))]
    pallas_call x0 -> x6, Pallas kernels: none -> 8.29 us  [the longest x2 2.69 us: shards(): pl.pallas_call(functools.partial(first_kernel, s), out_shape=tuple(outs),...]
    sub x31 -> x0, other arithmetic: 5.4 us -> none  [the longest x3 1.74 us: backward_z(): return jnp.concatenate([f[..., :1], f[..., 1:] - f[..., :-1]], axis=-1)]
    slice x18 -> x0, local copies, waits for them, and re-layouts: 3.3 us -> none  [the longest x9 1.85 us: backward_z(): return jnp.concatenate([f[..., :1], f[..., 1:] - f[..., :-1]], axis=-1)]
    another operation x10 -> x0, other arithmetic: 2.68 us -> none  [the longest x9 2.67 us: curl_curl(): return jnp.stack([curl_x, curl_y, curl_z], axis=-4)]
  transfers between devices with their start and end apart: 10 -> 6, of which waited for: 10 -> 1; matrix products, arithmetic and copies ran while one was open for 2% -> 4% of each run, Pallas kernels for 0% -> 9%
where the time goes in v2:
time: 43.1 us; the launch traced here: 42.8 us
  starting transfers between devices  16.3 us (38%)
  blocking collectives  14.3 us (33%)
  Pallas kernels  8.29 us (19%)
  local copies, waits for them, and re-layouts  1.53 us (4%)
  waiting for transfers between devices  0.93 us (2%)
  between operations  0.72 us (2%)
  other arithmetic  0.69 us (2%)
    all_to_all x1, blocking collectives, shards(): pieces = lax.all_to_all(partial_block, 'space', 0, 0)  12.4 us
    ppermute x2, starting transfers between devices, shards(): nears.append(lax.ppermute(result[1], 'space', near))  10 us
    ppermute x1, starting transfers between devices, shards(): from_near = lax.ppermute(to_near, 'space', near)  4.28 us
    pallas_call x2, Pallas kernels, shards(): pl.pallas_call(functools.partial(first_kernel, s), out_shape=tuple(outs),...  2.69 us
    pallas_call x2, Pallas kernels, shards(): pl.pallas_call(functools.partial(sweep_kernel, s, count), out_shape=outs,...  2.38 us
    all_gather x1, blocking collectives, shards(): every = lax.all_gather(rows, 'rx', axis=0)  1.93 us
    pallas_call x1, Pallas kernels, shards(): pl.pallas_call(functools.partial(stage_kernel, count, 2 + count), out_sha...  1.61 us
    pallas_call x1, Pallas kernels, shards(): pl.pallas_call(functools.partial(smooth_kernel, 1.0 / cells), out_shape=(...  1.6 us
  transfers between devices with their start and end apart: 6, of which 1 were waited for; matrix products, arithmetic and copies ran while one was open for 4% of the time, Pallas kernels for 9%

profile of v2, /device:TPU:0, one launch (start us, length us, event | category | flops | bytes accessed | tf_op | source)
XLA Modules:
  0.0 42.8 jit_solution(12342492243300964261)
XLA Ops:
  0.6 1.5 %first_sweep.2 = (bf16[13,32,128]{2,1,0:T(8,128)(2,1)S(1)}, bf16[13,32,128]{2,1,0:T(8,128)(2,1)S(1)}, f32[2,3,3,32,128]{4,3,2,1,0:T(8,128)S(1)}, f32[2,4,32,128]...) custom-call(f32[2,2,3,3,32,128]{5,4,3,2,1,0:T(8,128)} %refs_0_.1, ...), custom_call_target="tpu_custom_call" | custom-call | tf_op jit(solution)/shard_map/first_sweep/pallas_call | solution.py:420
  2.1 0.7 %collective-permute-start.2 = (bf16[13,32,128]{2,1,0:T(8,128)(2,1)S(1)}, bf16[13,32,128]{2,1,0:T(8,128)(2,1)S(1)}, u32[]{:S(2)}, u32[]{:S(2)}) collective-permute-start(bf16[13,32,128]{2,1,0:T(8,128)(2,1)S(1)} %get-tuple-element.23), channel_id=1, source_target_pairs={{1,2},{3,4},{5,6},{7,8},{9,10},{11,12},{13,14},{2,1},{4,3},{6,5},{... | collective-permute-start | bytes 319496 | tf_op jit(solution)/shard_map/ppermute | solution.py:433
  2.8 5.7 %collective-permute-start.3 = (bf16[13,32,128]{2,1,0:T(8,128)(2,1)S(1)}, bf16[13,32,128]{2,1,0:T(8,128)(2,1)S(1)}, u32[]{:S(2)}, u32[]{:S(2)}) collective-permute-start(bf16[13,32,128]{2,1,0:T(8,128)(2,1)S(1)} %get-tuple-element.24), channel_id=1, source_target_pairs={{0,1},{2,3},{4,5},{6,7},{8,9},{10,11},{12,13},{14,15},{1,0},{3,2},... | collective-permute-start | bytes 319496 | tf_op jit(solution)/shard_map/ppermute | solution.py:434
  8.5 1.2 %first_sweep.3 = (bf16[12,32,128]{2,1,0:T(8,128)(2,1)S(1)}, bf16[12,32,128]{2,1,0:T(8,128)(2,1)S(1)}, f32[2,3,3,32,128]{4,3,2,1,0:T(8,128)S(1)}, f32[2,4,32,128]{3,2,1,0:T(8,128)S(1)}) custom-call(f32[1,2,3,3,32,128]{5,4,3,2,1,0:T(8,128)S(1)} %get-tuple-element.17.refs_0_, f32[3,32,128]{2,1,0:T(8,128)S(1)} %get-tuple-element.18.refs_1_.refs_3_, ...), custom_call_target="tpu_custom_call" | custom-call | tf_op jit(solution)/shard_map/first_sweep/pallas_call | solution.py:420
  9.7 0.7 %collective-permute-start = (bf16[12,32,128]{2,1,0:T(8,128)(2,1)S(1)}, bf16[12,32,128]{2,1,0:T(8,128)(2,1)S(1)}, u32[]{:S(2)}, u32[]{:S(2)}) collective-permute-start(bf16[12,32,128]{2,1,0:T(8,128)(2,1)S(1)} %get-tuple-element.21), channel_id=1, source_target_pairs={{1,2},{3,4},{5,6},{7,8},{9,10},{11,12},{13,14},{2,1},{4,3},{6,5},{... | collective-permute-start | bytes 294920 | tf_op jit(solution)/shard_map/ppermute | solution.py:433
  10.4 4.3 %collective-permute-start.1 = (bf16[12,32,128]{2,1,0:T(8,128)(2,1)S(1)}, bf16[12,32,128]{2,1,0:T(8,128)(2,1)S(1)}, u32[]{:S(2)}, u32[]{:S(2)}) collective-permute-start(bf16[12,32,128]{2,1,0:T(8,128)(2,1)S(1)} %get-tuple-element.22), channel_id=1, source_target_pairs={{0,1},{2,3},{4,5},{6,7},{8,9},{10,11},{12,13},{14,15},{1,0},{3,2},... | collective-permute-start | bytes 294920 | tf_op jit(solution)/shard_map/ppermute | solution.py:434
  14.7 0.8 %reshape.7 = f32[12]{0:T(128)S(1)} reshape(f32[2,2,3]{2,1,0:T(2,128)} %refs_2_.3) | data formatting | bytes 96 | tf_op jit(solution)/shard_map/reshape | solution.py:394
  15.5 0.8 %concatenate.6 = s32[10]{0:T(128)S(1)} concatenate(s32[1]{0:T(128)} %bitcast, s32[1]{0:T(128)} %constant.2.clone.1, s32[2]{0:T(128)} %refs_3_.3, s32[2]{0:T(128)} %refs_4_.3, s32[4]{0:T(128)} %refs_5_.3), dimensions={0} | concatenate | bytes 80 | tf_op jit(solution)/shard_map/concatenate | solution.py:393
  16.2 0.1 pad_maximum_fusion.scalar_ref.refs_0_
  16.3 1.6 %stage_field.1.refs_4_ = f32[2,2,3,3,32,128]{5,4,3,2,1,0:T(8,128)S(1)} custom-call(f32[22]{0:T(128)S(1)} %pad_maximum_fusion.scalar_ref.refs_0_, f32[4,2,3,3,32,128]{5,4,3,2,1,0:T(8,128)} %field_ref.1), custom_call_target="tpu_custom_call" | custom-call | tf_op jit(solution)/shard_map/stage_field/pallas_call | solution.py:436
  17.9 0.0 collective-permute-done.2.refs_5_.refs_7_
  17.9 0.0 collective-permute-done.3.refs_6_.refs_8_
  18.0 1.2 %sweeps.2.refs_9_ = bf16[2,3,32,128]{3,2,1,0:T(8,128)(2,1)S(1)} custom-call(f32[22]{0:T(128)S(1)} %pad_maximum_fusion.scalar_ref.refs_0_, f32[2,3,3,32,128]{4,3,2,1,0:T(8,128)S(1)} %get-tuple-element.25.refs_1_, f32[2,4,32,128]{3,2,1,0:T(8,128)S(1)} %get-tuple-element.26.refs_2_, f32[3,32,128]{2,1,0:T(8,128)S(1)} %get-tuple-element.18.refs_1_.refs_3_, ...), custom_call_target="tpu_custom_call" | custom-call | tf_op jit(solution)/shard_map/sweeps/pallas_call | solution.py:465
  19.2 0.0 collective-permute-done.refs_5_
  19.2 0.0 collective-permute-done.1.refs_6_
  19.2 1.2 %sweeps.3 = (bf16[2,2,3,32,128]{4,3,2,1,0:T(8,128)(2,1)S(1)}, bf16[2,2,2,32,128]{4,3,2,1,0:T(8,128)(2,1)S(1)}, bf16[2,2,2,32,128]{4,3,2,1,0:T(8,128)(2,1)S(1)}) custom-call(f32[22]{0:T(128)S(1)} %pad_maximum_fusion.scalar_ref.refs_0_, f32[2,3,3,32,128]{4,3,2,1,0:T(8,128)S(1)} %get-tuple-element.19.refs_1_, f32[2,4,32,128]{3,2,1,0:T(8,128)S(1)} %get-tuple-element.20.refs_2_, ...), custom_call_target="tpu_custom_call" | custom-call | tf_op jit(solution)/shard_map/sweeps/pallas_call | solution.py:465
  20.4 0.7 %collective-permute-start.4 = (bf16[2,2,2,32,128]{4,3,2,1,0:T(8,128)(2,1)S(1)}, bf16[2,2,2,32,128]{4,3,2,1,0:T(8,128)(2,1)S(1)}, u32[]{:S(2)}, u32[]{:S(2)}) collective-permute-start(bf16[2,2,2,32,128]{4,3,2,1,0:T(8,128)(2,1)S(1)} %get-tuple-element.28), channel_id=1, source_target_pairs={{1,2},{3,4},{5,6},{7,8},{9,10},{11,12},{13,14},{2,1},{4,3},{6,5},{... | collective-permute-start | bytes 196616 | tf_op jit(solution)/shard_map/ppermute | solution.py:476
  21.0 4.3 %collective-permute-start.5 = (bf16[2,2,2,32,128]{4,3,2,1,0:T(8,128)(2,1)S(1)}, bf16[2,2,2,32,128]{4,3,2,1,0:T(8,128)(2,1)S(1)}, u32[]{:S(2)}, u32[]{:S(2)}) collective-permute-start(bf16[2,2,2,32,128]{4,3,2,1,0:T(8,128)(2,1)S(1)} %get-tuple-element.29), channel_id=1, source_target_pairs={{0,1},{2,3},{4,5},{6,7},{8,9},{10,11},{12,13},{14,15},{1,0},{3,2},... | collective-permute-start | bytes 196616 | tf_op jit(solution)/shard_map/ppermute | solution.py:477
  25.3 1.9 %all-gather = bf16[4,2,3,32,128]{4,3,2,1,0:T(8,128)(2,1)S(1)} all-gather(bf16[2,2,3,32,128]{4,3,2,1,0:T(8,128)(2,1)S(1)} %get-tuple-element.27.rows_ref), channel_id=2, replica_groups=mesh['rx'=2,'space'=16] {'rx'}, dimensions={0}, use_global_device_ids=true | all-gather | bytes 294912 | tf_op jit(solution)/shard_map/all_gather | solution.py:478
  27.3 0.0 collective-permute-done.4.far_in
  27.3 0.9 %collective-permute-done.5.near_in = bf16[2,2,2,32,128]{4,3,2,1,0:T(8,128)(2,1)S(1)} collective-permute-done((bf16[2,2,2,32,128]{4,3,2,1,0:T(8,128)(2,1)S(1)}, bf16[2,2,2,32,128]{4,3,2,1,0:T(8,128)(2,1)S(1)}, u32[]{:S(2)}, u32[]{:S(2)}) %collective-permute-start.5) | collective-permute-done | bytes 65568 | tf_op jit(solution)/shard_map/ppermute | solution.py:477
  28.2 1.6 %smooth.1 = (bf16[2,2,3,32,128]{4,3,2,1,0:T(8,128)(2,1)}, f32[16,4,8]{2,1,0:T(4,128)S(1)}) custom-call(f32[22]{0:T(128)S(1)} %pad_maximum_fusion.scalar_ref.refs_0_, bf16[2,2,3,32,128]{4,3,2,1,0:T(8,128)(2,1)S(1)} %get-tuple-element.27.rows_ref, bf16[2,2,2,32,128]{4,3,2,1,0:T(8,128)(2,1)S(1)} %collective-permute-done.4.far_in, ...), custom_call_target="tpu_custom_call" | custom-call | tf_op jit(solution)/shard_map/smooth/pallas_call | solution.py:481
  29.8 12.4 %all_to_all.5 = f32[16,4,8]{2,1,0:T(4,128)S(1)} all-to-all(f32[16,4,8]{2,1,0:T(4,128)S(1)} %get-tuple-element.30), channel_id=1, replica_groups=mesh['rx'=2,'space'=16] {'space'}, dimensions={0} | all-to-all | bytes 4096 | tf_op jit(solution)/shard_map/all_to_all | solution.py:490
  42.2 0.6 %reduce_sum.9 = f32[4,8]{1,0:T(4,128)} reduce(f32[16,4,8]{2,1,0:T(4,128)S(1)} %all_to_all.5, f32[]{:T(128)} %constant.3.clone.1), dimensions={0}, to_apply=%region_0.0 | reduce | flops 480 | bytes 2180 | tf_op jit(solution)/shard_map/reduce_sum | solution.py:491
  (1 shorter events, 0.0 us)
Async XLA Ops:
  2.1 15.8 %collective-permute-start.2 = (bf16[13,32,128]{2,1,0:T(8,128)(2,1)S(1)}, bf16[13,32,128]{2,1,0:T(8,128)(2,1)S(1)}, u32[]{:S(2)}, u32[]{:S(2)}) collective-permute-start(bf16[13,32,128]{2,1,0:T(8,128)(2,1)S(1)} %get-tuple-element.23), channel_id=1, source_target_pairs={{1,2},{3,4},{5,6},{7,8},{9,10},{11,12},{13,14},{2,1},{4,3},{6,5},{... | collective-permute-start | bytes 319496 | tf_op jit(solution)/shard_map/ppermute | solution.py:433
  2.8 15.2 %collective-permute-start.3 = (bf16[13,32,128]{2,1,0:T(8,128)(2,1)S(1)}, bf16[13,32,128]{2,1,0:T(8,128)(2,1)S(1)}, u32[]{:S(2)}, u32[]{:S(2)}) collective-permute-start(bf16[13,32,128]{2,1,0:T(8,128)(2,1)S(1)} %get-tuple-element.24), channel_id=1, source_target_pairs={{0,1},{2,3},{4,5},{6,7},{8,9},{10,11},{12,13},{14,15},{1,0},{3,2},... | collective-permute-start | bytes 319496 | tf_op jit(solution)/shard_map/ppermute | solution.py:434
  9.7 9.4 %collective-permute-start = (bf16[12,32,128]{2,1,0:T(8,128)(2,1)S(1)}, bf16[12,32,128]{2,1,0:T(8,128)(2,1)S(1)}, u32[]{:S(2)}, u32[]{:S(2)}) collective-permute-start(bf16[12,32,128]{2,1,0:T(8,128)(2,1)S(1)} %get-tuple-element.21), channel_id=1, source_target_pairs={{1,2},{3,4},{5,6},{7,8},{9,10},{11,12},{13,14},{2,1},{4,3},{6,5},{... | collective-permute-start | bytes 294920 | tf_op jit(solution)/shard_map/ppermute | solution.py:433
  10.4 8.8 %collective-permute-start.1 = (bf16[12,32,128]{2,1,0:T(8,128)(2,1)S(1)}, bf16[12,32,128]{2,1,0:T(8,128)(2,1)S(1)}, u32[]{:S(2)}, u32[]{:S(2)}) collective-permute-start(bf16[12,32,128]{2,1,0:T(8,128)(2,1)S(1)} %get-tuple-element.22), channel_id=1, source_target_pairs={{0,1},{2,3},{4,5},{6,7},{8,9},{10,11},{12,13},{14,15},{1,0},{3,2},... | collective-permute-start | bytes 294920 | tf_op jit(solution)/shard_map/ppermute | solution.py:434
  20.4 6.9 %collective-permute-start.4 = (bf16[2,2,2,32,128]{4,3,2,1,0:T(8,128)(2,1)S(1)}, bf16[2,2,2,32,128]{4,3,2,1,0:T(8,128)(2,1)S(1)}, u32[]{:S(2)}, u32[]{:S(2)}) collective-permute-start(bf16[2,2,2,32,128]{4,3,2,1,0:T(8,128)(2,1)S(1)} %get-tuple-element.28), channel_id=1, source_target_pairs={{1,2},{3,4},{5,6},{7,8},{9,10},{11,12},{13,14},{2,1},{4,3},{6,5},{... | collective-permute-start | bytes 196616 | tf_op jit(solution)/shard_map/ppermute | solution.py:476
  21.0 7.1 %collective-permute-start.5 = (bf16[2,2,2,32,128]{4,3,2,1,0:T(8,128)(2,1)S(1)}, bf16[2,2,2,32,128]{4,3,2,1,0:T(8,128)(2,1)S(1)}, u32[]{:S(2)}, u32[]{:S(2)}) collective-permute-start(bf16[2,2,2,32,128]{4,3,2,1,0:T(8,128)(2,1)S(1)} %get-tuple-element.29), channel_id=1, source_target_pairs={{0,1},{2,3},{4,5},{6,7},{8,9},{10,11},{12,13},{14,15},{1,0},{3,2},... | collective-permute-start | bytes 196616 | tf_op jit(solution)/shard_map/ppermute | solution.py:477

commit v3 on v0

v3 whole, which is shorter than its diff:
```python
import functools

import jax
import jax.numpy as jnp
from jax import lax
from jax.experimental import pallas as pl
from jax.experimental.pallas import tpu as pltpu
from jax.sharding import PartitionSpec as P

SENT = 6
RELAX = 0.2
KAPPA = 0.1
REACH = 2
FULL = pl.BlockSpec(memory_space=pltpu.VMEM)
HBM = pl.BlockSpec(memory_space=pltpu.HBM)
SCALARS = pl.BlockSpec(memory_space=pltpu.SMEM)
KERNEL = pltpu.CompilerParams(vmem_limit_bytes=8 * 2**20)
F32 = jnp.float32


class Steps:
    def __init__(self, height, breadth):
        self.height, self.breadth = height, breadth
        self.sub = lax.broadcasted_iota(jnp.int32, (8, breadth), 0)
        self.lane = lax.broadcasted_iota(jnp.int32, (height, breadth), 1)

    def after_y(self, f):
        f = pltpu.roll(f, self.height - 1, 0)
        return jnp.concatenate([f[:-8], jnp.where(self.sub < 7, f[-8:], 0.0)], axis=0)

    def before_y(self, f):
        f = pltpu.roll(f, 1, 0)
        return jnp.concatenate([jnp.where(self.sub > 0, f[:8], 0.0), f[8:]], axis=0)

    def after_z(self, f):
        return jnp.where(self.lane < self.breadth - 1, pltpu.roll(f, self.breadth - 1, 1), 0.0)

    def before_z(self, f):
        return jnp.where(self.lane > 0, pltpu.roll(f, 1, 1), 0.0)

    def up_y(self, f):
        return self.after_y(f) - f

    def up_z(self, f):
        return self.after_z(f) - f

    def down_y(self, f):
        return f - self.before_y(f)

    def down_z(self, f):
        return f - self.before_z(f)

    def magnetic_yz(self, e, e_next):
        ex, ey, ez = e
        if e_next is None:
            return self.up_z(ex) + ez, -ey - self.up_y(ex)
        return self.up_z(ex) - (e_next[2] - ez), (e_next[1] - ey) - self.up_y(ex)

    def magnetic_x(self, e):
        return self.up_y(e[2]) - self.up_z(e[1])

    def curl_back(self, comp, hx, hy, hz, before):
        if comp == 0:
            return self.down_y(hz) - self.down_z(hy)
        if comp == 1:
            return self.down_z(hx) - (hz - before[1])
        return (hy - before[0]) - self.down_y(hx)


def angular_of(freq):
    angular = F32(0.25)
    for bit, factor in ((1, 1.25), (2, 1.25**2), (4, 1.25**4)):
        angular = angular * jnp.where((freq & bit) != 0, F32(factor), F32(1.0))
    return angular


def split(number, size):
    if size & (size - 1):
        return number // size, number % size
    return number >> (size.bit_length() - 1), number & (size - 1)


class Point:
    def __init__(self, cell, first, steps):
        plane, inner = split(cell, steps.height * steps.breadth)
        row, lane = split(inner, steps.breadth)
        block, sub = split(row, 8)
        self.plane = plane - first
        self.rows = pl.ds(pl.multiple_of(block * 8, 8), 8)
        self.row, self.sub, self.lane, self.steps = row, sub, lane, steps

    def spread(self, value):
        here = (self.steps.sub == self.sub) & (self.steps.lane[:8] == self.lane)
        return jnp.where(here, RELAX * value, 0.0)

    def add_to(self, ref, low, high, shift, weight):
        @pl.when((self.plane >= low) & (self.plane < high))
        def _():
            for part in range(2):
                for comp in range(3):
                    at = (part, comp, self.plane + shift, self.rows)
                    ref[at] = ref[at] + self.spread(weight(part, comp))


def first_kernel(
    start_ref, cond_ref, back_ref, weight_ref, cell_ref, group_ref, freq_ref,
    far_ref, near_ref, own_ref, edge_ref, held_ref, field_ref,
    raw, weight, cell, group, freq, sent, sems,
):
    count, _, _, depth, height, breadth = start_ref.shape
    pairs = ((group_ref, group), (freq_ref, freq), (cell_ref, cell), (weight_ref, weight), (cond_ref, held_ref))
    copies = [pltpu.make_async_copy(a, b, sems.at[k]) for k, (a, b) in enumerate(pairs)]

    def start_of(s):
        return pltpu.make_async_copy(start_ref.at[s], raw.at[s], sems.at[len(pairs) + s])

    for copy in copies + [start_of(s) for s in range(count)]:
        copy.start()
    copies[0].wait()
    fields = [
        pltpu.make_async_copy(back_ref.at[group[s]], field_ref.at[s], sems.at[len(pairs) + count + s])
        for s in range(count)
    ]
    for copy in fields:
        copy.start()
    for copy in copies[1:]:
        copy.wait()
    steps = Steps(height, breadth)
    half = far_ref.dtype
    index = lax.axis_index("space")
    first = index * depth
    down = index & 1
    up = 1 - down
    row = lax.broadcasted_iota(jnp.int32, (height, breadth), 0)
    last = depth - 1
    sent[up, 2 * count * SENT] = held_ref[last].astype(half)
    sent[down, 2 * count * SENT] = held_ref[0].astype(half)

    def one_source(s, _):
        start_of(s).wait()
        scale = RELAX * angular_of(freq[group[s]])
        scales = scale, -scale
        point = Point(cell[s], first, steps)
        base = 2 * s * SENT
        before = []
        for part in range(2):
            ey, ez = raw[s, part, 1, 0], raw[s, part, 2, 0]
            for k, f in enumerate((ey, ez)):
                sent[down, base + part * SENT + k] = f.astype(half)
                edge_ref[s, part, k] = f
            before.append((-ez, ey))
        for p in range(depth):
            for part in range(2):
                e = [raw[s, part, comp, p] for comp in range(3)]
                e_next = None
                if p < last:
                    e_next = [None if comp == 0 else raw[s, part, comp, p + 1] for comp in range(3)]
                hy, hz = steps.magnetic_yz(e, e_next)
                if p == last:
                    for k, f in enumerate((hy, hz)):
                        sent[up, base + part * SENT + k] = f.astype(half)
                        edge_ref[s, part, 2 + k] = f
                hx = steps.magnetic_x(e)
                coef = scales[part] * held_ref[p]
                for comp in range(3):
                    curl = steps.curl_back(comp, hx, hy, hz, before[part])
                    own_ref[s, part, comp, p] = e[comp] - RELAX * curl + coef * raw[s, 1 - part, comp, p]
                before[part] = hy, hz
        point.add_to(own_ref.at[s], 0, depth, 0, lambda part, comp: weight[s, part, comp])

        at_last = jnp.where(point.plane == last, F32(1.0), F32(0.0))
        here = jnp.where((row == point.row) & (steps.lane == point.lane), RELAX * at_last, 0.0)
        for part in range(2):
            ex, ey, ez = [own_ref[s, part, comp, 0] for comp in range(3)]
            hy, hz = steps.up_z(ex) - own_ref[s, part, 2, 1], own_ref[s, part, 1, 1] - steps.up_y(ex)
            for k, f in enumerate((ey, ez, hy, hz)):
                sent[down, base + part * SENT + 2 + k] = f.astype(half)
            e = [own_ref[s, part, comp, last] for comp in range(3)]
            behind = steps.magnetic_yz([own_ref[s, part, comp, last - 1] for comp in range(3)], e)
            hy, hz = steps.magnetic_yz(e, None)
            hx = steps.magnetic_x(e)
            coef = scales[part] * held_ref[last]
            after = []
            for comp in range(3):
                curl = steps.curl_back(comp, hx, hy, hz, behind)
                value = e[comp] - RELAX * curl + coef * own_ref[s, 1 - part, comp, last]
                after.append(value + here * weight[s, part, comp])
            for k, f in enumerate((hy, hz) + steps.magnetic_yz(after, None)):
                sent[up, base + part * SENT + 2 + k] = f.astype(half)
        return 0

    lax.fori_loop(0, count, one_source, 0)
    far_ref[...] = sent[0]
    near_ref[...] = sent[1]
    for copy in fields:
        copy.wait()


def sweep_kernel(
    planes, scalar_ref, own_ref, edge_ref, held_ref, field_ref, far_in, near_in, rows_ref, far_ref, near_ref, one_, two_, got, sent,
):
    count, _, _, depth, height, breadth = own_ref.shape
    steps = Steps(height, breadth)
    index = lax.axis_index("space")
    first = index * depth
    relax_low = jnp.where(first > 0, F32(RELAX), F32(0.0))
    relax_high = jnp.where(first + depth < planes, F32(RELAX), F32(0.0))
    odd = index & 1
    low, high = odd, 1 - odd
    got[0] = far_in[...]
    got[1] = near_in[...]

    def conductivity(p):
        if p < 0:
            return got[low, 2 * count * SENT].astype(F32)
        if p >= depth:
            return got[high, 2 * count * SENT].astype(F32)
        return held_ref[p]

    def one_source(s, _):
        group = scalar_ref[count + s].astype(jnp.int32)
        angular = angular_of(scalar_ref[2 * count + group].astype(jnp.int32))
        scales = RELAX * angular, -RELAX * angular
        point = Point(scalar_ref[s].astype(jnp.int32), first, steps)
        weights_at = scalar_ref.shape[0] - 6 * count + 6 * s

        def received(side, part, k):
            return got[side, (2 * s + part) * SENT + k].astype(F32)

        for part in range(2):
            ey, ez, ly, lz = [edge_ref[s, part, k] for k in range(4)]
            one_[part, 0, 0] = -relax_low * (steps.down_y(ey) + steps.down_z(ez))
            one_[part, 1, 0] = relax_low * ey
            one_[part, 2, 0] = relax_low * ez
            e = [own_ref[s, part, comp, 0] for comp in range(3)]
            one_[part, 0, 1] = e[0]
            one_[part, 1, 1] = e[1] - RELAX * received(low, part, 1)
            one_[part, 2, 1] = e[2] + RELAX * received(low, part, 0)
            for p in range(1, depth - 1):
                for comp in range(3):
                    one_[part, comp, p + 1] = own_ref[s, part, comp, p]
            e = [own_ref[s, part, comp, depth - 1] for comp in range(3)]
            high_y, high_z = received(high, part, 0), received(high, part, 1)
            one_[part, 0, depth] = e[0] - RELAX * (steps.down_y(high_y) + steps.down_z(high_z))
            one_[part, 1, depth] = e[1] + RELAX * high_y
            one_[part, 2, depth] = e[2] + RELAX * high_z
            one_[part, 1, depth + 1] = received(high, part, 2) - relax_high * lz
            one_[part, 2, depth + 1] = received(high, part, 3) + relax_high * ly

        def sweep(ref, into, low_plane, planes_swept, k):
            if low_plane < 0:
                before = [(-ref[part, 2, 0], ref[part, 1, 0]) for part in range(2)]
            else:
                before = []
                for part in range(2):
                    e = [ref[part, comp, 0] for comp in range(3)]
                    hy, hz = steps.magnetic_yz(e, [None, ref[part, 1, 1], ref[part, 2, 1]])
                    before.append((hy + received(low, part, k), hz + received(low, part, k + 1)))
            for p in range(low_plane, planes_swept):
                relax = relax_low if p < 0 else relax_high if p == depth else F32(RELAX)
                for part in range(2):
                    e = [ref[part, comp, p + 1] if comp or p < depth else None for comp in range(3)]
                    if p < depth:
                        e_next = [None if comp == 0 else ref[part, comp, p + 2] for comp in range(3)]
                        hy, hz = steps.magnetic_yz(e, e_next)
                    else:
                        hy, hz = received(high, part, 4) + e[2], received(high, part, 5) - e[1]
                    hx = steps.magnetic_x(e)
                    coef = scales[part] * conductivity(p)
                    for comp in range(1 if p == depth else 0, 3):
                        curl = steps.curl_back(comp, hx, hy, hz, before[part])
                        into[part, comp, p + 1] = e[comp] - relax * curl + coef * ref[1 - part, comp, p + 1]
                    if p < 0:
                        hy, hz = hy + received(low, part, k), hz + received(low, part, k + 1)
                    before[part] = hy, hz
            point.add_to(into, 0, planes_swept, 1, lambda part, comp: scalar_ref[weights_at + part * 3 + comp])

        sweep(one_, two_, -1, depth + 1, 2)
        sweep(two_, one_, 0, depth, 4)

        for p in range(depth):
            row_re = row_im = None
            for comp in range(3):
                re, im = one_[0, comp, p + 1], one_[1, comp, p + 1]
                field_re, field_im = field_ref[s, 0, comp, p], field_ref[s, 1, comp, p]
                add_re, add_im = field_re * re - field_im * im, field_re * im + field_im * re
                row_re, row_im = (add_re, add_im) if comp == 0 else (row_re + add_re, row_im + add_im)
            coef = angular * held_ref[p]
            for part, value in enumerate((row_re, row_im)):
                value = (coef * value).astype(rows_ref.dtype)
                rows_ref[s, part, p] = value
                if p >= depth - REACH:
                    sent[high, s, part, p - depth + REACH] = value
                if p < REACH:
                    sent[low, s, part, p] = value
        return 0

    lax.fori_loop(0, count, one_source, 0)
    far_ref[...] = sent[0]
    near_ref[...] = sent[1]


def in_plane(steps, f):
    total = (steps.after_y(f) + steps.before_y(f)) + (steps.after_z(f) + steps.before_z(f))
    return (1.0 - 6.0 * KAPPA) * f + KAPPA * total


def smooth_kernel(planes, rows_ref, alone_ref):
    count, _, depth, height, breadth = rows_ref.shape
    steps = Steps(height, breadth)
    first = lax.axis_index("space") * depth
    below = jnp.where(first > 0, F32(KAPPA), F32(0.0))
    above = jnp.where(first + depth < planes, F32(KAPPA), F32(0.0))

    def one_row(i, _):
        s, part = i >> 1, i & 1
        value = [rows_ref[s, part, p].astype(F32) for p in range(depth)]
        once = []
        for p in range(depth):
            beside = [value[q] for q in (p - 1, p + 1) if 0 <= q < depth]
            once.append(in_plane(steps, value[p]) + KAPPA * functools.reduce(jnp.add, beside))
        once = [below * value[0]] + once + [above * value[-1]]
        for p in range(depth):
            alone_ref[s, part, p] = in_plane(steps, once[p + 1]) + KAPPA * (once[p] + once[p + 2])
        return 0

    lax.fori_loop(0, 2 * count, one_row, 0)


def block_kernel(cells, rows_ref, alone_ref, far_in, near_in, all_ref, smooth_ref, block_ref, got, rounded, sums, sem):
    count, _, depth, height, breadth = rows_ref.shape
    ranks = all_ref.shape[0]
    steps = Steps(height, breadth)
    many = ranks * count * 2
    got[0] = far_in[...]
    got[1] = near_in[...]
    odd = lax.axis_index("space") & 1
    low, high = odd, 1 - odd

    def one_row(i, _):
        s, part = i >> 1, i & 1
        value = [alone_ref[s, part, p] for p in range(depth)]
        for side, nearest, order in ((low, REACH - 1, 1), (high, 0, -1)):
            close = got[side, s, part, nearest].astype(F32)
            beyond = got[side, s, part, REACH - 1 - nearest].astype(F32)
            end = 0 if order > 0 else depth - 1
            value[end] = value[end] + (2.0 * KAPPA * in_plane(steps, close) + KAPPA * KAPPA * beyond)
            value[end + order] = value[end + order] + KAPPA * KAPPA * close
        for p in range(depth):
            rounded[s, part, p] = value[p].astype(rounded.dtype)
        return 0

    lax.fori_loop(0, 2 * count, one_row, 0)
    out = pltpu.make_async_copy(rounded, smooth_ref, sem)
    out.start()

    sums[...] = jnp.zeros_like(sums)

    def one_plane(p, _):
        mine = [rounded[a // 2, a % 2, p].astype(F32) for a in range(2 * count)]
        for b in range(many):
            r, t = divmod(b // 2, count)
            other = all_ref[r, t, b % 2, p].astype(F32)
            for a in range(2 * count):
                prod = mine[a] * other
                total = prod[:8]
                for k in range(8, height, 8):
                    total = total + prod[k : k + 8]
                sums[a * many + b] = sums[a * many + b] + total
        return 0

    lax.fori_loop(0, depth, one_plane, 0)
    half = jnp.bfloat16
    ones = jnp.ones((breadth, breadth), half)
    for a in range(2 * count):
        table = sums[a * many : (a + 1) * many].reshape(many * 8, breadth)
        coarse = table.astype(half)
        fine = (table - coarse.astype(F32)).astype(half)
        table = jnp.dot(coarse, ones, preferred_element_type=F32) + jnp.dot(fine, ones, preferred_element_type=F32)
        line = None
        for b in range(many):
            add = jnp.where(steps.lane[:8] == b, table[b * 8 : b * 8 + 8], 0.0)
            line = add if line is None else line + add
        line = jnp.sum(line, axis=0, keepdims=True) * (1.0 / cells)
        for peer in range(block_ref.shape[0]):
            block_ref[peer, a : a + 1, :] = line[:, :many]
    out.wait()


def in_hbm(x):
    return pltpu.with_memory_space_constraint(x, pltpu.HBM)


def shards(conductivity, background, warm_start, data_weight, recv_cell, src_group, group_freq):
    count = warm_start.shape[0]
    depth, height, breadth = conductivity.shape
    plane = (height, breadth)
    peers = lax.axis_size("space")
    ranks = lax.axis_size("rx")
    cells = depth * height * breadth * peers
    half = jnp.bfloat16
    integers = jnp.concatenate([recv_cell, src_group, group_freq]).astype(F32)
    scalars = jnp.concatenate([integers, data_weight.reshape(-1)])
    far = [(i, i + 1) for i in range(1, peers - 1, 2)]
    near = [(i, i + 1) for i in range(0, peers - 1, 2)]
    far, near = [pairs + [(j, i) for i, j in pairs] for pairs in (far, near)]
    shape = jax.ShapeDtypeStruct

    message = shape((2 * count * SENT + 1,) + plane, half)
    to_far, to_near, own, edge, held, field = pl.pallas_call(
        first_kernel,
        out_shape=(
            message,
            message,
            shape(warm_start.shape, F32),
            shape((count, 2, 4) + plane, F32),
            shape(conductivity.shape, F32),
            shape((count,) + background.shape[1:], F32),
        ),
        in_specs=[HBM] * 7,
        out_specs=(FULL,) * 6,
        scratch_shapes=[
            pltpu.VMEM(warm_start.shape, F32),
            pltpu.SMEM(data_weight.shape, F32),
            pltpu.SMEM(recv_cell.shape, jnp.int32),
            pltpu.SMEM(src_group.shape, jnp.int32),
            pltpu.SMEM(group_freq.shape, jnp.int32),
            pltpu.VMEM((2,) + message.shape, half),
            pltpu.SemaphoreType.DMA((5 + 2 * count,)),
        ],
        compiler_params=KERNEL,
        name="first_sweep",
    )(*[in_hbm(x) for x in (warm_start, conductivity, background, data_weight, recv_cell, src_group, group_freq)])
    from_far = lax.ppermute(to_far, "space", far)
    from_near = lax.ppermute(to_near, "space", near)

    rows_of = shape((count, 2, depth) + plane, half)
    ends_of = shape((count, 2, REACH) + plane, half)
    rows, to_far, to_near = pl.pallas_call(
        functools.partial(sweep_kernel, peers * depth),
        out_shape=(rows_of, ends_of, ends_of),
        in_specs=[SCALARS] + [FULL] * 6,
        out_specs=(FULL,) * 3,
        scratch_shapes=[
            pltpu.VMEM((2, 3, depth + 2) + plane, F32),
            pltpu.VMEM((2, 3, depth + 2) + plane, F32),
            pltpu.VMEM((2,) + message.shape, half),
            pltpu.VMEM((2,) + ends_of.shape, half),
        ],
        compiler_params=KERNEL,
        name="sweeps",
    )(scalars, own, edge, held, field, from_far, from_near)
    from_far = lax.ppermute(to_far, "space", far)
    from_near = lax.ppermute(to_near, "space", near)
    every = lax.all_gather(rows, "rx", axis=0)

    many = 2 * count * ranks
    alone = pl.pallas_call(
        functools.partial(smooth_kernel, peers * depth),
        out_shape=shape(rows_of.shape, F32),
        in_specs=[FULL],
        out_specs=FULL,
        compiler_params=KERNEL,
        name="smooth",
    )(rows)
    smoothed, partial_block = pl.pallas_call(
        functools.partial(block_kernel, cells),
        out_shape=(rows_of, shape((peers, 2 * count, many), F32)),
        in_specs=[FULL] * 5,
        out_specs=(HBM, FULL),
        scratch_shapes=[
            pltpu.VMEM((2,) + ends_of.shape, half),
            pltpu.VMEM(rows_of.shape, half),
            pltpu.VMEM((2 * count * many, 8, breadth), F32),
            pltpu.SemaphoreType.DMA,
        ],
        compiler_params=KERNEL,
        name="block",
    )(rows, alone, from_far, from_near, every)
    backwards = [list(range(peers - 1, -1, -1))]
    pieces = lax.all_to_all(partial_block, "space", 0, 0, axis_index_groups=backwards)
    return (jnp.sum(pieces, axis=0), smoothed)


def solution(mesh):
    in_specs = (
        P("space", None, None),
        P(None, None, None, "space", None, None),
        P("rx", None, None, "space", None, None),
        P("rx", None, None),
        P("rx"),
        P("rx"),
        P(),
    )
    out_specs = (P("rx", None), P("rx", None, "space", None, None))
    return jax.shard_map(shards, mesh=mesh, in_specs=in_specs, out_specs=out_specs, check_vma=False)
```

time: 124 us -> 39.7 us (0.32)
  blocking collectives: 41.4 us -> 13 us
  waiting for transfers between devices: 30.8 us -> 9.16 us
  starting transfers between devices: 28.4 us -> 10.2 us
  other arithmetic: 15.5 us -> 0.76 us
  local copies, waits for them, and re-layouts: 5.66 us -> 0.1 us
  Pallas kernels: 0 us -> 5.52 us
    psum x1 -> x0, blocking collectives: 39.5 us -> none  [shards(): total = lax.psum(partial_block, 'space')]
    ppermute x10 -> x4, waiting for transfers between devices: 30.8 us -> 9.16 us  [the longest x2 9.15 us: shards(): from_near = lax.ppermute(to_near, 'space', near)]
    ppermute x10 -> x4, starting transfers between devices: 28.4 us -> 10.2 us  [the longest x2 8.88 us: shards(): from_near = lax.ppermute(to_near, 'space', near)]
    all_to_all x0 -> x1, blocking collectives: none -> 11 us  [shards(): lax.all_to_all(partial_block, 'space', 0, 0, axis_index_groups=backwards)]
    pallas_call x0 -> x4, Pallas kernels: none -> 5.52 us  [the longest x1 2 us: shards(): pl.pallas_call(first_kernel, out_shape=(message, message, shape(warm_star...]
    sub x31 -> x0, other arithmetic: 5.4 us -> none  [the longest x3 1.74 us: backward_z(): return jnp.concatenate([f[..., :1], f[..., 1:] - f[..., :-1]], axis=-1)]
    slice x18 -> x0, local copies, waits for them, and re-layouts: 3.3 us -> none  [the longest x9 1.85 us: backward_z(): return jnp.concatenate([f[..., :1], f[..., 1:] - f[..., :-1]], axis=-1)]
    another operation x10 -> x0, other arithmetic: 2.68 us -> none  [the longest x9 2.67 us: curl_curl(): return jnp.stack([curl_x, curl_y, curl_z], axis=-4)]
  transfers between devices with their start and end apart: 10 -> 4, of which waited for: 10 -> 2; matrix products, arithmetic and copies ran while one was open for 2% -> 1% of each run, Pallas kernels for 0% -> 2%
where the time goes in v3:
time: 39.7 us; the launch traced here: 39.5 us
  blocking collectives  13 us (33%)
  starting transfers between devices  10.2 us (26%)
  waiting for transfers between devices  9.16 us (23%)
  Pallas kernels  5.52 us (14%)
  other arithmetic  0.76 us (2%)
  between operations  0.72 us (2%)
    all_to_all x1, blocking collectives, shards(): lax.all_to_all(partial_block, 'space', 0, 0, axis_index_groups=backwards)  11 us
    ppermute x2, waiting for transfers between devices, shards(): from_near = lax.ppermute(to_near, 'space', near)  9.15 us
    ppermute x2, starting transfers between devices, shards(): from_near = lax.ppermute(to_near, 'space', near)  8.88 us
    pallas_call x1, Pallas kernels, shards(): pl.pallas_call(first_kernel, out_shape=(message, message, shape(warm_star...  2 us
    all_gather x1, blocking collectives, shards(): every = lax.all_gather(rows, 'rx', axis=0)  1.95 us
    pallas_call x1, Pallas kernels, shards(): pl.pallas_call(functools.partial(sweep_kernel, peers * depth), out_shape=...  1.81 us
    ppermute x2, starting transfers between devices, shards(): from_far = lax.ppermute(to_far, 'space', far)  1.34 us
    pallas_call x1, Pallas kernels, shards(): pl.pallas_call(functools.partial(block_kernel, cells), out_shape=(rows_of...  1.01 us
  transfers between devices with their start and end apart: 4, of which 2 were waited for; matrix products, arithmetic and copies ran while one was open for 1% of the time, Pallas kernels for 2%

profile of v3, /device:TPU:0, one launch (start us, length us, event | category | flops | bytes accessed | tf_op | source)
XLA Modules:
  0.0 39.5 jit_solution(16138581886059938408)
XLA Ops:
  0.6 0.0 copy-start.1
  0.6 0.0 copy-start.2
  0.7 0.0 copy-start.3
  0.7 0.0 copy-start
  0.7 2.0 %first_sweep.1 = (bf16[25,32,128]{2,1,0:T(8,128)(2,1)S(1)}, bf16[25,32,128]{2,1,0:T(8,128)(2,1)S(1)}, f32[2,2,3,3,32,128]{5,4,3,2,1,0:T(8,128)S(1)}, f32[2,2,4,3...) custom-call(f32[2,2,3,3,32,128]{5,4,3,2,1,0:T(8,128)} %start_ref.1, ...), custom_call_target="tpu_custom_call" | custom-call | tf_op jit(solution)/shard_map/first_sweep/pallas_call | solution.py:410
  2.7 0.7 %collective-permute-start = (bf16[25,32,128]{2,1,0:T(8,128)(2,1)S(1)}, bf16[25,32,128]{2,1,0:T(8,128)(2,1)S(1)}, u32[]{:S(2)}, u32[]{:S(2)}) collective-permute-start(bf16[25,32,128]{2,1,0:T(8,128)(2,1)S(1)} %get-tuple-element.17), channel_id=1, source_target_pairs={{1,2},{3,4},{5,6},{7,8},{9,10},{11,12},{13,14},{2,1},{4,3},{6,5},{... | collective-permute-start | bytes 614408 | tf_op jit(solution)/shard_map/ppermute | solution.py:434
  3.4 5.7 %collective-permute-start.1 = (bf16[25,32,128]{2,1,0:T(8,128)(2,1)S(1)}, bf16[25,32,128]{2,1,0:T(8,128)(2,1)S(1)}, u32[]{:S(2)}, u32[]{:S(2)}) collective-permute-start(bf16[25,32,128]{2,1,0:T(8,128)(2,1)S(1)} %get-tuple-element.18), channel_id=1, source_target_pairs={{0,1},{2,3},{4,5},{6,7},{8,9},{10,11},{12,13},{14,15},{1,0},{3,2},... | collective-permute-start | bytes 614408 | tf_op jit(solution)/shard_map/ppermute | solution.py:435
  9.1 0.0 copy-done
  9.1 0.1 reshape.7
  9.2 0.0 copy-done.1
  9.2 0.0 copy-done.2
  9.2 0.0 copy-done.3
  9.2 0.1 add_convert_fusion
  9.3 0.1 pad_maximum_fusion.scalar_ref
  9.3 0.0 collective-permute-done.far_in
  9.3 8.8 %collective-permute-done.1.near_in = bf16[25,32,128]{2,1,0:T(8,128)(2,1)S(1)} collective-permute-done((bf16[25,32,128]{2,1,0:T(8,128)(2,1)S(1)}, bf16[25,32,128]{2,1,0:T(8,128)(2,1)S(1)}, u32[]{:S(2)}, u32[]{:S(2)}) %collective-permute-start.1) | collective-permute-done | bytes 204832 | tf_op jit(solution)/shard_map/ppermute | solution.py:435
  18.2 1.8 %sweeps.1 = (bf16[2,2,3,32,128]{4,3,2,1,0:T(8,128)(2,1)S(1)}, bf16[2,2,2,32,128]{4,3,2,1,0:T(8,128)(2,1)S(1)}, bf16[2,2,2,32,128]{4,3,2,1,0:T(8,128)(2,1)S(1)}) custom-call(f32[20]{0:T(128)S(1)} %pad_maximum_fusion.scalar_ref, f32[2,2,3,3,32,128]{5,4,3,2,1,0:T(8,128)S(1)} %get-tuple-element.13.own_ref, f32[2,2,4,32,128]{4,3,2,1,0:T(8,128)S(1)} %get-tuple-element.14.edge_ref, ...), custom_call_target="tpu_custom_call" | custom-call | tf_op jit(solution)/shard_map/sweeps/pallas_call | solution.py:439
  20.0 0.7 %collective-permute-start.2 = (bf16[2,2,2,32,128]{4,3,2,1,0:T(8,128)(2,1)S(1)}, bf16[2,2,2,32,128]{4,3,2,1,0:T(8,128)(2,1)S(1)}, u32[]{:S(2)}, u32[]{:S(2)}) collective-permute-start(bf16[2,2,2,32,128]{4,3,2,1,0:T(8,128)(2,1)S(1)} %get-tuple-element.20), channel_id=1, source_target_pairs={{1,2},{3,4},{5,6},{7,8},{9,10},{11,12},{13,14},{2,1},{4,3},{6,5},{... | collective-permute-start | bytes 196616 | tf_op jit(solution)/shard_map/ppermute | solution.py:453
  20.7 3.2 %collective-permute-start.3 = (bf16[2,2,2,32,128]{4,3,2,1,0:T(8,128)(2,1)S(1)}, bf16[2,2,2,32,128]{4,3,2,1,0:T(8,128)(2,1)S(1)}, u32[]{:S(2)}, u32[]{:S(2)}) collective-permute-start(bf16[2,2,2,32,128]{4,3,2,1,0:T(8,128)(2,1)S(1)} %get-tuple-element.21), channel_id=1, source_target_pairs={{0,1},{2,3},{4,5},{6,7},{8,9},{10,11},{12,13},{14,15},{1,0},{3,2},... | collective-permute-start | bytes 196616 | tf_op jit(solution)/shard_map/ppermute | solution.py:454
  23.8 0.7 %smooth.1.alone_ref = f32[2,2,3,32,128]{4,3,2,1,0:T(8,128)S(1)} custom-call(bf16[2,2,3,32,128]{4,3,2,1,0:T(8,128)(2,1)S(1)} %get-tuple-element.19.rows_ref), custom_call_target="tpu_custom_call" | custom-call | tf_op jit(solution)/shard_map/smooth/pallas_call | solution.py:458
  24.5 1.9 %all-gather = bf16[4,2,3,32,128]{4,3,2,1,0:T(8,128)(2,1)S(1)} all-gather(bf16[2,2,3,32,128]{4,3,2,1,0:T(8,128)(2,1)S(1)} %get-tuple-element.19.rows_ref), channel_id=2, replica_groups=mesh['rx'=2,'space'=16] {'rx'}, dimensions={0}, use_global_device_ids=true | all-gather | bytes 294912 | tf_op jit(solution)/shard_map/all_gather | solution.py:455
  26.5 0.0 collective-permute-done.2.far_in
  26.5 0.3 collective-permute-done.3.near_in
  26.8 1.0 %block.1 = (bf16[2,2,3,32,128]{4,3,2,1,0:T(8,128)(2,1)}, f32[16,4,8]{2,1,0:T(4,128)S(1)}) custom-call(bf16[2,2,3,32,128]{4,3,2,1,0:T(8,128)(2,1)S(1)} %get-tuple-element.19.rows_ref, f32[2,2,3,32,128]{4,3,2,1,0:T(8,128)S(1)} %smooth.1.alone_ref, bf16[2,2,2,32,128]{4,3,2,1,0:T(8,128)(2,1)S(1)} %collective-permute-done.2.far_in, ...), custom_call_target="tpu_custom_call" | custom-call | tf_op jit(solution)/shard_map/block/pallas_call | solution.py:466
  27.8 11.0 %all_to_all.5 = f32[16,4,8]{2,1,0:T(4,128)S(1)} all-to-all(f32[16,4,8]{2,1,0:T(4,128)S(1)} %get-tuple-element.22), channel_id=1, replica_groups={{15,14,13,12,11,10,9,8,7,6,5,4,3,2,1,0},{31,30,29,28,27,26,25,24,23,22,..., dimensions={0} | all-to-all | bytes 4096 | tf_op jit(solution)/shard_map/all_to_all | solution.py:481
  38.8 0.6 %reduce_sum.9 = f32[4,8]{1,0:T(4,128)} reduce(f32[16,4,8]{2,1,0:T(4,128)S(1)} %all_to_all.5, f32[]{:T(128)} %constant.0.clone.1), dimensions={0}, to_apply=%region_0.0 | reduce | flops 480 | bytes 2180 | tf_op jit(solution)/shard_map/reduce_sum | solution.py:482
Async XLA Ops:
  0.6 8.5 %copy-start.1 = (s32[4]{0:T(128)S(1)}, s32[4]{0:T(128)}, u32[]{:S(2)}) copy-start(s32[4]{0:T(128)} %freq_ref.1) | copy-start | bytes 52
  0.6 8.5 %copy-start.2 = (s32[2]{0:T(128)S(1)}, s32[2]{0:T(128)}, u32[]{:S(2)}) copy-start(s32[2]{0:T(128)} %group_ref.1) | copy-start | bytes 28
  0.7 8.5 %copy-start.3 = (s32[2]{0:T(128)S(1)}, s32[2]{0:T(128)}, u32[]{:S(2)}) copy-start(s32[2]{0:T(128)} %cell_ref.1) | copy-start | bytes 28
  0.7 8.4 %copy-start = (f32[2,2,3]{2,1,0:T(2,128)S(1)}, f32[2,2,3]{2,1,0:T(2,128)}, u32[]{:S(2)}) copy-start(f32[2,2,3]{2,1,0:T(2,128)} %weight_ref.1) | copy-start | bytes 148
  2.7 6.7 %collective-permute-start = (bf16[25,32,128]{2,1,0:T(8,128)(2,1)S(1)}, bf16[25,32,128]{2,1,0:T(8,128)(2,1)S(1)}, u32[]{:S(2)}, u32[]{:S(2)}) collective-permute-start(bf16[25,32,128]{2,1,0:T(8,128)(2,1)S(1)} %get-tuple-element.17), channel_id=1, source_target_pairs={{1,2},{3,4},{5,6},{7,8},{9,10},{11,12},{13,14},{2,1},{4,3},{6,5},{... | collective-permute-start | bytes 614408 | tf_op jit(solution)/shard_map/ppermute | solution.py:434
  3.4 14.8 %collective-permute-start.1 = (bf16[25,32,128]{2,1,0:T(8,128)(2,1)S(1)}, bf16[25,32,128]{2,1,0:T(8,128)(2,1)S(1)}, u32[]{:S(2)}, u32[]{:S(2)}) collective-permute-start(bf16[25,32,128]{2,1,0:T(8,128)(2,1)S(1)} %get-tuple-element.18), channel_id=1, source_target_pairs={{0,1},{2,3},{4,5},{6,7},{8,9},{10,11},{12,13},{14,15},{1,0},{3,2},... | collective-permute-start | bytes 614408 | tf_op jit(solution)/shard_map/ppermute | solution.py:435
  20.0 6.5 %collective-permute-start.2 = (bf16[2,2,2,32,128]{4,3,2,1,0:T(8,128)(2,1)S(1)}, bf16[2,2,2,32,128]{4,3,2,1,0:T(8,128)(2,1)S(1)}, u32[]{:S(2)}, u32[]{:S(2)}) collective-permute-start(bf16[2,2,2,32,128]{4,3,2,1,0:T(8,128)(2,1)S(1)} %get-tuple-element.20), channel_id=1, source_target_pairs={{1,2},{3,4},{5,6},{7,8},{9,10},{11,12},{13,14},{2,1},{4,3},{6,5},{... | collective-permute-start | bytes 196616 | tf_op jit(solution)/shard_map/ppermute | solution.py:453
  20.7 6.1 %collective-permute-start.3 = (bf16[2,2,2,32,128]{4,3,2,1,0:T(8,128)(2,1)S(1)}, bf16[2,2,2,32,128]{4,3,2,1,0:T(8,128)(2,1)S(1)}, u32[]{:S(2)}, u32[]{:S(2)}) collective-permute-start(bf16[2,2,2,32,128]{4,3,2,1,0:T(8,128)(2,1)S(1)} %get-tuple-element.21), channel_id=1, source_target_pairs={{0,1},{2,3},{4,5},{6,7},{8,9},{10,11},{12,13},{14,15},{1,0},{3,2},... | collective-permute-start | bytes 196616 | tf_op jit(solution)/shard_map/ppermute | solution.py:454

commit v4 on v3

--- a/solution.py
+++ b/solution.py
@@ -7,7 +7,7 @@
 from jax.experimental.pallas import tpu as pltpu
 from jax.sharding import PartitionSpec as P
 
-SENT = 6
+EARLY, LATE = 4, 2
 RELAX = 0.2
 KAPPA = 0.1
 REACH = 2
@@ -131,22 +131,20 @@
     first = index * depth
     down = index & 1
     up = 1 - down
-    row = lax.broadcasted_iota(jnp.int32, (height, breadth), 0)
     last = depth - 1
-    sent[up, 2 * count * SENT] = held_ref[last].astype(half)
-    sent[down, 2 * count * SENT] = held_ref[0].astype(half)
+    sent[up, 2 * count * EARLY] = held_ref[last].astype(half)
+    sent[down, 2 * count * EARLY] = held_ref[0].astype(half)
 
     def one_source(s, _):
         start_of(s).wait()
         scale = RELAX * angular_of(freq[group[s]])
         scales = scale, -scale
         point = Point(cell[s], first, steps)
-        base = 2 * s * SENT
         before = []
         for part in range(2):
             ey, ez = raw[s, part, 1, 0], raw[s, part, 2, 0]
             for k, f in enumerate((ey, ez)):
-                sent[down, base + part * SENT + k] = f.astype(half)
+                sent[down, (2 * s + part) * EARLY + k] = f.astype(half)
                 edge_ref[s, part, k] = f
             before.append((-ez, ey))
         for p in range(depth):
@@ -158,7 +156,7 @@
                 hy, hz = steps.magnetic_yz(e, e_next)
                 if p == last:
                     for k, f in enumerate((hy, hz)):
-                        sent[up, base + part * SENT + k] = f.astype(half)
+                        sent[up, (2 * s + part) * EARLY + k] = f.astype(half)
                         edge_ref[s, part, 2 + k] = f
                 hx = steps.magnetic_x(e)
                 coef = scales[part] * held_ref[p]
@@ -167,14 +165,58 @@
                     own_ref[s, part, comp, p] = e[comp] - RELAX * curl + coef * raw[s, 1 - part, comp, p]
                 before[part] = hy, hz
         point.add_to(own_ref.at[s], 0, depth, 0, lambda part, comp: weight[s, part, comp])
-
+        for part in range(2):
+            for k, f in enumerate((own_ref[s, part, 1, 0], own_ref[s, part, 2, 0])):
+                sent[down, (2 * s + part) * EARLY + 2 + k] = f.astype(half)
+            share = steps.magnetic_yz([own_ref[s, part, comp, last] for comp in range(3)], None)
+            for k, f in enumerate(share):
+                sent[up, (2 * s + part) * EARLY + 2 + k] = f.astype(half)
+        return 0
+
+    lax.fori_loop(0, count, one_source, 0)
+    far_ref[...] = sent[0]
+    near_ref[...] = sent[1]
+    for copy in fields:
+        copy.wait()
+
+
+class Sources:
+    def __init__(self, ref, count, steps, first):
+        self.ref, self.count, self.steps, self.first = ref, count, steps, first
+
+    def angular(self, s):
+        group = self.ref[self.count + s].astype(jnp.int32)
+        return angular_of(self.ref[2 * self.count + group].astype(jnp.int32))
+
+    def point(self, s):
+        return Point(self.ref[s].astype(jnp.int32), self.first, self.steps)
+
+    def weight(self, s, part, comp):
+        return self.ref[self.ref.shape[0] - 6 * self.count + 6 * s + part * 3 + comp]
+
+
+def second_kernel(scalar_ref, own_ref, held_ref, far_ref, near_ref, sent):
+    count, _, _, depth, height, breadth = own_ref.shape
+    steps = Steps(height, breadth)
+    half = far_ref.dtype
+    index = lax.axis_index("space")
+    down = index & 1
+    up = 1 - down
+    last = depth - 1
+    sources = Sources(scalar_ref, count, steps, index * depth)
+    row = lax.broadcasted_iota(jnp.int32, (height, breadth), 0)
+
+    def one_source(s, _):
+        scale = RELAX * sources.angular(s)
+        scales = scale, -scale
+        point = sources.point(s)
         at_last = jnp.where(point.plane == last, F32(1.0), F32(0.0))
         here = jnp.where((row == point.row) & (steps.lane == point.lane), RELAX * at_last, 0.0)
         for part in range(2):
-            ex, ey, ez = [own_ref[s, part, comp, 0] for comp in range(3)]
-            hy, hz = steps.up_z(ex) - own_ref[s, part, 2, 1], own_ref[s, part, 1, 1] - steps.up_y(ex)
-            for k, f in enumerate((ey, ez, hy, hz)):
-                sent[down, base + part * SENT + 2 + k] = f.astype(half)
+            base = (2 * s + part) * LATE
+            ex = own_ref[s, part, 0, 0]
+            sent[down, base] = (steps.up_z(ex) - own_ref[s, part, 2, 1]).astype(half)
+            sent[down, base + 1] = (own_ref[s, part, 1, 1] - steps.up_y(ex)).astype(half)
             e = [own_ref[s, part, comp, last] for comp in range(3)]
             behind = steps.magnetic_yz([own_ref[s, part, comp, last - 1] for comp in range(3)], e)
             hy, hz = steps.magnetic_yz(e, None)
@@ -184,48 +226,35 @@
             for comp in range(3):
                 curl = steps.curl_back(comp, hx, hy, hz, behind)
                 value = e[comp] - RELAX * curl + coef * own_ref[s, 1 - part, comp, last]
-                after.append(value + here * weight[s, part, comp])
-            for k, f in enumerate((hy, hz) + steps.magnetic_yz(after, None)):
-                sent[up, base + part * SENT + 2 + k] = f.astype(half)
+                after.append(value + here * sources.weight(s, part, comp))
+            for k, f in enumerate(steps.magnetic_yz(after, None)):
+                sent[up, base + k] = f.astype(half)
         return 0
 
     lax.fori_loop(0, count, one_source, 0)
     far_ref[...] = sent[0]
     near_ref[...] = sent[1]
-    for copy in fields:
-        copy.wait()
-
-
-def sweep_kernel(
-    planes, scalar_ref, own_ref, edge_ref, held_ref, field_ref, far_in, near_in, rows_ref, far_ref, near_ref, one_, two_, got, sent,
-):
+
+
+def sweep_two_kernel(planes, scalar_ref, own_ref, edge_ref, held_ref, far_in, near_in, two_ref, top_ref, one_, got):
     count, _, _, depth, height, breadth = own_ref.shape
     steps = Steps(height, breadth)
     index = lax.axis_index("space")
     first = index * depth
     relax_low = jnp.where(first > 0, F32(RELAX), F32(0.0))
     relax_high = jnp.where(first + depth < planes, F32(RELAX), F32(0.0))
-    odd = index & 1
-    low, high = odd, 1 - odd
+    low = index & 1
+    high = 1 - low
     got[0] = far_in[...]
     got[1] = near_in[...]
-
-    def conductivity(p):
-        if p < 0:
-            return got[low, 2 * count * SENT].astype(F32)
-        if p >= depth:
-            return got[high, 2 * count * SENT].astype(F32)
-        return held_ref[p]
+    sources = Sources(scalar_ref, count, steps, first)
 
     def one_source(s, _):
-        group = scalar_ref[count + s].astype(jnp.int32)
-        angular = angular_of(scalar_ref[2 * count + group].astype(jnp.int32))
-        scales = RELAX * angular, -RELAX * angular
-        point = Point(scalar_ref[s].astype(jnp.int32), first, steps)
-        weights_at = scalar_ref.shape[0] - 6 * count + 6 * s
+        scale = RELAX * sources.angular(s)
+        scales = scale, -scale
 
         def received(side, part, k):
-            return got[side, (2 * s + part) * SENT + k].astype(F32)
+            return got[side, (2 * s + part) * EARLY + k].astype(F32)
 
         for part in range(2):
             ey, ez, ly, lz = [edge_ref[s, part, k] for k in range(4)]
@@ -244,44 +273,100 @@
             one_[part, 0, depth] = e[0] - RELAX * (steps.down_y(high_y) + steps.down_z(high_z))
             one_[part, 1, depth] = e[1] + RELAX * high_y
             one_[part, 2, depth] = e[2] + RELAX * high_z
-            one_[part, 1, depth + 1] = received(high, part, 2) - relax_high * lz
-            one_[part, 2, depth + 1] = received(high, part, 3) + relax_high * ly
-
-        def sweep(ref, into, low_plane, planes_swept, k):
-            if low_plane < 0:
-                before = [(-ref[part, 2, 0], ref[part, 1, 0]) for part in range(2)]
-            else:
-                before = []
-                for part in range(2):
-                    e = [ref[part, comp, 0] for comp in range(3)]
-                    hy, hz = steps.magnetic_yz(e, [None, ref[part, 1, 1], ref[part, 2, 1]])
-                    before.append((hy + received(low, part, k), hz + received(low, part, k + 1)))
-            for p in range(low_plane, planes_swept):
-                relax = relax_low if p < 0 else relax_high if p == depth else F32(RELAX)
-                for part in range(2):
-                    e = [ref[part, comp, p + 1] if comp or p < depth else None for comp in range(3)]
-                    if p < depth:
-                        e_next = [None if comp == 0 else ref[part, comp, p + 2] for comp in range(3)]
-                        hy, hz = steps.magnetic_yz(e, e_next)
-                    else:
-                        hy, hz = received(high, part, 4) + e[2], received(high, part, 5) - e[1]
-                    hx = steps.magnetic_x(e)
-                    coef = scales[part] * conductivity(p)
-                    for comp in range(1 if p == depth else 0, 3):
-                        curl = steps.curl_back(comp, hx, hy, hz, before[part])
-                        into[part, comp, p + 1] = e[comp] - relax * curl + coef * ref[1 - part, comp, p + 1]
-                    if p < 0:
-                        hy, hz = hy + received(low, part, k), hz + received(low, part, k + 1)
-                    before[part] = hy, hz
-            point.add_to(into, 0, planes_swept, 1, lambda part, comp: scalar_ref[weights_at + part * 3 + comp])
-
-        sweep(one_, two_, -1, depth + 1, 2)
-        sweep(two_, one_, 0, depth, 4)
+            top_y = received(high, part, 2) - relax_high * lz
+            top_z = received(high, part, 3) + relax_high * ly
+            one_[part, 1, depth + 1] = top_y
+            one_[part, 2, depth + 1] = top_z
+            top_ref[s, part, 0] = top_y
+            top_ref[s, part, 1] = top_z
+
+        before = [(-one_[part, 2, 0], one_[part, 1, 0]) for part in range(2)]
+        for p in range(-1, depth):
+            relax = relax_low if p < 0 else F32(RELAX)
+            for part in range(2):
+                e = [one_[part, comp, p + 1] for comp in range(3)]
+                hy, hz = steps.magnetic_yz(e, [None, one_[part, 1, p + 2], one_[part, 2, p + 2]])
+                hx = steps.magnetic_x(e)
+                held = got[low, 2 * count * EARLY].astype(F32) if p < 0 else held_ref[p]
+                coef = scales[part] * held
+                for comp in range(3):
+                    curl = steps.curl_back(comp, hx, hy, hz, before[part])
+                    two_ref[s, part, comp, p + 1] = e[comp] - relax * curl + coef * one_[1 - part, comp, p + 1]
+                if p < 0:
+                    hy, hz = hy + received(low, part, 2), hz + received(low, part, 3)
+                before[part] = hy, hz
+        for part in range(2):
+            for k, f in enumerate(before[part]):
+                top_ref[s, part, 2 + k] = f
+        sources.point(s).add_to(two_ref.at[s], 0, depth, 1, functools.partial(sources.weight, s))
+        return 0
+
+    lax.fori_loop(0, count, one_source, 0)
+
+
+def sweep_three_kernel(
+    planes, scalar_ref, two_ref, top_ref, held_ref, field_ref, far_cond, near_cond, far_in, near_in,
+    rows_ref, far_ref, near_ref, above, last_, got, conds, sent,
+):
+    count, _, _, _, height, breadth = two_ref.shape
+    depth = held_ref.shape[0]
+    steps = Steps(height, breadth)
+    index = lax.axis_index("space")
+    first = index * depth
+    relax_high = jnp.where(first + depth < planes, F32(RELAX), F32(0.0))
+    low = index & 1
+    high = 1 - low
+    got[0] = far_in[...]
+    got[1] = near_in[...]
+    conds[0] = far_cond[2 * count * EARLY]
+    conds[1] = near_cond[2 * count * EARLY]
+    sources = Sources(scalar_ref, count, steps, first)
+
+    def one_source(s, _):
+        angular = sources.angular(s)
+        scales = RELAX * angular, -RELAX * angular
+        point = sources.point(s)
+        weight = functools.partial(sources.weight, s)
+
+        def received(side, part, k):
+            return got[side, (2 * s + part) * LATE + k].astype(F32)
+
+        held_above = conds[high].astype(F32)
+        for part in range(2):
+            ey, ez, hy_before, hz_before = [top_ref[s, part, k] for k in range(4)]
+            hy, hz = received(high, part, 0) + ez, received(high, part, 1) - ey
+            hx = steps.magnetic_x((None, ey, ez))
+            coef = scales[part] * held_above
+            for k, e in enumerate((ey, ez)):
+                curl = steps.curl_back(1 + k, hx, hy, hz, (hy_before, hz_before))
+                above[part, 1 + k, 0] = e - relax_high * curl + coef * top_ref[s, 1 - part, k]
+        point.add_to(above, depth, depth + 1, -depth, weight)
+
+        before = []
+        for part in range(2):
+            e = [two_ref[s, part, comp, 0] for comp in range(3)]
+            hy, hz = steps.magnetic_yz(e, [None, two_ref[s, part, 1, 1], two_ref[s, part, 2, 1]])
+            before.append((hy + received(low, part, 0), hz + received(low, part, 1)))
+        for p in range(depth):
+            for part in range(2):
+                e = [two_ref[s, part, comp, p + 1] for comp in range(3)]
+                if p < depth - 1:
+                    e_next = [None, two_ref[s, part, 1, p + 2], two_ref[s, part, 2, p + 2]]
+                else:
+                    e_next = [None, above[part, 1, 0], above[part, 2, 0]]
+                hy, hz = steps.magnetic_yz(e, e_next)
+                hx = steps.magnetic_x(e)
+                coef = scales[part] * held_ref[p]
+                for comp in range(3):
+                    curl = steps.curl_back(comp, hx, hy, hz, before[part])
+                    last_[part, comp, p] = e[comp] - RELAX * curl + coef * two_ref[s, 1 - part, comp, p + 1]
+                before[part] = hy, hz
+        point.add_to(last_, 0, depth, 0, weight)
 
         for p in range(depth):
             row_re = row_im = None
             for comp in range(3):
-                re, im = one_[0, comp, p + 1], one_[1, comp, p + 1]
+                re, im = last_[0, comp, p], last_[1, comp, p]
                 field_re, field_im = field_ref[s, 0, comp, p], field_ref[s, 1, comp, p]
                 add_re, add_im = field_re * re - field_im * im, field_re * im + field_im * re
                 row_re, row_im = (add_re, add_im) if comp == 0 else (row_re + add_re, row_im + add_im)
@@ -406,12 +491,13 @@
     far, near = [pairs + [(j, i) for i, j in pairs] for pairs in (far, near)]
     shape = jax.ShapeDtypeStruct
 
-    message = shape((2 * count * SENT + 1,) + plane, half)
+    early = shape((2 * count * EARLY + 1,) + plane, half)
+    late = shape((2 * count * LATE,) + plane, half)
     to_far, to_near, own, edge, held, field = pl.pallas_call(
         first_kernel,
         out_shape=(
-            message,
-            message,
+            early,
+            early,
             shape(warm_start.shape, F32),
             shape((count, 2, 4) + plane, F32),
             shape(conductivity.shape, F32),
@@ -425,31 +511,57 @@
             pltpu.SMEM(recv_cell.shape, jnp.int32),
             pltpu.SMEM(src_group.shape, jnp.int32),
             pltpu.SMEM(group_freq.shape, jnp.int32),
-            pltpu.VMEM((2,) + message.shape, half),
+            pltpu.VMEM((2,) + early.shape, half),
             pltpu.SemaphoreType.DMA((5 + 2 * count,)),
         ],
         compiler_params=KERNEL,
         name="first_sweep",
     )(*[in_hbm(x) for x in (warm_start, conductivity, background, data_weight, recv_cell, src_group, group_freq)])
-    from_far = lax.ppermute(to_far, "space", far)
-    from_near = lax.ppermute(to_near, "space", near)
+    far_early = lax.ppermute(to_far, "space", far)
+    near_early = lax.ppermute(to_near, "space", near)
+
+    to_far, to_near = pl.pallas_call(
+        second_kernel,
+        out_shape=(late, late),
+        in_specs=[SCALARS] + [FULL] * 2,
+        out_specs=(FULL,) * 2,
+        scratch_shapes=[pltpu.VMEM((2,) + late.shape, half)],
+        compiler_params=KERNEL,
+        name="late_message",
+    )(scalars, own, held)
+    far_late = lax.ppermute(to_far, "space", far)
+    near_late = lax.ppermute(to_near, "space", near)
+
+    two, top = pl.pallas_call(
+        functools.partial(sweep_two_kernel, peers * depth),
+        out_shape=(shape((count, 2, 3, depth + 1) + plane, F32), shape((count, 2, 4) + plane, F32)),
+        in_specs=[SCALARS] + [FULL] * 5,
+        out_specs=(FULL,) * 2,
+        scratch_shapes=[
+            pltpu.VMEM((2, 3, depth + 2) + plane, F32),
+            pltpu.VMEM((2,) + early.shape, half),
+        ],
+        compiler_params=KERNEL,
+        name="sweep_two",
+    )(scalars, own, edge, held, far_early, near_early)
 
     rows_of = shape((count, 2, depth) + plane, half)
     ends_of = shape((count, 2, REACH) + plane, half)
     rows, to_far, to_near = pl.pallas_call(
-        functools.partial(sweep_kernel, peers * depth),
+        functools.partial(sweep_three_kernel, peers * depth),
         out_shape=(rows_of, ends_of, ends_of),
-        in_specs=[SCALARS] + [FULL] * 6,
+        in_specs=[SCALARS] + [FULL] * 8,
         out_specs=(FULL,) * 3,
         scratch_shapes=[
-            pltpu.VMEM((2, 3, depth + 2) + plane, F32),
-            pltpu.VMEM((2, 3, depth + 2) + plane, F32),
-            pltpu.VMEM((2,) + message.shape, half),
+            pltpu.VMEM((2, 3, 1) + plane, F32),
+            pltpu.VMEM((2, 3, depth) + plane, F32),
+            pltpu.VMEM((2,) + late.shape, half),
+            pltpu.VMEM((2,) + plane, half),
             pltpu.VMEM((2,) + ends_of.shape, half),
         ],
         compiler_params=KERNEL,
-        name="sweeps",
-    )(scalars, own, edge, held, field, from_far, from_near)
+        name="sweep_three",
+    )(scalars, two, top, held, field, far_early, near_early, far_late, near_late)
     from_far = lax.ppermute(to_far, "space", far)
     from_near = lax.ppermute(to_near, "space", near)
     every = lax.all_gather(rows, "rx", axis=0)

time: 39.7 us -> 39.7 us (level)
  waiting for transfers between devices: 9.16 us -> 1.83 us
  starting transfers between devices: 10.2 us -> 15.7 us
  Pallas kernels: 5.52 us -> 7.38 us
    ppermute x0 -> x4, starting transfers between devices: none -> 11.4 us  [the longest x1 5.73 us: shards(): near_early = lax.ppermute(to_near, 'space', near)]
    ppermute x2 -> x1, waiting for transfers between devices: 9.15 us -> 0.2 us  [shards(): from_near = lax.ppermute(to_near, 'space', near)]
    ppermute x2 -> x1, starting transfers between devices: 8.88 us -> 3.67 us  [shards(): from_near = lax.ppermute(to_near, 'space', near)]
    pallas_call x2 -> x4, Pallas kernels: 3.81 us -> 5.67 us  [the longest x1 1.98 us: shards(): pl.pallas_call(first_kernel, out_shape=(early, early, shape(warm_start.sh...]
    ppermute x0 -> x4, waiting for transfers between devices: none -> 1.63 us  [the longest x1 1.07 us: shards(): near_late = lax.ppermute(to_near, 'space', near)]
    ppermute x2 -> x1, starting transfers between devices: 1.34 us -> 0.66 us  [shards(): from_far = lax.ppermute(to_far, 'space', far)]
  transfers between devices with their start and end apart: 4 -> 6, of which waited for: 2 -> 3; matrix products, arithmetic and copies ran while one was open for 1% -> 1% of each run, Pallas kernels for 2% -> 7%
where the time goes in v4:
time: 39.7 us; the launch traced here: 39.4 us
  starting transfers between devices  15.7 us (40%)
  blocking collectives  12.9 us (32%)
  Pallas kernels  7.38 us (19%)
  waiting for transfers between devices  1.83 us (5%)
  other arithmetic  0.76 us (2%)
  between operations  0.75 us (2%)
    all_to_all x1, blocking collectives, shards(): lax.all_to_all(partial_block, 'space', 0, 0, axis_index_groups=backwards)  11 us
    ppermute x1, starting transfers between devices, shards(): near_early = lax.ppermute(to_near, 'space', near)  5.73 us
    ppermute x1, starting transfers between devices, shards(): near_late = lax.ppermute(to_near, 'space', near)  4.29 us
    ppermute x1, starting transfers between devices, shards(): from_near = lax.ppermute(to_near, 'space', near)  3.67 us
    pallas_call x1, Pallas kernels, shards(): pl.pallas_call(first_kernel, out_shape=(early, early, shape(warm_start.sh...  1.98 us
    all_gather x1, blocking collectives, shards(): every = lax.all_gather(rows, 'rx', axis=0)  1.95 us
    pallas_call x1, Pallas kernels, shards(): pl.pallas_call(functools.partial(sweep_three_kernel, peers * depth), out_...  1.46 us
    pallas_call x1, Pallas kernels, shards(): pl.pallas_call(functools.partial(sweep_two_kernel, peers * depth), out_sh...  1.21 us
  transfers between devices with their start and end apart: 6, of which 3 were waited for; matrix products, arithmetic and copies ran while one was open for 1% of the time, Pallas kernels for 7%

profile of v4, /device:TPU:0, one launch (start us, length us, event | category | flops | bytes accessed | tf_op | source)
XLA Modules:
  0.0 39.4 jit_solution(15455097255962461231)
XLA Ops:
  0.6 0.0 copy-start
  0.6 0.0 copy-start.3
  0.7 0.0 copy-start.2
  0.7 0.0 copy-start.1
  0.7 2.0 %first_sweep.1 = (bf16[17,32,128]{2,1,0:T(8,128)(2,1)S(1)}, bf16[17,32,128]{2,1,0:T(8,128)(2,1)S(1)}, f32[2,2,3,3,32,128]{5,4,3,2,1,0:T(8,128)S(1)}, f32[2,2,4,3...) custom-call(f32[2,2,3,3,32,128]{5,4,3,2,1,0:T(8,128)} %start_ref.1, ...), custom_call_target="tpu_custom_call" | custom-call | tf_op jit(solution)/shard_map/first_sweep/pallas_call | solution.py:496
  2.7 0.7 %collective-permute-start = (bf16[17,32,128]{2,1,0:T(8,128)(2,1)S(1)}, bf16[17,32,128]{2,1,0:T(8,128)(2,1)S(1)}, u32[]{:S(2)}, u32[]{:S(2)}) collective-permute-start(bf16[17,32,128]{2,1,0:T(8,128)(2,1)S(1)} %get-tuple-element.20), channel_id=1, source_target_pairs={{1,2},{3,4},{5,6},{7,8},{9,10},{11,12},{13,14},{2,1},{4,3},{6,5},{... | collective-permute-start | bytes 417800 | tf_op jit(solution)/shard_map/ppermute | solution.py:520
  3.3 5.7 %collective-permute-start.1 = (bf16[17,32,128]{2,1,0:T(8,128)(2,1)S(1)}, bf16[17,32,128]{2,1,0:T(8,128)(2,1)S(1)}, u32[]{:S(2)}, u32[]{:S(2)}) collective-permute-start(bf16[17,32,128]{2,1,0:T(8,128)(2,1)S(1)} %get-tuple-element.21), channel_id=1, source_target_pairs={{0,1},{2,3},{4,5},{6,7},{8,9},{10,11},{12,13},{14,15},{1,0},{3,2},... | collective-permute-start | bytes 417800 | tf_op jit(solution)/shard_map/ppermute | solution.py:521
  9.1 0.0 copy-done.3
  9.1 0.0 copy-done.2
  9.1 0.0 copy-done.1
  9.1 0.1 add_convert_fusion
  9.2 0.0 copy-done
  9.2 0.1 reshape.7
  9.2 0.1 pad_maximum_fusion.scalar_ref
  9.3 1.0 %late_message.1 = (bf16[8,32,128]{2,1,0:T(8,128)(2,1)S(1)}, bf16[8,32,128]{2,1,0:T(8,128)(2,1)S(1)}) custom-call(f32[20]{0:T(128)S(1)} %pad_maximum_fusion.scalar_ref, f32[2,2,3,3,32,128]{5,4,3,2,1,0:T(8,128)S(1)} %get-tuple-element.17.own_ref, f32[3,32,128]{2,1,0:T(8,128)S(1)} %get-tuple-element.19.held_ref), custom_call_target="tpu_custom_call" | custom-call | tf_op jit(solution)/shard_map/late_message/pallas_call | solution.py:523
  10.3 0.7 %collective-permute-start.2 = (bf16[8,32,128]{2,1,0:T(8,128)(2,1)S(1)}, bf16[8,32,128]{2,1,0:T(8,128)(2,1)S(1)}, u32[]{:S(2)}, u32[]{:S(2)}) collective-permute-start(bf16[8,32,128]{2,1,0:T(8,128)(2,1)S(1)} %get-tuple-element.25), channel_id=1, source_target_pairs={{1,2},{3,4},{5,6},{7,8},{9,10},{11,12},{13,14},{2,1},{4,3},{6,5},{... | collective-permute-start | bytes 196616 | tf_op jit(solution)/shard_map/ppermute | solution.py:532
  11.0 4.3 %collective-permute-start.3 = (bf16[8,32,128]{2,1,0:T(8,128)(2,1)S(1)}, bf16[8,32,128]{2,1,0:T(8,128)(2,1)S(1)}, u32[]{:S(2)}, u32[]{:S(2)}) collective-permute-start(bf16[8,32,128]{2,1,0:T(8,128)(2,1)S(1)} %get-tuple-element.26), channel_id=1, source_target_pairs={{0,1},{2,3},{4,5},{6,7},{8,9},{10,11},{12,13},{14,15},{1,0},{3,2},... | collective-permute-start | bytes 196616 | tf_op jit(solution)/shard_map/ppermute | solution.py:533
  15.3 0.0 collective-permute-done.far_in.far_cond
  15.3 0.6 %collective-permute-done.1.near_in.near_cond = bf16[17,32,128]{2,1,0:T(8,128)(2,1)S(1)} collective-permute-done((bf16[17,32,128]{2,1,0:T(8,128)(2,1)S(1)}, bf16[17,32,128]{2,1,0:T(8,128)(2,1)S(1)}, u32[]{:S(2)}, u32[]{:S(2)}) %collective-permute-start.1) | collective-permute-done | bytes 139296 | tf_op jit(solution)/shard_map/ppermute | solution.py:521
  15.9 1.2 %sweep_two.1 = (f32[2,2,3,4,32,128]{5,4,3,2,1,0:T(8,128)S(1)}, f32[2,2,4,32,128]{4,3,2,1,0:T(8,128)S(1)}) custom-call(f32[20]{0:T(128)S(1)} %pad_maximum_fusion.scalar_ref, f32[2,2,3,3,32,128]{5,4,3,2,1,0:T(8,128)S(1)} %get-tuple-element.17.own_ref, f32[2,2,4,32,128]{4,3,2,1,0:T(8,128)S(1)} %get-tuple-element.18.edge_ref, ...), custom_call_target="tpu_custom_call" | custom-call | tf_op jit(solution)/shard_map/sweep_two/pallas_call | solution.py:535
  17.1 0.0 collective-permute-done.2.far_in
  17.1 1.1 %collective-permute-done.3.near_in = bf16[8,32,128]{2,1,0:T(8,128)(2,1)S(1)} collective-permute-done((bf16[8,32,128]{2,1,0:T(8,128)(2,1)S(1)}, bf16[8,32,128]{2,1,0:T(8,128)(2,1)S(1)}, u32[]{:S(2)}, u32[]{:S(2)}) %collective-permute-start.3) | collective-permute-done | bytes 65568 | tf_op jit(solution)/shard_map/ppermute | solution.py:533
  18.2 1.5 %sweep_three.1 = (bf16[2,2,3,32,128]{4,3,2,1,0:T(8,128)(2,1)S(1)}, bf16[2,2,2,32,128]{4,3,2,1,0:T(8,128)(2,1)S(1)}, bf16[2,2,2,32,128]{4,3,2,1,0:T(8,128)(2,1)S(1)}) custom-call(f32[20]{0:T(128)S(1)} %pad_maximum_fusion.scalar_ref, f32[2,2,3,4,32,128]{5,4,3,2,1,0:T(8,128)S(1)} %get-tuple-element.22.two_ref, ...), custom_call_target="tpu_custom_call" | custom-call | tf_op jit(solution)/shard_map/sweep_three/pallas_call | solution.py:550
  19.6 0.7 %collective-permute-start.4 = (bf16[2,2,2,32,128]{4,3,2,1,0:T(8,128)(2,1)S(1)}, bf16[2,2,2,32,128]{4,3,2,1,0:T(8,128)(2,1)S(1)}, u32[]{:S(2)}, u32[]{:S(2)}) collective-permute-start(bf16[2,2,2,32,128]{4,3,2,1,0:T(8,128)(2,1)S(1)} %get-tuple-element.28), channel_id=1, source_target_pairs={{1,2},{3,4},{5,6},{7,8},{9,10},{11,12},{13,14},{2,1},{4,3},{6,5},{... | collective-permute-start | bytes 196616 | tf_op jit(solution)/shard_map/ppermute | solution.py:565
  20.3 3.7 %collective-permute-start.5 = (bf16[2,2,2,32,128]{4,3,2,1,0:T(8,128)(2,1)S(1)}, bf16[2,2,2,32,128]{4,3,2,1,0:T(8,128)(2,1)S(1)}, u32[]{:S(2)}, u32[]{:S(2)}) collective-permute-start(bf16[2,2,2,32,128]{4,3,2,1,0:T(8,128)(2,1)S(1)} %get-tuple-element.29), channel_id=1, source_target_pairs={{0,1},{2,3},{4,5},{6,7},{8,9},{10,11},{12,13},{14,15},{1,0},{3,2},... | collective-permute-start | bytes 196616 | tf_op jit(solution)/shard_map/ppermute | solution.py:566
  24.0 0.7 %smooth.1.alone_ref = f32[2,2,3,32,128]{4,3,2,1,0:T(8,128)S(1)} custom-call(bf16[2,2,3,32,128]{4,3,2,1,0:T(8,128)(2,1)S(1)} %get-tuple-element.27.rows_ref), custom_call_target="tpu_custom_call" | custom-call | tf_op jit(solution)/shard_map/smooth/pallas_call | solution.py:570
  24.7 1.9 %all-gather = bf16[4,2,3,32,128]{4,3,2,1,0:T(8,128)(2,1)S(1)} all-gather(bf16[2,2,3,32,128]{4,3,2,1,0:T(8,128)(2,1)S(1)} %get-tuple-element.27.rows_ref), channel_id=2, replica_groups=mesh['rx'=2,'space'=16] {'rx'}, dimensions={0}, use_global_device_ids=true | all-gather | bytes 294912 | tf_op jit(solution)/shard_map/all_gather | solution.py:567
  26.6 0.0 collective-permute-done.4.far_in
  26.6 0.2 collective-permute-done.5.near_in
  26.8 1.0 %block.1 = (bf16[2,2,3,32,128]{4,3,2,1,0:T(8,128)(2,1)}, f32[16,4,8]{2,1,0:T(4,128)S(1)}) custom-call(bf16[2,2,3,32,128]{4,3,2,1,0:T(8,128)(2,1)S(1)} %get-tuple-element.27.rows_ref, f32[2,2,3,32,128]{4,3,2,1,0:T(8,128)S(1)} %smooth.1.alone_ref, bf16[2,2,2,32,128]{4,3,2,1,0:T(8,128)(2,1)S(1)} %collective-permute-done.4.far_in, ...), custom_call_target="tpu_custom_call" | custom-call | tf_op jit(solution)/shard_map/block/pallas_call | solution.py:578
  27.9 11.0 %all_to_all.5 = f32[16,4,8]{2,1,0:T(4,128)S(1)} all-to-all(f32[16,4,8]{2,1,0:T(4,128)S(1)} %get-tuple-element.30), channel_id=1, replica_groups={{15,14,13,12,11,10,9,8,7,6,5,4,3,2,1,0},{31,30,29,28,27,26,25,24,23,22,..., dimensions={0} | all-to-all | bytes 4096 | tf_op jit(solution)/shard_map/all_to_all | solution.py:593
  38.8 0.6 %reduce_sum.9 = f32[4,8]{1,0:T(4,128)} reduce(f32[16,4,8]{2,1,0:T(4,128)S(1)} %all_to_all.5, f32[]{:T(128)} %constant.0.clone.1), dimensions={0}, to_apply=%region_0.0 | reduce | flops 480 | bytes 2180 | tf_op jit(solution)/shard_map/reduce_sum | solution.py:594
Async XLA Ops:
  0.6 8.5 %copy-start = (f32[2,2,3]{2,1,0:T(2,128)S(1)}, f32[2,2,3]{2,1,0:T(2,128)}, u32[]{:S(2)}) copy-start(f32[2,2,3]{2,1,0:T(2,128)} %weight_ref.1) | copy-start | bytes 148
  0.6 8.4 %copy-start.3 = (s32[2]{0:T(128)S(1)}, s32[2]{0:T(128)}, u32[]{:S(2)}) copy-start(s32[2]{0:T(128)} %cell_ref.1) | copy-start | bytes 28
  0.7 8.4 %copy-start.2 = (s32[2]{0:T(128)S(1)}, s32[2]{0:T(128)}, u32[]{:S(2)}) copy-start(s32[2]{0:T(128)} %group_ref.1) | copy-start | bytes 28
  0.7 8.4 %copy-start.1 = (s32[4]{0:T(128)S(1)}, s32[4]{0:T(128)}, u32[]{:S(2)}) copy-start(s32[4]{0:T(128)} %freq_ref.1) | copy-start | bytes 52
  2.7 12.6 %collective-permute-start = (bf16[17,32,128]{2,1,0:T(8,128)(2,1)S(1)}, bf16[17,32,128]{2,1,0:T(8,128)(2,1)S(1)}, u32[]{:S(2)}, u32[]{:S(2)}) collective-permute-start(bf16[17,32,128]{2,1,0:T(8,128)(2,1)S(1)} %get-tuple-element.20), channel_id=1, source_target_pairs={{1,2},{3,4},{5,6},{7,8},{9,10},{11,12},{13,14},{2,1},{4,3},{6,5},{... | collective-permute-start | bytes 417800 | tf_op jit(solution)/shard_map/ppermute | solution.py:520
  3.3 12.5 %collective-permute-start.1 = (bf16[17,32,128]{2,1,0:T(8,128)(2,1)S(1)}, bf16[17,32,128]{2,1,0:T(8,128)(2,1)S(1)}, u32[]{:S(2)}, u32[]{:S(2)}) collective-permute-start(bf16[17,32,128]{2,1,0:T(8,128)(2,1)S(1)} %get-tuple-element.21), channel_id=1, source_target_pairs={{0,1},{2,3},{4,5},{6,7},{8,9},{10,11},{12,13},{14,15},{1,0},{3,2},... | collective-permute-start | bytes 417800 | tf_op jit(solution)/shard_map/ppermute | solution.py:521
  10.3 6.7 %collective-permute-start.2 = (bf16[8,32,128]{2,1,0:T(8,128)(2,1)S(1)}, bf16[8,32,128]{2,1,0:T(8,128)(2,1)S(1)}, u32[]{:S(2)}, u32[]{:S(2)}) collective-permute-start(bf16[8,32,128]{2,1,0:T(8,128)(2,1)S(1)} %get-tuple-element.25), channel_id=1, source_target_pairs={{1,2},{3,4},{5,6},{7,8},{9,10},{11,12},{13,14},{2,1},{4,3},{6,5},{... | collective-permute-start | bytes 196616 | tf_op jit(solution)/shard_map/ppermute | solution.py:532
  11.0 7.1 %collective-permute-start.3 = (bf16[8,32,128]{2,1,0:T(8,128)(2,1)S(1)}, bf16[8,32,128]{2,1,0:T(8,128)(2,1)S(1)}, u32[]{:S(2)}, u32[]{:S(2)}) collective-permute-start(bf16[8,32,128]{2,1,0:T(8,128)(2,1)S(1)} %get-tuple-element.26), channel_id=1, source_target_pairs={{0,1},{2,3},{4,5},{6,7},{8,9},{10,11},{12,13},{14,15},{1,0},{3,2},... | collective-permute-start | bytes 196616 | tf_op jit(solution)/shard_map/ppermute | solution.py:533
  19.6 7.0 %collective-permute-start.4 = (bf16[2,2,2,32,128]{4,3,2,1,0:T(8,128)(2,1)S(1)}, bf16[2,2,2,32,128]{4,3,2,1,0:T(8,128)(2,1)S(1)}, u32[]{:S(2)}, u32[]{:S(2)}) collective-permute-start(bf16[2,2,2,32,128]{4,3,2,1,0:T(8,128)(2,1)S(1)} %get-tuple-element.28), channel_id=1, source_target_pairs={{1,2},{3,4},{5,6},{7,8},{9,10},{11,12},{13,14},{2,1},{4,3},{6,5},{... | collective-permute-start | bytes 196616 | tf_op jit(solution)/shard_map/ppermute | solution.py:565
  20.3 6.5 %collective-permute-start.5 = (bf16[2,2,2,32,128]{4,3,2,1,0:T(8,128)(2,1)S(1)}, bf16[2,2,2,32,128]{4,3,2,1,0:T(8,128)(2,1)S(1)}, u32[]{:S(2)}, u32[]{:S(2)}) collective-permute-start(bf16[2,2,2,32,128]{4,3,2,1,0:T(8,128)(2,1)S(1)} %get-tuple-element.29), channel_id=1, source_target_pairs={{0,1},{2,3},{4,5},{6,7},{8,9},{10,11},{12,13},{14,15},{1,0},{3,2},... | collective-permute-start | bytes 196616 | tf_op jit(solution)/shard_map/ppermute | solution.py:566

commit v5 on v3

--- a/solution.py
+++ b/solution.py
@@ -89,17 +89,15 @@
         self.rows = pl.ds(pl.multiple_of(block * 8, 8), 8)
         self.row, self.sub, self.lane, self.steps = row, sub, lane, steps
 
-    def spread(self, value):
+    def add_to(self, ref, low, high, shift, weight):
+        reached = (self.plane >= low) & (self.plane < high)
         here = (self.steps.sub == self.sub) & (self.steps.lane[:8] == self.lane)
-        return jnp.where(here, RELAX * value, 0.0)
-
-    def add_to(self, ref, low, high, shift, weight):
-        @pl.when((self.plane >= low) & (self.plane < high))
-        def _():
-            for part in range(2):
-                for comp in range(3):
-                    at = (part, comp, self.plane + shift, self.rows)
-                    ref[at] = ref[at] + self.spread(weight(part, comp))
+        amount = jnp.where(here, jnp.where(reached, F32(RELAX), F32(0.0)), 0.0)
+        plane = jnp.clip(self.plane, low, high - 1) + shift
+        for part in range(2):
+            for comp in range(3):
+                at = (part, comp, plane, self.rows)
+                ref[at] = ref[at] + amount * weight(part, comp)
 
 
 def first_kernel(
@@ -244,6 +242,7 @@
             one_[part, 0, depth] = e[0] - RELAX * (steps.down_y(high_y) + steps.down_z(high_z))
             one_[part, 1, depth] = e[1] + RELAX * high_y
             one_[part, 2, depth] = e[2] + RELAX * high_z
+            two_[part, 0, depth + 1] = jnp.zeros((height, breadth), F32)
             one_[part, 1, depth + 1] = received(high, part, 2) - relax_high * lz
             one_[part, 2, depth + 1] = received(high, part, 3) + relax_high * ly
 
@@ -312,8 +311,7 @@
     below = jnp.where(first > 0, F32(KAPPA), F32(0.0))
     above = jnp.where(first + depth < planes, F32(KAPPA), F32(0.0))
 
-    def one_row(i, _):
-        s, part = i >> 1, i & 1
+    def one_row(s, part):
         value = [rows_ref[s, part, p].astype(F32) for p in range(depth)]
         once = []
         for p in range(depth):
@@ -322,9 +320,13 @@
         once = [below * value[0]] + once + [above * value[-1]]
         for p in range(depth):
             alone_ref[s, part, p] = in_plane(steps, once[p + 1]) + KAPPA * (once[p] + once[p + 2])
+
+    def one_source(s, _):
+        for part in range(2):
+            one_row(s, part)
         return 0
 
-    lax.fori_loop(0, 2 * count, one_row, 0)
+    lax.fori_loop(0, count, one_source, 0)
 
 
 def block_kernel(cells, rows_ref, alone_ref, far_in, near_in, all_ref, smooth_ref, block_ref, got, rounded, sums, sem):
@@ -337,8 +339,7 @@
     odd = lax.axis_index("space") & 1
     low, high = odd, 1 - odd
 
-    def one_row(i, _):
-        s, part = i >> 1, i & 1
+    def one_row(s, part):
         value = [alone_ref[s, part, p] for p in range(depth)]
         for side, nearest, order in ((low, REACH - 1, 1), (high, 0, -1)):
             close = got[side, s, part, nearest].astype(F32)
@@ -348,9 +349,13 @@
             value[end + order] = value[end + order] + KAPPA * KAPPA * close
         for p in range(depth):
             rounded[s, part, p] = value[p].astype(rounded.dtype)
+
+    def one_source(s, _):
+        for part in range(2):
+            one_row(s, part)
         return 0
 
-    lax.fori_loop(0, 2 * count, one_row, 0)
+    lax.fori_loop(0, count, one_source, 0)
     out = pltpu.make_async_copy(rounded, smooth_ref, sem)
     out.start()
 

time: 39.7 us -> 39.5 us (level)
  Pallas kernels: 5.52 us -> 5.11 us
  transfers between devices with their start and end apart: 4 -> 4, of which waited for: 2 -> 2; matrix products, arithmetic and copies ran while one was open for 1% -> 1% of each run, Pallas kernels for 2% -> 1%
where the time goes in v5:
time: 39.5 us; the launch traced here: 39.3 us
  blocking collectives  13 us (33%)
  starting transfers between devices  10.2 us (26%)
  waiting for transfers between devices  9.44 us (24%)
  Pallas kernels  5.11 us (13%)
  other arithmetic  0.76 us (2%)
  between operations  0.72 us (2%)
    all_to_all x1, blocking collectives, shards(): lax.all_to_all(partial_block, 'space', 0, 0, axis_index_groups=backwards)  11 us
    ppermute x2, waiting for transfers between devices, shards(): from_near = lax.ppermute(to_near, 'space', near)  9.44 us
    ppermute x2, starting transfers between devices, shards(): from_near = lax.ppermute(to_near, 'space', near)  8.89 us
    pallas_call x1, Pallas kernels, shards(): pl.pallas_call(first_kernel, out_shape=(message, message, shape(warm_star...  2 us
    all_gather x1, blocking collectives, shards(): every = lax.all_gather(rows, 'rx', axis=0)  1.95 us
    pallas_call x1, Pallas kernels, shards(): pl.pallas_call(functools.partial(sweep_kernel, peers * depth), out_shape=...  1.83 us
    ppermute x2, starting transfers between devices, shards(): from_far = lax.ppermute(to_far, 'space', far)  1.34 us
    pallas_call x1, Pallas kernels, shards(): pl.pallas_call(functools.partial(block_kernel, cells), out_shape=(rows_of...  0.87 us
  transfers between devices with their start and end apart: 4, of which 2 were waited for; matrix products, arithmetic and copies ran while one was open for 1% of the time, Pallas kernels for 1%

profile of v5, /device:TPU:0, one launch (start us, length us, event | category | flops | bytes accessed | tf_op | source)
XLA Modules:
  0.0 39.3 jit_solution(13613539353283904772)
XLA Ops:
  0.6 0.0 copy-start.1
  0.6 0.0 copy-start.2
  0.7 0.0 copy-start.3
  0.7 0.0 copy-start
  0.7 2.0 %first_sweep.1 = (bf16[25,32,128]{2,1,0:T(8,128)(2,1)S(1)}, bf16[25,32,128]{2,1,0:T(8,128)(2,1)S(1)}, f32[2,2,3,3,32,128]{5,4,3,2,1,0:T(8,128)S(1)}, f32[2,2,4,3...) custom-call(f32[2,2,3,3,32,128]{5,4,3,2,1,0:T(8,128)} %start_ref.1, ...), custom_call_target="tpu_custom_call" | custom-call | tf_op jit(solution)/shard_map/first_sweep/pallas_call | solution.py:415
  2.7 0.7 %collective-permute-start = (bf16[25,32,128]{2,1,0:T(8,128)(2,1)S(1)}, bf16[25,32,128]{2,1,0:T(8,128)(2,1)S(1)}, u32[]{:S(2)}, u32[]{:S(2)}) collective-permute-start(bf16[25,32,128]{2,1,0:T(8,128)(2,1)S(1)} %get-tuple-element.17), channel_id=1, source_target_pairs={{1,2},{3,4},{5,6},{7,8},{9,10},{11,12},{13,14},{2,1},{4,3},{6,5},{... | collective-permute-start | bytes 614408 | tf_op jit(solution)/shard_map/ppermute | solution.py:439
  3.4 5.7 %collective-permute-start.1 = (bf16[25,32,128]{2,1,0:T(8,128)(2,1)S(1)}, bf16[25,32,128]{2,1,0:T(8,128)(2,1)S(1)}, u32[]{:S(2)}, u32[]{:S(2)}) collective-permute-start(bf16[25,32,128]{2,1,0:T(8,128)(2,1)S(1)} %get-tuple-element.18), channel_id=1, source_target_pairs={{0,1},{2,3},{4,5},{6,7},{8,9},{10,11},{12,13},{14,15},{1,0},{3,2},... | collective-permute-start | bytes 614408 | tf_op jit(solution)/shard_map/ppermute | solution.py:440
  9.1 0.0 copy-done
  9.1 0.1 reshape.7
  9.2 0.0 copy-done.1
  9.2 0.0 copy-done.2
  9.2 0.0 copy-done.3
  9.2 0.1 add_convert_fusion
  9.3 0.1 pad_maximum_fusion.scalar_ref
  9.3 0.0 collective-permute-done.far_in
  9.3 8.8 %collective-permute-done.1.near_in = bf16[25,32,128]{2,1,0:T(8,128)(2,1)S(1)} collective-permute-done((bf16[25,32,128]{2,1,0:T(8,128)(2,1)S(1)}, bf16[25,32,128]{2,1,0:T(8,128)(2,1)S(1)}, u32[]{:S(2)}, u32[]{:S(2)}) %collective-permute-start.1) | collective-permute-done | bytes 204832 | tf_op jit(solution)/shard_map/ppermute | solution.py:440
  18.2 1.8 %sweeps.1 = (bf16[2,2,3,32,128]{4,3,2,1,0:T(8,128)(2,1)S(1)}, bf16[2,2,2,32,128]{4,3,2,1,0:T(8,128)(2,1)S(1)}, bf16[2,2,2,32,128]{4,3,2,1,0:T(8,128)(2,1)S(1)}) custom-call(f32[20]{0:T(128)S(1)} %pad_maximum_fusion.scalar_ref, f32[2,2,3,3,32,128]{5,4,3,2,1,0:T(8,128)S(1)} %get-tuple-element.13.own_ref, f32[2,2,4,32,128]{4,3,2,1,0:T(8,128)S(1)} %get-tuple-element.14.edge_ref, ...), custom_call_target="tpu_custom_call" | custom-call | tf_op jit(solution)/shard_map/sweeps/pallas_call | solution.py:444
  20.0 0.7 %collective-permute-start.2 = (bf16[2,2,2,32,128]{4,3,2,1,0:T(8,128)(2,1)S(1)}, bf16[2,2,2,32,128]{4,3,2,1,0:T(8,128)(2,1)S(1)}, u32[]{:S(2)}, u32[]{:S(2)}) collective-permute-start(bf16[2,2,2,32,128]{4,3,2,1,0:T(8,128)(2,1)S(1)} %get-tuple-element.20), channel_id=1, source_target_pairs={{1,2},{3,4},{5,6},{7,8},{9,10},{11,12},{13,14},{2,1},{4,3},{6,5},{... | collective-permute-start | bytes 196616 | tf_op jit(solution)/shard_map/ppermute | solution.py:458
  20.7 3.2 %collective-permute-start.3 = (bf16[2,2,2,32,128]{4,3,2,1,0:T(8,128)(2,1)S(1)}, bf16[2,2,2,32,128]{4,3,2,1,0:T(8,128)(2,1)S(1)}, u32[]{:S(2)}, u32[]{:S(2)}) collective-permute-start(bf16[2,2,2,32,128]{4,3,2,1,0:T(8,128)(2,1)S(1)} %get-tuple-element.21), channel_id=1, source_target_pairs={{0,1},{2,3},{4,5},{6,7},{8,9},{10,11},{12,13},{14,15},{1,0},{3,2},... | collective-permute-start | bytes 196616 | tf_op jit(solution)/shard_map/ppermute | solution.py:459
  23.8 0.4 %smooth.1.alone_ref = f32[2,2,3,32,128]{4,3,2,1,0:T(8,128)S(1)} custom-call(bf16[2,2,3,32,128]{4,3,2,1,0:T(8,128)(2,1)S(1)} %get-tuple-element.19.rows_ref), custom_call_target="tpu_custom_call" | custom-call | tf_op jit(solution)/shard_map/smooth/pallas_call | solution.py:463
  24.3 1.9 %all-gather = bf16[4,2,3,32,128]{4,3,2,1,0:T(8,128)(2,1)S(1)} all-gather(bf16[2,2,3,32,128]{4,3,2,1,0:T(8,128)(2,1)S(1)} %get-tuple-element.19.rows_ref), channel_id=2, replica_groups=mesh['rx'=2,'space'=16] {'rx'}, dimensions={0}, use_global_device_ids=true | all-gather | bytes 294912 | tf_op jit(solution)/shard_map/all_gather | solution.py:460
  26.2 0.0 collective-permute-done.2.far_in
  26.2 0.6 %collective-permute-done.3.near_in = bf16[2,2,2,32,128]{4,3,2,1,0:T(8,128)(2,1)S(1)} collective-permute-done((bf16[2,2,2,32,128]{4,3,2,1,0:T(8,128)(2,1)S(1)}, bf16[2,2,2,32,128]{4,3,2,1,0:T(8,128)(2,1)S(1)}, u32[]{:S(2)}, u32[]{:S(2)}) %collective-permute-start.3) | collective-permute-done | bytes 65568 | tf_op jit(solution)/shard_map/ppermute | solution.py:459
  26.8 0.9 %block.1 = (bf16[2,2,3,32,128]{4,3,2,1,0:T(8,128)(2,1)}, f32[16,4,8]{2,1,0:T(4,128)S(1)}) custom-call(bf16[2,2,3,32,128]{4,3,2,1,0:T(8,128)(2,1)S(1)} %get-tuple-element.19.rows_ref, f32[2,2,3,32,128]{4,3,2,1,0:T(8,128)S(1)} %smooth.1.alone_ref, bf16[2,2,2,32,128]{4,3,2,1,0:T(8,128)(2,1)S(1)} %collective-permute-done.2.far_in, ...), custom_call_target="tpu_custom_call" | custom-call | tf_op jit(solution)/shard_map/block/pallas_call | solution.py:471
  27.7 11.0 %all_to_all.5 = f32[16,4,8]{2,1,0:T(4,128)S(1)} all-to-all(f32[16,4,8]{2,1,0:T(4,128)S(1)} %get-tuple-element.22), channel_id=1, replica_groups={{15,14,13,12,11,10,9,8,7,6,5,4,3,2,1,0},{31,30,29,28,27,26,25,24,23,22,..., dimensions={0} | all-to-all | bytes 4096 | tf_op jit(solution)/shard_map/all_to_all | solution.py:486
  38.7 0.6 %reduce_sum.9 = f32[4,8]{1,0:T(4,128)} reduce(f32[16,4,8]{2,1,0:T(4,128)S(1)} %all_to_all.5, f32[]{:T(128)} %constant.0.clone.1), dimensions={0}, to_apply=%region_0.0 | reduce | flops 480 | bytes 2180 | tf_op jit(solution)/shard_map/reduce_sum | solution.py:487
Async XLA Ops:
  0.6 8.5 %copy-start.1 = (s32[4]{0:T(128)S(1)}, s32[4]{0:T(128)}, u32[]{:S(2)}) copy-start(s32[4]{0:T(128)} %freq_ref.1) | copy-start | bytes 52
  0.6 8.5 %copy-start.2 = (s32[2]{0:T(128)S(1)}, s32[2]{0:T(128)}, u32[]{:S(2)}) copy-start(s32[2]{0:T(128)} %group_ref.1) | copy-start | bytes 28
  0.7 8.5 %copy-start.3 = (s32[2]{0:T(128)S(1)}, s32[2]{0:T(128)}, u32[]{:S(2)}) copy-start(s32[2]{0:T(128)} %cell_ref.1) | copy-start | bytes 28
  0.7 8.4 %copy-start = (f32[2,2,3]{2,1,0:T(2,128)S(1)}, f32[2,2,3]{2,1,0:T(2,128)}, u32[]{:S(2)}) copy-start(f32[2,2,3]{2,1,0:T(2,128)} %weight_ref.1) | copy-start | bytes 148
  2.7 6.7 %collective-permute-start = (bf16[25,32,128]{2,1,0:T(8,128)(2,1)S(1)}, bf16[25,32,128]{2,1,0:T(8,128)(2,1)S(1)}, u32[]{:S(2)}, u32[]{:S(2)}) collective-permute-start(bf16[25,32,128]{2,1,0:T(8,128)(2,1)S(1)} %get-tuple-element.17), channel_id=1, source_target_pairs={{1,2},{3,4},{5,6},{7,8},{9,10},{11,12},{13,14},{2,1},{4,3},{6,5},{... | collective-permute-start | bytes 614408 | tf_op jit(solution)/shard_map/ppermute | solution.py:439
  3.4 14.8 %collective-permute-start.1 = (bf16[25,32,128]{2,1,0:T(8,128)(2,1)S(1)}, bf16[25,32,128]{2,1,0:T(8,128)(2,1)S(1)}, u32[]{:S(2)}, u32[]{:S(2)}) collective-permute-start(bf16[25,32,128]{2,1,0:T(8,128)(2,1)S(1)} %get-tuple-element.18), channel_id=1, source_target_pairs={{0,1},{2,3},{4,5},{6,7},{8,9},{10,11},{12,13},{14,15},{1,0},{3,2},... | collective-permute-start | bytes 614408 | tf_op jit(solution)/shard_map/ppermute | solution.py:440
  20.0 6.2 %collective-permute-start.2 = (bf16[2,2,2,32,128]{4,3,2,1,0:T(8,128)(2,1)S(1)}, bf16[2,2,2,32,128]{4,3,2,1,0:T(8,128)(2,1)S(1)}, u32[]{:S(2)}, u32[]{:S(2)}) collective-permute-start(bf16[2,2,2,32,128]{4,3,2,1,0:T(8,128)(2,1)S(1)} %get-tuple-element.20), channel_id=1, source_target_pairs={{1,2},{3,4},{5,6},{7,8},{9,10},{11,12},{13,14},{2,1},{4,3},{6,5},{... | collective-permute-start | bytes 196616 | tf_op jit(solution)/shard_map/ppermute | solution.py:458
  20.7 6.1 %collective-permute-start.3 = (bf16[2,2,2,32,128]{4,3,2,1,0:T(8,128)(2,1)S(1)}, bf16[2,2,2,32,128]{4,3,2,1,0:T(8,128)(2,1)S(1)}, u32[]{:S(2)}, u32[]{:S(2)}) collective-permute-start(bf16[2,2,2,32,128]{4,3,2,1,0:T(8,128)(2,1)S(1)} %get-tuple-element.21), channel_id=1, source_target_pairs={{0,1},{2,3},{4,5},{6,7},{8,9},{10,11},{12,13},{14,15},{1,0},{3,2},... | collective-permute-start | bytes 196616 | tf_op jit(solution)/shard_map/ppermute | solution.py:459

commit v6 on v5

--- a/solution.py
+++ b/solution.py
@@ -102,17 +102,18 @@
 
 def first_kernel(
     start_ref, cond_ref, back_ref, weight_ref, cell_ref, group_ref, freq_ref,
-    far_ref, near_ref, own_ref, edge_ref, held_ref, field_ref,
-    raw, weight, cell, group, freq, sent, sems,
+    *refs,
 ):
     count, _, _, depth, height, breadth = start_ref.shape
+    fars, nears = refs[:count], refs[count : 2 * count]
+    own_ref, edge_ref, held_ref, field_ref, raw, weight, cell, group, freq, sent, sems = refs[2 * count :]
     pairs = ((group_ref, group), (freq_ref, freq), (cell_ref, cell), (weight_ref, weight), (cond_ref, held_ref))
     copies = [pltpu.make_async_copy(a, b, sems.at[k]) for k, (a, b) in enumerate(pairs)]
 
     def start_of(s):
         return pltpu.make_async_copy(start_ref.at[s], raw.at[s], sems.at[len(pairs) + s])
 
-    for copy in copies + [start_of(s) for s in range(count)]:
+    for copy in [start_of(0)] + copies + [start_of(s) for s in range(1, count)]:
         copy.start()
     copies[0].wait()
     fields = [
@@ -124,27 +125,26 @@
     for copy in copies[1:]:
         copy.wait()
     steps = Steps(height, breadth)
-    half = far_ref.dtype
+    half = sent.dtype
     index = lax.axis_index("space")
     first = index * depth
     down = index & 1
     up = 1 - down
     row = lax.broadcasted_iota(jnp.int32, (height, breadth), 0)
     last = depth - 1
-    sent[up, 2 * count * SENT] = held_ref[last].astype(half)
-    sent[down, 2 * count * SENT] = held_ref[0].astype(half)
+    sent[up, 0, 2 * SENT] = held_ref[last].astype(half)
+    sent[down, 0, 2 * SENT] = held_ref[0].astype(half)
 
     def one_source(s, _):
         start_of(s).wait()
         scale = RELAX * angular_of(freq[group[s]])
         scales = scale, -scale
         point = Point(cell[s], first, steps)
-        base = 2 * s * SENT
         before = []
         for part in range(2):
             ey, ez = raw[s, part, 1, 0], raw[s, part, 2, 0]
             for k, f in enumerate((ey, ez)):
-                sent[down, base + part * SENT + k] = f.astype(half)
+                sent[down, s, part * SENT + k] = f.astype(half)
                 edge_ref[s, part, k] = f
             before.append((-ez, ey))
         for p in range(depth):
@@ -156,7 +156,7 @@
                 hy, hz = steps.magnetic_yz(e, e_next)
                 if p == last:
                     for k, f in enumerate((hy, hz)):
-                        sent[up, base + part * SENT + k] = f.astype(half)
+                        sent[up, s, part * SENT + k] = f.astype(half)
                         edge_ref[s, part, 2 + k] = f
                 hx = steps.magnetic_x(e)
                 coef = scales[part] * held_ref[p]
@@ -172,7 +172,7 @@
             ex, ey, ez = [own_ref[s, part, comp, 0] for comp in range(3)]
             hy, hz = steps.up_z(ex) - own_ref[s, part, 2, 1], own_ref[s, part, 1, 1] - steps.up_y(ex)
             for k, f in enumerate((ey, ez, hy, hz)):
-                sent[down, base + part * SENT + 2 + k] = f.astype(half)
+                sent[down, s, part * SENT + 2 + k] = f.astype(half)
             e = [own_ref[s, part, comp, last] for comp in range(3)]
             behind = steps.magnetic_yz([own_ref[s, part, comp, last - 1] for comp in range(3)], e)
             hy, hz = steps.magnetic_yz(e, None)
@@ -184,119 +184,140 @@
                 value = e[comp] - RELAX * curl + coef * own_ref[s, 1 - part, comp, last]
                 after.append(value + here * weight[s, part, comp])
             for k, f in enumerate((hy, hz) + steps.magnetic_yz(after, None)):
-                sent[up, base + part * SENT + 2 + k] = f.astype(half)
+                sent[up, s, part * SENT + 2 + k] = f.astype(half)
         return 0
 
     lax.fori_loop(0, count, one_source, 0)
-    far_ref[...] = sent[0]
-    near_ref[...] = sent[1]
+    for s in range(count):
+        fars[s][...] = sent[0, s, : fars[s].shape[0]]
+        nears[s][...] = sent[1, s, : nears[s].shape[0]]
     for copy in fields:
         copy.wait()
 
 
-def sweep_kernel(
-    planes, scalar_ref, own_ref, edge_ref, held_ref, field_ref, far_in, near_in, rows_ref, far_ref, near_ref, one_, two_, got, sent,
-):
+def sweep_kernel(s, planes, scalar_ref, own_ref, edge_ref, held_ref, field_ref, far_in, near_in, far_cond, near_cond, *refs):
     count, _, _, depth, height, breadth = own_ref.shape
+    final = s == count - 1
+    if final:
+        earlier = refs[:s]
+        rows_ref, far_ref, near_ref, one_, two_, got, conds, sent = refs[s:]
+    else:
+        rows_ref, one_, two_, got, conds = refs
     steps = Steps(height, breadth)
     index = lax.axis_index("space")
     first = index * depth
     relax_low = jnp.where(first > 0, F32(RELAX), F32(0.0))
     relax_high = jnp.where(first + depth < planes, F32(RELAX), F32(0.0))
-    odd = index & 1
-    low, high = odd, 1 - odd
-    got[0] = far_in[...]
-    got[1] = near_in[...]
+    low = index & 1
+    high = 1 - low
+    got[0] = far_in[: 2 * SENT]
+    got[1] = near_in[: 2 * SENT]
+    conds[0] = far_cond[2 * SENT]
+    conds[1] = near_cond[2 * SENT]
+    group = scalar_ref[count + s].astype(jnp.int32)
+    angular = angular_of(scalar_ref[2 * count + group].astype(jnp.int32))
+    scales = RELAX * angular, -RELAX * angular
+    point = Point(scalar_ref[s].astype(jnp.int32), first, steps)
+    weights_at = scalar_ref.shape[0] - 6 * count + 6 * s
 
     def conductivity(p):
         if p < 0:
-            return got[low, 2 * count * SENT].astype(F32)
+            return conds[low].astype(F32)
         if p >= depth:
-            return got[high, 2 * count * SENT].astype(F32)
+            return conds[high].astype(F32)
         return held_ref[p]
 
-    def one_source(s, _):
-        group = scalar_ref[count + s].astype(jnp.int32)
-        angular = angular_of(scalar_ref[2 * count + group].astype(jnp.int32))
-        scales = RELAX * angular, -RELAX * angular
-        point = Point(scalar_ref[s].astype(jnp.int32), first, steps)
-        weights_at = scalar_ref.shape[0] - 6 * count + 6 * s
-
-        def received(side, part, k):
-            return got[side, (2 * s + part) * SENT + k].astype(F32)
-
-        for part in range(2):
-            ey, ez, ly, lz = [edge_ref[s, part, k] for k in range(4)]
-            one_[part, 0, 0] = -relax_low * (steps.down_y(ey) + steps.down_z(ez))
-            one_[part, 1, 0] = relax_low * ey
-            one_[part, 2, 0] = relax_low * ez
-            e = [own_ref[s, part, comp, 0] for comp in range(3)]
-            one_[part, 0, 1] = e[0]
-            one_[part, 1, 1] = e[1] - RELAX * received(low, part, 1)
-            one_[part, 2, 1] = e[2] + RELAX * received(low, part, 0)
-            for p in range(1, depth - 1):
-                for comp in range(3):
-                    one_[part, comp, p + 1] = own_ref[s, part, comp, p]
-            e = [own_ref[s, part, comp, depth - 1] for comp in range(3)]
-            high_y, high_z = received(high, part, 0), received(high, part, 1)
-            one_[part, 0, depth] = e[0] - RELAX * (steps.down_y(high_y) + steps.down_z(high_z))
-            one_[part, 1, depth] = e[1] + RELAX * high_y
-            one_[part, 2, depth] = e[2] + RELAX * high_z
-            two_[part, 0, depth + 1] = jnp.zeros((height, breadth), F32)
-            one_[part, 1, depth + 1] = received(high, part, 2) - relax_high * lz
-            one_[part, 2, depth + 1] = received(high, part, 3) + relax_high * ly
-
-        def sweep(ref, into, low_plane, planes_swept, k):
-            if low_plane < 0:
-                before = [(-ref[part, 2, 0], ref[part, 1, 0]) for part in range(2)]
+    def received(side, part, k):
+        return got[side, part * SENT + k].astype(F32)
+
+    def weight(part, comp):
+        return scalar_ref[weights_at + part * 3 + comp]
+
+    for part in range(2):
+        ey, ez, ly, lz = [edge_ref[s, part, k] for k in range(4)]
+        one_[part, 0, 0] = -relax_low * (steps.down_y(ey) + steps.down_z(ez))
+        one_[part, 1, 0] = relax_low * ey
+        one_[part, 2, 0] = relax_low * ez
+        e = [own_ref[s, part, comp, 0] for comp in range(3)]
+        one_[part, 0, 1] = e[0]
+        one_[part, 1, 1] = e[1] - RELAX * received(low, part, 1)
+        one_[part, 2, 1] = e[2] + RELAX * received(low, part, 0)
+        for p in range(1, depth - 1):
+            for comp in range(3):
+                one_[part, comp, p + 1] = own_ref[s, part, comp, p]
+        e = [own_ref[s, part, comp, depth - 1] for comp in range(3)]
+        high_y, high_z = received(high, part, 0), received(high, part, 1)
+        one_[part, 0, depth] = e[0] - RELAX * (steps.down_y(high_y) + steps.down_z(high_z))
+        one_[part, 1, depth] = e[1] + RELAX * high_y
+        one_[part, 2, depth] = e[2] + RELAX * high_z
+        one_[part, 1, depth + 1] = received(high, part, 2) - relax_high * lz
+        one_[part, 2, depth + 1] = received(high, part, 3) + relax_high * ly
+
+    before = [(-one_[part, 2, 0], one_[part, 1, 0]) for part in range(2)]
+    for p in range(-1, depth + 1):
+        relax = relax_low if p < 0 else relax_high if p == depth else F32(RELAX)
+        for part in range(2):
+            e = [one_[part, comp, p + 1] if comp or p < depth else None for comp in range(3)]
+            if p < depth:
+                hy, hz = steps.magnetic_yz(e, [None, one_[part, 1, p + 2], one_[part, 2, p + 2]])
             else:
-                before = []
-                for part in range(2):
-                    e = [ref[part, comp, 0] for comp in range(3)]
-                    hy, hz = steps.magnetic_yz(e, [None, ref[part, 1, 1], ref[part, 2, 1]])
-                    before.append((hy + received(low, part, k), hz + received(low, part, k + 1)))
-            for p in range(low_plane, planes_swept):
-                relax = relax_low if p < 0 else relax_high if p == depth else F32(RELAX)
-                for part in range(2):
-                    e = [ref[part, comp, p + 1] if comp or p < depth else None for comp in range(3)]
-                    if p < depth:
-                        e_next = [None if comp == 0 else ref[part, comp, p + 2] for comp in range(3)]
-                        hy, hz = steps.magnetic_yz(e, e_next)
-                    else:
-                        hy, hz = received(high, part, 4) + e[2], received(high, part, 5) - e[1]
-                    hx = steps.magnetic_x(e)
-                    coef = scales[part] * conductivity(p)
-                    for comp in range(1 if p == depth else 0, 3):
-                        curl = steps.curl_back(comp, hx, hy, hz, before[part])
-                        into[part, comp, p + 1] = e[comp] - relax * curl + coef * ref[1 - part, comp, p + 1]
-                    if p < 0:
-                        hy, hz = hy + received(low, part, k), hz + received(low, part, k + 1)
-                    before[part] = hy, hz
-            point.add_to(into, 0, planes_swept, 1, lambda part, comp: scalar_ref[weights_at + part * 3 + comp])
-
-        sweep(one_, two_, -1, depth + 1, 2)
-        sweep(two_, one_, 0, depth, 4)
-
-        for p in range(depth):
-            row_re = row_im = None
+                hy, hz = received(high, part, 4) + e[2], received(high, part, 5) - e[1]
+            hx = steps.magnetic_x(e)
+            coef = scales[part] * conductivity(p)
+            for comp in range(1 if p == depth else 0, 3):
+                curl = steps.curl_back(comp, hx, hy, hz, before[part])
+                two_[part, comp, p + 1] = e[comp] - relax * curl + coef * one_[1 - part, comp, p + 1]
+            if p < 0:
+                hy, hz = hy + received(low, part, 2), hz + received(low, part, 3)
+            before[part] = hy, hz
+    for part in range(2):
+        two_[part, 0, depth + 1] = jnp.zeros((height, breadth), F32)
+    point.add_to(two_, 0, depth + 1, 1, weight)
+
+    row = lax.broadcasted_iota(jnp.int32, (height, breadth), 0)
+    here = (row == point.row) & (steps.lane == point.lane)
+    before = []
+    for part in range(2):
+        e = [two_[part, comp, 0] for comp in range(3)]
+        hy, hz = steps.magnetic_yz(e, [None, two_[part, 1, 1], two_[part, 2, 1]])
+        before.append((hy + received(low, part, 4), hz + received(low, part, 5)))
+    for p in range(depth):
+        spot = jnp.where(here, jnp.where(point.plane == p, F32(RELAX), F32(0.0)), 0.0)
+        after = []
+        for part in range(2):
+            e = [two_[part, comp, p + 1] for comp in range(3)]
+            hy, hz = steps.magnetic_yz(e, [None, two_[part, 1, p + 2], two_[part, 2, p + 2]])
+            hx = steps.magnetic_x(e)
+            coef = scales[part] * held_ref[p]
             for comp in range(3):
-                re, im = one_[0, comp, p + 1], one_[1, comp, p + 1]
-                field_re, field_im = field_ref[s, 0, comp, p], field_ref[s, 1, comp, p]
-                add_re, add_im = field_re * re - field_im * im, field_re * im + field_im * re
-                row_re, row_im = (add_re, add_im) if comp == 0 else (row_re + add_re, row_im + add_im)
-            coef = angular * held_ref[p]
-            for part, value in enumerate((row_re, row_im)):
-                value = (coef * value).astype(rows_ref.dtype)
-                rows_ref[s, part, p] = value
-                if p >= depth - REACH:
-                    sent[high, s, part, p - depth + REACH] = value
-                if p < REACH:
-                    sent[low, s, part, p] = value
-        return 0
-
-    lax.fori_loop(0, count, one_source, 0)
-    far_ref[...] = sent[0]
-    near_ref[...] = sent[1]
+                curl = steps.curl_back(comp, hx, hy, hz, before[part])
+                value = e[comp] - RELAX * curl + coef * two_[1 - part, comp, p + 1]
+                after.append(value + spot * weight(part, comp))
+            before[part] = hy, hz
+        row_re = row_im = None
+        for comp in range(3):
+            re, im = after[comp], after[3 + comp]
+            field_re, field_im = field_ref[s, 0, comp, p], field_ref[s, 1, comp, p]
+            add_re, add_im = field_re * re - field_im * im, field_re * im + field_im * re
+            row_re, row_im = (add_re, add_im) if comp == 0 else (row_re + add_re, row_im + add_im)
+        coef = angular * held_ref[p]
+        for part, value in enumerate((row_re, row_im)):
+            value = (coef * value).astype(rows_ref.dtype)
+            if not final:
+                rows_ref[part, p] = value
+                continue
+            rows_ref[s, part, p] = value
+            if p >= depth - REACH:
+                sent[high, s, part, p - depth + REACH] = value
+            if p < REACH:
+                sent[low, s, part, p] = value
+    if final:
+        for t, ref in enumerate(earlier):
+            rows_ref[t] = ref[...]
+            sent[high, t] = ref[:, depth - REACH :]
+            sent[low, t] = ref[:, :REACH]
+        far_ref[...] = sent[0]
+        near_ref[...] = sent[1]
 
 
 def in_plane(steps, f):
@@ -411,50 +432,64 @@
     far, near = [pairs + [(j, i) for i, j in pairs] for pairs in (far, near)]
     shape = jax.ShapeDtypeStruct
 
-    message = shape((2 * count * SENT + 1,) + plane, half)
-    to_far, to_near, own, edge, held, field = pl.pallas_call(
+    messages = [shape((2 * SENT + (s == 0),) + plane, half) for s in range(count)]
+    outs = pl.pallas_call(
         first_kernel,
-        out_shape=(
-            message,
-            message,
+        out_shape=tuple(messages)
+        + tuple(messages)
+        + (
             shape(warm_start.shape, F32),
             shape((count, 2, 4) + plane, F32),
             shape(conductivity.shape, F32),
             shape((count,) + background.shape[1:], F32),
         ),
         in_specs=[HBM] * 7,
-        out_specs=(FULL,) * 6,
+        out_specs=(FULL,) * (2 * count + 4),
         scratch_shapes=[
             pltpu.VMEM(warm_start.shape, F32),
             pltpu.SMEM(data_weight.shape, F32),
             pltpu.SMEM(recv_cell.shape, jnp.int32),
             pltpu.SMEM(src_group.shape, jnp.int32),
             pltpu.SMEM(group_freq.shape, jnp.int32),
-            pltpu.VMEM((2,) + message.shape, half),
+            pltpu.VMEM((2, count) + messages[0].shape, half),
             pltpu.SemaphoreType.DMA((5 + 2 * count,)),
         ],
         compiler_params=KERNEL,
         name="first_sweep",
     )(*[in_hbm(x) for x in (warm_start, conductivity, background, data_weight, recv_cell, src_group, group_freq)])
-    from_far = lax.ppermute(to_far, "space", far)
-    from_near = lax.ppermute(to_near, "space", near)
+    own, edge, held, field = outs[2 * count :]
+    fars, nears = [], []
+    for s in range(count):
+        fars.append(lax.ppermute(outs[s], "space", far))
+        nears.append(lax.ppermute(outs[count + s], "space", near))
 
     rows_of = shape((count, 2, depth) + plane, half)
     ends_of = shape((count, 2, REACH) + plane, half)
-    rows, to_far, to_near = pl.pallas_call(
-        functools.partial(sweep_kernel, peers * depth),
-        out_shape=(rows_of, ends_of, ends_of),
-        in_specs=[SCALARS] + [FULL] * 6,
-        out_specs=(FULL,) * 3,
-        scratch_shapes=[
+    earlier = []
+    for s in range(count):
+        operands = [scalars, own, edge, held, field, fars[s], nears[s], fars[0], nears[0]]
+        scratch = [
             pltpu.VMEM((2, 3, depth + 2) + plane, F32),
             pltpu.VMEM((2, 3, depth + 2) + plane, F32),
-            pltpu.VMEM((2,) + message.shape, half),
-            pltpu.VMEM((2,) + ends_of.shape, half),
-        ],
-        compiler_params=KERNEL,
-        name="sweeps",
-    )(scalars, own, edge, held, field, from_far, from_near)
+            pltpu.VMEM((2, 2 * SENT) + plane, half),
+            pltpu.VMEM((2,) + plane, half),
+        ]
+        results = (shape((2, depth) + plane, half),)
+        if s == count - 1:
+            operands += earlier
+            results = (rows_of, ends_of, ends_of)
+            scratch.append(pltpu.VMEM((2,) + ends_of.shape, half))
+        results = pl.pallas_call(
+            functools.partial(sweep_kernel, s, peers * depth),
+            out_shape=results,
+            in_specs=[SCALARS] + [FULL] * (len(operands) - 1),
+            out_specs=(FULL,) * len(results),
+            scratch_shapes=scratch,
+            compiler_params=KERNEL,
+            name="sweeps",
+        )(*operands)
+        earlier.append(results[0])
+    rows, to_far, to_near = results
     from_far = lax.ppermute(to_far, "space", far)
     from_near = lax.ppermute(to_near, "space", near)
     every = lax.all_gather(rows, "rx", axis=0)

time: 39.5 us -> 40.1 us (1.015)
  starting transfers between devices: 10.2 us -> 15.1 us
  waiting for transfers between devices: 9.44 us -> 4.82 us
  Pallas kernels: 5.11 us -> 5.63 us
    ppermute x0 -> x4, starting transfers between devices: none -> 11.3 us  [the longest x2 10 us: shards(): nears.append(lax.ppermute(outs[count + s], 'space', near))]
    ppermute x2 -> x1, waiting for transfers between devices: 9.44 us -> 0.74 us  [shards(): from_near = lax.ppermute(to_near, 'space', near)]
    ppermute x2 -> x1, starting transfers between devices: 8.89 us -> 3.1 us  [shards(): from_near = lax.ppermute(to_near, 'space', near)]
    ppermute x0 -> x4, waiting for transfers between devices: none -> 4.07 us  [the longest x2 4.07 us: shards(): nears.append(lax.ppermute(outs[count + s], 'space', near))]
    ppermute x2 -> x1, starting transfers between devices: 1.34 us -> 0.66 us  [shards(): from_far = lax.ppermute(to_far, 'space', far)]
    pallas_call x2 -> x3, Pallas kernels: 3.83 us -> 4.35 us  [the longest x2 2.37 us: shards(): pl.pallas_call(functools.partial(sweep_kernel, s, peers * depth), out_sha...]
  transfers between devices with their start and end apart: 4 -> 6, of which waited for: 2 -> 2; matrix products, arithmetic and copies ran while one was open for 1% -> 1% of each run, Pallas kernels for 1% -> 4%
where the time goes in v6:
time: 40.1 us; the launch traced here: 39.9 us
  starting transfers between devices  15.1 us (38%)
  blocking collectives  12.7 us (32%)
  Pallas kernels  5.63 us (14%)
  waiting for transfers between devices  4.82 us (12%)
  other arithmetic  0.76 us (2%)
  between operations  0.75 us (2%)
    all_to_all x1, blocking collectives, shards(): lax.all_to_all(partial_block, 'space', 0, 0, axis_index_groups=backwards)  10.8 us
    ppermute x2, starting transfers between devices, shards(): nears.append(lax.ppermute(outs[count + s], 'space', near))  10 us
    ppermute x2, waiting for transfers between devices, shards(): nears.append(lax.ppermute(outs[count + s], 'space', near))  4.07 us
    ppermute x1, starting transfers between devices, shards(): from_near = lax.ppermute(to_near, 'space', near)  3.1 us
    pallas_call x2, Pallas kernels, shards(): pl.pallas_call(functools.partial(sweep_kernel, s, peers * depth), out_sha...  2.37 us
    pallas_call x1, Pallas kernels, shards(): pl.pallas_call(first_kernel, out_shape=tuple(messages) + tuple(messages)...  1.98 us
    all_gather x1, blocking collectives, shards(): every = lax.all_gather(rows, 'rx', axis=0)  1.95 us
    ppermute x2, starting transfers between devices, shards(): fars.append(lax.ppermute(outs[s], 'space', far))  1.32 us
  transfers between devices with their start and end apart: 6, of which 2 were waited for; matrix products, arithmetic and copies ran while one was open for 1% of the time, Pallas kernels for 4%

profile of v6, /device:TPU:0, one launch (start us, length us, event | category | flops | bytes accessed | tf_op | source)
XLA Modules:
  0.0 39.9 jit_solution(7835143460820806792)
XLA Ops:
  0.6 0.0 copy-start.1
  0.6 0.0 copy-start.2
  0.7 0.0 copy-start.3
  0.7 0.0 copy-start
  0.7 2.0 %first_sweep.1 = (bf16[13,32,128]{2,1,0:T(8,128)(2,1)S(1)}, bf16[12,32,128]{2,1,0:T(8,128)(2,1)S(1)}, bf16[13,32,128]{2,1,0:T(8,128)(2,1)S(1)}, bf16[12,32,128]{...) custom-call(f32[2,2,3,3,32,128]{5,4,3,2,1,0:T(8,128)} %start_ref.1, ...), custom_call_target="tpu_custom_call" | custom-call | tf_op jit(solution)/shard_map/first_sweep/pallas_call | solution.py:436
  2.7 0.7 %collective-permute-start = (bf16[12,32,128]{2,1,0:T(8,128)(2,1)S(1)}, bf16[12,32,128]{2,1,0:T(8,128)(2,1)S(1)}, u32[]{:S(2)}, u32[]{:S(2)}) collective-permute-start(bf16[12,32,128]{2,1,0:T(8,128)(2,1)S(1)} %get-tuple-element.19), channel_id=1, source_target_pairs={{1,2},{3,4},{5,6},{7,8},{9,10},{11,12},{13,14},{2,1},{4,3},{6,5},{... | collective-permute-start | bytes 294920 | tf_op jit(solution)/shard_map/ppermute | solution.py:463
  3.3 5.7 %collective-permute-start.1 = (bf16[12,32,128]{2,1,0:T(8,128)(2,1)S(1)}, bf16[12,32,128]{2,1,0:T(8,128)(2,1)S(1)}, u32[]{:S(2)}, u32[]{:S(2)}) collective-permute-start(bf16[12,32,128]{2,1,0:T(8,128)(2,1)S(1)} %get-tuple-element.20), channel_id=1, source_target_pairs={{0,1},{2,3},{4,5},{6,7},{8,9},{10,11},{12,13},{14,15},{1,0},{3,2},... | collective-permute-start | bytes 294920 | tf_op jit(solution)/shard_map/ppermute | solution.py:464
  9.1 0.7 %collective-permute-start.2 = (bf16[13,32,128]{2,1,0:T(8,128)(2,1)S(1)}, bf16[13,32,128]{2,1,0:T(8,128)(2,1)S(1)}, u32[]{:S(2)}, u32[]{:S(2)}) collective-permute-start(bf16[13,32,128]{2,1,0:T(8,128)(2,1)S(1)} %get-tuple-element.21), channel_id=1, source_target_pairs={{1,2},{3,4},{5,6},{7,8},{9,10},{11,12},{13,14},{2,1},{4,3},{6,5},{... | collective-permute-start | bytes 319496 | tf_op jit(solution)/shard_map/ppermute | solution.py:463
  9.7 4.3 %collective-permute-start.3 = (bf16[13,32,128]{2,1,0:T(8,128)(2,1)S(1)}, bf16[13,32,128]{2,1,0:T(8,128)(2,1)S(1)}, u32[]{:S(2)}, u32[]{:S(2)}) collective-permute-start(bf16[13,32,128]{2,1,0:T(8,128)(2,1)S(1)} %get-tuple-element.22), channel_id=1, source_target_pairs={{0,1},{2,3},{4,5},{6,7},{8,9},{10,11},{12,13},{14,15},{1,0},{3,2},... | collective-permute-start | bytes 319496 | tf_op jit(solution)/shard_map/ppermute | solution.py:464
  14.0 0.0 copy-done
  14.0 0.1 reshape.7
  14.1 0.0 copy-done.1
  14.1 0.0 copy-done.2
  14.1 0.0 copy-done.3
  14.1 0.1 add_convert_fusion
  14.2 0.1 pad_maximum_fusion.scalar_ref
  14.3 0.0 collective-permute-done.2.far_in.far_cond
  14.3 4.1 %collective-permute-done.3.near_in.near_cond = bf16[13,32,128]{2,1,0:T(8,128)(2,1)S(1)} collective-permute-done((bf16[13,32,128]{2,1,0:T(8,128)(2,1)S(1)}, bf16[13,32,128]{2,1,0:T(8,128)(2,1)S(1)}, u32[]{:S(2)}, u32[]{:S(2)}) %collective-permute-start.3) | collective-permute-done | bytes 106528 | tf_op jit(solution)/shard_map/ppermute | solution.py:464
  18.3 1.2 %sweeps.2.refs_0_ = bf16[2,3,32,128]{3,2,1,0:T(8,128)(2,1)S(1)} custom-call(f32[20]{0:T(128)S(1)} %pad_maximum_fusion.scalar_ref, f32[2,2,3,3,32,128]{5,4,3,2,1,0:T(8,128)S(1)} %get-tuple-element.15.own_ref, f32[2,2,4,32,128]{4,3,2,1,0:T(8,128)S(1)} %get-tuple-element.16.edge_ref, f32[3,32,128]{2,1,0:T(8,128)S(1)} %get-tuple-element.17.held_ref, ...), custom_call_target="tpu_custom_call" | custom-call | tf_op jit(solution)/shard_map/sweeps/pallas_call | solution.py:482
  19.5 0.0 collective-permute-done.far_in
  19.5 0.0 collective-permute-done.1.near_in
  19.5 1.2 %sweeps.3 = (bf16[2,2,3,32,128]{4,3,2,1,0:T(8,128)(2,1)S(1)}, bf16[2,2,2,32,128]{4,3,2,1,0:T(8,128)(2,1)S(1)}, bf16[2,2,2,32,128]{4,3,2,1,0:T(8,128)(2,1)S(1)}) custom-call(f32[20]{0:T(128)S(1)} %pad_maximum_fusion.scalar_ref, f32[2,2,3,3,32,128]{5,4,3,2,1,0:T(8,128)S(1)} %get-tuple-element.15.own_ref, f32[2,2,4,32,128]{4,3,2,1,0:T(8,128)S(1)} %get-tuple-element.16.edge_ref, ...), custom_call_target="tpu_custom_call" | custom-call | tf_op jit(solution)/shard_map/sweeps/pallas_call | solution.py:482
  20.7 0.7 %collective-permute-start.4 = (bf16[2,2,2,32,128]{4,3,2,1,0:T(8,128)(2,1)S(1)}, bf16[2,2,2,32,128]{4,3,2,1,0:T(8,128)(2,1)S(1)}, u32[]{:S(2)}, u32[]{:S(2)}) collective-permute-start(bf16[2,2,2,32,128]{4,3,2,1,0:T(8,128)(2,1)S(1)} %get-tuple-element.24), channel_id=1, source_target_pairs={{1,2},{3,4},{5,6},{7,8},{9,10},{11,12},{13,14},{2,1},{4,3},{6,5},{... | collective-permute-start | bytes 196616 | tf_op jit(solution)/shard_map/ppermute | solution.py:493
  21.4 3.1 %collective-permute-start.5 = (bf16[2,2,2,32,128]{4,3,2,1,0:T(8,128)(2,1)S(1)}, bf16[2,2,2,32,128]{4,3,2,1,0:T(8,128)(2,1)S(1)}, u32[]{:S(2)}, u32[]{:S(2)}) collective-permute-start(bf16[2,2,2,32,128]{4,3,2,1,0:T(8,128)(2,1)S(1)} %get-tuple-element.25), channel_id=1, source_target_pairs={{0,1},{2,3},{4,5},{6,7},{8,9},{10,11},{12,13},{14,15},{1,0},{3,2},... | collective-permute-start | bytes 196616 | tf_op jit(solution)/shard_map/ppermute | solution.py:494
  24.5 0.4 %smooth.1.alone_ref = f32[2,2,3,32,128]{4,3,2,1,0:T(8,128)S(1)} custom-call(bf16[2,2,3,32,128]{4,3,2,1,0:T(8,128)(2,1)S(1)} %get-tuple-element.23.rows_ref), custom_call_target="tpu_custom_call" | custom-call | tf_op jit(solution)/shard_map/smooth/pallas_call | solution.py:498
  24.9 1.9 %all-gather = bf16[4,2,3,32,128]{4,3,2,1,0:T(8,128)(2,1)S(1)} all-gather(bf16[2,2,3,32,128]{4,3,2,1,0:T(8,128)(2,1)S(1)} %get-tuple-element.23.rows_ref), channel_id=2, replica_groups=mesh['rx'=2,'space'=16] {'rx'}, dimensions={0}, use_global_device_ids=true | all-gather | bytes 294912 | tf_op jit(solution)/shard_map/all_gather | solution.py:495
  26.9 0.0 collective-permute-done.4.far_in
  26.9 0.7 %collective-permute-done.5.near_in = bf16[2,2,2,32,128]{4,3,2,1,0:T(8,128)(2,1)S(1)} collective-permute-done((bf16[2,2,2,32,128]{4,3,2,1,0:T(8,128)(2,1)S(1)}, bf16[2,2,2,32,128]{4,3,2,1,0:T(8,128)(2,1)S(1)}, u32[]{:S(2)}, u32[]{:S(2)}) %collective-permute-start.5) | collective-permute-done | bytes 65568 | tf_op jit(solution)/shard_map/ppermute | solution.py:494
  27.6 0.9 %block.1 = (bf16[2,2,3,32,128]{4,3,2,1,0:T(8,128)(2,1)}, f32[16,4,8]{2,1,0:T(4,128)S(1)}) custom-call(bf16[2,2,3,32,128]{4,3,2,1,0:T(8,128)(2,1)S(1)} %get-tuple-element.23.rows_ref, f32[2,2,3,32,128]{4,3,2,1,0:T(8,128)S(1)} %smooth.1.alone_ref, bf16[2,2,2,32,128]{4,3,2,1,0:T(8,128)(2,1)S(1)} %collective-permute-done.4.far_in, ...), custom_call_target="tpu_custom_call" | custom-call | tf_op jit(solution)/shard_map/block/pallas_call | solution.py:506
  28.5 10.8 %all_to_all.5 = f32[16,4,8]{2,1,0:T(4,128)S(1)} all-to-all(f32[16,4,8]{2,1,0:T(4,128)S(1)} %get-tuple-element.26), channel_id=1, replica_groups={{15,14,13,12,11,10,9,8,7,6,5,4,3,2,1,0},{31,30,29,28,27,26,25,24,23,22,..., dimensions={0} | all-to-all | bytes 4096 | tf_op jit(solution)/shard_map/all_to_all | solution.py:521
  39.3 0.6 %reduce_sum.9 = f32[4,8]{1,0:T(4,128)} reduce(f32[16,4,8]{2,1,0:T(4,128)S(1)} %all_to_all.5, f32[]{:T(128)} %constant.0.clone.1), dimensions={0}, to_apply=%region_0.0 | reduce | flops 480 | bytes 2180 | tf_op jit(solution)/shard_map/reduce_sum | solution.py:522
Async XLA Ops:
  0.6 13.5 %copy-start.1 = (s32[4]{0:T(128)S(1)}, s32[4]{0:T(128)}, u32[]{:S(2)}) copy-start(s32[4]{0:T(128)} %freq_ref.1) | copy-start | bytes 52
  0.6 13.5 %copy-start.2 = (s32[2]{0:T(128)S(1)}, s32[2]{0:T(128)}, u32[]{:S(2)}) copy-start(s32[2]{0:T(128)} %group_ref.1) | copy-start | bytes 28
  0.7 13.5 %copy-start.3 = (s32[2]{0:T(128)S(1)}, s32[2]{0:T(128)}, u32[]{:S(2)}) copy-start(s32[2]{0:T(128)} %cell_ref.1) | copy-start | bytes 28
  0.7 13.4 %copy-start = (f32[2,2,3]{2,1,0:T(2,128)S(1)}, f32[2,2,3]{2,1,0:T(2,128)}, u32[]{:S(2)}) copy-start(f32[2,2,3]{2,1,0:T(2,128)} %weight_ref.1) | copy-start | bytes 148
  2.7 16.9 %collective-permute-start = (bf16[12,32,128]{2,1,0:T(8,128)(2,1)S(1)}, bf16[12,32,128]{2,1,0:T(8,128)(2,1)S(1)}, u32[]{:S(2)}, u32[]{:S(2)}) collective-permute-start(bf16[12,32,128]{2,1,0:T(8,128)(2,1)S(1)} %get-tuple-element.19), channel_id=1, source_target_pairs={{1,2},{3,4},{5,6},{7,8},{9,10},{11,12},{13,14},{2,1},{4,3},{6,5},{... | collective-permute-start | bytes 294920 | tf_op jit(solution)/shard_map/ppermute | solution.py:463
  3.3 16.2 %collective-permute-start.1 = (bf16[12,32,128]{2,1,0:T(8,128)(2,1)S(1)}, bf16[12,32,128]{2,1,0:T(8,128)(2,1)S(1)}, u32[]{:S(2)}, u32[]{:S(2)}) collective-permute-start(bf16[12,32,128]{2,1,0:T(8,128)(2,1)S(1)} %get-tuple-element.20), channel_id=1, source_target_pairs={{0,1},{2,3},{4,5},{6,7},{8,9},{10,11},{12,13},{14,15},{1,0},{3,2},... | collective-permute-start | bytes 294920 | tf_op jit(solution)/shard_map/ppermute | solution.py:464
  9.1 5.2 %collective-permute-start.2 = (bf16[13,32,128]{2,1,0:T(8,128)(2,1)S(1)}, bf16[13,32,128]{2,1,0:T(8,128)(2,1)S(1)}, u32[]{:S(2)}, u32[]{:S(2)}) collective-permute-start(bf16[13,32,128]{2,1,0:T(8,128)(2,1)S(1)} %get-tuple-element.21), channel_id=1, source_target_pairs={{1,2},{3,4},{5,6},{7,8},{9,10},{11,12},{13,14},{2,1},{4,3},{6,5},{... | collective-permute-start | bytes 319496 | tf_op jit(solution)/shard_map/ppermute | solution.py:463
  9.7 8.6 %collective-permute-start.3 = (bf16[13,32,128]{2,1,0:T(8,128)(2,1)S(1)}, bf16[13,32,128]{2,1,0:T(8,128)(2,1)S(1)}, u32[]{:S(2)}, u32[]{:S(2)}) collective-permute-start(bf16[13,32,128]{2,1,0:T(8,128)(2,1)S(1)} %get-tuple-element.22), channel_id=1, source_target_pairs={{0,1},{2,3},{4,5},{6,7},{8,9},{10,11},{12,13},{14,15},{1,0},{3,2},... | collective-permute-start | bytes 319496 | tf_op jit(solution)/shard_map/ppermute | solution.py:464
  20.7 6.1 %collective-permute-start.4 = (bf16[2,2,2,32,128]{4,3,2,1,0:T(8,128)(2,1)S(1)}, bf16[2,2,2,32,128]{4,3,2,1,0:T(8,128)(2,1)S(1)}, u32[]{:S(2)}, u32[]{:S(2)}) collective-permute-start(bf16[2,2,2,32,128]{4,3,2,1,0:T(8,128)(2,1)S(1)} %get-tuple-element.24), channel_id=1, source_target_pairs={{1,2},{3,4},{5,6},{7,8},{9,10},{11,12},{13,14},{2,1},{4,3},{6,5},{... | collective-permute-start | bytes 196616 | tf_op jit(solution)/shard_map/ppermute | solution.py:493
  21.4 6.2 %collective-permute-start.5 = (bf16[2,2,2,32,128]{4,3,2,1,0:T(8,128)(2,1)S(1)}, bf16[2,2,2,32,128]{4,3,2,1,0:T(8,128)(2,1)S(1)}, u32[]{:S(2)}, u32[]{:S(2)}) collective-permute-start(bf16[2,2,2,32,128]{4,3,2,1,0:T(8,128)(2,1)S(1)} %get-tuple-element.25), channel_id=1, source_target_pairs={{0,1},{2,3},{4,5},{6,7},{8,9},{10,11},{12,13},{14,15},{1,0},{3,2},... | collective-permute-start | bytes 196616 | tf_op jit(solution)/shard_map/ppermute | solution.py:494

commit v7 on v5

--- a/solution.py
+++ b/solution.py
@@ -98,6 +98,18 @@
             for comp in range(3):
                 at = (part, comp, plane, self.rows)
                 ref[at] = ref[at] + amount * weight(part, comp)
+
+
+def receive(got, far_in, near_in, at_end):
+    got[1] = near_in[...]
+
+    @pl.when(at_end)
+    def _():
+        got[0] = jnp.zeros(far_in.shape, far_in.dtype)
+
+    @pl.when(jnp.logical_not(at_end))
+    def _():
+        got[0] = far_in[...]
 
 
 def first_kernel(
@@ -205,8 +217,7 @@
     relax_high = jnp.where(first + depth < planes, F32(RELAX), F32(0.0))
     odd = index & 1
     low, high = odd, 1 - odd
-    got[0] = far_in[...]
-    got[1] = near_in[...]
+    receive(got, far_in, near_in, (first == 0) | (first + depth == planes))
 
     def conductivity(p):
         if p < 0:
@@ -334,9 +345,9 @@
     ranks = all_ref.shape[0]
     steps = Steps(height, breadth)
     many = ranks * count * 2
-    got[0] = far_in[...]
-    got[1] = near_in[...]
-    odd = lax.axis_index("space") & 1
+    index = lax.axis_index("space")
+    receive(got, far_in, near_in, (index == 0) | (index == lax.axis_size("space") - 1))
+    odd = index & 1
     low, high = odd, 1 - odd
 
     def one_row(s, part):
@@ -406,8 +417,9 @@
     half = jnp.bfloat16
     integers = jnp.concatenate([recv_cell, src_group, group_freq]).astype(F32)
     scalars = jnp.concatenate([integers, data_weight.reshape(-1)])
-    far = [(i, i + 1) for i in range(1, peers - 1, 2)]
-    near = [(i, i + 1) for i in range(0, peers - 1, 2)]
+    assert peers % 2 == 0
+    far = [(i, (i + 1) % peers) for i in range(1, peers, 2)]
+    near = [(i, i + 1) for i in range(0, peers, 2)]
     far, near = [pairs + [(j, i) for i, j in pairs] for pairs in (far, near)]
     shape = jax.ShapeDtypeStruct
 

time: 39.5 us -> 38 us (0.962)
  blocking collectives: 13 us -> 11.3 us
  starting transfers between devices: 10.2 us -> 11.5 us
  waiting for transfers between devices: 9.44 us -> 8.32 us
    ppermute x2, starting transfers between devices: 1.34 us -> 11.5 us  [shards(): from_far = lax.ppermute(to_far, 'space', far)]
    ppermute x2, starting transfers between devices: 8.89 us -> 0.01 us  [shards(): from_near = lax.ppermute(to_near, 'space', near)]
    ppermute x2, waiting for transfers between devices: 9.44 us -> 2.32 us  [shards(): from_near = lax.ppermute(to_near, 'space', near)]
    ppermute x2, waiting for transfers between devices: 0.01 us -> 6 us  [shards(): from_far = lax.ppermute(to_far, 'space', far)]
    all_to_all x1, blocking collectives: 11 us -> 9.34 us  [shards(): lax.all_to_all(partial_block, 'space', 0, 0, axis_index_groups=backwards)]
  transfers between devices with their start and end apart: 4 -> 4, of which waited for: 2 -> 4; matrix products, arithmetic and copies ran while one was open for 1% -> 1% of each run, Pallas kernels for 1% -> 1%
where the time goes in v7:
time: 38 us; the launch traced here: 37.8 us
  starting transfers between devices  11.5 us (30%)
  blocking collectives  11.3 us (30%)
  waiting for transfers between devices  8.32 us (22%)
  Pallas kernels  5.13 us (14%)
  other arithmetic  0.76 us (2%)
  between operations  0.7 us (2%)
    ppermute x2, starting transfers between devices, shards(): from_far = lax.ppermute(to_far, 'space', far)  11.5 us
    all_to_all x1, blocking collectives, shards(): lax.all_to_all(partial_block, 'space', 0, 0, axis_index_groups=backwards)  9.34 us
    ppermute x2, waiting for transfers between devices, shards(): from_far = lax.ppermute(to_far, 'space', far)  6 us
    ppermute x2, waiting for transfers between devices, shards(): from_near = lax.ppermute(to_near, 'space', near)  2.32 us
    pallas_call x1, Pallas kernels, shards(): pl.pallas_call(first_kernel, out_shape=(message, message, shape(warm_star...  2 us
    all_gather x1, blocking collectives, shards(): every = lax.all_gather(rows, 'rx', axis=0)  1.95 us
    pallas_call x1, Pallas kernels, shards(): pl.pallas_call(functools.partial(sweep_kernel, peers * depth), out_shape=...  1.84 us
    pallas_call x1, Pallas kernels, shards(): pl.pallas_call(functools.partial(block_kernel, cells), out_shape=(rows_of...  0.87 us
  transfers between devices with their start and end apart: 4, of which 4 were waited for; matrix products, arithmetic and copies ran while one was open for 1% of the time, Pallas kernels for 1%

profile of v7, /device:TPU:0, one launch (start us, length us, event | category | flops | bytes accessed | tf_op | source)
XLA Modules:
  0.0 37.8 jit_solution(4763444771240424781)
XLA Ops:
  0.6 0.0 copy-start.1
  0.6 0.0 copy-start.2
  0.7 0.0 copy-start.3
  0.7 0.0 copy-start
  0.7 2.0 %first_sweep.1 = (bf16[25,32,128]{2,1,0:T(8,128)(2,1)S(1)}, bf16[25,32,128]{2,1,0:T(8,128)(2,1)S(1)}, f32[2,2,3,3,32,128]{5,4,3,2,1,0:T(8,128)S(1)}, f32[2,2,4,3...) custom-call(f32[2,2,3,3,32,128]{5,4,3,2,1,0:T(8,128)} %start_ref.1, ...), custom_call_target="tpu_custom_call" | custom-call | tf_op jit(solution)/shard_map/first_sweep/pallas_call | solution.py:427
  2.7 7.0 %collective-permute-start = (bf16[25,32,128]{2,1,0:T(8,128)(2,1)S(1)}, bf16[25,32,128]{2,1,0:T(8,128)(2,1)S(1)}, u32[]{:S(2)}, u32[]{:S(2)}) collective-permute-start(bf16[25,32,128]{2,1,0:T(8,128)(2,1)S(1)} %get-tuple-element.17), channel_id=1, source_target_pairs={{1,2},{3,4},{5,6},{7,8},{9,10},{11,12},{13,14},{15,0},{2,1},{4,3},... | collective-permute-start | bytes 614408 | tf_op jit(solution)/shard_map/ppermute | solution.py:451
  9.7 0.0 collective-permute-start.1
  9.7 0.0 copy-done
  9.7 0.1 reshape.7
  9.8 0.0 copy-done.1
  9.8 0.0 copy-done.2
  9.8 0.0 copy-done.3
  9.8 0.1 add_convert_fusion
  9.8 0.1 pad_maximum_fusion.scalar_ref
  9.9 4.9 %collective-permute-done.far_in = bf16[25,32,128]{2,1,0:T(8,128)(2,1)S(1)} collective-permute-done((bf16[25,32,128]{2,1,0:T(8,128)(2,1)S(1)}, bf16[25,32,128]{2,1,0:T(8,128)(2,1)S(1)}, u32[]{:S(2)}, u32[]{:S(2)}) %collective-permute-start) | collective-permute-done | bytes 204832 | tf_op jit(solution)/shard_map/ppermute | solution.py:451
  14.9 1.5 %collective-permute-done.1.near_in = bf16[25,32,128]{2,1,0:T(8,128)(2,1)S(1)} collective-permute-done((bf16[25,32,128]{2,1,0:T(8,128)(2,1)S(1)}, bf16[25,32,128]{2,1,0:T(8,128)(2,1)S(1)}, u32[]{:S(2)}, u32[]{:S(2)}) %collective-permute-start.1) | collective-permute-done | bytes 204832 | tf_op jit(solution)/shard_map/ppermute | solution.py:452
  16.4 1.8 %sweeps.1 = (bf16[2,2,3,32,128]{4,3,2,1,0:T(8,128)(2,1)S(1)}, bf16[2,2,2,32,128]{4,3,2,1,0:T(8,128)(2,1)S(1)}, bf16[2,2,2,32,128]{4,3,2,1,0:T(8,128)(2,1)S(1)}) custom-call(f32[20]{0:T(128)S(1)} %pad_maximum_fusion.scalar_ref, f32[2,2,3,3,32,128]{5,4,3,2,1,0:T(8,128)S(1)} %get-tuple-element.13.own_ref, f32[2,2,4,32,128]{4,3,2,1,0:T(8,128)S(1)} %get-tuple-element.14.edge_ref, ...), custom_call_target="tpu_custom_call" | custom-call | tf_op jit(solution)/shard_map/sweeps/pallas_call | solution.py:456
  18.2 4.5 %collective-permute-start.2 = (bf16[2,2,2,32,128]{4,3,2,1,0:T(8,128)(2,1)S(1)}, bf16[2,2,2,32,128]{4,3,2,1,0:T(8,128)(2,1)S(1)}, u32[]{:S(2)}, u32[]{:S(2)}) collective-permute-start(bf16[2,2,2,32,128]{4,3,2,1,0:T(8,128)(2,1)S(1)} %get-tuple-element.20), channel_id=1, source_target_pairs={{1,2},{3,4},{5,6},{7,8},{9,10},{11,12},{13,14},{15,0},{2,1},{4,3},... | collective-permute-start | bytes 196616 | tf_op jit(solution)/shard_map/ppermute | solution.py:470
  22.7 0.0 collective-permute-start.3
  22.8 0.4 %smooth.1.alone_ref = f32[2,2,3,32,128]{4,3,2,1,0:T(8,128)S(1)} custom-call(bf16[2,2,3,32,128]{4,3,2,1,0:T(8,128)(2,1)S(1)} %get-tuple-element.19.rows_ref), custom_call_target="tpu_custom_call" | custom-call | tf_op jit(solution)/shard_map/smooth/pallas_call | solution.py:475
  23.2 1.9 %all-gather = bf16[4,2,3,32,128]{4,3,2,1,0:T(8,128)(2,1)S(1)} all-gather(bf16[2,2,3,32,128]{4,3,2,1,0:T(8,128)(2,1)S(1)} %get-tuple-element.19.rows_ref), channel_id=2, replica_groups=mesh['rx'=2,'space'=16] {'rx'}, dimensions={0}, use_global_device_ids=true | all-gather | bytes 294912 | tf_op jit(solution)/shard_map/all_gather | solution.py:472
  25.1 1.1 %collective-permute-done.2.far_in = bf16[2,2,2,32,128]{4,3,2,1,0:T(8,128)(2,1)S(1)} collective-permute-done((bf16[2,2,2,32,128]{4,3,2,1,0:T(8,128)(2,1)S(1)}, bf16[2,2,2,32,128]{4,3,2,1,0:T(8,128)(2,1)S(1)}, u32[]{:S(2)}, u32[]{:S(2)}) %collective-permute-start.2) | collective-permute-done | bytes 65568 | tf_op jit(solution)/shard_map/ppermute | solution.py:470
  26.2 0.8 %collective-permute-done.3.near_in = bf16[2,2,2,32,128]{4,3,2,1,0:T(8,128)(2,1)S(1)} collective-permute-done((bf16[2,2,2,32,128]{4,3,2,1,0:T(8,128)(2,1)S(1)}, bf16[2,2,2,32,128]{4,3,2,1,0:T(8,128)(2,1)S(1)}, u32[]{:S(2)}, u32[]{:S(2)}) %collective-permute-start.3) | collective-permute-done | bytes 65568 | tf_op jit(solution)/shard_map/ppermute | solution.py:471
  27.0 0.9 %block.1 = (bf16[2,2,3,32,128]{4,3,2,1,0:T(8,128)(2,1)}, f32[16,4,8]{2,1,0:T(4,128)S(1)}) custom-call(bf16[2,2,3,32,128]{4,3,2,1,0:T(8,128)(2,1)S(1)} %get-tuple-element.19.rows_ref, f32[2,2,3,32,128]{4,3,2,1,0:T(8,128)S(1)} %smooth.1.alone_ref, bf16[2,2,2,32,128]{4,3,2,1,0:T(8,128)(2,1)S(1)} %collective-permute-done.2.far_in, ...), custom_call_target="tpu_custom_call" | custom-call | tf_op jit(solution)/shard_map/block/pallas_call | solution.py:483
  27.9 9.3 %all_to_all.5 = f32[16,4,8]{2,1,0:T(4,128)S(1)} all-to-all(f32[16,4,8]{2,1,0:T(4,128)S(1)} %get-tuple-element.22), channel_id=1, replica_groups={{15,14,13,12,11,10,9,8,7,6,5,4,3,2,1,0},{31,30,29,28,27,26,25,24,23,22,..., dimensions={0} | all-to-all | bytes 4096 | tf_op jit(solution)/shard_map/all_to_all | solution.py:498
  37.2 0.6 %reduce_sum.9 = f32[4,8]{1,0:T(4,128)} reduce(f32[16,4,8]{2,1,0:T(4,128)S(1)} %all_to_all.5, f32[]{:T(128)} %constant.0.clone.1), dimensions={0}, to_apply=%region_0.0 | reduce | flops 480 | bytes 2180 | tf_op jit(solution)/shard_map/reduce_sum | solution.py:499
Async XLA Ops:
  0.6 9.1 %copy-start.1 = (s32[4]{0:T(128)S(1)}, s32[4]{0:T(128)}, u32[]{:S(2)}) copy-start(s32[4]{0:T(128)} %freq_ref.1) | copy-start | bytes 52
  0.6 9.1 %copy-start.2 = (s32[2]{0:T(128)S(1)}, s32[2]{0:T(128)}, u32[]{:S(2)}) copy-start(s32[2]{0:T(128)} %group_ref.1) | copy-start | bytes 28
  0.7 9.1 %copy-start.3 = (s32[2]{0:T(128)S(1)}, s32[2]{0:T(128)}, u32[]{:S(2)}) copy-start(s32[2]{0:T(128)} %cell_ref.1) | copy-start | bytes 28
  0.7 9.0 %copy-start = (f32[2,2,3]{2,1,0:T(2,128)S(1)}, f32[2,2,3]{2,1,0:T(2,128)}, u32[]{:S(2)}) copy-start(f32[2,2,3]{2,1,0:T(2,128)} %weight_ref.1) | copy-start | bytes 148
  2.7 12.2 %collective-permute-start = (bf16[25,32,128]{2,1,0:T(8,128)(2,1)S(1)}, bf16[25,32,128]{2,1,0:T(8,128)(2,1)S(1)}, u32[]{:S(2)}, u32[]{:S(2)}) collective-permute-start(bf16[25,32,128]{2,1,0:T(8,128)(2,1)S(1)} %get-tuple-element.17), channel_id=1, source_target_pairs={{1,2},{3,4},{5,6},{7,8},{9,10},{11,12},{13,14},{15,0},{2,1},{4,3},... | collective-permute-start | bytes 614408 | tf_op jit(solution)/shard_map/ppermute | solution.py:451
  9.7 6.7 %collective-permute-start.1 = (bf16[25,32,128]{2,1,0:T(8,128)(2,1)S(1)}, bf16[25,32,128]{2,1,0:T(8,128)(2,1)S(1)}, u32[]{:S(2)}, u32[]{:S(2)}) collective-permute-start(bf16[25,32,128]{2,1,0:T(8,128)(2,1)S(1)} %get-tuple-element.18), channel_id=1, source_target_pairs={{0,1},{2,3},{4,5},{6,7},{8,9},{10,11},{12,13},{14,15},{1,0},{3,2},... | collective-permute-start | bytes 614408 | tf_op jit(solution)/shard_map/ppermute | solution.py:452
  18.2 8.0 %collective-permute-start.2 = (bf16[2,2,2,32,128]{4,3,2,1,0:T(8,128)(2,1)S(1)}, bf16[2,2,2,32,128]{4,3,2,1,0:T(8,128)(2,1)S(1)}, u32[]{:S(2)}, u32[]{:S(2)}) collective-permute-start(bf16[2,2,2,32,128]{4,3,2,1,0:T(8,128)(2,1)S(1)} %get-tuple-element.20), channel_id=1, source_target_pairs={{1,2},{3,4},{5,6},{7,8},{9,10},{11,12},{13,14},{15,0},{2,1},{4,3},... | collective-permute-start | bytes 196616 | tf_op jit(solution)/shard_map/ppermute | solution.py:470
  22.7 4.3 %collective-permute-start.3 = (bf16[2,2,2,32,128]{4,3,2,1,0:T(8,128)(2,1)S(1)}, bf16[2,2,2,32,128]{4,3,2,1,0:T(8,128)(2,1)S(1)}, u32[]{:S(2)}, u32[]{:S(2)}) collective-permute-start(bf16[2,2,2,32,128]{4,3,2,1,0:T(8,128)(2,1)S(1)} %get-tuple-element.21), channel_id=1, source_target_pairs={{0,1},{2,3},{4,5},{6,7},{8,9},{10,11},{12,13},{14,15},{1,0},{3,2},... | collective-permute-start | bytes 196616 | tf_op jit(solution)/shard_map/ppermute | solution.py:471

commit v8 on v7

--- a/solution.py
+++ b/solution.py
@@ -417,8 +417,10 @@
     half = jnp.bfloat16
     integers = jnp.concatenate([recv_cell, src_group, group_freq]).astype(F32)
     scalars = jnp.concatenate([integers, data_weight.reshape(-1)])
-    assert peers % 2 == 0
-    far = [(i, (i + 1) % peers) for i in range(1, peers, 2)]
+    assert peers % 2 == 0 and ranks % 2 == 0
+    both = ("rx", "space")
+    far = [(r * peers + i, r * peers + i + 1) for r in range(ranks) for i in range(1, peers - 1, 2)]
+    far += [(r * peers + i, (r + 1) * peers + i) for r in range(0, ranks, 2) for i in (0, peers - 1)]
     near = [(i, i + 1) for i in range(0, peers, 2)]
     far, near = [pairs + [(j, i) for i, j in pairs] for pairs in (far, near)]
     shape = jax.ShapeDtypeStruct
@@ -448,7 +450,7 @@
         compiler_params=KERNEL,
         name="first_sweep",
     )(*[in_hbm(x) for x in (warm_start, conductivity, background, data_weight, recv_cell, src_group, group_freq)])
-    from_far = lax.ppermute(to_far, "space", far)
+    from_far = lax.ppermute(to_far, both, far)
     from_near = lax.ppermute(to_near, "space", near)
 
     rows_of = shape((count, 2, depth) + plane, half)
@@ -467,7 +469,7 @@
         compiler_params=KERNEL,
         name="sweeps",
     )(scalars, own, edge, held, field, from_far, from_near)
-    from_far = lax.ppermute(to_far, "space", far)
+    from_far = lax.ppermute(to_far, both, far)
     from_near = lax.ppermute(to_near, "space", near)
     every = lax.all_gather(rows, "rx", axis=0)
 

time: 38 us -> 35.9 us (0.945)
  starting transfers between devices: 11.5 us -> 6.37 us
  waiting for transfers between devices: 8.32 us -> 9.97 us
  blocking collectives: 11.3 us -> 12.6 us
    ppermute x2, starting transfers between devices: 11.5 us -> 0.59 us  [shards(): from_far = lax.ppermute(to_far, both, far)]
    ppermute x2, waiting for transfers between devices: 2.32 us -> 9.96 us  [shards(): from_near = lax.ppermute(to_near, 'space', near)]
    ppermute x2, waiting for transfers between devices: 6 us -> 0.01 us  [shards(): from_far = lax.ppermute(to_far, both, far)]
    ppermute x2, starting transfers between devices: 0.01 us -> 5.78 us  [shards(): from_near = lax.ppermute(to_near, 'space', near)]
    all_to_all x1, blocking collectives: 9.34 us -> 10.7 us  [shards(): lax.all_to_all(partial_block, 'space', 0, 0, axis_index_groups=backwards)]
  transfers between devices with their start and end apart: 4 -> 4, of which waited for: 4 -> 2; matrix products, arithmetic and copies ran while one was open for 1% -> 1% of each run, Pallas kernels for 1% -> 1%
where the time goes in v8:
time: 35.9 us; the launch traced here: 35.7 us
  blocking collectives  12.6 us (35%)
  waiting for transfers between devices  9.97 us (28%)
  starting transfers between devices  6.37 us (18%)
  Pallas kernels  5.13 us (14%)
  other arithmetic  0.76 us (2%)
  between operations  0.71 us (2%)
    all_to_all x1, blocking collectives, shards(): lax.all_to_all(partial_block, 'space', 0, 0, axis_index_groups=backwards)  10.7 us
    ppermute x2, waiting for transfers between devices, shards(): from_near = lax.ppermute(to_near, 'space', near)  9.96 us
    ppermute x2, starting transfers between devices, shards(): from_near = lax.ppermute(to_near, 'space', near)  5.78 us
    pallas_call x1, Pallas kernels, shards(): pl.pallas_call(first_kernel, out_shape=(message, message, shape(warm_star...  2 us
    all_gather x1, blocking collectives, shards(): every = lax.all_gather(rows, 'rx', axis=0)  1.95 us
    pallas_call x1, Pallas kernels, shards(): pl.pallas_call(functools.partial(sweep_kernel, peers * depth), out_shape=...  1.84 us
    pallas_call x1, Pallas kernels, shards(): pl.pallas_call(functools.partial(block_kernel, cells), out_shape=(rows_of...  0.87 us
  transfers between devices with their start and end apart: 4, of which 2 were waited for; matrix products, arithmetic and copies ran while one was open for 1% of the time, Pallas kernels for 1%

profile of v8, /device:TPU:0, one launch (start us, length us, event | category | flops | bytes accessed | tf_op | source)
XLA Modules:
  0.0 35.7 jit_solution(6095965311502295763)
XLA Ops:
  0.6 0.0 copy-start.1
  0.6 0.0 copy-start.2
  0.7 0.0 copy-start.3
  0.7 0.0 copy-start
  0.7 2.0 %first_sweep.1 = (bf16[25,32,128]{2,1,0:T(8,128)(2,1)S(1)}, bf16[25,32,128]{2,1,0:T(8,128)(2,1)S(1)}, f32[2,2,3,3,32,128]{5,4,3,2,1,0:T(8,128)S(1)}, f32[2,2,4,3...) custom-call(f32[2,2,3,3,32,128]{5,4,3,2,1,0:T(8,128)} %start_ref.1, ...), custom_call_target="tpu_custom_call" | custom-call | tf_op jit(solution)/shard_map/first_sweep/pallas_call | solution.py:429
  2.7 0.5 %collective-permute-start = (bf16[25,32,128]{2,1,0:T(8,128)(2,1)S(1)}, bf16[25,32,128]{2,1,0:T(8,128)(2,1)S(1)}, u32[]{:S(2)}, u32[]{:S(2)}) collective-permute-start(bf16[25,32,128]{2,1,0:T(8,128)(2,1)S(1)} %get-tuple-element.17), channel_id=1, source_target_pairs={{1,2},{3,4},{5,6},{7,8},{9,10},{11,12},{13,14},{17,18},{19,20},{21... | collective-permute-start | bytes 614408 | tf_op jit(solution)/shard_map/ppermute | solution.py:453
  3.2 4.0 %collective-permute-start.1 = (bf16[25,32,128]{2,1,0:T(8,128)(2,1)S(1)}, bf16[25,32,128]{2,1,0:T(8,128)(2,1)S(1)}, u32[]{:S(2)}, u32[]{:S(2)}) collective-permute-start(bf16[25,32,128]{2,1,0:T(8,128)(2,1)S(1)} %get-tuple-element.18), channel_id=1, source_target_pairs={{0,1},{2,3},{4,5},{6,7},{8,9},{10,11},{12,13},{14,15},{1,0},{3,2},... | collective-permute-start | bytes 614408 | tf_op jit(solution)/shard_map/ppermute | solution.py:454
  7.2 0.0 copy-done
  7.2 0.1 reshape.7
  7.3 0.0 copy-done.1
  7.3 0.0 copy-done.2
  7.3 0.0 copy-done.3
  7.3 0.1 add_convert_fusion
  7.3 0.1 pad_maximum_fusion.scalar_ref
  7.4 0.0 collective-permute-done.far_in
  7.4 8.9 %collective-permute-done.1.near_in = bf16[25,32,128]{2,1,0:T(8,128)(2,1)S(1)} collective-permute-done((bf16[25,32,128]{2,1,0:T(8,128)(2,1)S(1)}, bf16[25,32,128]{2,1,0:T(8,128)(2,1)S(1)}, u32[]{:S(2)}, u32[]{:S(2)}) %collective-permute-start.1) | collective-permute-done | bytes 204832 | tf_op jit(solution)/shard_map/ppermute | solution.py:454
  16.4 1.8 %sweeps.1 = (bf16[2,2,3,32,128]{4,3,2,1,0:T(8,128)(2,1)S(1)}, bf16[2,2,2,32,128]{4,3,2,1,0:T(8,128)(2,1)S(1)}, bf16[2,2,2,32,128]{4,3,2,1,0:T(8,128)(2,1)S(1)}) custom-call(f32[20]{0:T(128)S(1)} %pad_maximum_fusion.scalar_ref, f32[2,2,3,3,32,128]{5,4,3,2,1,0:T(8,128)S(1)} %get-tuple-element.13.own_ref, f32[2,2,4,32,128]{4,3,2,1,0:T(8,128)S(1)} %get-tuple-element.14.edge_ref, ...), custom_call_target="tpu_custom_call" | custom-call | tf_op jit(solution)/shard_map/sweeps/pallas_call | solution.py:458
  18.2 0.1 collective-permute-start.2
  18.3 1.8 %collective-permute-start.3 = (bf16[2,2,2,32,128]{4,3,2,1,0:T(8,128)(2,1)S(1)}, bf16[2,2,2,32,128]{4,3,2,1,0:T(8,128)(2,1)S(1)}, u32[]{:S(2)}, u32[]{:S(2)}) collective-permute-start(bf16[2,2,2,32,128]{4,3,2,1,0:T(8,128)(2,1)S(1)} %get-tuple-element.21), channel_id=1, source_target_pairs={{0,1},{2,3},{4,5},{6,7},{8,9},{10,11},{12,13},{14,15},{1,0},{3,2},... | collective-permute-start | bytes 196616 | tf_op jit(solution)/shard_map/ppermute | solution.py:473
  20.1 0.4 %smooth.1.alone_ref = f32[2,2,3,32,128]{4,3,2,1,0:T(8,128)S(1)} custom-call(bf16[2,2,3,32,128]{4,3,2,1,0:T(8,128)(2,1)S(1)} %get-tuple-element.19.rows_ref), custom_call_target="tpu_custom_call" | custom-call | tf_op jit(solution)/shard_map/smooth/pallas_call | solution.py:477
  20.5 1.9 %all-gather = bf16[4,2,3,32,128]{4,3,2,1,0:T(8,128)(2,1)S(1)} all-gather(bf16[2,2,3,32,128]{4,3,2,1,0:T(8,128)(2,1)S(1)} %get-tuple-element.19.rows_ref), channel_id=2, replica_groups=mesh['rx'=2,'space'=16] {'rx'}, dimensions={0}, use_global_device_ids=true | all-gather | bytes 294912 | tf_op jit(solution)/shard_map/all_gather | solution.py:474
  22.5 0.0 collective-permute-done.2.far_in
  22.5 1.0 %collective-permute-done.3.near_in = bf16[2,2,2,32,128]{4,3,2,1,0:T(8,128)(2,1)S(1)} collective-permute-done((bf16[2,2,2,32,128]{4,3,2,1,0:T(8,128)(2,1)S(1)}, bf16[2,2,2,32,128]{4,3,2,1,0:T(8,128)(2,1)S(1)}, u32[]{:S(2)}, u32[]{:S(2)}) %collective-permute-start.3) | collective-permute-done | bytes 65568 | tf_op jit(solution)/shard_map/ppermute | solution.py:473
  23.5 0.9 %block.1 = (bf16[2,2,3,32,128]{4,3,2,1,0:T(8,128)(2,1)}, f32[16,4,8]{2,1,0:T(4,128)S(1)}) custom-call(bf16[2,2,3,32,128]{4,3,2,1,0:T(8,128)(2,1)S(1)} %get-tuple-element.19.rows_ref, f32[2,2,3,32,128]{4,3,2,1,0:T(8,128)S(1)} %smooth.1.alone_ref, bf16[2,2,2,32,128]{4,3,2,1,0:T(8,128)(2,1)S(1)} %collective-permute-done.2.far_in, ...), custom_call_target="tpu_custom_call" | custom-call | tf_op jit(solution)/shard_map/block/pallas_call | solution.py:485
  24.4 10.7 %all_to_all.5 = f32[16,4,8]{2,1,0:T(4,128)S(1)} all-to-all(f32[16,4,8]{2,1,0:T(4,128)S(1)} %get-tuple-element.22), channel_id=1, replica_groups={{15,14,13,12,11,10,9,8,7,6,5,4,3,2,1,0},{31,30,29,28,27,26,25,24,23,22,..., dimensions={0} | all-to-all | bytes 4096 | tf_op jit(solution)/shard_map/all_to_all | solution.py:500
  35.1 0.6 %reduce_sum.9 = f32[4,8]{1,0:T(4,128)} reduce(f32[16,4,8]{2,1,0:T(4,128)S(1)} %all_to_all.5, f32[]{:T(128)} %constant.0.clone.1), dimensions={0}, to_apply=%region_0.0 | reduce | flops 480 | bytes 2180 | tf_op jit(solution)/shard_map/reduce_sum | solution.py:501
Async XLA Ops:
  0.6 6.6 %copy-start.1 = (s32[4]{0:T(128)S(1)}, s32[4]{0:T(128)}, u32[]{:S(2)}) copy-start(s32[4]{0:T(128)} %freq_ref.1) | copy-start | bytes 52
  0.6 6.6 %copy-start.2 = (s32[2]{0:T(128)S(1)}, s32[2]{0:T(128)}, u32[]{:S(2)}) copy-start(s32[2]{0:T(128)} %group_ref.1) | copy-start | bytes 28
  0.7 6.6 %copy-start.3 = (s32[2]{0:T(128)S(1)}, s32[2]{0:T(128)}, u32[]{:S(2)}) copy-start(s32[2]{0:T(128)} %cell_ref.1) | copy-start | bytes 28
  0.7 6.5 %copy-start = (f32[2,2,3]{2,1,0:T(2,128)S(1)}, f32[2,2,3]{2,1,0:T(2,128)}, u32[]{:S(2)}) copy-start(f32[2,2,3]{2,1,0:T(2,128)} %weight_ref.1) | copy-start | bytes 148
  2.7 4.7 %collective-permute-start = (bf16[25,32,128]{2,1,0:T(8,128)(2,1)S(1)}, bf16[25,32,128]{2,1,0:T(8,128)(2,1)S(1)}, u32[]{:S(2)}, u32[]{:S(2)}) collective-permute-start(bf16[25,32,128]{2,1,0:T(8,128)(2,1)S(1)} %get-tuple-element.17), channel_id=1, source_target_pairs={{1,2},{3,4},{5,6},{7,8},{9,10},{11,12},{13,14},{17,18},{19,20},{21... | collective-permute-start | bytes 614408 | tf_op jit(solution)/shard_map/ppermute | solution.py:453
  3.2 13.2 %collective-permute-start.1 = (bf16[25,32,128]{2,1,0:T(8,128)(2,1)S(1)}, bf16[25,32,128]{2,1,0:T(8,128)(2,1)S(1)}, u32[]{:S(2)}, u32[]{:S(2)}) collective-permute-start(bf16[25,32,128]{2,1,0:T(8,128)(2,1)S(1)} %get-tuple-element.18), channel_id=1, source_target_pairs={{0,1},{2,3},{4,5},{6,7},{8,9},{10,11},{12,13},{14,15},{1,0},{3,2},... | collective-permute-start | bytes 614408 | tf_op jit(solution)/shard_map/ppermute | solution.py:454
  18.2 4.3 %collective-permute-start.2 = (bf16[2,2,2,32,128]{4,3,2,1,0:T(8,128)(2,1)S(1)}, bf16[2,2,2,32,128]{4,3,2,1,0:T(8,128)(2,1)S(1)}, u32[]{:S(2)}, u32[]{:S(2)}) collective-permute-start(bf16[2,2,2,32,128]{4,3,2,1,0:T(8,128)(2,1)S(1)} %get-tuple-element.20), channel_id=1, source_target_pairs={{1,2},{3,4},{5,6},{7,8},{9,10},{11,12},{13,14},{17,18},{19,20},{21... | collective-permute-start | bytes 196616 | tf_op jit(solution)/shard_map/ppermute | solution.py:472
  18.3 5.2 %collective-permute-start.3 = (bf16[2,2,2,32,128]{4,3,2,1,0:T(8,128)(2,1)S(1)}, bf16[2,2,2,32,128]{4,3,2,1,0:T(8,128)(2,1)S(1)}, u32[]{:S(2)}, u32[]{:S(2)}) collective-permute-start(bf16[2,2,2,32,128]{4,3,2,1,0:T(8,128)(2,1)S(1)} %get-tuple-element.21), channel_id=1, source_target_pairs={{0,1},{2,3},{4,5},{6,7},{8,9},{10,11},{12,13},{14,15},{1,0},{3,2},... | collective-permute-start | bytes 196616 | tf_op jit(solution)/shard_map/ppermute | solution.py:473

commit v9 on v6

--- a/solution.py
+++ b/solution.py
@@ -100,103 +100,122 @@
                 ref[at] = ref[at] + amount * weight(part, comp)
 
 
-def first_kernel(
-    start_ref, cond_ref, back_ref, weight_ref, cell_ref, group_ref, freq_ref,
-    *refs,
-):
-    count, _, _, depth, height, breadth = start_ref.shape
-    fars, nears = refs[:count], refs[count : 2 * count]
-    own_ref, edge_ref, held_ref, field_ref, raw, weight, cell, group, freq, sent, sems = refs[2 * count :]
-    pairs = ((group_ref, group), (freq_ref, freq), (cell_ref, cell), (weight_ref, weight), (cond_ref, held_ref))
-    copies = [pltpu.make_async_copy(a, b, sems.at[k]) for k, (a, b) in enumerate(pairs)]
-
-    def start_of(s):
-        return pltpu.make_async_copy(start_ref.at[s], raw.at[s], sems.at[len(pairs) + s])
-
-    for copy in [start_of(0)] + copies + [start_of(s) for s in range(1, count)]:
-        copy.start()
-    copies[0].wait()
-    fields = [
-        pltpu.make_async_copy(back_ref.at[group[s]], field_ref.at[s], sems.at[len(pairs) + count + s])
-        for s in range(count)
-    ]
-    for copy in fields:
-        copy.start()
-    for copy in copies[1:]:
-        copy.wait()
+def receive(got, far_in, near_in, at_end):
+    got[1] = near_in[: got.shape[1]]
+
+    @pl.when(at_end)
+    def _():
+        got[0] = jnp.zeros(got.shape[1:], got.dtype)
+
+    @pl.when(jnp.logical_not(at_end))
+    def _():
+        got[0] = far_in[: got.shape[1]]
+
+
+def first_kernel(s, planes_ref, *refs):
+    if s == 0:
+        cond_ref, back_ref, weight_ref, cell_ref, group_ref, freq_ref = refs[:6]
+        far_ref, near_ref, own_ref, edge_ref, held_ref, later_ref, field_ref = refs[6:13]
+        raw, weight_of, cell, group, freq, sent, sems = refs[13:]
+        count = planes_ref.shape[0]
+        small = ((group_ref, group), (freq_ref, freq), (cell_ref, cell), (weight_ref, weight_of), (cond_ref, held_ref))
+        copies = [pltpu.make_async_copy(planes_ref.at[0], raw, sems.at[0])]
+        copies += [pltpu.make_async_copy(a, b, sems.at[k + 1]) for k, (a, b) in enumerate(small)]
+        others = [pltpu.make_async_copy(planes_ref.at[pl.ds(1, count - 1)], later_ref, sems.at[len(copies)])]
+        for copy in copies + others:
+            copy.start()
+        copies[1].wait()
+        for t in range(count):
+            field = pltpu.make_async_copy(back_ref.at[group[t]], field_ref.at[t], sems.at[len(copies) + 1 + t])
+            field.start()
+            others.append(field)
+        for copy in copies[:1] + copies[2:]:
+            copy.wait()
+        angular = angular_of(freq[group[s]])
+        cell_at = cell[s]
+
+        def weight(part, comp):
+            return weight_of[s, part, comp]
+    else:
+        scalar_ref, held_ref, far_ref, near_ref, own_ref, edge_ref, sent = refs
+        raw = planes_ref.at[s - 1]
+        count = planes_ref.shape[0] + 1
+        others = []
+        group = scalar_ref[count + s].astype(jnp.int32)
+        angular = angular_of(scalar_ref[2 * count + group].astype(jnp.int32))
+        cell_at = scalar_ref[s].astype(jnp.int32)
+        weights_at = scalar_ref.shape[0] - 6 * count + 6 * s
+
+        def weight(part, comp):
+            return scalar_ref[weights_at + part * 3 + comp]
+
+    depth, height, breadth = held_ref.shape
     steps = Steps(height, breadth)
     half = sent.dtype
     index = lax.axis_index("space")
     first = index * depth
     down = index & 1
     up = 1 - down
+    last = depth - 1
+    scales = RELAX * angular, -RELAX * angular
+    point = Point(cell_at, first, steps)
+    if s == 0:
+        sent[up, 2 * SENT] = held_ref[last].astype(half)
+        sent[down, 2 * SENT] = held_ref[0].astype(half)
+
+    before = []
+    for part in range(2):
+        ey, ez = raw[part, 1, 0], raw[part, 2, 0]
+        for k, f in enumerate((ey, ez)):
+            sent[down, part * SENT + k] = f.astype(half)
+            edge_ref[part, k] = f
+        before.append((-ez, ey))
+    for p in range(depth):
+        for part in range(2):
+            e = [raw[part, comp, p] for comp in range(3)]
+            e_next = [None if comp == 0 else raw[part, comp, p + 1] for comp in range(3)] if p < last else None
+            hy, hz = steps.magnetic_yz(e, e_next)
+            if p == last:
+                for k, f in enumerate((hy, hz)):
+                    sent[up, part * SENT + k] = f.astype(half)
+                    edge_ref[part, 2 + k] = f
+            hx = steps.magnetic_x(e)
+            coef = scales[part] * held_ref[p]
+            for comp in range(3):
+                curl = steps.curl_back(comp, hx, hy, hz, before[part])
+                own_ref[part, comp, p] = e[comp] - RELAX * curl + coef * raw[1 - part, comp, p]
+            before[part] = hy, hz
+    point.add_to(own_ref, 0, depth, 0, weight)
+
     row = lax.broadcasted_iota(jnp.int32, (height, breadth), 0)
-    last = depth - 1
-    sent[up, 0, 2 * SENT] = held_ref[last].astype(half)
-    sent[down, 0, 2 * SENT] = held_ref[0].astype(half)
-
-    def one_source(s, _):
-        start_of(s).wait()
-        scale = RELAX * angular_of(freq[group[s]])
-        scales = scale, -scale
-        point = Point(cell[s], first, steps)
-        before = []
-        for part in range(2):
-            ey, ez = raw[s, part, 1, 0], raw[s, part, 2, 0]
-            for k, f in enumerate((ey, ez)):
-                sent[down, s, part * SENT + k] = f.astype(half)
-                edge_ref[s, part, k] = f
-            before.append((-ez, ey))
-        for p in range(depth):
-            for part in range(2):
-                e = [raw[s, part, comp, p] for comp in range(3)]
-                e_next = None
-                if p < last:
-                    e_next = [None if comp == 0 else raw[s, part, comp, p + 1] for comp in range(3)]
-                hy, hz = steps.magnetic_yz(e, e_next)
-                if p == last:
-                    for k, f in enumerate((hy, hz)):
-                        sent[up, s, part * SENT + k] = f.astype(half)
-                        edge_ref[s, part, 2 + k] = f
-                hx = steps.magnetic_x(e)
-                coef = scales[part] * held_ref[p]
-                for comp in range(3):
-                    curl = steps.curl_back(comp, hx, hy, hz, before[part])
-                    own_ref[s, part, comp, p] = e[comp] - RELAX * curl + coef * raw[s, 1 - part, comp, p]
-                before[part] = hy, hz
-        point.add_to(own_ref.at[s], 0, depth, 0, lambda part, comp: weight[s, part, comp])
-
-        at_last = jnp.where(point.plane == last, F32(1.0), F32(0.0))
-        here = jnp.where((row == point.row) & (steps.lane == point.lane), RELAX * at_last, 0.0)
-        for part in range(2):
-            ex, ey, ez = [own_ref[s, part, comp, 0] for comp in range(3)]
-            hy, hz = steps.up_z(ex) - own_ref[s, part, 2, 1], own_ref[s, part, 1, 1] - steps.up_y(ex)
-            for k, f in enumerate((ey, ez, hy, hz)):
-                sent[down, s, part * SENT + 2 + k] = f.astype(half)
-            e = [own_ref[s, part, comp, last] for comp in range(3)]
-            behind = steps.magnetic_yz([own_ref[s, part, comp, last - 1] for comp in range(3)], e)
-            hy, hz = steps.magnetic_yz(e, None)
-            hx = steps.magnetic_x(e)
-            coef = scales[part] * held_ref[last]
-            after = []
-            for comp in range(3):
-                curl = steps.curl_back(comp, hx, hy, hz, behind)
-                value = e[comp] - RELAX * curl + coef * own_ref[s, 1 - part, comp, last]
-                after.append(value + here * weight[s, part, comp])
-            for k, f in enumerate((hy, hz) + steps.magnetic_yz(after, None)):
-                sent[up, s, part * SENT + 2 + k] = f.astype(half)
-        return 0
-
-    lax.fori_loop(0, count, one_source, 0)
-    for s in range(count):
-        fars[s][...] = sent[0, s, : fars[s].shape[0]]
-        nears[s][...] = sent[1, s, : nears[s].shape[0]]
-    for copy in fields:
+    at_last = jnp.where(point.plane == last, F32(1.0), F32(0.0))
+    here = jnp.where((row == point.row) & (steps.lane == point.lane), RELAX * at_last, 0.0)
+    for part in range(2):
+        ex, ey, ez = [own_ref[part, comp, 0] for comp in range(3)]
+        hy, hz = steps.up_z(ex) - own_ref[part, 2, 1], own_ref[part, 1, 1] - steps.up_y(ex)
+        for k, f in enumerate((ey, ez, hy, hz)):
+            sent[down, part * SENT + 2 + k] = f.astype(half)
+        e = [own_ref[part, comp, last] for comp in range(3)]
+        behind = steps.magnetic_yz([own_ref[part, comp, last - 1] for comp in range(3)], e)
+        hy, hz = steps.magnetic_yz(e, None)
+        hx = steps.magnetic_x(e)
+        coef = scales[part] * held_ref[last]
+        after = []
+        for comp in range(3):
+            curl = steps.curl_back(comp, hx, hy, hz, behind)
+            value = e[comp] - RELAX * curl + coef * own_ref[1 - part, comp, last]
+            after.append(value + here * weight(part, comp))
+        for k, f in enumerate((hy, hz) + steps.magnetic_yz(after, None)):
+            sent[up, part * SENT + 2 + k] = f.astype(half)
+    far_ref[...] = sent[0]
+    near_ref[...] = sent[1]
+    for copy in others:
         copy.wait()
 
 
 def sweep_kernel(s, planes, scalar_ref, own_ref, edge_ref, held_ref, field_ref, far_in, near_in, far_cond, near_cond, *refs):
-    count, _, _, depth, height, breadth = own_ref.shape
+    depth, height, breadth = held_ref.shape
+    count = field_ref.shape[0]
     final = s == count - 1
     if final:
         earlier = refs[:s]
@@ -210,8 +229,7 @@
     relax_high = jnp.where(first + depth < planes, F32(RELAX), F32(0.0))
     low = index & 1
     high = 1 - low
-    got[0] = far_in[: 2 * SENT]
-    got[1] = near_in[: 2 * SENT]
+    receive(got, far_in, near_in, (first == 0) | (first + depth == planes))
     conds[0] = far_cond[2 * SENT]
     conds[1] = near_cond[2 * SENT]
     group = scalar_ref[count + s].astype(jnp.int32)
@@ -234,18 +252,18 @@
         return scalar_ref[weights_at + part * 3 + comp]
 
     for part in range(2):
-        ey, ez, ly, lz = [edge_ref[s, part, k] for k in range(4)]
+        ey, ez, ly, lz = [edge_ref[part, k] for k in range(4)]
         one_[part, 0, 0] = -relax_low * (steps.down_y(ey) + steps.down_z(ez))
         one_[part, 1, 0] = relax_low * ey
         one_[part, 2, 0] = relax_low * ez
-        e = [own_ref[s, part, comp, 0] for comp in range(3)]
+        e = [own_ref[part, comp, 0] for comp in range(3)]
         one_[part, 0, 1] = e[0]
         one_[part, 1, 1] = e[1] - RELAX * received(low, part, 1)
         one_[part, 2, 1] = e[2] + RELAX * received(low, part, 0)
         for p in range(1, depth - 1):
             for comp in range(3):
-                one_[part, comp, p + 1] = own_ref[s, part, comp, p]
-        e = [own_ref[s, part, comp, depth - 1] for comp in range(3)]
+                one_[part, comp, p + 1] = own_ref[part, comp, p]
+        e = [own_ref[part, comp, depth - 1] for comp in range(3)]
         high_y, high_z = received(high, part, 0), received(high, part, 1)
         one_[part, 0, depth] = e[0] - RELAX * (steps.down_y(high_y) + steps.down_z(high_z))
         one_[part, 1, depth] = e[1] + RELAX * high_y
@@ -355,9 +373,9 @@
     ranks = all_ref.shape[0]
     steps = Steps(height, breadth)
     many = ranks * count * 2
-    got[0] = far_in[...]
-    got[1] = near_in[...]
-    odd = lax.axis_index("space") & 1
+    index = lax.axis_index("space")
+    receive(got, far_in, near_in, (index == 0) | (index == lax.axis_size("space") - 1))
+    odd = index & 1
     low, high = odd, 1 - odd
 
     def one_row(s, part):
@@ -427,47 +445,59 @@
     half = jnp.bfloat16
     integers = jnp.concatenate([recv_cell, src_group, group_freq]).astype(F32)
     scalars = jnp.concatenate([integers, data_weight.reshape(-1)])
-    far = [(i, i + 1) for i in range(1, peers - 1, 2)]
-    near = [(i, i + 1) for i in range(0, peers - 1, 2)]
+    assert peers % 2 == 0 and ranks % 2 == 0
+    both = ("rx", "space")
+    far = [(r * peers + i, r * peers + i + 1) for r in range(ranks) for i in range(1, peers - 1, 2)]
+    far += [(r * peers + i, (r + 1) * peers + i) for r in range(0, ranks, 2) for i in (0, peers - 1)]
+    near = [(i, i + 1) for i in range(0, peers, 2)]
     far, near = [pairs + [(j, i) for i, j in pairs] for pairs in (far, near)]
     shape = jax.ShapeDtypeStruct
 
-    messages = [shape((2 * SENT + (s == 0),) + plane, half) for s in range(count)]
-    outs = pl.pallas_call(
-        first_kernel,
-        out_shape=tuple(messages)
-        + tuple(messages)
-        + (
-            shape(warm_start.shape, F32),
-            shape((count, 2, 4) + plane, F32),
-            shape(conductivity.shape, F32),
-            shape((count,) + background.shape[1:], F32),
-        ),
-        in_specs=[HBM] * 7,
-        out_specs=(FULL,) * (2 * count + 4),
-        scratch_shapes=[
-            pltpu.VMEM(warm_start.shape, F32),
-            pltpu.SMEM(data_weight.shape, F32),
-            pltpu.SMEM(recv_cell.shape, jnp.int32),
-            pltpu.SMEM(src_group.shape, jnp.int32),
-            pltpu.SMEM(group_freq.shape, jnp.int32),
-            pltpu.VMEM((2, count) + messages[0].shape, half),
-            pltpu.SemaphoreType.DMA((5 + 2 * count,)),
-        ],
-        compiler_params=KERNEL,
-        name="first_sweep",
-    )(*[in_hbm(x) for x in (warm_start, conductivity, background, data_weight, recv_cell, src_group, group_freq)])
-    own, edge, held, field = outs[2 * count :]
-    fars, nears = [], []
+    own, edges, fars, nears = [], [], [], []
     for s in range(count):
-        fars.append(lax.ppermute(outs[s], "space", far))
-        nears.append(lax.ppermute(outs[count + s], "space", near))
+        message = shape((2 * SENT + (s == 0),) + plane, half)
+        outs = [message, message, shape(warm_start.shape[1:], F32), shape((2, 4) + plane, F32)]
+        scratch = [pltpu.VMEM((2,) + message.shape, half)]
+        if s == 0:
+            operands = [warm_start, conductivity, background, data_weight, recv_cell, src_group, group_freq]
+            operands = [in_hbm(x) for x in operands]
+            specs = [HBM] * 7
+            outs += [
+                shape(conductivity.shape, F32),
+                shape((count - 1,) + warm_start.shape[1:], F32),
+                shape((count,) + background.shape[1:], F32),
+            ]
+            scratch = [
+                pltpu.VMEM(warm_start.shape[1:], F32),
+                pltpu.SMEM(data_weight.shape, F32),
+                pltpu.SMEM(recv_cell.shape, jnp.int32),
+                pltpu.SMEM(src_group.shape, jnp.int32),
+                pltpu.SMEM(group_freq.shape, jnp.int32),
+            ] + scratch + [pltpu.SemaphoreType.DMA((7 + count,))]
+        else:
+            operands = [later, scalars, held]
+            specs = [FULL, SCALARS, FULL]
+        result = pl.pallas_call(
+            functools.partial(first_kernel, s),
+            out_shape=tuple(outs),
+            in_specs=specs,
+            out_specs=(FULL,) * len(outs),
+            scratch_shapes=scratch,
+            compiler_params=KERNEL,
+            name="first_sweep",
+        )(*operands)
+        if s == 0:
+            held, later, field = result[4:]
+        own.append(result[2])
+        edges.append(result[3])
+        fars.append(lax.ppermute(result[0], both, far))
+        nears.append(lax.ppermute(result[1], "space", near))
 
     rows_of = shape((count, 2, depth) + plane, half)
     ends_of = shape((count, 2, REACH) + plane, half)
     earlier = []
     for s in range(count):
-        operands = [scalars, own, edge, held, field, fars[s], nears[s], fars[0], nears[0]]
+        operands = [scalars, own[s], edges[s], held, field, fars[s], nears[s], fars[0], nears[0]]
         scratch = [
             pltpu.VMEM((2, 3, depth + 2) + plane, F32),
             pltpu.VMEM((2, 3, depth + 2) + plane, F32),
@@ -490,7 +520,7 @@
         )(*operands)
         earlier.append(results[0])
     rows, to_far, to_near = results
-    from_far = lax.ppermute(to_far, "space", far)
+    from_far = lax.ppermute(to_far, both, far)
     from_near = lax.ppermute(to_near, "space", near)
     every = lax.all_gather(rows, "rx", axis=0)
 

time: 40.1 us -> 35.3 us (0.88)
  starting transfers between devices: 15.1 us -> 9.41 us
  Pallas kernels: 5.63 us -> 6.77 us
    ppermute x5, starting transfers between devices: 12 us -> 7.61 us  [the longest x2 6.95 us: shards(): nears.append(lax.ppermute(result[1], 'space', near))]
    ppermute x1, starting transfers between devices: 3.1 us -> 1.81 us  [shards(): from_near = lax.ppermute(to_near, 'space', near)]
    pallas_call x1 -> x2, Pallas kernels: 1.98 us -> 2.97 us  [shards(): pl.pallas_call(functools.partial(first_kernel, s), out_shape=tuple(outs),...]
    ppermute x5, waiting for transfers between devices: 4.08 us -> 3.63 us  [the longest x2 3.62 us: shards(): nears.append(lax.ppermute(result[1], 'space', near))]
  transfers between devices with their start and end apart: 6 -> 6, of which waited for: 2 -> 3; matrix products, arithmetic and copies ran while one was open for 1% -> 1% of each run, Pallas kernels for 4% -> 8%
where the time goes in v9:
time: 35.3 us; the launch traced here: 35.1 us
  blocking collectives  12.7 us (36%)
  starting transfers between devices  9.41 us (27%)
  Pallas kernels  6.77 us (19%)
  waiting for transfers between devices  4.66 us (13%)
  other arithmetic  0.76 us (2%)
  between operations  0.74 us (2%)
    all_to_all x1, blocking collectives, shards(): lax.all_to_all(partial_block, 'space', 0, 0, axis_index_groups=backwards)  10.7 us
    ppermute x2, starting transfers between devices, shards(): nears.append(lax.ppermute(result[1], 'space', near))  6.95 us
    ppermute x2, waiting for transfers between devices, shards(): nears.append(lax.ppermute(result[1], 'space', near))  3.62 us
    pallas_call x2, Pallas kernels, shards(): pl.pallas_call(functools.partial(first_kernel, s), out_shape=tuple(outs),...  2.97 us
    pallas_call x2, Pallas kernels, shards(): pl.pallas_call(functools.partial(sweep_kernel, s, peers * depth), out_sha...  2.51 us
    all_gather x1, blocking collectives, shards(): every = lax.all_gather(rows, 'rx', axis=0)  1.95 us
    ppermute x1, starting transfers between devices, shards(): from_near = lax.ppermute(to_near, 'space', near)  1.81 us
    ppermute x1, waiting for transfers between devices, shards(): from_near = lax.ppermute(to_near, 'space', near)  1.03 us
  transfers between devices with their start and end apart: 6, of which 3 were waited for; matrix products, arithmetic and copies ran while one was open for 1% of the time, Pallas kernels for 8%

profile of v9, /device:TPU:0, one launch (start us, length us, event | category | flops | bytes accessed | tf_op | source)
XLA Modules:
  0.0 35.1 jit_solution(9076123458295035910)
XLA Ops:
  0.6 0.0 copy-start.1
  0.6 0.0 copy-start.2
  0.7 0.0 copy-start.3
  0.7 0.0 copy-start
  0.7 2.0 %first_sweep.2 = (bf16[13,32,128]{2,1,0:T(8,128)(2,1)S(1)}, bf16[13,32,128]{2,1,0:T(8,128)(2,1)S(1)}, f32[2,3,3,32,128]{4,3,2,1,0:T(8,128)S(1)}, f32[2,4,32,128]...) custom-call(f32[2,2,3,3,32,128]{5,4,3,2,1,0:T(8,128)} %planes_ref.1,, ...), custom_call_target="tpu_custom_call" | custom-call | tf_op jit(solution)/shard_map/first_sweep/pallas_call | solution.py:480
  2.7 0.5 %collective-permute-start.2 = (bf16[13,32,128]{2,1,0:T(8,128)(2,1)S(1)}, bf16[13,32,128]{2,1,0:T(8,128)(2,1)S(1)}, u32[]{:S(2)}, u32[]{:S(2)}) collective-permute-start(bf16[13,32,128]{2,1,0:T(8,128)(2,1)S(1)} %get-tuple-element.25), channel_id=1, source_target_pairs={{1,2},{3,4},{5,6},{7,8},{9,10},{11,12},{13,14},{17,18},{19,20},{21... | collective-permute-start | bytes 319496 | tf_op jit(solution)/shard_map/ppermute | solution.py:493
  3.2 4.0 %collective-permute-start.3 = (bf16[13,32,128]{2,1,0:T(8,128)(2,1)S(1)}, bf16[13,32,128]{2,1,0:T(8,128)(2,1)S(1)}, u32[]{:S(2)}, u32[]{:S(2)}) collective-permute-start(bf16[13,32,128]{2,1,0:T(8,128)(2,1)S(1)} %get-tuple-element.26), channel_id=1, source_target_pairs={{0,1},{2,3},{4,5},{6,7},{8,9},{10,11},{12,13},{14,15},{1,0},{3,2},... | collective-permute-start | bytes 319496 | tf_op jit(solution)/shard_map/ppermute | solution.py:494
  7.2 0.0 copy-done
  7.2 0.1 reshape.7
  7.2 0.0 copy-done.1
  7.2 0.0 copy-done.2
  7.2 0.0 copy-done.3
  7.2 0.1 add_convert_fusion
  7.3 0.1 pad_maximum_fusion.refs_0_.scalar_ref
  7.4 1.0 %first_sweep.3 = (bf16[12,32,128]{2,1,0:T(8,128)(2,1)S(1)}, bf16[12,32,128]{2,1,0:T(8,128)(2,1)S(1)}, f32[2,3,3,32,128]{4,3,2,1,0:T(8,128)S(1)}, f32[2,4,32,128]{3,2,1,0:T(8,128)S(1)}) custom-call(f32[1,2,3,3,32,128]{5,4,3,2,1,0:T(8,128)S(1)} %get-tuple-element.18.planes_ref, f32[20]{0:T(128)S(1)} %pad_maximum_fusion.refs_0_.scalar_ref, ...), custom_call_target="tpu_custom_call" | custom-call | tf_op jit(solution)/shard_map/first_sweep/pallas_call | solution.py:480
  8.4 0.1 collective-permute-start
  8.5 3.0 %collective-permute-start.1 = (bf16[12,32,128]{2,1,0:T(8,128)(2,1)S(1)}, bf16[12,32,128]{2,1,0:T(8,128)(2,1)S(1)}, u32[]{:S(2)}, u32[]{:S(2)}) collective-permute-start(bf16[12,32,128]{2,1,0:T(8,128)(2,1)S(1)} %get-tuple-element.24), channel_id=1, source_target_pairs={{0,1},{2,3},{4,5},{6,7},{8,9},{10,11},{12,13},{14,15},{1,0},{3,2},... | collective-permute-start | bytes 294920 | tf_op jit(solution)/shard_map/ppermute | solution.py:494
  11.4 0.0 collective-permute-done.2.far_in.far_cond
  11.5 2.8 %collective-permute-done.3.near_in.near_cond = bf16[13,32,128]{2,1,0:T(8,128)(2,1)S(1)} collective-permute-done((bf16[13,32,128]{2,1,0:T(8,128)(2,1)S(1)}, bf16[13,32,128]{2,1,0:T(8,128)(2,1)S(1)}, u32[]{:S(2)}, u32[]{:S(2)}) %collective-permute-start.3) | collective-permute-done | bytes 106528 | tf_op jit(solution)/shard_map/ppermute | solution.py:494
  14.3 1.2 %sweeps.2.refs_0_ = bf16[2,3,32,128]{3,2,1,0:T(8,128)(2,1)S(1)} custom-call(f32[20]{0:T(128)S(1)} %pad_maximum_fusion.refs_0_.scalar_ref, f32[2,3,3,32,128]{4,3,2,1,0:T(8,128)S(1)} %get-tuple-element.27.own_ref, f32[2,4,32,128]{3,2,1,0:T(8,128)S(1)} %get-tuple-element.28.edge_ref, f32[3,32,128]{2,1,0:T(8,128)S(1)} %get-tuple-element.19.refs_1_.held_ref, ...), custom_call_target="tpu_custom_call" | custom-call | tf_op jit(solution)/shard_map/sweeps/pallas_call | solution.py:512
  15.5 0.0 collective-permute-done.far_in
  15.6 0.8 %collective-permute-done.1.near_in = bf16[12,32,128]{2,1,0:T(8,128)(2,1)S(1)} collective-permute-done((bf16[12,32,128]{2,1,0:T(8,128)(2,1)S(1)}, bf16[12,32,128]{2,1,0:T(8,128)(2,1)S(1)}, u32[]{:S(2)}, u32[]{:S(2)}) %collective-permute-start.1) | collective-permute-done | bytes 98336 | tf_op jit(solution)/shard_map/ppermute | solution.py:494
  16.3 1.3 %sweeps.3 = (bf16[2,2,3,32,128]{4,3,2,1,0:T(8,128)(2,1)S(1)}, bf16[2,2,2,32,128]{4,3,2,1,0:T(8,128)(2,1)S(1)}, bf16[2,2,2,32,128]{4,3,2,1,0:T(8,128)(2,1)S(1)}) custom-call(f32[20]{0:T(128)S(1)} %pad_maximum_fusion.refs_0_.scalar_ref, f32[2,3,3,32,128]{4,3,2,1,0:T(8,128)S(1)} %get-tuple-element.20.own_ref, f32[2,4,32,128]{3,2,1,0:T(8,128)S(1)} %get-tuple-element.21.edge_ref, ...), custom_call_target="tpu_custom_call" | custom-call | tf_op jit(solution)/shard_map/sweeps/pallas_call | solution.py:512
  17.6 0.1 collective-permute-start.4
  17.7 1.8 %collective-permute-start.5 = (bf16[2,2,2,32,128]{4,3,2,1,0:T(8,128)(2,1)S(1)}, bf16[2,2,2,32,128]{4,3,2,1,0:T(8,128)(2,1)S(1)}, u32[]{:S(2)}, u32[]{:S(2)}) collective-permute-start(bf16[2,2,2,32,128]{4,3,2,1,0:T(8,128)(2,1)S(1)} %get-tuple-element.31), channel_id=1, source_target_pairs={{0,1},{2,3},{4,5},{6,7},{8,9},{10,11},{12,13},{14,15},{1,0},{3,2},... | collective-permute-start | bytes 196616 | tf_op jit(solution)/shard_map/ppermute | solution.py:524
  19.5 0.4 %smooth.1.alone_ref = f32[2,2,3,32,128]{4,3,2,1,0:T(8,128)S(1)} custom-call(bf16[2,2,3,32,128]{4,3,2,1,0:T(8,128)(2,1)S(1)} %get-tuple-element.29.rows_ref), custom_call_target="tpu_custom_call" | custom-call | tf_op jit(solution)/shard_map/smooth/pallas_call | solution.py:528
  19.9 1.9 %all-gather = bf16[4,2,3,32,128]{4,3,2,1,0:T(8,128)(2,1)S(1)} all-gather(bf16[2,2,3,32,128]{4,3,2,1,0:T(8,128)(2,1)S(1)} %get-tuple-element.29.rows_ref), channel_id=2, replica_groups=mesh['rx'=2,'space'=16] {'rx'}, dimensions={0}, use_global_device_ids=true | all-gather | bytes 294912 | tf_op jit(solution)/shard_map/all_gather | solution.py:525
  21.9 0.0 collective-permute-done.4.far_in
  21.9 1.0 %collective-permute-done.5.near_in = bf16[2,2,2,32,128]{4,3,2,1,0:T(8,128)(2,1)S(1)} collective-permute-done((bf16[2,2,2,32,128]{4,3,2,1,0:T(8,128)(2,1)S(1)}, bf16[2,2,2,32,128]{4,3,2,1,0:T(8,128)(2,1)S(1)}, u32[]{:S(2)}, u32[]{:S(2)}) %collective-permute-start.5) | collective-permute-done | bytes 65568 | tf_op jit(solution)/shard_map/ppermute | solution.py:524
  22.9 0.9 %block.1 = (bf16[2,2,3,32,128]{4,3,2,1,0:T(8,128)(2,1)}, f32[16,4,8]{2,1,0:T(4,128)S(1)}) custom-call(bf16[2,2,3,32,128]{4,3,2,1,0:T(8,128)(2,1)S(1)} %get-tuple-element.29.rows_ref, f32[2,2,3,32,128]{4,3,2,1,0:T(8,128)S(1)} %smooth.1.alone_ref, bf16[2,2,2,32,128]{4,3,2,1,0:T(8,128)(2,1)S(1)} %collective-permute-done.4.far_in, ...), custom_call_target="tpu_custom_call" | custom-call | tf_op jit(solution)/shard_map/block/pallas_call | solution.py:536
  23.8 10.7 %all_to_all.5 = f32[16,4,8]{2,1,0:T(4,128)S(1)} all-to-all(f32[16,4,8]{2,1,0:T(4,128)S(1)} %get-tuple-element.32), channel_id=1, replica_groups={{15,14,13,12,11,10,9,8,7,6,5,4,3,2,1,0},{31,30,29,28,27,26,25,24,23,22,..., dimensions={0} | all-to-all | bytes 4096 | tf_op jit(solution)/shard_map/all_to_all | solution.py:551
  34.5 0.6 %reduce_sum.9 = f32[4,8]{1,0:T(4,128)} reduce(f32[16,4,8]{2,1,0:T(4,128)S(1)} %all_to_all.5, f32[]{:T(128)} %constant.0.clone.1), dimensions={0}, to_apply=%region_0.0 | reduce | flops 480 | bytes 2180 | tf_op jit(solution)/shard_map/reduce_sum | solution.py:552
Async XLA Ops:
  0.6 6.6 %copy-start.1 = (s32[4]{0:T(128)S(1)}, s32[4]{0:T(128)}, u32[]{:S(2)}) copy-start(s32[4]{0:T(128)} %refs_5_.1) | copy-start | bytes 52
  0.6 6.6 %copy-start.2 = (s32[2]{0:T(128)S(1)}, s32[2]{0:T(128)}, u32[]{:S(2)}) copy-start(s32[2]{0:T(128)} %refs_4_.1) | copy-start | bytes 28
  0.7 6.6 %copy-start.3 = (s32[2]{0:T(128)S(1)}, s32[2]{0:T(128)}, u32[]{:S(2)}) copy-start(s32[2]{0:T(128)} %refs_3_.1) | copy-start | bytes 28
  0.7 6.5 %copy-start = (f32[2,2,3]{2,1,0:T(2,128)S(1)}, f32[2,2,3]{2,1,0:T(2,128)}, u32[]{:S(2)}) copy-start(f32[2,2,3]{2,1,0:T(2,128)} %refs_2_.1) | copy-start | bytes 148
  2.7 8.8 %collective-permute-start.2 = (bf16[13,32,128]{2,1,0:T(8,128)(2,1)S(1)}, bf16[13,32,128]{2,1,0:T(8,128)(2,1)S(1)}, u32[]{:S(2)}, u32[]{:S(2)}) collective-permute-start(bf16[13,32,128]{2,1,0:T(8,128)(2,1)S(1)} %get-tuple-element.25), channel_id=1, source_target_pairs={{1,2},{3,4},{5,6},{7,8},{9,10},{11,12},{13,14},{17,18},{19,20},{21... | collective-permute-start | bytes 319496 | tf_op jit(solution)/shard_map/ppermute | solution.py:493
  3.2 11.1 %collective-permute-start.3 = (bf16[13,32,128]{2,1,0:T(8,128)(2,1)S(1)}, bf16[13,32,128]{2,1,0:T(8,128)(2,1)S(1)}, u32[]{:S(2)}, u32[]{:S(2)}) collective-permute-start(bf16[13,32,128]{2,1,0:T(8,128)(2,1)S(1)} %get-tuple-element.26), channel_id=1, source_target_pairs={{0,1},{2,3},{4,5},{6,7},{8,9},{10,11},{12,13},{14,15},{1,0},{3,2},... | collective-permute-start | bytes 319496 | tf_op jit(solution)/shard_map/ppermute | solution.py:494
  8.4 7.1 %collective-permute-start = (bf16[12,32,128]{2,1,0:T(8,128)(2,1)S(1)}, bf16[12,32,128]{2,1,0:T(8,128)(2,1)S(1)}, u32[]{:S(2)}, u32[]{:S(2)}) collective-permute-start(bf16[12,32,128]{2,1,0:T(8,128)(2,1)S(1)} %get-tuple-element.23), channel_id=1, source_target_pairs={{1,2},{3,4},{5,6},{7,8},{9,10},{11,12},{13,14},{17,18},{19,20},{21... | collective-permute-start | bytes 294920 | tf_op jit(solution)/shard_map/ppermute | solution.py:493
  8.5 7.9 %collective-permute-start.1 = (bf16[12,32,128]{2,1,0:T(8,128)(2,1)S(1)}, bf16[12,32,128]{2,1,0:T(8,128)(2,1)S(1)}, u32[]{:S(2)}, u32[]{:S(2)}) collective-permute-start(bf16[12,32,128]{2,1,0:T(8,128)(2,1)S(1)} %get-tuple-element.24), channel_id=1, source_target_pairs={{0,1},{2,3},{4,5},{6,7},{8,9},{10,11},{12,13},{14,15},{1,0},{3,2},... | collective-permute-start | bytes 294920 | tf_op jit(solution)/shard_map/ppermute | solution.py:494
  17.6 4.3 %collective-permute-start.4 = (bf16[2,2,2,32,128]{4,3,2,1,0:T(8,128)(2,1)S(1)}, bf16[2,2,2,32,128]{4,3,2,1,0:T(8,128)(2,1)S(1)}, u32[]{:S(2)}, u32[]{:S(2)}) collective-permute-start(bf16[2,2,2,32,128]{4,3,2,1,0:T(8,128)(2,1)S(1)} %get-tuple-element.30), channel_id=1, source_target_pairs={{1,2},{3,4},{5,6},{7,8},{9,10},{11,12},{13,14},{17,18},{19,20},{21... | collective-permute-start | bytes 196616 | tf_op jit(solution)/shard_map/ppermute | solution.py:523
  17.7 5.2 %collective-permute-start.5 = (bf16[2,2,2,32,128]{4,3,2,1,0:T(8,128)(2,1)S(1)}, bf16[2,2,2,32,128]{4,3,2,1,0:T(8,128)(2,1)S(1)}, u32[]{:S(2)}, u32[]{:S(2)}) collective-permute-start(bf16[2,2,2,32,128]{4,3,2,1,0:T(8,128)(2,1)S(1)} %get-tuple-element.31), channel_id=1, source_target_pairs={{0,1},{2,3},{4,5},{6,7},{8,9},{10,11},{12,13},{14,15},{1,0},{3,2},... | collective-permute-start | bytes 196616 | tf_op jit(solution)/shard_map/ppermute | solution.py:524

commit v10 on v9

--- a/solution.py
+++ b/solution.py
@@ -114,9 +114,9 @@
 
 def first_kernel(s, planes_ref, *refs):
     if s == 0:
-        cond_ref, back_ref, weight_ref, cell_ref, group_ref, freq_ref = refs[:6]
-        far_ref, near_ref, own_ref, edge_ref, held_ref, later_ref, field_ref = refs[6:13]
-        raw, weight_of, cell, group, freq, sent, sems = refs[13:]
+        cond_ref, weight_ref, cell_ref, group_ref, freq_ref = refs[:5]
+        far_ref, near_ref, own_ref, edge_ref, held_ref, later_ref = refs[5:11]
+        raw, weight_of, cell, group, freq, sent, sems = refs[11:]
         count = planes_ref.shape[0]
         small = ((group_ref, group), (freq_ref, freq), (cell_ref, cell), (weight_ref, weight_of), (cond_ref, held_ref))
         copies = [pltpu.make_async_copy(planes_ref.at[0], raw, sems.at[0])]
@@ -124,12 +124,7 @@
         others = [pltpu.make_async_copy(planes_ref.at[pl.ds(1, count - 1)], later_ref, sems.at[len(copies)])]
         for copy in copies + others:
             copy.start()
-        copies[1].wait()
-        for t in range(count):
-            field = pltpu.make_async_copy(back_ref.at[group[t]], field_ref.at[t], sems.at[len(copies) + 1 + t])
-            field.start()
-            others.append(field)
-        for copy in copies[:1] + copies[2:]:
+        for copy in copies:
             copy.wait()
         angular = angular_of(freq[group[s]])
         cell_at = cell[s]
@@ -137,10 +132,14 @@
         def weight(part, comp):
             return weight_of[s, part, comp]
     else:
-        scalar_ref, held_ref, far_ref, near_ref, own_ref, edge_ref, sent = refs
+        scalar_ref, held_ref, back_ref, far_ref, near_ref, own_ref, edge_ref, field_ref, sent, sems = refs
         raw = planes_ref.at[s - 1]
         count = planes_ref.shape[0] + 1
         others = []
+        for k, t in enumerate((0, 1) if s == 1 else (s,)):
+            group = scalar_ref[count + t].astype(jnp.int32)
+            others.append(pltpu.make_async_copy(back_ref.at[group], field_ref.at[k], sems.at[k]))
+            others[-1].start()
         group = scalar_ref[count + s].astype(jnp.int32)
         angular = angular_of(scalar_ref[2 * count + group].astype(jnp.int32))
         cell_at = scalar_ref[s].astype(jnp.int32)
@@ -213,9 +212,8 @@
         copy.wait()
 
 
-def sweep_kernel(s, planes, scalar_ref, own_ref, edge_ref, held_ref, field_ref, far_in, near_in, far_cond, near_cond, *refs):
+def sweep_kernel(s, count, field_at, planes, scalar_ref, own_ref, edge_ref, held_ref, field_ref, far_in, near_in, far_cond, near_cond, *refs):
     depth, height, breadth = held_ref.shape
-    count = field_ref.shape[0]
     final = s == count - 1
     if final:
         earlier = refs[:s]
@@ -315,7 +313,7 @@
         row_re = row_im = None
         for comp in range(3):
             re, im = after[comp], after[3 + comp]
-            field_re, field_im = field_ref[s, 0, comp, p], field_ref[s, 1, comp, p]
+            field_re, field_im = field_ref[field_at, 0, comp, p], field_ref[field_at, 1, comp, p]
             add_re, add_im = field_re * re - field_im * im, field_re * im + field_im * re
             row_re, row_im = (add_re, add_im) if comp == 0 else (row_re + add_re, row_im + add_im)
         coef = angular * held_ref[p]
@@ -452,20 +450,20 @@
     near = [(i, i + 1) for i in range(0, peers, 2)]
     far, near = [pairs + [(j, i) for i, j in pairs] for pairs in (far, near)]
     shape = jax.ShapeDtypeStruct
-
-    own, edges, fars, nears = [], [], [], []
+    assert count > 1
+
+    own, edges, fars, nears, fields = [], [], [], [], []
     for s in range(count):
         message = shape((2 * SENT + (s == 0),) + plane, half)
         outs = [message, message, shape(warm_start.shape[1:], F32), shape((2, 4) + plane, F32)]
         scratch = [pltpu.VMEM((2,) + message.shape, half)]
         if s == 0:
-            operands = [warm_start, conductivity, background, data_weight, recv_cell, src_group, group_freq]
+            operands = [warm_start, conductivity, data_weight, recv_cell, src_group, group_freq]
             operands = [in_hbm(x) for x in operands]
-            specs = [HBM] * 7
+            specs = [HBM] * 6
             outs += [
                 shape(conductivity.shape, F32),
                 shape((count - 1,) + warm_start.shape[1:], F32),
-                shape((count,) + background.shape[1:], F32),
             ]
             scratch = [
                 pltpu.VMEM(warm_start.shape[1:], F32),
@@ -473,10 +471,12 @@
                 pltpu.SMEM(recv_cell.shape, jnp.int32),
                 pltpu.SMEM(src_group.shape, jnp.int32),
                 pltpu.SMEM(group_freq.shape, jnp.int32),
-            ] + scratch + [pltpu.SemaphoreType.DMA((7 + count,))]
+            ] + scratch + [pltpu.SemaphoreType.DMA((7,))]
         else:
-            operands = [later, scalars, held]
-            specs = [FULL, SCALARS, FULL]
+            operands = [later, scalars, held, in_hbm(background)]
+            specs = [FULL, SCALARS, FULL, HBM]
+            outs.append(shape((1 + (s == 1),) + background.shape[1:], F32))
+            scratch.append(pltpu.SemaphoreType.DMA((2,)))
         result = pl.pallas_call(
             functools.partial(first_kernel, s),
             out_shape=tuple(outs),
@@ -487,7 +487,9 @@
             name="first_sweep",
         )(*operands)
         if s == 0:
-            held, later, field = result[4:]
+            held, later = result[4:]
+        else:
+            fields += [(result[4], k) for k in range(result[4].shape[0])]
         own.append(result[2])
         edges.append(result[3])
         fars.append(lax.ppermute(result[0], both, far))
@@ -497,7 +499,7 @@
     ends_of = shape((count, 2, REACH) + plane, half)
     earlier = []
     for s in range(count):
-        operands = [scalars, own[s], edges[s], held, field, fars[s], nears[s], fars[0], nears[0]]
+        operands = [scalars, own[s], edges[s], held, fields[s][0], fars[s], nears[s], fars[0], nears[0]]
         scratch = [
             pltpu.VMEM((2, 3, depth + 2) + plane, F32),
             pltpu.VMEM((2, 3, depth + 2) + plane, F32),
@@ -510,7 +512,7 @@
             results = (rows_of, ends_of, ends_of)
             scratch.append(pltpu.VMEM((2,) + ends_of.shape, half))
         results = pl.pallas_call(
-            functools.partial(sweep_kernel, s, peers * depth),
+            functools.partial(sweep_kernel, s, count, fields[s][1], peers * depth),
             out_shape=results,
             in_specs=[SCALARS] + [FULL] * (len(operands) - 1),
             out_specs=(FULL,) * len(results),

time: 35.3 us -> 36.1 us (1.023)
  waiting for transfers between devices: 4.66 us -> 3.76 us
  other arithmetic: 0.76 us -> 1.45 us
  local copies, waits for them, and re-layouts: 0.1 us -> 0.76 us
  Pallas kernels: 6.77 us -> 7.35 us
    ppermute x2, waiting for transfers between devices: 3.62 us -> 2.77 us  [shards(): nears.append(lax.ppermute(result[1], 'space', near))]
    convert_element_type x1, other arithmetic: 0.08 us -> 0.76 us  [shards(): integers = jnp.concatenate([recv_cell, src_group, group_freq]).astype(F32)]
    reshape x1, local copies, waits for them, and re-layouts: 0.08 us -> 0.76 us  [shards(): scalars = jnp.concatenate([integers, data_weight.reshape(-1)])]
    pallas_call x2, Pallas kernels: 2.97 us -> 3.51 us  [shards(): pl.pallas_call(functools.partial(first_kernel, s), out_shape=tuple(outs),...]
  transfers between devices with their start and end apart: 6 -> 6, of which waited for: 3 -> 2; matrix products, arithmetic and copies ran while one was open for 1% -> 4% of each run, Pallas kernels for 8% -> 10%
where the time goes in v10:
time: 36.1 us; the launch traced here: 35.9 us
  blocking collectives  12.4 us (34%)
  starting transfers between devices  9.46 us (26%)
  Pallas kernels  7.35 us (20%)
  waiting for transfers between devices  3.76 us (10%)
  other arithmetic  1.45 us (4%)
  local copies, waits for them, and re-layouts  0.76 us (2%)
  between operations  0.7 us (2%)
    all_to_all x1, blocking collectives, shards(): lax.all_to_all(partial_block, 'space', 0, 0, axis_index_groups=backwards)  10.4 us
    ppermute x2, starting transfers between devices, shards(): nears.append(lax.ppermute(result[1], 'space', near))  6.95 us
    pallas_call x2, Pallas kernels, shards(): pl.pallas_call(functools.partial(first_kernel, s), out_shape=tuple(outs),...  3.51 us
    ppermute x2, waiting for transfers between devices, shards(): nears.append(lax.ppermute(result[1], 'space', near))  2.77 us
    pallas_call x2, Pallas kernels, shards(): pl.pallas_call(functools.partial(sweep_kernel, s, count, fields[s][1], pe...  2.55 us
    all_gather x1, blocking collectives, shards(): every = lax.all_gather(rows, 'rx', axis=0)  1.95 us
    ppermute x1, starting transfers between devices, shards(): from_near = lax.ppermute(to_near, 'space', near)  1.86 us
    ppermute x1, waiting for transfers between devices, shards(): from_near = lax.ppermute(to_near, 'space', near)  0.98 us
  transfers between devices with their start and end apart: 6, of which 2 were waited for; matrix products, arithmetic and copies ran while one was open for 4% of the time, Pallas kernels for 10%

profile of v10, /device:TPU:0, one launch (start us, length us, event | category | flops | bytes accessed | tf_op | source)
XLA Modules:
  0.0 35.9 jit_solution(2718772284425904310)
XLA Ops:
  0.6 1.5 %first_sweep.2 = (bf16[13,32,128]{2,1,0:T(8,128)(2,1)S(1)}, bf16[13,32,128]{2,1,0:T(8,128)(2,1)S(1)}, f32[2,3,3,32,128]{4,3,2,1,0:T(8,128)S(1)}, f32[2,4,32,128]...) custom-call(f32[2,2,3,3,32,128]{5,4,3,2,1,0:T(8,128)} %planes_ref.1, ...), custom_call_target="tpu_custom_call" | custom-call | tf_op jit(solution)/shard_map/first_sweep/pallas_call | solution.py:480
  2.1 0.5 %collective-permute-start.2 = (bf16[13,32,128]{2,1,0:T(8,128)(2,1)S(1)}, bf16[13,32,128]{2,1,0:T(8,128)(2,1)S(1)}, u32[]{:S(2)}, u32[]{:S(2)}) collective-permute-start(bf16[13,32,128]{2,1,0:T(8,128)(2,1)S(1)} %get-tuple-element.25), channel_id=1, source_target_pairs={{1,2},{3,4},{5,6},{7,8},{9,10},{11,12},{13,14},{17,18},{19,20},{21... | collective-permute-start | bytes 319496 | tf_op jit(solution)/shard_map/ppermute | solution.py:495
  2.7 4.0 %collective-permute-start.3 = (bf16[13,32,128]{2,1,0:T(8,128)(2,1)S(1)}, bf16[13,32,128]{2,1,0:T(8,128)(2,1)S(1)}, u32[]{:S(2)}, u32[]{:S(2)}) collective-permute-start(bf16[13,32,128]{2,1,0:T(8,128)(2,1)S(1)} %get-tuple-element.26), channel_id=1, source_target_pairs={{0,1},{2,3},{4,5},{6,7},{8,9},{10,11},{12,13},{14,15},{1,0},{3,2},... | collective-permute-start | bytes 319496 | tf_op jit(solution)/shard_map/ppermute | solution.py:496
  6.6 0.8 %reshape.7 = f32[12]{0:T(128)S(1)} reshape(f32[2,2,3]{2,1,0:T(2,128)} %refs_1_.1) | data formatting | bytes 96 | tf_op jit(solution)/shard_map/reshape | solution.py:445
  7.4 0.8 %add_convert_fusion = f32[8]{0:T(128)S(1)} fusion(s32[4]{0:T(128)} %refs_4_.1, s32[2]{0:T(128)} %refs_3_.1, s32[2]{0:T(128)} %refs_2_.2), kind=kLoop, calls=%fused_computation | loop fusion | flops 24 | bytes 64 | tf_op jit(solution)/shard_map/convert_element_type | solution.py:444
  8.2 0.1 pad_maximum_fusion.refs_0_.scalar_ref
  8.3 2.0 %first_sweep.3 = (bf16[12,32,128]{2,1,0:T(8,128)(2,1)S(1)}, bf16[12,32,128]{2,1,0:T(8,128)(2,1)S(1)}, f32[2,3,3,32,128]{4,3,2,1,0:T(8,128)S(1)}, f32[2,4,32,128]...) custom-call(f32[1,2,3,3,32,128]{5,4,3,2,1,0:T(8,128)S(1)} %get-tuple-element.18.planes_ref, ...), custom_call_target="tpu_custom_call" | custom-call | tf_op jit(solution)/shard_map/first_sweep/pallas_call | solution.py:480
  10.3 0.1 collective-permute-start
  10.3 3.0 %collective-permute-start.1 = (bf16[12,32,128]{2,1,0:T(8,128)(2,1)S(1)}, bf16[12,32,128]{2,1,0:T(8,128)(2,1)S(1)}, u32[]{:S(2)}, u32[]{:S(2)}) collective-permute-start(bf16[12,32,128]{2,1,0:T(8,128)(2,1)S(1)} %get-tuple-element.24), channel_id=1, source_target_pairs={{0,1},{2,3},{4,5},{6,7},{8,9},{10,11},{12,13},{14,15},{1,0},{3,2},... | collective-permute-start | bytes 294920 | tf_op jit(solution)/shard_map/ppermute | solution.py:496
  13.3 0.0 collective-permute-done.2.far_in.far_cond
  13.3 0.0 collective-permute-done.3.near_in.near_cond
  13.3 1.3 %sweeps.2.refs_0_ = bf16[2,3,32,128]{3,2,1,0:T(8,128)(2,1)S(1)} custom-call(f32[20]{0:T(128)S(1)} %pad_maximum_fusion.refs_0_.scalar_ref, f32[2,3,3,32,128]{4,3,2,1,0:T(8,128)S(1)} %get-tuple-element.27.own_ref, f32[2,4,32,128]{3,2,1,0:T(8,128)S(1)} %get-tuple-element.28.edge_ref, f32[3,32,128]{2,1,0:T(8,128)S(1)} %get-tuple-element.19.refs_1_.held_ref, ...), custom_call_target="tpu_custom_call" | custom-call | tf_op jit(solution)/shard_map/sweeps/pallas_call | solution.py:514
  14.6 0.0 collective-permute-done.far_in
  14.6 2.8 %collective-permute-done.1.near_in = bf16[12,32,128]{2,1,0:T(8,128)(2,1)S(1)} collective-permute-done((bf16[12,32,128]{2,1,0:T(8,128)(2,1)S(1)}, bf16[12,32,128]{2,1,0:T(8,128)(2,1)S(1)}, u32[]{:S(2)}, u32[]{:S(2)}) %collective-permute-start.1) | collective-permute-done | bytes 98336 | tf_op jit(solution)/shard_map/ppermute | solution.py:496
  17.4 1.3 %sweeps.3 = (bf16[2,2,3,32,128]{4,3,2,1,0:T(8,128)(2,1)S(1)}, bf16[2,2,2,32,128]{4,3,2,1,0:T(8,128)(2,1)S(1)}, bf16[2,2,2,32,128]{4,3,2,1,0:T(8,128)(2,1)S(1)}) custom-call(f32[20]{0:T(128)S(1)} %pad_maximum_fusion.refs_0_.scalar_ref, f32[2,3,3,32,128]{4,3,2,1,0:T(8,128)S(1)} %get-tuple-element.20.own_ref, f32[2,4,32,128]{3,2,1,0:T(8,128)S(1)} %get-tuple-element.21.edge_ref, ...), custom_call_target="tpu_custom_call" | custom-call | tf_op jit(solution)/shard_map/sweeps/pallas_call | solution.py:514
  18.7 0.1 collective-permute-start.4
  18.7 1.9 %collective-permute-start.5 = (bf16[2,2,2,32,128]{4,3,2,1,0:T(8,128)(2,1)S(1)}, bf16[2,2,2,32,128]{4,3,2,1,0:T(8,128)(2,1)S(1)}, u32[]{:S(2)}, u32[]{:S(2)}) collective-permute-start(bf16[2,2,2,32,128]{4,3,2,1,0:T(8,128)(2,1)S(1)} %get-tuple-element.31), channel_id=1, source_target_pairs={{0,1},{2,3},{4,5},{6,7},{8,9},{10,11},{12,13},{14,15},{1,0},{3,2},... | collective-permute-start | bytes 196616 | tf_op jit(solution)/shard_map/ppermute | solution.py:526
  20.6 0.4 %smooth.1.alone_ref = f32[2,2,3,32,128]{4,3,2,1,0:T(8,128)S(1)} custom-call(bf16[2,2,3,32,128]{4,3,2,1,0:T(8,128)(2,1)S(1)} %get-tuple-element.29.rows_ref), custom_call_target="tpu_custom_call" | custom-call | tf_op jit(solution)/shard_map/smooth/pallas_call | solution.py:530
  21.0 1.9 %all-gather = bf16[4,2,3,32,128]{4,3,2,1,0:T(8,128)(2,1)S(1)} all-gather(bf16[2,2,3,32,128]{4,3,2,1,0:T(8,128)(2,1)S(1)} %get-tuple-element.29.rows_ref), channel_id=2, replica_groups=mesh['rx'=2,'space'=16] {'rx'}, dimensions={0}, use_global_device_ids=true | all-gather | bytes 294912 | tf_op jit(solution)/shard_map/all_gather | solution.py:527
  23.0 0.0 collective-permute-done.4.far_in
  23.0 1.0 %collective-permute-done.5.near_in = bf16[2,2,2,32,128]{4,3,2,1,0:T(8,128)(2,1)S(1)} collective-permute-done((bf16[2,2,2,32,128]{4,3,2,1,0:T(8,128)(2,1)S(1)}, bf16[2,2,2,32,128]{4,3,2,1,0:T(8,128)(2,1)S(1)}, u32[]{:S(2)}, u32[]{:S(2)}) %collective-permute-start.5) | collective-permute-done | bytes 65568 | tf_op jit(solution)/shard_map/ppermute | solution.py:526
  23.9 0.9 %block.1 = (bf16[2,2,3,32,128]{4,3,2,1,0:T(8,128)(2,1)}, f32[16,4,8]{2,1,0:T(4,128)S(1)}) custom-call(bf16[2,2,3,32,128]{4,3,2,1,0:T(8,128)(2,1)S(1)} %get-tuple-element.29.rows_ref, f32[2,2,3,32,128]{4,3,2,1,0:T(8,128)S(1)} %smooth.1.alone_ref, bf16[2,2,2,32,128]{4,3,2,1,0:T(8,128)(2,1)S(1)} %collective-permute-done.4.far_in, ...), custom_call_target="tpu_custom_call" | custom-call | tf_op jit(solution)/shard_map/block/pallas_call | solution.py:538
  24.8 10.4 %all_to_all.5 = f32[16,4,8]{2,1,0:T(4,128)S(1)} all-to-all(f32[16,4,8]{2,1,0:T(4,128)S(1)} %get-tuple-element.32), channel_id=1, replica_groups={{15,14,13,12,11,10,9,8,7,6,5,4,3,2,1,0},{31,30,29,28,27,26,25,24,23,22,..., dimensions={0} | all-to-all | bytes 4096 | tf_op jit(solution)/shard_map/all_to_all | solution.py:553
  35.2 0.6 %reduce_sum.9 = f32[4,8]{1,0:T(4,128)} reduce(f32[16,4,8]{2,1,0:T(4,128)S(1)} %all_to_all.5, f32[]{:T(128)} %constant.0.clone.1), dimensions={0}, to_apply=%region_0.0 | reduce | flops 480 | bytes 2180 | tf_op jit(solution)/shard_map/reduce_sum | solution.py:554
Async XLA Ops:
  2.1 11.2 %collective-permute-start.2 = (bf16[13,32,128]{2,1,0:T(8,128)(2,1)S(1)}, bf16[13,32,128]{2,1,0:T(8,128)(2,1)S(1)}, u32[]{:S(2)}, u32[]{:S(2)}) collective-permute-start(bf16[13,32,128]{2,1,0:T(8,128)(2,1)S(1)} %get-tuple-element.25), channel_id=1, source_target_pairs={{1,2},{3,4},{5,6},{7,8},{9,10},{11,12},{13,14},{17,18},{19,20},{21... | collective-permute-start | bytes 319496 | tf_op jit(solution)/shard_map/ppermute | solution.py:495
  2.7 10.6 %collective-permute-start.3 = (bf16[13,32,128]{2,1,0:T(8,128)(2,1)S(1)}, bf16[13,32,128]{2,1,0:T(8,128)(2,1)S(1)}, u32[]{:S(2)}, u32[]{:S(2)}) collective-permute-start(bf16[13,32,128]{2,1,0:T(8,128)(2,1)S(1)} %get-tuple-element.26), channel_id=1, source_target_pairs={{0,1},{2,3},{4,5},{6,7},{8,9},{10,11},{12,13},{14,15},{1,0},{3,2},... | collective-permute-start | bytes 319496 | tf_op jit(solution)/shard_map/ppermute | solution.py:496
  10.3 4.3 %collective-permute-start = (bf16[12,32,128]{2,1,0:T(8,128)(2,1)S(1)}, bf16[12,32,128]{2,1,0:T(8,128)(2,1)S(1)}, u32[]{:S(2)}, u32[]{:S(2)}) collective-permute-start(bf16[12,32,128]{2,1,0:T(8,128)(2,1)S(1)} %get-tuple-element.23), channel_id=1, source_target_pairs={{1,2},{3,4},{5,6},{7,8},{9,10},{11,12},{13,14},{17,18},{19,20},{21... | collective-permute-start | bytes 294920 | tf_op jit(solution)/shard_map/ppermute | solution.py:495
  10.3 7.0 %collective-permute-start.1 = (bf16[12,32,128]{2,1,0:T(8,128)(2,1)S(1)}, bf16[12,32,128]{2,1,0:T(8,128)(2,1)S(1)}, u32[]{:S(2)}, u32[]{:S(2)}) collective-permute-start(bf16[12,32,128]{2,1,0:T(8,128)(2,1)S(1)} %get-tuple-element.24), channel_id=1, source_target_pairs={{0,1},{2,3},{4,5},{6,7},{8,9},{10,11},{12,13},{14,15},{1,0},{3,2},... | collective-permute-start | bytes 294920 | tf_op jit(solution)/shard_map/ppermute | solution.py:496
  18.7 4.3 %collective-permute-start.4 = (bf16[2,2,2,32,128]{4,3,2,1,0:T(8,128)(2,1)S(1)}, bf16[2,2,2,32,128]{4,3,2,1,0:T(8,128)(2,1)S(1)}, u32[]{:S(2)}, u32[]{:S(2)}) collective-permute-start(bf16[2,2,2,32,128]{4,3,2,1,0:T(8,128)(2,1)S(1)} %get-tuple-element.30), channel_id=1, source_target_pairs={{1,2},{3,4},{5,6},{7,8},{9,10},{11,12},{13,14},{17,18},{19,20},{21... | collective-permute-start | bytes 196616 | tf_op jit(solution)/shard_map/ppermute | solution.py:525
  18.7 5.2 %collective-permute-start.5 = (bf16[2,2,2,32,128]{4,3,2,1,0:T(8,128)(2,1)S(1)}, bf16[2,2,2,32,128]{4,3,2,1,0:T(8,128)(2,1)S(1)}, u32[]{:S(2)}, u32[]{:S(2)}) collective-permute-start(bf16[2,2,2,32,128]{4,3,2,1,0:T(8,128)(2,1)S(1)} %get-tuple-element.31), channel_id=1, source_target_pairs={{0,1},{2,3},{4,5},{6,7},{8,9},{10,11},{12,13},{14,15},{1,0},{3,2},... | collective-permute-start | bytes 196616 | tf_op jit(solution)/shard_map/ppermute | solution.py:526

commit v11 on v9

--- a/solution.py
+++ b/solution.py
@@ -122,14 +122,10 @@
         copies = [pltpu.make_async_copy(planes_ref.at[0], raw, sems.at[0])]
         copies += [pltpu.make_async_copy(a, b, sems.at[k + 1]) for k, (a, b) in enumerate(small)]
         others = [pltpu.make_async_copy(planes_ref.at[pl.ds(1, count - 1)], later_ref, sems.at[len(copies)])]
+        others.append(pltpu.make_async_copy(back_ref, field_ref, sems.at[len(copies) + 1]))
         for copy in copies + others:
             copy.start()
-        copies[1].wait()
-        for t in range(count):
-            field = pltpu.make_async_copy(back_ref.at[group[t]], field_ref.at[t], sems.at[len(copies) + 1 + t])
-            field.start()
-            others.append(field)
-        for copy in copies[:1] + copies[2:]:
+        for copy in copies:
             copy.wait()
         angular = angular_of(freq[group[s]])
         cell_at = cell[s]
@@ -213,9 +209,8 @@
         copy.wait()
 
 
-def sweep_kernel(s, planes, scalar_ref, own_ref, edge_ref, held_ref, field_ref, far_in, near_in, far_cond, near_cond, *refs):
+def sweep_kernel(s, count, planes, scalar_ref, own_ref, edge_ref, held_ref, field_ref, far_in, near_in, far_cond, near_cond, *refs):
     depth, height, breadth = held_ref.shape
-    count = field_ref.shape[0]
     final = s == count - 1
     if final:
         earlier = refs[:s]
@@ -315,7 +310,7 @@
         row_re = row_im = None
         for comp in range(3):
             re, im = after[comp], after[3 + comp]
-            field_re, field_im = field_ref[s, 0, comp, p], field_ref[s, 1, comp, p]
+            field_re, field_im = field_ref[group, 0, comp, p], field_ref[group, 1, comp, p]
             add_re, add_im = field_re * re - field_im * im, field_re * im + field_im * re
             row_re, row_im = (add_re, add_im) if comp == 0 else (row_re + add_re, row_im + add_im)
         coef = angular * held_ref[p]
@@ -465,7 +460,7 @@
             outs += [
                 shape(conductivity.shape, F32),
                 shape((count - 1,) + warm_start.shape[1:], F32),
-                shape((count,) + background.shape[1:], F32),
+                shape(background.shape, F32),
             ]
             scratch = [
                 pltpu.VMEM(warm_start.shape[1:], F32),
@@ -473,7 +468,7 @@
                 pltpu.SMEM(recv_cell.shape, jnp.int32),
                 pltpu.SMEM(src_group.shape, jnp.int32),
                 pltpu.SMEM(group_freq.shape, jnp.int32),
-            ] + scratch + [pltpu.SemaphoreType.DMA((7 + count,))]
+            ] + scratch + [pltpu.SemaphoreType.DMA((8,))]
         else:
             operands = [later, scalars, held]
             specs = [FULL, SCALARS, FULL]
@@ -510,7 +505,7 @@
             results = (rows_of, ends_of, ends_of)
             scratch.append(pltpu.VMEM((2,) + ends_of.shape, half))
         results = pl.pallas_call(
-            functools.partial(sweep_kernel, s, peers * depth),
+            functools.partial(sweep_kernel, s, count, peers * depth),
             out_shape=results,
             in_specs=[SCALARS] + [FULL] * (len(operands) - 1),
             out_specs=(FULL,) * len(results),

time: 35.3 us -> 34.9 us (0.989)
  Pallas kernels: 6.77 us -> 6.38 us
    pallas_call x2, Pallas kernels: 2.97 us -> 2.57 us  [shards(): pl.pallas_call(functools.partial(first_kernel, s), out_shape=tuple(outs),...]
where the time goes in v11:
time: 34.9 us; the launch traced here: 34.7 us
  blocking collectives  12.7 us (36%)
  starting transfers between devices  9.41 us (27%)
  Pallas kernels  6.38 us (18%)
  waiting for transfers between devices  4.66 us (13%)
  other arithmetic  0.76 us (2%)
  between operations  0.73 us (2%)
    all_to_all x1, blocking collectives, shards(): lax.all_to_all(partial_block, 'space', 0, 0, axis_index_groups=backwards)  10.7 us
    ppermute x2, starting transfers between devices, shards(): nears.append(lax.ppermute(result[1], 'space', near))  6.95 us
    ppermute x2, waiting for transfers between devices, shards(): nears.append(lax.ppermute(result[1], 'space', near))  3.62 us
    pallas_call x2, Pallas kernels, shards(): pl.pallas_call(functools.partial(first_kernel, s), out_shape=tuple(outs),...  2.57 us
    pallas_call x2, Pallas kernels, shards(): pl.pallas_call(functools.partial(sweep_kernel, s, count, peers * depth),...  2.52 us
    all_gather x1, blocking collectives, shards(): every = lax.all_gather(rows, 'rx', axis=0)  1.95 us
    ppermute x1, starting transfers between devices, shards(): from_near = lax.ppermute(to_near, 'space', near)  1.81 us
    ppermute x1, waiting for transfers between devices, shards(): from_near = lax.ppermute(to_near, 'space', near)  1.03 us
  transfers between devices with their start and end apart: 6, of which 3 were waited for; matrix products, arithmetic and copies ran while one was open for 1% of the time, Pallas kernels for 8%

profile of v11, /device:TPU:0, one launch (start us, length us, event | category | flops | bytes accessed | tf_op | source)
XLA Modules:
  0.0 34.7 jit_solution(5517503002490607433)
XLA Ops:
  0.6 0.0 copy-start.1
  0.6 0.0 copy-start.2
  0.7 0.0 copy-start.3
  0.7 0.0 copy-start
  0.7 1.6 %first_sweep.2 = (bf16[13,32,128]{2,1,0:T(8,128)(2,1)S(1)}, bf16[13,32,128]{2,1,0:T(8,128)(2,1)S(1)}, f32[2,3,3,32,128]{4,3,2,1,0:T(8,128)S(1)}, f32[2,4,32,128]...) custom-call(f32[2,2,3,3,32,128]{5,4,3,2,1,0:T(8,128)} %planes_ref.1,, ...), custom_call_target="tpu_custom_call" | custom-call | tf_op jit(solution)/shard_map/first_sweep/pallas_call | solution.py:475
  2.3 0.5 %collective-permute-start.2 = (bf16[13,32,128]{2,1,0:T(8,128)(2,1)S(1)}, bf16[13,32,128]{2,1,0:T(8,128)(2,1)S(1)}, u32[]{:S(2)}, u32[]{:S(2)}) collective-permute-start(bf16[13,32,128]{2,1,0:T(8,128)(2,1)S(1)} %get-tuple-element.25), channel_id=1, source_target_pairs={{1,2},{3,4},{5,6},{7,8},{9,10},{11,12},{13,14},{17,18},{19,20},{21... | collective-permute-start | bytes 319496 | tf_op jit(solution)/shard_map/ppermute | solution.py:488
  2.8 4.0 %collective-permute-start.3 = (bf16[13,32,128]{2,1,0:T(8,128)(2,1)S(1)}, bf16[13,32,128]{2,1,0:T(8,128)(2,1)S(1)}, u32[]{:S(2)}, u32[]{:S(2)}) collective-permute-start(bf16[13,32,128]{2,1,0:T(8,128)(2,1)S(1)} %get-tuple-element.26), channel_id=1, source_target_pairs={{0,1},{2,3},{4,5},{6,7},{8,9},{10,11},{12,13},{14,15},{1,0},{3,2},... | collective-permute-start | bytes 319496 | tf_op jit(solution)/shard_map/ppermute | solution.py:489
  6.8 0.0 copy-done
  6.8 0.1 reshape.7
  6.8 0.0 copy-done.1
  6.8 0.0 copy-done.2
  6.8 0.0 copy-done.3
  6.8 0.1 add_convert_fusion
  6.9 0.1 pad_maximum_fusion.refs_0_.scalar_ref
  7.0 1.0 %first_sweep.3 = (bf16[12,32,128]{2,1,0:T(8,128)(2,1)S(1)}, bf16[12,32,128]{2,1,0:T(8,128)(2,1)S(1)}, f32[2,3,3,32,128]{4,3,2,1,0:T(8,128)S(1)}, f32[2,4,32,128]{3,2,1,0:T(8,128)S(1)}) custom-call(f32[1,2,3,3,32,128]{5,4,3,2,1,0:T(8,128)S(1)} %get-tuple-element.18.planes_ref, f32[20]{0:T(128)S(1)} %pad_maximum_fusion.refs_0_.scalar_ref, ...), custom_call_target="tpu_custom_call" | custom-call | tf_op jit(solution)/shard_map/first_sweep/pallas_call | solution.py:475
  8.0 0.1 collective-permute-start
  8.1 3.0 %collective-permute-start.1 = (bf16[12,32,128]{2,1,0:T(8,128)(2,1)S(1)}, bf16[12,32,128]{2,1,0:T(8,128)(2,1)S(1)}, u32[]{:S(2)}, u32[]{:S(2)}) collective-permute-start(bf16[12,32,128]{2,1,0:T(8,128)(2,1)S(1)} %get-tuple-element.24), channel_id=1, source_target_pairs={{0,1},{2,3},{4,5},{6,7},{8,9},{10,11},{12,13},{14,15},{1,0},{3,2},... | collective-permute-start | bytes 294920 | tf_op jit(solution)/shard_map/ppermute | solution.py:489
  11.0 0.0 collective-permute-done.2.far_in.far_cond
  11.0 2.8 %collective-permute-done.3.near_in.near_cond = bf16[13,32,128]{2,1,0:T(8,128)(2,1)S(1)} collective-permute-done((bf16[13,32,128]{2,1,0:T(8,128)(2,1)S(1)}, bf16[13,32,128]{2,1,0:T(8,128)(2,1)S(1)}, u32[]{:S(2)}, u32[]{:S(2)}) %collective-permute-start.3) | collective-permute-done | bytes 106528 | tf_op jit(solution)/shard_map/ppermute | solution.py:489
  13.9 1.2 %sweeps.2.refs_0_ = bf16[2,3,32,128]{3,2,1,0:T(8,128)(2,1)S(1)} custom-call(f32[20]{0:T(128)S(1)} %pad_maximum_fusion.refs_0_.scalar_ref, f32[2,3,3,32,128]{4,3,2,1,0:T(8,128)S(1)} %get-tuple-element.27.own_ref, f32[2,4,32,128]{3,2,1,0:T(8,128)S(1)} %get-tuple-element.28.edge_ref, f32[3,32,128]{2,1,0:T(8,128)S(1)} %get-tuple-element.19.refs_1_.held_ref, ...), custom_call_target="tpu_custom_call" | custom-call | tf_op jit(solution)/shard_map/sweeps/pallas_call | solution.py:507
  15.1 0.0 collective-permute-done.far_in
  15.1 0.8 %collective-permute-done.1.near_in = bf16[12,32,128]{2,1,0:T(8,128)(2,1)S(1)} collective-permute-done((bf16[12,32,128]{2,1,0:T(8,128)(2,1)S(1)}, bf16[12,32,128]{2,1,0:T(8,128)(2,1)S(1)}, u32[]{:S(2)}, u32[]{:S(2)}) %collective-permute-start.1) | collective-permute-done | bytes 98336 | tf_op jit(solution)/shard_map/ppermute | solution.py:489
  15.9 1.3 %sweeps.3 = (bf16[2,2,3,32,128]{4,3,2,1,0:T(8,128)(2,1)S(1)}, bf16[2,2,2,32,128]{4,3,2,1,0:T(8,128)(2,1)S(1)}, bf16[2,2,2,32,128]{4,3,2,1,0:T(8,128)(2,1)S(1)}) custom-call(f32[20]{0:T(128)S(1)} %pad_maximum_fusion.refs_0_.scalar_ref, f32[2,3,3,32,128]{4,3,2,1,0:T(8,128)S(1)} %get-tuple-element.20.own_ref, f32[2,4,32,128]{3,2,1,0:T(8,128)S(1)} %get-tuple-element.21.edge_ref, ...), custom_call_target="tpu_custom_call" | custom-call | tf_op jit(solution)/shard_map/sweeps/pallas_call | solution.py:507
  17.2 0.1 collective-permute-start.4
  17.3 1.8 %collective-permute-start.5 = (bf16[2,2,2,32,128]{4,3,2,1,0:T(8,128)(2,1)S(1)}, bf16[2,2,2,32,128]{4,3,2,1,0:T(8,128)(2,1)S(1)}, u32[]{:S(2)}, u32[]{:S(2)}) collective-permute-start(bf16[2,2,2,32,128]{4,3,2,1,0:T(8,128)(2,1)S(1)} %get-tuple-element.31), channel_id=1, source_target_pairs={{0,1},{2,3},{4,5},{6,7},{8,9},{10,11},{12,13},{14,15},{1,0},{3,2},... | collective-permute-start | bytes 196616 | tf_op jit(solution)/shard_map/ppermute | solution.py:519
  19.1 0.4 %smooth.1.alone_ref = f32[2,2,3,32,128]{4,3,2,1,0:T(8,128)S(1)} custom-call(bf16[2,2,3,32,128]{4,3,2,1,0:T(8,128)(2,1)S(1)} %get-tuple-element.29.rows_ref), custom_call_target="tpu_custom_call" | custom-call | tf_op jit(solution)/shard_map/smooth/pallas_call | solution.py:523
  19.5 1.9 %all-gather = bf16[4,2,3,32,128]{4,3,2,1,0:T(8,128)(2,1)S(1)} all-gather(bf16[2,2,3,32,128]{4,3,2,1,0:T(8,128)(2,1)S(1)} %get-tuple-element.29.rows_ref), channel_id=2, replica_groups=mesh['rx'=2,'space'=16] {'rx'}, dimensions={0}, use_global_device_ids=true | all-gather | bytes 294912 | tf_op jit(solution)/shard_map/all_gather | solution.py:520
  21.5 0.0 collective-permute-done.4.far_in
  21.5 1.0 %collective-permute-done.5.near_in = bf16[2,2,2,32,128]{4,3,2,1,0:T(8,128)(2,1)S(1)} collective-permute-done((bf16[2,2,2,32,128]{4,3,2,1,0:T(8,128)(2,1)S(1)}, bf16[2,2,2,32,128]{4,3,2,1,0:T(8,128)(2,1)S(1)}, u32[]{:S(2)}, u32[]{:S(2)}) %collective-permute-start.5) | collective-permute-done | bytes 65568 | tf_op jit(solution)/shard_map/ppermute | solution.py:519
  22.5 0.9 %block.1 = (bf16[2,2,3,32,128]{4,3,2,1,0:T(8,128)(2,1)}, f32[16,4,8]{2,1,0:T(4,128)S(1)}) custom-call(bf16[2,2,3,32,128]{4,3,2,1,0:T(8,128)(2,1)S(1)} %get-tuple-element.29.rows_ref, f32[2,2,3,32,128]{4,3,2,1,0:T(8,128)S(1)} %smooth.1.alone_ref, bf16[2,2,2,32,128]{4,3,2,1,0:T(8,128)(2,1)S(1)} %collective-permute-done.4.far_in, ...), custom_call_target="tpu_custom_call" | custom-call | tf_op jit(solution)/shard_map/block/pallas_call | solution.py:531
  23.4 10.7 %all_to_all.5 = f32[16,4,8]{2,1,0:T(4,128)S(1)} all-to-all(f32[16,4,8]{2,1,0:T(4,128)S(1)} %get-tuple-element.32), channel_id=1, replica_groups={{15,14,13,12,11,10,9,8,7,6,5,4,3,2,1,0},{31,30,29,28,27,26,25,24,23,22,..., dimensions={0} | all-to-all | bytes 4096 | tf_op jit(solution)/shard_map/all_to_all | solution.py:546
  34.1 0.6 %reduce_sum.9 = f32[4,8]{1,0:T(4,128)} reduce(f32[16,4,8]{2,1,0:T(4,128)S(1)} %all_to_all.5, f32[]{:T(128)} %constant.0.clone.1), dimensions={0}, to_apply=%region_0.0 | reduce | flops 480 | bytes 2180 | tf_op jit(solution)/shard_map/reduce_sum | solution.py:547
Async XLA Ops:
  0.6 6.2 %copy-start.1 = (s32[4]{0:T(128)S(1)}, s32[4]{0:T(128)}, u32[]{:S(2)}) copy-start(s32[4]{0:T(128)} %refs_5_.1) | copy-start | bytes 52
  0.6 6.2 %copy-start.2 = (s32[2]{0:T(128)S(1)}, s32[2]{0:T(128)}, u32[]{:S(2)}) copy-start(s32[2]{0:T(128)} %refs_4_.1) | copy-start | bytes 28
  0.7 6.2 %copy-start.3 = (s32[2]{0:T(128)S(1)}, s32[2]{0:T(128)}, u32[]{:S(2)}) copy-start(s32[2]{0:T(128)} %refs_3_.1) | copy-start | bytes 28
  0.7 6.1 %copy-start = (f32[2,2,3]{2,1,0:T(2,128)S(1)}, f32[2,2,3]{2,1,0:T(2,128)}, u32[]{:S(2)}) copy-start(f32[2,2,3]{2,1,0:T(2,128)} %refs_2_.1) | copy-start | bytes 148
  2.3 8.8 %collective-permute-start.2 = (bf16[13,32,128]{2,1,0:T(8,128)(2,1)S(1)}, bf16[13,32,128]{2,1,0:T(8,128)(2,1)S(1)}, u32[]{:S(2)}, u32[]{:S(2)}) collective-permute-start(bf16[13,32,128]{2,1,0:T(8,128)(2,1)S(1)} %get-tuple-element.25), channel_id=1, source_target_pairs={{1,2},{3,4},{5,6},{7,8},{9,10},{11,12},{13,14},{17,18},{19,20},{21... | collective-permute-start | bytes 319496 | tf_op jit(solution)/shard_map/ppermute | solution.py:488
  2.8 11.1 %collective-permute-start.3 = (bf16[13,32,128]{2,1,0:T(8,128)(2,1)S(1)}, bf16[13,32,128]{2,1,0:T(8,128)(2,1)S(1)}, u32[]{:S(2)}, u32[]{:S(2)}) collective-permute-start(bf16[13,32,128]{2,1,0:T(8,128)(2,1)S(1)} %get-tuple-element.26), channel_id=1, source_target_pairs={{0,1},{2,3},{4,5},{6,7},{8,9},{10,11},{12,13},{14,15},{1,0},{3,2},... | collective-permute-start | bytes 319496 | tf_op jit(solution)/shard_map/ppermute | solution.py:489
  8.0 7.1 %collective-permute-start = (bf16[12,32,128]{2,1,0:T(8,128)(2,1)S(1)}, bf16[12,32,128]{2,1,0:T(8,128)(2,1)S(1)}, u32[]{:S(2)}, u32[]{:S(2)}) collective-permute-start(bf16[12,32,128]{2,1,0:T(8,128)(2,1)S(1)} %get-tuple-element.23), channel_id=1, source_target_pairs={{1,2},{3,4},{5,6},{7,8},{9,10},{11,12},{13,14},{17,18},{19,20},{21... | collective-permute-start | bytes 294920 | tf_op jit(solution)/shard_map/ppermute | solution.py:488
  8.1 7.9 %collective-permute-start.1 = (bf16[12,32,128]{2,1,0:T(8,128)(2,1)S(1)}, bf16[12,32,128]{2,1,0:T(8,128)(2,1)S(1)}, u32[]{:S(2)}, u32[]{:S(2)}) collective-permute-start(bf16[12,32,128]{2,1,0:T(8,128)(2,1)S(1)} %get-tuple-element.24), channel_id=1, source_target_pairs={{0,1},{2,3},{4,5},{6,7},{8,9},{10,11},{12,13},{14,15},{1,0},{3,2},... | collective-permute-start | bytes 294920 | tf_op jit(solution)/shard_map/ppermute | solution.py:489
  17.2 4.3 %collective-permute-start.4 = (bf16[2,2,2,32,128]{4,3,2,1,0:T(8,128)(2,1)S(1)}, bf16[2,2,2,32,128]{4,3,2,1,0:T(8,128)(2,1)S(1)}, u32[]{:S(2)}, u32[]{:S(2)}) collective-permute-start(bf16[2,2,2,32,128]{4,3,2,1,0:T(8,128)(2,1)S(1)} %get-tuple-element.30), channel_id=1, source_target_pairs={{1,2},{3,4},{5,6},{7,8},{9,10},{11,12},{13,14},{17,18},{19,20},{21... | collective-permute-start | bytes 196616 | tf_op jit(solution)/shard_map/ppermute | solution.py:518
  17.3 5.2 %collective-permute-start.5 = (bf16[2,2,2,32,128]{4,3,2,1,0:T(8,128)(2,1)S(1)}, bf16[2,2,2,32,128]{4,3,2,1,0:T(8,128)(2,1)S(1)}, u32[]{:S(2)}, u32[]{:S(2)}) collective-permute-start(bf16[2,2,2,32,128]{4,3,2,1,0:T(8,128)(2,1)S(1)} %get-tuple-element.31), channel_id=1, source_target_pairs={{0,1},{2,3},{4,5},{6,7},{8,9},{10,11},{12,13},{14,15},{1,0},{3,2},... | collective-permute-start | bytes 196616 | tf_op jit(solution)/shard_map/ppermute | solution.py:519

commit v12 on v11

--- a/solution.py
+++ b/solution.py
@@ -212,11 +212,8 @@
 def sweep_kernel(s, count, planes, scalar_ref, own_ref, edge_ref, held_ref, field_ref, far_in, near_in, far_cond, near_cond, *refs):
     depth, height, breadth = held_ref.shape
     final = s == count - 1
-    if final:
-        earlier = refs[:s]
-        rows_ref, far_ref, near_ref, one_, two_, got, conds, sent = refs[s:]
-    else:
-        rows_ref, one_, two_, got, conds = refs
+    earlier = refs[:s] if final else ()
+    rows_ref, far_ref, near_ref, one_, two_, got, conds, sent = refs[len(earlier) :]
     steps = Steps(height, breadth)
     index = lax.axis_index("space")
     first = index * depth
@@ -316,21 +313,18 @@
         coef = angular * held_ref[p]
         for part, value in enumerate((row_re, row_im)):
             value = (coef * value).astype(rows_ref.dtype)
-            if not final:
+            if final:
+                rows_ref[s, part, p] = value
+            else:
                 rows_ref[part, p] = value
-                continue
-            rows_ref[s, part, p] = value
             if p >= depth - REACH:
-                sent[high, s, part, p - depth + REACH] = value
+                sent[high, part, p - depth + REACH] = value
             if p < REACH:
-                sent[low, s, part, p] = value
-    if final:
-        for t, ref in enumerate(earlier):
-            rows_ref[t] = ref[...]
-            sent[high, t] = ref[:, depth - REACH :]
-            sent[low, t] = ref[:, :REACH]
-        far_ref[...] = sent[0]
-        near_ref[...] = sent[1]
+                sent[low, part, p] = value
+    for t, ref in enumerate(earlier):
+        rows_ref[t] = ref[...]
+    far_ref[...] = sent[0]
+    near_ref[...] = sent[1]
 
 
 def in_plane(steps, f):
@@ -363,21 +357,25 @@
     lax.fori_loop(0, count, one_source, 0)
 
 
-def block_kernel(cells, rows_ref, alone_ref, far_in, near_in, all_ref, smooth_ref, block_ref, got, rounded, sums, sem):
+def block_kernel(cells, rows_ref, alone_ref, all_ref, *refs):
     count, _, depth, height, breadth = rows_ref.shape
     ranks = all_ref.shape[0]
     steps = Steps(height, breadth)
     many = ranks * count * 2
+    fars, nears = refs[:count], refs[count : 2 * count]
+    smooth_ref, block_ref, got, rounded, sums, sem = refs[2 * count :]
     index = lax.axis_index("space")
-    receive(got, far_in, near_in, (index == 0) | (index == lax.axis_size("space") - 1))
+    at_end = (index == 0) | (index == lax.axis_size("space") - 1)
+    for s in range(count):
+        receive(got.at[s], fars[s], nears[s], at_end)
     odd = index & 1
     low, high = odd, 1 - odd
 
     def one_row(s, part):
         value = [alone_ref[s, part, p] for p in range(depth)]
         for side, nearest, order in ((low, REACH - 1, 1), (high, 0, -1)):
-            close = got[side, s, part, nearest].astype(F32)
-            beyond = got[side, s, part, REACH - 1 - nearest].astype(F32)
+            close = got[s, side, part, nearest].astype(F32)
+            beyond = got[s, side, part, REACH - 1 - nearest].astype(F32)
             end = 0 if order > 0 else depth - 1
             value[end] = value[end] + (2.0 * KAPPA * in_plane(steps, close) + KAPPA * KAPPA * beyond)
             value[end + order] = value[end + order] + KAPPA * KAPPA * close
@@ -489,34 +487,31 @@
         nears.append(lax.ppermute(result[1], "space", near))
 
     rows_of = shape((count, 2, depth) + plane, half)
-    ends_of = shape((count, 2, REACH) + plane, half)
-    earlier = []
+    ends_of = shape((2, REACH) + plane, half)
+    earlier, far_ends, near_ends = [], [], []
     for s in range(count):
         operands = [scalars, own[s], edges[s], held, field, fars[s], nears[s], fars[0], nears[0]]
-        scratch = [
-            pltpu.VMEM((2, 3, depth + 2) + plane, F32),
-            pltpu.VMEM((2, 3, depth + 2) + plane, F32),
-            pltpu.VMEM((2, 2 * SENT) + plane, half),
-            pltpu.VMEM((2,) + plane, half),
-        ]
-        results = (shape((2, depth) + plane, half),)
         if s == count - 1:
             operands += earlier
-            results = (rows_of, ends_of, ends_of)
-            scratch.append(pltpu.VMEM((2,) + ends_of.shape, half))
         results = pl.pallas_call(
             functools.partial(sweep_kernel, s, count, peers * depth),
-            out_shape=results,
+            out_shape=(rows_of if s == count - 1 else shape(rows_of.shape[1:], half), ends_of, ends_of),
             in_specs=[SCALARS] + [FULL] * (len(operands) - 1),
-            out_specs=(FULL,) * len(results),
-            scratch_shapes=scratch,
+            out_specs=(FULL,) * 3,
+            scratch_shapes=[
+                pltpu.VMEM((2, 3, depth + 2) + plane, F32),
+                pltpu.VMEM((2, 3, depth + 2) + plane, F32),
+                pltpu.VMEM((2, 2 * SENT) + plane, half),
+                pltpu.VMEM((2,) + plane, half),
+                pltpu.VMEM((2,) + ends_of.shape, half),
+            ],
             compiler_params=KERNEL,
             name="sweeps",
         )(*operands)
         earlier.append(results[0])
-    rows, to_far, to_near = results
-    from_far = lax.ppermute(to_far, both, far)
-    from_near = lax.ppermute(to_near, "space", near)
+        far_ends.append(lax.ppermute(results[1], both, far))
+        near_ends.append(lax.ppermute(results[2], "space", near))
+    rows = earlier[-1]
     every = lax.all_gather(rows, "rx", axis=0)
 
     many = 2 * count * ranks
@@ -531,17 +526,17 @@
     smoothed, partial_block = pl.pallas_call(
         functools.partial(block_kernel, cells),
         out_shape=(rows_of, shape((peers, 2 * count, many), F32)),
-        in_specs=[FULL] * 5,
+        in_specs=[FULL] * (3 + 2 * count),
         out_specs=(HBM, FULL),
         scratch_shapes=[
-            pltpu.VMEM((2,) + ends_of.shape, half),
+            pltpu.VMEM((count, 2) + ends_of.shape, half),
             pltpu.VMEM(rows_of.shape, half),
             pltpu.VMEM((2 * count * many, 8, breadth), F32),
             pltpu.SemaphoreType.DMA,
         ],
         compiler_params=KERNEL,
         name="block",
-    )(rows, alone, from_far, from_near, every)
+    )(rows, alone, every, *far_ends, *near_ends)
     backwards = [list(range(peers - 1, -1, -1))]
     pieces = lax.all_to_all(partial_block, "space", 0, 0, axis_index_groups=backwards)
     return (jnp.sum(pieces, axis=0), smoothed)

time: 34.9 us -> 37.1 us (1.063)
  starting transfers between devices: 9.41 us -> 13.6 us
  waiting for transfers between devices: 4.66 us -> 2.86 us
    ppermute x2 -> x4, starting transfers between devices: 1.88 us -> 6.07 us  [the longest x2 5.93 us: shards(): near_ends.append(lax.ppermute(results[2], 'space', near))]
    ppermute x2 -> x4, waiting for transfers between devices: 1.03 us -> 0.01 us  [the longest x2 0.01 us: shards(): far_ends.append(lax.ppermute(results[1], both, far))]
    ppermute x2, waiting for transfers between devices: 3.62 us -> 2.84 us  [shards(): nears.append(lax.ppermute(result[1], 'space', near))]
  transfers between devices with their start and end apart: 6 -> 8, of which waited for: 3 -> 1; matrix products, arithmetic and copies ran while one was open for 1% -> 1% of each run, Pallas kernels for 8% -> 11%
where the time goes in v12:
time: 37.1 us; the launch traced here: 36.9 us
  starting transfers between devices  13.6 us (37%)
  blocking collectives  12.5 us (34%)
  Pallas kernels  6.4 us (17%)
  waiting for transfers between devices  2.86 us (8%)
  other arithmetic  0.76 us (2%)
  between operations  0.74 us (2%)
    all_to_all x1, blocking collectives, shards(): lax.all_to_all(partial_block, 'space', 0, 0, axis_index_groups=backwards)  10.5 us
    ppermute x2, starting transfers between devices, shards(): nears.append(lax.ppermute(result[1], 'space', near))  6.95 us
    ppermute x2, starting transfers between devices, shards(): near_ends.append(lax.ppermute(results[2], 'space', near))  5.93 us
    ppermute x2, waiting for transfers between devices, shards(): nears.append(lax.ppermute(result[1], 'space', near))  2.84 us
    pallas_call x2, Pallas kernels, shards(): pl.pallas_call(functools.partial(first_kernel, s), out_shape=tuple(outs),...  2.57 us
    pallas_call x2, Pallas kernels, shards(): pl.pallas_call(functools.partial(sweep_kernel, s, count, peers * depth),...  2.53 us
    all_gather x1, blocking collectives, shards(): every = lax.all_gather(rows, 'rx', axis=0)  1.95 us
    pallas_call x1, Pallas kernels, shards(): pl.pallas_call(functools.partial(block_kernel, cells), out_shape=(rows_of...  0.89 us
  transfers between devices with their start and end apart: 8, of which 1 were waited for; matrix products, arithmetic and copies ran while one was open for 1% of the time, Pallas kernels for 11%

profile of v12, /device:TPU:0, one launch (start us, length us, event | category | flops | bytes accessed | tf_op | source)
XLA Modules:
  0.0 36.9 jit_solution(14364495917868154994)
XLA Ops:
  0.6 0.0 copy-start.1
  0.6 0.0 copy-start.2
  0.7 0.0 copy-start.3
  0.7 0.0 copy-start
  0.7 1.6 %first_sweep.2 = (bf16[13,32,128]{2,1,0:T(8,128)(2,1)S(1)}, bf16[13,32,128]{2,1,0:T(8,128)(2,1)S(1)}, f32[2,3,3,32,128]{4,3,2,1,0:T(8,128)S(1)}, f32[2,4,32,128]...) custom-call(f32[2,2,3,3,32,128]{5,4,3,2,1,0:T(8,128)} %planes_ref.1,, ...), custom_call_target="tpu_custom_call" | custom-call | tf_op jit(solution)/shard_map/first_sweep/pallas_call | solution.py:473
  2.3 0.5 %collective-permute-start.2 = (bf16[13,32,128]{2,1,0:T(8,128)(2,1)S(1)}, bf16[13,32,128]{2,1,0:T(8,128)(2,1)S(1)}, u32[]{:S(2)}, u32[]{:S(2)}) collective-permute-start(bf16[13,32,128]{2,1,0:T(8,128)(2,1)S(1)} %get-tuple-element.28), channel_id=1, source_target_pairs={{1,2},{3,4},{5,6},{7,8},{9,10},{11,12},{13,14},{17,18},{19,20},{21... | collective-permute-start | bytes 319496 | tf_op jit(solution)/shard_map/ppermute | solution.py:486
  2.8 4.0 %collective-permute-start.3 = (bf16[13,32,128]{2,1,0:T(8,128)(2,1)S(1)}, bf16[13,32,128]{2,1,0:T(8,128)(2,1)S(1)}, u32[]{:S(2)}, u32[]{:S(2)}) collective-permute-start(bf16[13,32,128]{2,1,0:T(8,128)(2,1)S(1)} %get-tuple-element.29), channel_id=1, source_target_pairs={{0,1},{2,3},{4,5},{6,7},{8,9},{10,11},{12,13},{14,15},{1,0},{3,2},... | collective-permute-start | bytes 319496 | tf_op jit(solution)/shard_map/ppermute | solution.py:487
  6.8 0.0 copy-done
  6.8 0.1 reshape.7
  6.8 0.0 copy-done.1
  6.8 0.0 copy-done.2
  6.8 0.0 copy-done.3
  6.8 0.1 add_convert_fusion
  6.9 0.1 pad_maximum_fusion.refs_0_.scalar_ref
  7.0 1.0 %first_sweep.3 = (bf16[12,32,128]{2,1,0:T(8,128)(2,1)S(1)}, bf16[12,32,128]{2,1,0:T(8,128)(2,1)S(1)}, f32[2,3,3,32,128]{4,3,2,1,0:T(8,128)S(1)}, f32[2,4,32,128]{3,2,1,0:T(8,128)S(1)}) custom-call(f32[1,2,3,3,32,128]{5,4,3,2,1,0:T(8,128)S(1)} %get-tuple-element.21.planes_ref, f32[20]{0:T(128)S(1)} %pad_maximum_fusion.refs_0_.scalar_ref, ...), custom_call_target="tpu_custom_call" | custom-call | tf_op jit(solution)/shard_map/first_sweep/pallas_call | solution.py:473
  8.0 0.1 collective-permute-start
  8.1 3.0 %collective-permute-start.1 = (bf16[12,32,128]{2,1,0:T(8,128)(2,1)S(1)}, bf16[12,32,128]{2,1,0:T(8,128)(2,1)S(1)}, u32[]{:S(2)}, u32[]{:S(2)}) collective-permute-start(bf16[12,32,128]{2,1,0:T(8,128)(2,1)S(1)} %get-tuple-element.27), channel_id=1, source_target_pairs={{0,1},{2,3},{4,5},{6,7},{8,9},{10,11},{12,13},{14,15},{1,0},{3,2},... | collective-permute-start | bytes 294920 | tf_op jit(solution)/shard_map/ppermute | solution.py:487
  11.0 0.0 collective-permute-done.2.far_in.far_cond
  11.0 2.8 %collective-permute-done.3.near_in.near_cond = bf16[13,32,128]{2,1,0:T(8,128)(2,1)S(1)} collective-permute-done((bf16[13,32,128]{2,1,0:T(8,128)(2,1)S(1)}, bf16[13,32,128]{2,1,0:T(8,128)(2,1)S(1)}, u32[]{:S(2)}, u32[]{:S(2)}) %collective-permute-start.3) | collective-permute-done | bytes 106528 | tf_op jit(solution)/shard_map/ppermute | solution.py:487
  13.9 1.3 %sweeps.2 = (bf16[2,3,32,128]{3,2,1,0:T(8,128)(2,1)S(1)}, bf16[2,2,32,128]{3,2,1,0:T(8,128)(2,1)S(1)}, bf16[2,2,32,128]{3,2,1,0:T(8,128)(2,1)S(1)}) custom-call(f32[20]{0:T(128)S(1)} %pad_maximum_fusion.refs_0_.scalar_ref, f32[2,3,3,32,128]{4,3,2,1,0:T(8,128)S(1)} %get-tuple-element.30.own_ref, f32[2,4,32,128]{3,2,1,0:T(8,128)S(1)} %get-tuple-element.31.edge_ref, ...), custom_call_target="tpu_custom_call" | custom-call | tf_op jit(solution)/shard_map/sweeps/pallas_call | solution.py:496
  15.1 0.1 collective-permute-start.4
  15.2 2.5 %collective-permute-start.6 = (bf16[2,2,32,128]{3,2,1,0:T(8,128)(2,1)S(1)}, bf16[2,2,32,128]{3,2,1,0:T(8,128)(2,1)S(1)}, u32[]{:S(2)}, u32[]{:S(2)}) collective-permute-start(bf16[2,2,32,128]{3,2,1,0:T(8,128)(2,1)S(1)} %get-tuple-element.36), channel_id=1, source_target_pairs={{0,1},{2,3},{4,5},{6,7},{8,9},{10,11},{12,13},{14,15},{1,0},{3,2},... | collective-permute-start | bytes 98312 | tf_op jit(solution)/shard_map/ppermute | solution.py:513
  17.8 0.0 collective-permute-done.far_in
  17.8 0.0 collective-permute-done.1.near_in
  17.8 1.3 %sweeps.3 = (bf16[2,2,3,32,128]{4,3,2,1,0:T(8,128)(2,1)S(1)}, bf16[2,2,32,128]{3,2,1,0:T(8,128)(2,1)S(1)}, bf16[2,2,32,128]{3,2,1,0:T(8,128)(2,1)S(1)}) custom-call(f32[20]{0:T(128)S(1)} %pad_maximum_fusion.refs_0_.scalar_ref, f32[2,3,3,32,128]{4,3,2,1,0:T(8,128)S(1)} %get-tuple-element.23.own_ref, f32[2,4,32,128]{3,2,1,0:T(8,128)S(1)} %get-tuple-element.24.edge_ref, ...), custom_call_target="tpu_custom_call" | custom-call | tf_op jit(solution)/shard_map/sweeps/pallas_call | solution.py:496
  19.0 0.1 collective-permute-start.5
  19.1 3.4 %collective-permute-start.7 = (bf16[2,2,32,128]{3,2,1,0:T(8,128)(2,1)S(1)}, bf16[2,2,32,128]{3,2,1,0:T(8,128)(2,1)S(1)}, u32[]{:S(2)}, u32[]{:S(2)}) collective-permute-start(bf16[2,2,32,128]{3,2,1,0:T(8,128)(2,1)S(1)} %get-tuple-element.37), channel_id=1, source_target_pairs={{0,1},{2,3},{4,5},{6,7},{8,9},{10,11},{12,13},{14,15},{1,0},{3,2},... | collective-permute-start | bytes 98312 | tf_op jit(solution)/shard_map/ppermute | solution.py:513
  22.5 0.4 %smooth.1.alone_ref = f32[2,2,3,32,128]{4,3,2,1,0:T(8,128)S(1)} custom-call(bf16[2,2,3,32,128]{4,3,2,1,0:T(8,128)(2,1)S(1)} %get-tuple-element.33.rows_ref), custom_call_target="tpu_custom_call" | custom-call | tf_op jit(solution)/shard_map/smooth/pallas_call | solution.py:518
  22.9 1.9 %all-gather = bf16[4,2,3,32,128]{4,3,2,1,0:T(8,128)(2,1)S(1)} all-gather(bf16[2,2,3,32,128]{4,3,2,1,0:T(8,128)(2,1)S(1)} %get-tuple-element.33.rows_ref), channel_id=2, replica_groups=mesh['rx'=2,'space'=16] {'rx'}, dimensions={0}, use_global_device_ids=true | all-gather | bytes 294912 | tf_op jit(solution)/shard_map/all_gather | solution.py:515
  24.9 0.0 collective-permute-done.4.refs_0_
  24.9 0.0 collective-permute-done.6.refs_2_
  24.9 0.0 collective-permute-done.5.refs_1_
  24.9 0.0 collective-permute-done.7.refs_3_
  24.9 0.9 %block.1 = (bf16[2,2,3,32,128]{4,3,2,1,0:T(8,128)(2,1)}, f32[16,4,8]{2,1,0:T(4,128)S(1)}) custom-call(bf16[2,2,3,32,128]{4,3,2,1,0:T(8,128)(2,1)S(1)} %get-tuple-element.33.rows_ref, f32[2,2,3,32,128]{4,3,2,1,0:T(8,128)S(1)} %smooth.1.alone_ref, bf16[2,2,2,3,32,128]{5,4,3,2,1,0:T(8,128)(2,1)S(1)} %bitcast.1, ...), custom_call_target="tpu_custom_call" | custom-call | tf_op jit(solution)/shard_map/block/pallas_call | solution.py:526
  25.8 10.5 %all_to_all.5 = f32[16,4,8]{2,1,0:T(4,128)S(1)} all-to-all(f32[16,4,8]{2,1,0:T(4,128)S(1)} %get-tuple-element.38), channel_id=1, replica_groups={{15,14,13,12,11,10,9,8,7,6,5,4,3,2,1,0},{31,30,29,28,27,26,25,24,23,22,..., dimensions={0} | all-to-all | bytes 4096 | tf_op jit(solution)/shard_map/all_to_all | solution.py:541
  36.3 0.6 %reduce_sum.9 = f32[4,8]{1,0:T(4,128)} reduce(f32[16,4,8]{2,1,0:T(4,128)S(1)} %all_to_all.5, f32[]{:T(128)} %constant.0.clone.1), dimensions={0}, to_apply=%region_0.0 | reduce | flops 480 | bytes 2180 | tf_op jit(solution)/shard_map/reduce_sum | solution.py:542
Async XLA Ops:
  0.6 6.2 %copy-start.1 = (s32[4]{0:T(128)S(1)}, s32[4]{0:T(128)}, u32[]{:S(2)}) copy-start(s32[4]{0:T(128)} %refs_5_.1) | copy-start | bytes 52
  0.6 6.2 %copy-start.2 = (s32[2]{0:T(128)S(1)}, s32[2]{0:T(128)}, u32[]{:S(2)}) copy-start(s32[2]{0:T(128)} %refs_4_.1) | copy-start | bytes 28
  0.7 6.2 %copy-start.3 = (s32[2]{0:T(128)S(1)}, s32[2]{0:T(128)}, u32[]{:S(2)}) copy-start(s32[2]{0:T(128)} %refs_3_.1) | copy-start | bytes 28
  0.7 6.1 %copy-start = (f32[2,2,3]{2,1,0:T(2,128)S(1)}, f32[2,2,3]{2,1,0:T(2,128)}, u32[]{:S(2)}) copy-start(f32[2,2,3]{2,1,0:T(2,128)} %refs_2_.1) | copy-start | bytes 148
  2.3 8.8 %collective-permute-start.2 = (bf16[13,32,128]{2,1,0:T(8,128)(2,1)S(1)}, bf16[13,32,128]{2,1,0:T(8,128)(2,1)S(1)}, u32[]{:S(2)}, u32[]{:S(2)}) collective-permute-start(bf16[13,32,128]{2,1,0:T(8,128)(2,1)S(1)} %get-tuple-element.28), channel_id=1, source_target_pairs={{1,2},{3,4},{5,6},{7,8},{9,10},{11,12},{13,14},{17,18},{19,20},{21... | collective-permute-start | bytes 319496 | tf_op jit(solution)/shard_map/ppermute | solution.py:486
  2.8 11.1 %collective-permute-start.3 = (bf16[13,32,128]{2,1,0:T(8,128)(2,1)S(1)}, bf16[13,32,128]{2,1,0:T(8,128)(2,1)S(1)}, u32[]{:S(2)}, u32[]{:S(2)}) collective-permute-start(bf16[13,32,128]{2,1,0:T(8,128)(2,1)S(1)} %get-tuple-element.29), channel_id=1, source_target_pairs={{0,1},{2,3},{4,5},{6,7},{8,9},{10,11},{12,13},{14,15},{1,0},{3,2},... | collective-permute-start | bytes 319496 | tf_op jit(solution)/shard_map/ppermute | solution.py:487
  8.0 9.8 %collective-permute-start = (bf16[12,32,128]{2,1,0:T(8,128)(2,1)S(1)}, bf16[12,32,128]{2,1,0:T(8,128)(2,1)S(1)}, u32[]{:S(2)}, u32[]{:S(2)}) collective-permute-start(bf16[12,32,128]{2,1,0:T(8,128)(2,1)S(1)} %get-tuple-element.26), channel_id=1, source_target_pairs={{1,2},{3,4},{5,6},{7,8},{9,10},{11,12},{13,14},{17,18},{19,20},{21... | collective-permute-start | bytes 294920 | tf_op jit(solution)/shard_map/ppermute | solution.py:486
  8.1 9.7 %collective-permute-start.1 = (bf16[12,32,128]{2,1,0:T(8,128)(2,1)S(1)}, bf16[12,32,128]{2,1,0:T(8,128)(2,1)S(1)}, u32[]{:S(2)}, u32[]{:S(2)}) collective-permute-start(bf16[12,32,128]{2,1,0:T(8,128)(2,1)S(1)} %get-tuple-element.27), channel_id=1, source_target_pairs={{0,1},{2,3},{4,5},{6,7},{8,9},{10,11},{12,13},{14,15},{1,0},{3,2},... | collective-permute-start | bytes 294920 | tf_op jit(solution)/shard_map/ppermute | solution.py:487
  15.1 9.7 %collective-permute-start.4 = (bf16[2,2,32,128]{3,2,1,0:T(8,128)(2,1)S(1)}, bf16[2,2,32,128]{3,2,1,0:T(8,128)(2,1)S(1)}, u32[]{:S(2)}, u32[]{:S(2)}) collective-permute-start(bf16[2,2,32,128]{3,2,1,0:T(8,128)(2,1)S(1)} %get-tuple-element.34), channel_id=1, source_target_pairs={{1,2},{3,4},{5,6},{7,8},{9,10},{11,12},{13,14},{17,18},{19,20},{21... | collective-permute-start | bytes 98312 | tf_op jit(solution)/shard_map/ppermute | solution.py:512
  15.2 9.7 %collective-permute-start.6 = (bf16[2,2,32,128]{3,2,1,0:T(8,128)(2,1)S(1)}, bf16[2,2,32,128]{3,2,1,0:T(8,128)(2,1)S(1)}, u32[]{:S(2)}, u32[]{:S(2)}) collective-permute-start(bf16[2,2,32,128]{3,2,1,0:T(8,128)(2,1)S(1)} %get-tuple-element.36), channel_id=1, source_target_pairs={{0,1},{2,3},{4,5},{6,7},{8,9},{10,11},{12,13},{14,15},{1,0},{3,2},... | collective-permute-start | bytes 98312 | tf_op jit(solution)/shard_map/ppermute | solution.py:513
  19.0 5.8 %collective-permute-start.5 = (bf16[2,2,32,128]{3,2,1,0:T(8,128)(2,1)S(1)}, bf16[2,2,32,128]{3,2,1,0:T(8,128)(2,1)S(1)}, u32[]{:S(2)}, u32[]{:S(2)}) collective-permute-start(bf16[2,2,32,128]{3,2,1,0:T(8,128)(2,1)S(1)} %get-tuple-element.35), channel_id=1, source_target_pairs={{1,2},{3,4},{5,6},{7,8},{9,10},{11,12},{13,14},{17,18},{19,20},{21... | collective-permute-start | bytes 98312 | tf_op jit(solution)/shard_map/ppermute | solution.py:512
  19.1 5.8 %collective-permute-start.7 = (bf16[2,2,32,128]{3,2,1,0:T(8,128)(2,1)S(1)}, bf16[2,2,32,128]{3,2,1,0:T(8,128)(2,1)S(1)}, u32[]{:S(2)}, u32[]{:S(2)}) collective-permute-start(bf16[2,2,32,128]{3,2,1,0:T(8,128)(2,1)S(1)} %get-tuple-element.37), channel_id=1, source_target_pairs={{0,1},{2,3},{4,5},{6,7},{8,9},{10,11},{12,13},{14,15},{1,0},{3,2},... | collective-permute-start | bytes 98312 | tf_op jit(solution)/shard_map/ppermute | solution.py:513

commit v13 on v11

--- a/solution.py
+++ b/solution.py
@@ -100,23 +100,23 @@
                 ref[at] = ref[at] + amount * weight(part, comp)
 
 
-def receive(got, far_in, near_in, at_end):
-    got[1] = near_in[: got.shape[1]]
-
-    @pl.when(at_end)
+def by_parity(far_ref, near_ref, body):
+    odd = lax.axis_index("space") & 1
+
+    @pl.when(odd == 0)
     def _():
-        got[0] = jnp.zeros(got.shape[1:], got.dtype)
-
-    @pl.when(jnp.logical_not(at_end))
+        body(far_ref, near_ref)
+
+    @pl.when(odd == 1)
     def _():
-        got[0] = far_in[: got.shape[1]]
+        body(near_ref, far_ref)
 
 
 def first_kernel(s, planes_ref, *refs):
     if s == 0:
         cond_ref, back_ref, weight_ref, cell_ref, group_ref, freq_ref = refs[:6]
         far_ref, near_ref, own_ref, edge_ref, held_ref, later_ref, field_ref = refs[6:13]
-        raw, weight_of, cell, group, freq, sent, sems = refs[13:]
+        raw, weight_of, cell, group, freq, sems = refs[13:]
         count = planes_ref.shape[0]
         small = ((group_ref, group), (freq_ref, freq), (cell_ref, cell), (weight_ref, weight_of), (cond_ref, held_ref))
         copies = [pltpu.make_async_copy(planes_ref.at[0], raw, sems.at[0])]
@@ -133,7 +133,7 @@
         def weight(part, comp):
             return weight_of[s, part, comp]
     else:
-        scalar_ref, held_ref, far_ref, near_ref, own_ref, edge_ref, sent = refs
+        scalar_ref, held_ref, far_ref, near_ref, own_ref, edge_ref = refs
         raw = planes_ref.at[s - 1]
         count = planes_ref.shape[0] + 1
         others = []
@@ -147,64 +147,63 @@
 
     depth, height, breadth = held_ref.shape
     steps = Steps(height, breadth)
-    half = sent.dtype
+    half = far_ref.dtype
     index = lax.axis_index("space")
     first = index * depth
-    down = index & 1
-    up = 1 - down
     last = depth - 1
     scales = RELAX * angular, -RELAX * angular
     point = Point(cell_at, first, steps)
-    if s == 0:
-        sent[up, 2 * SENT] = held_ref[last].astype(half)
-        sent[down, 2 * SENT] = held_ref[0].astype(half)
-
-    before = []
-    for part in range(2):
-        ey, ez = raw[part, 1, 0], raw[part, 2, 0]
-        for k, f in enumerate((ey, ez)):
-            sent[down, part * SENT + k] = f.astype(half)
-            edge_ref[part, k] = f
-        before.append((-ez, ey))
-    for p in range(depth):
-        for part in range(2):
-            e = [raw[part, comp, p] for comp in range(3)]
-            e_next = [None if comp == 0 else raw[part, comp, p + 1] for comp in range(3)] if p < last else None
-            hy, hz = steps.magnetic_yz(e, e_next)
-            if p == last:
-                for k, f in enumerate((hy, hz)):
-                    sent[up, part * SENT + k] = f.astype(half)
-                    edge_ref[part, 2 + k] = f
+    def sweep_and_send(down_ref, up_ref):
+        if s == 0:
+            up_ref[2 * SENT] = held_ref[last].astype(half)
+            down_ref[2 * SENT] = held_ref[0].astype(half)
+
+        before = []
+        for part in range(2):
+            ey, ez = raw[part, 1, 0], raw[part, 2, 0]
+            for k, f in enumerate((ey, ez)):
+                down_ref[part * SENT + k] = f.astype(half)
+                edge_ref[part, k] = f
+            before.append((-ez, ey))
+        for p in range(depth):
+            for part in range(2):
+                e = [raw[part, comp, p] for comp in range(3)]
+                e_next = [None if comp == 0 else raw[part, comp, p + 1] for comp in range(3)] if p < last else None
+                hy, hz = steps.magnetic_yz(e, e_next)
+                if p == last:
+                    for k, f in enumerate((hy, hz)):
+                        up_ref[part * SENT + k] = f.astype(half)
+                        edge_ref[part, 2 + k] = f
+                hx = steps.magnetic_x(e)
+                coef = scales[part] * held_ref[p]
+                for comp in range(3):
+                    curl = steps.curl_back(comp, hx, hy, hz, before[part])
+                    own_ref[part, comp, p] = e[comp] - RELAX * curl + coef * raw[1 - part, comp, p]
+                before[part] = hy, hz
+        point.add_to(own_ref, 0, depth, 0, weight)
+
+        row = lax.broadcasted_iota(jnp.int32, (height, breadth), 0)
+        at_last = jnp.where(point.plane == last, F32(1.0), F32(0.0))
+        here = jnp.where((row == point.row) & (steps.lane == point.lane), RELAX * at_last, 0.0)
+        for part in range(2):
+            ex, ey, ez = [own_ref[part, comp, 0] for comp in range(3)]
+            hy, hz = steps.up_z(ex) - own_ref[part, 2, 1], own_ref[part, 1, 1] - steps.up_y(ex)
+            for k, f in enumerate((ey, ez, hy, hz)):
+                down_ref[part * SENT + 2 + k] = f.astype(half)
+            e = [own_ref[part, comp, last] for comp in range(3)]
+            behind = steps.magnetic_yz([own_ref[part, comp, last - 1] for comp in range(3)], e)
+            hy, hz = steps.magnetic_yz(e, None)
             hx = steps.magnetic_x(e)
-            coef = scales[part] * held_ref[p]
+            coef = scales[part] * held_ref[last]
+            after = []
             for comp in range(3):
-                curl = steps.curl_back(comp, hx, hy, hz, before[part])
-                own_ref[part, comp, p] = e[comp] - RELAX * curl + coef * raw[1 - part, comp, p]
-            before[part] = hy, hz
-    point.add_to(own_ref, 0, depth, 0, weight)
-
-    row = lax.broadcasted_iota(jnp.int32, (height, breadth), 0)
-    at_last = jnp.where(point.plane == last, F32(1.0), F32(0.0))
-    here = jnp.where((row == point.row) & (steps.lane == point.lane), RELAX * at_last, 0.0)
-    for part in range(2):
-        ex, ey, ez = [own_ref[part, comp, 0] for comp in range(3)]
-        hy, hz = steps.up_z(ex) - own_ref[part, 2, 1], own_ref[part, 1, 1] - steps.up_y(ex)
-        for k, f in enumerate((ey, ez, hy, hz)):
-            sent[down, part * SENT + 2 + k] = f.astype(half)
-        e = [own_ref[part, comp, last] for comp in range(3)]
-        behind = steps.magnetic_yz([own_ref[part, comp, last - 1] for comp in range(3)], e)
-        hy, hz = steps.magnetic_yz(e, None)
-        hx = steps.magnetic_x(e)
-        coef = scales[part] * held_ref[last]
-        after = []
-        for comp in range(3):
-            curl = steps.curl_back(comp, hx, hy, hz, behind)
-            value = e[comp] - RELAX * curl + coef * own_ref[1 - part, comp, last]
-            after.append(value + here * weight(part, comp))
-        for k, f in enumerate((hy, hz) + steps.magnetic_yz(after, None)):
-            sent[up, part * SENT + 2 + k] = f.astype(half)
-    far_ref[...] = sent[0]
-    near_ref[...] = sent[1]
+                curl = steps.curl_back(comp, hx, hy, hz, behind)
+                value = e[comp] - RELAX * curl + coef * own_ref[1 - part, comp, last]
+                after.append(value + here * weight(part, comp))
+            for k, f in enumerate((hy, hz) + steps.magnetic_yz(after, None)):
+                up_ref[part * SENT + 2 + k] = f.astype(half)
+
+    by_parity(far_ref, near_ref, sweep_and_send)
     for copy in others:
         copy.wait()
 
@@ -214,123 +213,123 @@
     final = s == count - 1
     if final:
         earlier = refs[:s]
-        rows_ref, far_ref, near_ref, one_, two_, got, conds, sent = refs[s:]
+        rows_ref, far_ref, near_ref, one_, two_ = refs[s:]
     else:
-        rows_ref, one_, two_, got, conds = refs
+        rows_ref, one_, two_ = refs
     steps = Steps(height, breadth)
     index = lax.axis_index("space")
     first = index * depth
     relax_low = jnp.where(first > 0, F32(RELAX), F32(0.0))
     relax_high = jnp.where(first + depth < planes, F32(RELAX), F32(0.0))
-    low = index & 1
-    high = 1 - low
-    receive(got, far_in, near_in, (first == 0) | (first + depth == planes))
-    conds[0] = far_cond[2 * SENT]
-    conds[1] = near_cond[2 * SENT]
+    inside_low = jnp.where(first > 0, F32(1.0), F32(0.0))
+    inside_high = jnp.where(first + depth < planes, F32(1.0), F32(0.0))
     group = scalar_ref[count + s].astype(jnp.int32)
     angular = angular_of(scalar_ref[2 * count + group].astype(jnp.int32))
     scales = RELAX * angular, -RELAX * angular
     point = Point(scalar_ref[s].astype(jnp.int32), first, steps)
     weights_at = scalar_ref.shape[0] - 6 * count + 6 * s
 
-    def conductivity(p):
-        if p < 0:
-            return conds[low].astype(F32)
-        if p >= depth:
-            return conds[high].astype(F32)
-        return held_ref[p]
-
-    def received(side, part, k):
-        return got[side, part * SENT + k].astype(F32)
-
-    def weight(part, comp):
-        return scalar_ref[weights_at + part * 3 + comp]
-
-    for part in range(2):
-        ey, ez, ly, lz = [edge_ref[part, k] for k in range(4)]
-        one_[part, 0, 0] = -relax_low * (steps.down_y(ey) + steps.down_z(ez))
-        one_[part, 1, 0] = relax_low * ey
-        one_[part, 2, 0] = relax_low * ez
-        e = [own_ref[part, comp, 0] for comp in range(3)]
-        one_[part, 0, 1] = e[0]
-        one_[part, 1, 1] = e[1] - RELAX * received(low, part, 1)
-        one_[part, 2, 1] = e[2] + RELAX * received(low, part, 0)
-        for p in range(1, depth - 1):
+    def sweeps(low_in, high_in, low_cond, high_cond, to_low, to_high):
+        def conductivity(p):
+            if p < 0:
+                return low_cond[2 * SENT].astype(F32)
+            if p >= depth:
+                return high_cond[2 * SENT].astype(F32)
+            return held_ref[p]
+
+        def received(side, part, k):
+            return side[part * SENT + k].astype(F32)
+
+        def weight(part, comp):
+            return scalar_ref[weights_at + part * 3 + comp]
+
+        for part in range(2):
+            ey, ez, ly, lz = [edge_ref[part, k] for k in range(4)]
+            one_[part, 0, 0] = -relax_low * (steps.down_y(ey) + steps.down_z(ez))
+            one_[part, 1, 0] = relax_low * ey
+            one_[part, 2, 0] = relax_low * ez
+            e = [own_ref[part, comp, 0] for comp in range(3)]
+            one_[part, 0, 1] = e[0]
+            one_[part, 1, 1] = e[1] - relax_low * received(low_in, part, 1)
+            one_[part, 2, 1] = e[2] + relax_low * received(low_in, part, 0)
+            for p in range(1, depth - 1):
+                for comp in range(3):
+                    one_[part, comp, p + 1] = own_ref[part, comp, p]
+            e = [own_ref[part, comp, depth - 1] for comp in range(3)]
+            high_y, high_z = received(high_in, part, 0), received(high_in, part, 1)
+            one_[part, 0, depth] = e[0] - relax_high * (steps.down_y(high_y) + steps.down_z(high_z))
+            one_[part, 1, depth] = e[1] + relax_high * high_y
+            one_[part, 2, depth] = e[2] + relax_high * high_z
+            one_[part, 1, depth + 1] = inside_high * received(high_in, part, 2) - relax_high * lz
+            one_[part, 2, depth + 1] = inside_high * received(high_in, part, 3) + relax_high * ly
+
+        before = [(-one_[part, 2, 0], one_[part, 1, 0]) for part in range(2)]
+        for p in range(-1, depth + 1):
+            relax = relax_low if p < 0 else relax_high if p == depth else F32(RELAX)
+            for part in range(2):
+                e = [one_[part, comp, p + 1] if comp or p < depth else None for comp in range(3)]
+                if p < depth:
+                    hy, hz = steps.magnetic_yz(e, [None, one_[part, 1, p + 2], one_[part, 2, p + 2]])
+                else:
+                    hy, hz = received(high_in, part, 4) + e[2], received(high_in, part, 5) - e[1]
+                hx = steps.magnetic_x(e)
+                coef = scales[part] * conductivity(p)
+                for comp in range(1 if p == depth else 0, 3):
+                    curl = steps.curl_back(comp, hx, hy, hz, before[part])
+                    two_[part, comp, p + 1] = e[comp] - relax * curl + coef * one_[1 - part, comp, p + 1]
+                if p < 0:
+                    hy, hz = hy + inside_low * received(low_in, part, 2), hz + inside_low * received(low_in, part, 3)
+                before[part] = hy, hz
+        for part in range(2):
+            two_[part, 0, depth + 1] = jnp.zeros((height, breadth), F32)
+        point.add_to(two_, 0, depth + 1, 1, weight)
+
+        row = lax.broadcasted_iota(jnp.int32, (height, breadth), 0)
+        here = (row == point.row) & (steps.lane == point.lane)
+        before = []
+        for part in range(2):
+            e = [two_[part, comp, 0] for comp in range(3)]
+            hy, hz = steps.magnetic_yz(e, [None, two_[part, 1, 1], two_[part, 2, 1]])
+            before.append((hy + inside_low * received(low_in, part, 4), hz + inside_low * received(low_in, part, 5)))
+        for p in range(depth):
+            spot = jnp.where(here, jnp.where(point.plane == p, F32(RELAX), F32(0.0)), 0.0)
+            after = []
+            for part in range(2):
+                e = [two_[part, comp, p + 1] for comp in range(3)]
+                hy, hz = steps.magnetic_yz(e, [None, two_[part, 1, p + 2], two_[part, 2, p + 2]])
+                hx = steps.magnetic_x(e)
+                coef = scales[part] * held_ref[p]
+                for comp in range(3):
+                    curl = steps.curl_back(comp, hx, hy, hz, before[part])
+                    value = e[comp] - RELAX * curl + coef * two_[1 - part, comp, p + 1]
+                    after.append(value + spot * weight(part, comp))
+                before[part] = hy, hz
+            row_re = row_im = None
             for comp in range(3):
-                one_[part, comp, p + 1] = own_ref[part, comp, p]
-        e = [own_ref[part, comp, depth - 1] for comp in range(3)]
-        high_y, high_z = received(high, part, 0), received(high, part, 1)
-        one_[part, 0, depth] = e[0] - RELAX * (steps.down_y(high_y) + steps.down_z(high_z))
-        one_[part, 1, depth] = e[1] + RELAX * high_y
-        one_[part, 2, depth] = e[2] + RELAX * high_z
-        one_[part, 1, depth + 1] = received(high, part, 2) - relax_high * lz
-        one_[part, 2, depth + 1] = received(high, part, 3) + relax_high * ly
-
-    before = [(-one_[part, 2, 0], one_[part, 1, 0]) for part in range(2)]
-    for p in range(-1, depth + 1):
-        relax = relax_low if p < 0 else relax_high if p == depth else F32(RELAX)
-        for part in range(2):
-            e = [one_[part, comp, p + 1] if comp or p < depth else None for comp in range(3)]
-            if p < depth:
-                hy, hz = steps.magnetic_yz(e, [None, one_[part, 1, p + 2], one_[part, 2, p + 2]])
-            else:
-                hy, hz = received(high, part, 4) + e[2], received(high, part, 5) - e[1]
-            hx = steps.magnetic_x(e)
-            coef = scales[part] * conductivity(p)
-            for comp in range(1 if p == depth else 0, 3):
-                curl = steps.curl_back(comp, hx, hy, hz, before[part])
-                two_[part, comp, p + 1] = e[comp] - relax * curl + coef * one_[1 - part, comp, p + 1]
-            if p < 0:
-                hy, hz = hy + received(low, part, 2), hz + received(low, part, 3)
-            before[part] = hy, hz
-    for part in range(2):
-        two_[part, 0, depth + 1] = jnp.zeros((height, breadth), F32)
-    point.add_to(two_, 0, depth + 1, 1, weight)
-
-    row = lax.broadcasted_iota(jnp.int32, (height, breadth), 0)
-    here = (row == point.row) & (steps.lane == point.lane)
-    before = []
-    for part in range(2):
-        e = [two_[part, comp, 0] for comp in range(3)]
-        hy, hz = steps.magnetic_yz(e, [None, two_[part, 1, 1], two_[part, 2, 1]])
-        before.append((hy + received(low, part, 4), hz + received(low, part, 5)))
-    for p in range(depth):
-        spot = jnp.where(here, jnp.where(point.plane == p, F32(RELAX), F32(0.0)), 0.0)
-        after = []
-        for part in range(2):
-            e = [two_[part, comp, p + 1] for comp in range(3)]
-            hy, hz = steps.magnetic_yz(e, [None, two_[part, 1, p + 2], two_[part, 2, p + 2]])
-            hx = steps.magnetic_x(e)
-            coef = scales[part] * held_ref[p]
-            for comp in range(3):
-                curl = steps.curl_back(comp, hx, hy, hz, before[part])
-                value = e[comp] - RELAX * curl + coef * two_[1 - part, comp, p + 1]
-                after.append(value + spot * weight(part, comp))
-            before[part] = hy, hz
-        row_re = row_im = None
-        for comp in range(3):
-            re, im = after[comp], after[3 + comp]
-            field_re, field_im = field_ref[group, 0, comp, p], field_ref[group, 1, comp, p]
-            add_re, add_im = field_re * re - field_im * im, field_re * im + field_im * re
-            row_re, row_im = (add_re, add_im) if comp == 0 else (row_re + add_re, row_im + add_im)
-        coef = angular * held_ref[p]
-        for part, value in enumerate((row_re, row_im)):
-            value = (coef * value).astype(rows_ref.dtype)
-            if not final:
-                rows_ref[part, p] = value
-                continue
-            rows_ref[s, part, p] = value
-            if p >= depth - REACH:
-                sent[high, s, part, p - depth + REACH] = value
-            if p < REACH:
-                sent[low, s, part, p] = value
-    if final:
-        for t, ref in enumerate(earlier):
-            rows_ref[t] = ref[...]
-            sent[high, t] = ref[:, depth - REACH :]
-            sent[low, t] = ref[:, :REACH]
-        far_ref[...] = sent[0]
-        near_ref[...] = sent[1]
+                re, im = after[comp], after[3 + comp]
+                field_re, field_im = field_ref[group, 0, comp, p], field_ref[group, 1, comp, p]
+                add_re, add_im = field_re * re - field_im * im, field_re * im + field_im * re
+                row_re, row_im = (add_re, add_im) if comp == 0 else (row_re + add_re, row_im + add_im)
+            coef = angular * held_ref[p]
+            for part, value in enumerate((row_re, row_im)):
+                value = (coef * value).astype(rows_ref.dtype)
+                if not final:
+                    rows_ref[part, p] = value
+                    continue
+                rows_ref[s, part, p] = value
+                if p >= depth - REACH:
+                    to_high[s, part, p - depth + REACH] = value
+                if p < REACH:
+                    to_low[s, part, p] = value
+        if final:
+            for t, ref in enumerate(earlier):
+                rows_ref[t] = ref[...]
+                to_high[t] = ref[:, depth - REACH :]
+                to_low[t] = ref[:, :REACH]
+
+    far = far_in, far_cond, far_ref if final else None
+    near = near_in, near_cond, near_ref if final else None
+    by_parity(far, near, lambda low, high: sweeps(low[0], high[0], low[1], high[1], low[2], high[2]))
 
 
 def in_plane(steps, f):
@@ -363,33 +362,36 @@
     lax.fori_loop(0, count, one_source, 0)
 
 
-def block_kernel(cells, rows_ref, alone_ref, far_in, near_in, all_ref, smooth_ref, block_ref, got, rounded, sums, sem):
+def block_kernel(cells, rows_ref, alone_ref, far_in, near_in, all_ref, smooth_ref, block_ref, rounded, sums, sem):
     count, _, depth, height, breadth = rows_ref.shape
     ranks = all_ref.shape[0]
     steps = Steps(height, breadth)
     many = ranks * count * 2
     index = lax.axis_index("space")
-    receive(got, far_in, near_in, (index == 0) | (index == lax.axis_size("space") - 1))
-    odd = index & 1
-    low, high = odd, 1 - odd
-
-    def one_row(s, part):
+    inside_low = jnp.where(index > 0, F32(KAPPA), F32(0.0))
+    inside_high = jnp.where(index < lax.axis_size("space") - 1, F32(KAPPA), F32(0.0))
+
+    def one_row(low_in, high_in, s, part):
         value = [alone_ref[s, part, p] for p in range(depth)]
-        for side, nearest, order in ((low, REACH - 1, 1), (high, 0, -1)):
-            close = got[side, s, part, nearest].astype(F32)
-            beyond = got[side, s, part, REACH - 1 - nearest].astype(F32)
+        ends = (low_in, REACH - 1, 1, inside_low), (high_in, 0, -1, inside_high)
+        for side, nearest, order, kappa in ends:
+            close = side[s, part, nearest].astype(F32)
+            beyond = side[s, part, REACH - 1 - nearest].astype(F32)
             end = 0 if order > 0 else depth - 1
-            value[end] = value[end] + (2.0 * KAPPA * in_plane(steps, close) + KAPPA * KAPPA * beyond)
-            value[end + order] = value[end + order] + KAPPA * KAPPA * close
+            value[end] = value[end] + kappa * (2.0 * in_plane(steps, close) + KAPPA * beyond)
+            value[end + order] = value[end + order] + kappa * (KAPPA * close)
         for p in range(depth):
             rounded[s, part, p] = value[p].astype(rounded.dtype)
 
-    def one_source(s, _):
-        for part in range(2):
-            one_row(s, part)
-        return 0
-
-    lax.fori_loop(0, count, one_source, 0)
+    def join_rows(low_in, high_in):
+        def one_source(s, _):
+            for part in range(2):
+                one_row(low_in, high_in, s, part)
+            return 0
+
+        lax.fori_loop(0, count, one_source, 0)
+
+    by_parity(far_in, near_in, join_rows)
     out = pltpu.make_async_copy(rounded, smooth_ref, sem)
     out.start()
 
@@ -452,7 +454,7 @@
     for s in range(count):
         message = shape((2 * SENT + (s == 0),) + plane, half)
         outs = [message, message, shape(warm_start.shape[1:], F32), shape((2, 4) + plane, F32)]
-        scratch = [pltpu.VMEM((2,) + message.shape, half)]
+        scratch = []
         if s == 0:
             operands = [warm_start, conductivity, background, data_weight, recv_cell, src_group, group_freq]
             operands = [in_hbm(x) for x in operands]
@@ -496,14 +498,11 @@
         scratch = [
             pltpu.VMEM((2, 3, depth + 2) + plane, F32),
             pltpu.VMEM((2, 3, depth + 2) + plane, F32),
-            pltpu.VMEM((2, 2 * SENT) + plane, half),
-            pltpu.VMEM((2,) + plane, half),
         ]
         results = (shape((2, depth) + plane, half),)
         if s == count - 1:
             operands += earlier
             results = (rows_of, ends_of, ends_of)
-            scratch.append(pltpu.VMEM((2,) + ends_of.shape, half))
         results = pl.pallas_call(
             functools.partial(sweep_kernel, s, count, peers * depth),
             out_shape=results,
@@ -534,7 +533,6 @@
         in_specs=[FULL] * 5,
         out_specs=(HBM, FULL),
         scratch_shapes=[
-            pltpu.VMEM((2,) + ends_of.shape, half),
             pltpu.VMEM(rows_of.shape, half),
             pltpu.VMEM((2 * count * many, 8, breadth), F32),
             pltpu.SemaphoreType.DMA,

time: 34.9 us -> 34.8 us (level)
  no operation moved by 1% of the time
where the time goes in v13:
time: 34.8 us; the launch traced here: 34.6 us
  blocking collectives  12.7 us (36%)
  starting transfers between devices  9.4 us (27%)
  Pallas kernels  6.28 us (18%)
  waiting for transfers between devices  4.7 us (14%)
  other arithmetic  0.76 us (2%)
  between operations  0.74 us (2%)
    all_to_all x1, blocking collectives, shards(): lax.all_to_all(partial_block, 'space', 0, 0, axis_index_groups=backwards)  10.7 us
    ppermute x2, starting transfers between devices, shards(): nears.append(lax.ppermute(result[1], 'space', near))  6.95 us
    ppermute x2, waiting for transfers between devices, shards(): nears.append(lax.ppermute(result[1], 'space', near))  3.65 us
    pallas_call x2, Pallas kernels, shards(): pl.pallas_call(functools.partial(first_kernel, s), out_shape=tuple(outs),...  2.58 us
    pallas_call x2, Pallas kernels, shards(): pl.pallas_call(functools.partial(sweep_kernel, s, count, peers * depth),...  2.41 us
    all_gather x1, blocking collectives, shards(): every = lax.all_gather(rows, 'rx', axis=0)  1.95 us
    ppermute x1, starting transfers between devices, shards(): from_near = lax.ppermute(to_near, 'space', near)  1.8 us
    ppermute x1, waiting for transfers between devices, shards(): from_near = lax.ppermute(to_near, 'space', near)  1.04 us
  transfers between devices with their start and end apart: 6, of which 3 were waited for; matrix products, arithmetic and copies ran while one was open for 1% of the time, Pallas kernels for 8%

profile of v13, /device:TPU:0, one launch (start us, length us, event | category | flops | bytes accessed | tf_op | source)
XLA Modules:
  0.0 34.6 jit_solution(1687745481846726004)
XLA Ops:
  0.6 0.0 copy-start.1
  0.6 0.0 copy-start.2
  0.7 0.0 copy-start.3
  0.7 0.0 copy-start
  0.7 1.6 %first_sweep.2 = (bf16[13,32,128]{2,1,0:T(8,128)(2,1)S(1)}, bf16[13,32,128]{2,1,0:T(8,128)(2,1)S(1)}, f32[2,3,3,32,128]{4,3,2,1,0:T(8,128)S(1)}, f32[2,4,32,128]...) custom-call(f32[2,2,3,3,32,128]{5,4,3,2,1,0:T(8,128)} %planes_ref.1,, ...), custom_call_target="tpu_custom_call" | custom-call | tf_op jit(solution)/shard_map/first_sweep/pallas_call | solution.py:477
  2.3 0.5 %collective-permute-start.2 = (bf16[13,32,128]{2,1,0:T(8,128)(2,1)S(1)}, bf16[13,32,128]{2,1,0:T(8,128)(2,1)S(1)}, u32[]{:S(2)}, u32[]{:S(2)}) collective-permute-start(bf16[13,32,128]{2,1,0:T(8,128)(2,1)S(1)} %get-tuple-element.25), channel_id=1, source_target_pairs={{1,2},{3,4},{5,6},{7,8},{9,10},{11,12},{13,14},{17,18},{19,20},{21... | collective-permute-start | bytes 319496 | tf_op jit(solution)/shard_map/ppermute | solution.py:490
  2.8 4.0 %collective-permute-start.3 = (bf16[13,32,128]{2,1,0:T(8,128)(2,1)S(1)}, bf16[13,32,128]{2,1,0:T(8,128)(2,1)S(1)}, u32[]{:S(2)}, u32[]{:S(2)}) collective-permute-start(bf16[13,32,128]{2,1,0:T(8,128)(2,1)S(1)} %get-tuple-element.26), channel_id=1, source_target_pairs={{0,1},{2,3},{4,5},{6,7},{8,9},{10,11},{12,13},{14,15},{1,0},{3,2},... | collective-permute-start | bytes 319496 | tf_op jit(solution)/shard_map/ppermute | solution.py:491
  6.8 0.0 copy-done
  6.8 0.1 reshape.7
  6.8 0.0 copy-done.1
  6.8 0.0 copy-done.2
  6.8 0.0 copy-done.3
  6.8 0.1 add_convert_fusion
  6.9 0.1 pad_maximum_fusion.refs_0_.scalar_ref
  7.0 1.0 %first_sweep.3 = (bf16[12,32,128]{2,1,0:T(8,128)(2,1)S(1)}, bf16[12,32,128]{2,1,0:T(8,128)(2,1)S(1)}, f32[2,3,3,32,128]{4,3,2,1,0:T(8,128)S(1)}, f32[2,4,32,128]{3,2,1,0:T(8,128)S(1)}) custom-call(f32[1,2,3,3,32,128]{5,4,3,2,1,0:T(8,128)S(1)} %get-tuple-element.18.planes_ref, f32[20]{0:T(128)S(1)} %pad_maximum_fusion.refs_0_.scalar_ref, ...), custom_call_target="tpu_custom_call" | custom-call | tf_op jit(solution)/shard_map/first_sweep/pallas_call | solution.py:477
  8.0 0.1 collective-permute-start
  8.1 3.0 %collective-permute-start.1 = (bf16[12,32,128]{2,1,0:T(8,128)(2,1)S(1)}, bf16[12,32,128]{2,1,0:T(8,128)(2,1)S(1)}, u32[]{:S(2)}, u32[]{:S(2)}) collective-permute-start(bf16[12,32,128]{2,1,0:T(8,128)(2,1)S(1)} %get-tuple-element.24), channel_id=1, source_target_pairs={{0,1},{2,3},{4,5},{6,7},{8,9},{10,11},{12,13},{14,15},{1,0},{3,2},... | collective-permute-start | bytes 294920 | tf_op jit(solution)/shard_map/ppermute | solution.py:491
  11.1 0.0 collective-permute-done.2.far_in.far_cond
  11.1 2.8 %collective-permute-done.3.near_in.near_cond = bf16[13,32,128]{2,1,0:T(8,128)(2,1)S(1)} collective-permute-done((bf16[13,32,128]{2,1,0:T(8,128)(2,1)S(1)}, bf16[13,32,128]{2,1,0:T(8,128)(2,1)S(1)}, u32[]{:S(2)}, u32[]{:S(2)}) %collective-permute-start.3) | collective-permute-done | bytes 106528 | tf_op jit(solution)/shard_map/ppermute | solution.py:491
  13.9 1.2 %sweeps.2.refs_0_ = bf16[2,3,32,128]{3,2,1,0:T(8,128)(2,1)S(1)} custom-call(f32[20]{0:T(128)S(1)} %pad_maximum_fusion.refs_0_.scalar_ref, f32[2,3,3,32,128]{4,3,2,1,0:T(8,128)S(1)} %get-tuple-element.27.own_ref, f32[2,4,32,128]{3,2,1,0:T(8,128)S(1)} %get-tuple-element.28.edge_ref, f32[3,32,128]{2,1,0:T(8,128)S(1)} %get-tuple-element.19.refs_1_.held_ref, ...), custom_call_target="tpu_custom_call" | custom-call | tf_op jit(solution)/shard_map/sweeps/pallas_call | solution.py:506
  15.1 0.0 collective-permute-done.far_in
  15.1 0.8 %collective-permute-done.1.near_in = bf16[12,32,128]{2,1,0:T(8,128)(2,1)S(1)} collective-permute-done((bf16[12,32,128]{2,1,0:T(8,128)(2,1)S(1)}, bf16[12,32,128]{2,1,0:T(8,128)(2,1)S(1)}, u32[]{:S(2)}, u32[]{:S(2)}) %collective-permute-start.1) | collective-permute-done | bytes 98336 | tf_op jit(solution)/shard_map/ppermute | solution.py:491
  15.9 1.2 %sweeps.3 = (bf16[2,2,3,32,128]{4,3,2,1,0:T(8,128)(2,1)S(1)}, bf16[2,2,2,32,128]{4,3,2,1,0:T(8,128)(2,1)S(1)}, bf16[2,2,2,32,128]{4,3,2,1,0:T(8,128)(2,1)S(1)}) custom-call(f32[20]{0:T(128)S(1)} %pad_maximum_fusion.refs_0_.scalar_ref, f32[2,3,3,32,128]{4,3,2,1,0:T(8,128)S(1)} %get-tuple-element.20.own_ref, f32[2,4,32,128]{3,2,1,0:T(8,128)S(1)} %get-tuple-element.21.edge_ref, ...), custom_call_target="tpu_custom_call" | custom-call | tf_op jit(solution)/shard_map/sweeps/pallas_call | solution.py:506
  17.2 0.1 collective-permute-start.4
  17.2 1.8 %collective-permute-start.5 = (bf16[2,2,2,32,128]{4,3,2,1,0:T(8,128)(2,1)S(1)}, bf16[2,2,2,32,128]{4,3,2,1,0:T(8,128)(2,1)S(1)}, u32[]{:S(2)}, u32[]{:S(2)}) collective-permute-start(bf16[2,2,2,32,128]{4,3,2,1,0:T(8,128)(2,1)S(1)} %get-tuple-element.31), channel_id=1, source_target_pairs={{0,1},{2,3},{4,5},{6,7},{8,9},{10,11},{12,13},{14,15},{1,0},{3,2},... | collective-permute-start | bytes 196616 | tf_op jit(solution)/shard_map/ppermute | solution.py:518
  19.0 0.4 %smooth.1.alone_ref = f32[2,2,3,32,128]{4,3,2,1,0:T(8,128)S(1)} custom-call(bf16[2,2,3,32,128]{4,3,2,1,0:T(8,128)(2,1)S(1)} %get-tuple-element.29.rows_ref), custom_call_target="tpu_custom_call" | custom-call | tf_op jit(solution)/shard_map/smooth/pallas_call | solution.py:522
  19.5 1.9 %all-gather = bf16[4,2,3,32,128]{4,3,2,1,0:T(8,128)(2,1)S(1)} all-gather(bf16[2,2,3,32,128]{4,3,2,1,0:T(8,128)(2,1)S(1)} %get-tuple-element.29.rows_ref), channel_id=2, replica_groups=mesh['rx'=2,'space'=16] {'rx'}, dimensions={0}, use_global_device_ids=true | all-gather | bytes 294912 | tf_op jit(solution)/shard_map/all_gather | solution.py:519
  21.4 0.0 collective-permute-done.4.far_in
  21.4 1.0 %collective-permute-done.5.near_in = bf16[2,2,2,32,128]{4,3,2,1,0:T(8,128)(2,1)S(1)} collective-permute-done((bf16[2,2,2,32,128]{4,3,2,1,0:T(8,128)(2,1)S(1)}, bf16[2,2,2,32,128]{4,3,2,1,0:T(8,128)(2,1)S(1)}, u32[]{:S(2)}, u32[]{:S(2)}) %collective-permute-start.5) | collective-permute-done | bytes 65568 | tf_op jit(solution)/shard_map/ppermute | solution.py:518
  22.4 0.9 %block.1 = (bf16[2,2,3,32,128]{4,3,2,1,0:T(8,128)(2,1)}, f32[16,4,8]{2,1,0:T(4,128)S(1)}) custom-call(bf16[2,2,3,32,128]{4,3,2,1,0:T(8,128)(2,1)S(1)} %get-tuple-element.29.rows_ref, f32[2,2,3,32,128]{4,3,2,1,0:T(8,128)S(1)} %smooth.1.alone_ref, bf16[2,2,2,32,128]{4,3,2,1,0:T(8,128)(2,1)S(1)} %collective-permute-done.4.far_in, ...), custom_call_target="tpu_custom_call" | custom-call | tf_op jit(solution)/shard_map/block/pallas_call | solution.py:530
  23.3 10.7 %all_to_all.5 = f32[16,4,8]{2,1,0:T(4,128)S(1)} all-to-all(f32[16,4,8]{2,1,0:T(4,128)S(1)} %get-tuple-element.32), channel_id=1, replica_groups={{15,14,13,12,11,10,9,8,7,6,5,4,3,2,1,0},{31,30,29,28,27,26,25,24,23,22,..., dimensions={0} | all-to-all | bytes 4096 | tf_op jit(solution)/shard_map/all_to_all | solution.py:544
  34.0 0.6 %reduce_sum.9 = f32[4,8]{1,0:T(4,128)} reduce(f32[16,4,8]{2,1,0:T(4,128)S(1)} %all_to_all.5, f32[]{:T(128)} %constant.0.clone.1), dimensions={0}, to_apply=%region_0.0 | reduce | flops 480 | bytes 2180 | tf_op jit(solution)/shard_map/reduce_sum | solution.py:545
Async XLA Ops:
  0.6 6.2 %copy-start.1 = (s32[4]{0:T(128)S(1)}, s32[4]{0:T(128)}, u32[]{:S(2)}) copy-start(s32[4]{0:T(128)} %refs_5_.1) | copy-start | bytes 52
  0.6 6.2 %copy-start.2 = (s32[2]{0:T(128)S(1)}, s32[2]{0:T(128)}, u32[]{:S(2)}) copy-start(s32[2]{0:T(128)} %refs_4_.1) | copy-start | bytes 28
  0.7 6.2 %copy-start.3 = (s32[2]{0:T(128)S(1)}, s32[2]{0:T(128)}, u32[]{:S(2)}) copy-start(s32[2]{0:T(128)} %refs_3_.1) | copy-start | bytes 28
  0.7 6.1 %copy-start = (f32[2,2,3]{2,1,0:T(2,128)S(1)}, f32[2,2,3]{2,1,0:T(2,128)}, u32[]{:S(2)}) copy-start(f32[2,2,3]{2,1,0:T(2,128)} %refs_2_.1) | copy-start | bytes 148
  2.3 8.8 %collective-permute-start.2 = (bf16[13,32,128]{2,1,0:T(8,128)(2,1)S(1)}, bf16[13,32,128]{2,1,0:T(8,128)(2,1)S(1)}, u32[]{:S(2)}, u32[]{:S(2)}) collective-permute-start(bf16[13,32,128]{2,1,0:T(8,128)(2,1)S(1)} %get-tuple-element.25), channel_id=1, source_target_pairs={{1,2},{3,4},{5,6},{7,8},{9,10},{11,12},{13,14},{17,18},{19,20},{21... | collective-permute-start | bytes 319496 | tf_op jit(solution)/shard_map/ppermute | solution.py:490
  2.8 11.1 %collective-permute-start.3 = (bf16[13,32,128]{2,1,0:T(8,128)(2,1)S(1)}, bf16[13,32,128]{2,1,0:T(8,128)(2,1)S(1)}, u32[]{:S(2)}, u32[]{:S(2)}) collective-permute-start(bf16[13,32,128]{2,1,0:T(8,128)(2,1)S(1)} %get-tuple-element.26), channel_id=1, source_target_pairs={{0,1},{2,3},{4,5},{6,7},{8,9},{10,11},{12,13},{14,15},{1,0},{3,2},... | collective-permute-start | bytes 319496 | tf_op jit(solution)/shard_map/ppermute | solution.py:491
  8.0 7.1 %collective-permute-start = (bf16[12,32,128]{2,1,0:T(8,128)(2,1)S(1)}, bf16[12,32,128]{2,1,0:T(8,128)(2,1)S(1)}, u32[]{:S(2)}, u32[]{:S(2)}) collective-permute-start(bf16[12,32,128]{2,1,0:T(8,128)(2,1)S(1)} %get-tuple-element.23), channel_id=1, source_target_pairs={{1,2},{3,4},{5,6},{7,8},{9,10},{11,12},{13,14},{17,18},{19,20},{21... | collective-permute-start | bytes 294920 | tf_op jit(solution)/shard_map/ppermute | solution.py:490
  8.1 7.8 %collective-permute-start.1 = (bf16[12,32,128]{2,1,0:T(8,128)(2,1)S(1)}, bf16[12,32,128]{2,1,0:T(8,128)(2,1)S(1)}, u32[]{:S(2)}, u32[]{:S(2)}) collective-permute-start(bf16[12,32,128]{2,1,0:T(8,128)(2,1)S(1)} %get-tuple-element.24), channel_id=1, source_target_pairs={{0,1},{2,3},{4,5},{6,7},{8,9},{10,11},{12,13},{14,15},{1,0},{3,2},... | collective-permute-start | bytes 294920 | tf_op jit(solution)/shard_map/ppermute | solution.py:491
  17.2 4.3 %collective-permute-start.4 = (bf16[2,2,2,32,128]{4,3,2,1,0:T(8,128)(2,1)S(1)}, bf16[2,2,2,32,128]{4,3,2,1,0:T(8,128)(2,1)S(1)}, u32[]{:S(2)}, u32[]{:S(2)}) collective-permute-start(bf16[2,2,2,32,128]{4,3,2,1,0:T(8,128)(2,1)S(1)} %get-tuple-element.30), channel_id=1, source_target_pairs={{1,2},{3,4},{5,6},{7,8},{9,10},{11,12},{13,14},{17,18},{19,20},{21... | collective-permute-start | bytes 196616 | tf_op jit(solution)/shard_map/ppermute | solution.py:517
  17.2 5.2 %collective-permute-start.5 = (bf16[2,2,2,32,128]{4,3,2,1,0:T(8,128)(2,1)S(1)}, bf16[2,2,2,32,128]{4,3,2,1,0:T(8,128)(2,1)S(1)}, u32[]{:S(2)}, u32[]{:S(2)}) collective-permute-start(bf16[2,2,2,32,128]{4,3,2,1,0:T(8,128)(2,1)S(1)} %get-tuple-element.31), channel_id=1, source_target_pairs={{0,1},{2,3},{4,5},{6,7},{8,9},{10,11},{12,13},{14,15},{1,0},{3,2},... | collective-permute-start | bytes 196616 | tf_op jit(solution)/shard_map/ppermute | solution.py:518

commit v14 on v11

--- a/solution.py
+++ b/solution.py
@@ -209,7 +209,7 @@
         copy.wait()
 
 
-def sweep_kernel(s, count, planes, scalar_ref, own_ref, edge_ref, held_ref, field_ref, far_in, near_in, far_cond, near_cond, *refs):
+def sweep_kernel(s, count, planes, scalar_ref, own_ref, edge_ref, held_ref, field_ref, near_in, far_in, near_cond, far_cond, *refs):
     depth, height, breadth = held_ref.shape
     final = s == count - 1
     if final:
@@ -485,14 +485,14 @@
             held, later, field = result[4:]
         own.append(result[2])
         edges.append(result[3])
+        nears.append(lax.ppermute(result[1], "space", near))
         fars.append(lax.ppermute(result[0], both, far))
-        nears.append(lax.ppermute(result[1], "space", near))
 
     rows_of = shape((count, 2, depth) + plane, half)
     ends_of = shape((count, 2, REACH) + plane, half)
     earlier = []
     for s in range(count):
-        operands = [scalars, own[s], edges[s], held, field, fars[s], nears[s], fars[0], nears[0]]
+        operands = [scalars, own[s], edges[s], held, field, nears[s], fars[s], nears[0], fars[0]]
         scratch = [
             pltpu.VMEM((2, 3, depth + 2) + plane, F32),
             pltpu.VMEM((2, 3, depth + 2) + plane, F32),

time: 34.9 us -> 34.7 us (level)
  waiting for transfers between devices: 4.66 us -> 3.87 us
  starting transfers between devices: 9.41 us -> 10 us
    ppermute x1, starting transfers between devices: 1.81 us -> 3.91 us  [shards(): from_near = lax.ppermute(to_near, 'space', near)]
    ppermute x2, starting transfers between devices: 6.95 us -> 6.05 us  [shards(): nears.append(lax.ppermute(result[1], 'space', near))]
    ppermute x2, starting transfers between devices: 0.59 us -> 0.01 us  [shards(): fars.append(lax.ppermute(result[0], both, far))]
    ppermute x1, waiting for transfers between devices: 1.03 us -> 0.57 us  [shards(): from_near = lax.ppermute(to_near, 'space', near)]
  transfers between devices with their start and end apart: 6 -> 6, of which waited for: 3 -> 2; matrix products, arithmetic and copies ran while one was open for 1% -> 1% of each run, Pallas kernels for 8% -> 8%
where the time goes in v14:
time: 34.7 us; the launch traced here: 34.6 us
  blocking collectives  12.7 us (37%)
  starting transfers between devices  10 us (29%)
  Pallas kernels  6.38 us (18%)
  waiting for transfers between devices  3.87 us (11%)
  other arithmetic  0.76 us (2%)
  between operations  0.72 us (2%)
    all_to_all x1, blocking collectives, shards(): lax.all_to_all(partial_block, 'space', 0, 0, axis_index_groups=backwards)  10.7 us
    ppermute x2, starting transfers between devices, shards(): nears.append(lax.ppermute(result[1], 'space', near))  6.05 us
    ppermute x1, starting transfers between devices, shards(): from_near = lax.ppermute(to_near, 'space', near)  3.91 us
    ppermute x2, waiting for transfers between devices, shards(): nears.append(lax.ppermute(result[1], 'space', near))  3.3 us
    pallas_call x2, Pallas kernels, shards(): pl.pallas_call(functools.partial(first_kernel, s), out_shape=tuple(outs),...  2.57 us
    pallas_call x2, Pallas kernels, shards(): pl.pallas_call(functools.partial(sweep_kernel, s, count, peers * depth),...  2.52 us
    all_gather x1, blocking collectives, shards(): every = lax.all_gather(rows, 'rx', axis=0)  1.95 us
    pallas_call x1, Pallas kernels, shards(): pl.pallas_call(functools.partial(block_kernel, cells), out_shape=(rows_of...  0.87 us
  transfers between devices with their start and end apart: 6, of which 2 were waited for; matrix products, arithmetic and copies ran while one was open for 1% of the time, Pallas kernels for 8%

profile of v14, /device:TPU:0, one launch (start us, length us, event | category | flops | bytes accessed | tf_op | source)
XLA Modules:
  0.0 34.6 jit_solution(116348211210259398)
XLA Ops:
  0.6 0.0 copy-start.1
  0.6 0.0 copy-start.2
  0.7 0.0 copy-start.3
  0.7 0.0 copy-start
  0.7 1.6 %first_sweep.2 = (bf16[13,32,128]{2,1,0:T(8,128)(2,1)S(1)}, bf16[13,32,128]{2,1,0:T(8,128)(2,1)S(1)}, f32[2,3,3,32,128]{4,3,2,1,0:T(8,128)S(1)}, f32[2,4,32,128]...) custom-call(f32[2,2,3,3,32,128]{5,4,3,2,1,0:T(8,128)} %planes_ref.1,, ...), custom_call_target="tpu_custom_call" | custom-call | tf_op jit(solution)/shard_map/first_sweep/pallas_call | solution.py:475
  2.3 3.0 %collective-permute-start.2 = (bf16[13,32,128]{2,1,0:T(8,128)(2,1)S(1)}, bf16[13,32,128]{2,1,0:T(8,128)(2,1)S(1)}, u32[]{:S(2)}, u32[]{:S(2)}) collective-permute-start(bf16[13,32,128]{2,1,0:T(8,128)(2,1)S(1)} %get-tuple-element.25), channel_id=1, source_target_pairs={{0,1},{2,3},{4,5},{6,7},{8,9},{10,11},{12,13},{14,15},{1,0},{3,2},... | collective-permute-start | bytes 319496 | tf_op jit(solution)/shard_map/ppermute | solution.py:488
  5.3 0.0 collective-permute-start.3
  5.3 0.0 copy-done
  5.3 0.1 reshape.7
  5.3 0.0 copy-done.1
  5.4 0.0 copy-done.2
  5.4 0.0 copy-done.3
  5.4 0.1 add_convert_fusion
  5.4 0.1 pad_maximum_fusion.refs_0_.scalar_ref
  5.5 1.0 %first_sweep.3 = (bf16[12,32,128]{2,1,0:T(8,128)(2,1)S(1)}, bf16[12,32,128]{2,1,0:T(8,128)(2,1)S(1)}, f32[2,3,3,32,128]{4,3,2,1,0:T(8,128)S(1)}, f32[2,4,32,128]{3,2,1,0:T(8,128)S(1)}) custom-call(f32[1,2,3,3,32,128]{5,4,3,2,1,0:T(8,128)S(1)} %get-tuple-element.18.planes_ref, f32[20]{0:T(128)S(1)} %pad_maximum_fusion.refs_0_.scalar_ref, ...), custom_call_target="tpu_custom_call" | custom-call | tf_op jit(solution)/shard_map/first_sweep/pallas_call | solution.py:475
  6.5 3.0 %collective-permute-start = (bf16[12,32,128]{2,1,0:T(8,128)(2,1)S(1)}, bf16[12,32,128]{2,1,0:T(8,128)(2,1)S(1)}, u32[]{:S(2)}, u32[]{:S(2)}) collective-permute-start(bf16[12,32,128]{2,1,0:T(8,128)(2,1)S(1)} %get-tuple-element.23), channel_id=1, source_target_pairs={{0,1},{2,3},{4,5},{6,7},{8,9},{10,11},{12,13},{14,15},{1,0},{3,2},... | collective-permute-start | bytes 294920 | tf_op jit(solution)/shard_map/ppermute | solution.py:488
  9.6 0.0 collective-permute-start.1
  9.6 0.0 collective-permute-done.2.near_in.near_cond
  9.6 0.0 collective-permute-done.3.far_in.far_cond
  9.6 1.2 %sweeps.2.refs_0_ = bf16[2,3,32,128]{3,2,1,0:T(8,128)(2,1)S(1)} custom-call(f32[20]{0:T(128)S(1)} %pad_maximum_fusion.refs_0_.scalar_ref, f32[2,3,3,32,128]{4,3,2,1,0:T(8,128)S(1)} %get-tuple-element.27.own_ref, f32[2,4,32,128]{3,2,1,0:T(8,128)S(1)} %get-tuple-element.28.edge_ref, f32[3,32,128]{2,1,0:T(8,128)S(1)} %get-tuple-element.19.refs_1_.held_ref, ...), custom_call_target="tpu_custom_call" | custom-call | tf_op jit(solution)/shard_map/sweeps/pallas_call | solution.py:507
  10.8 3.3 %collective-permute-done.near_in = bf16[12,32,128]{2,1,0:T(8,128)(2,1)S(1)} collective-permute-done((bf16[12,32,128]{2,1,0:T(8,128)(2,1)S(1)}, bf16[12,32,128]{2,1,0:T(8,128)(2,1)S(1)}, u32[]{:S(2)}, u32[]{:S(2)}) %collective-permute-start) | collective-permute-done | bytes 98336 | tf_op jit(solution)/shard_map/ppermute | solution.py:488
  14.1 0.0 collective-permute-done.1.far_in
  14.1 1.3 %sweeps.3 = (bf16[2,2,3,32,128]{4,3,2,1,0:T(8,128)(2,1)S(1)}, bf16[2,2,2,32,128]{4,3,2,1,0:T(8,128)(2,1)S(1)}, bf16[2,2,2,32,128]{4,3,2,1,0:T(8,128)(2,1)S(1)}) custom-call(f32[20]{0:T(128)S(1)} %pad_maximum_fusion.refs_0_.scalar_ref, f32[2,3,3,32,128]{4,3,2,1,0:T(8,128)S(1)} %get-tuple-element.20.own_ref, f32[2,4,32,128]{3,2,1,0:T(8,128)S(1)} %get-tuple-element.21.edge_ref, ...), custom_call_target="tpu_custom_call" | custom-call | tf_op jit(solution)/shard_map/sweeps/pallas_call | solution.py:507
  15.4 0.1 collective-permute-start.4
  15.5 3.9 %collective-permute-start.5 = (bf16[2,2,2,32,128]{4,3,2,1,0:T(8,128)(2,1)S(1)}, bf16[2,2,2,32,128]{4,3,2,1,0:T(8,128)(2,1)S(1)}, u32[]{:S(2)}, u32[]{:S(2)}) collective-permute-start(bf16[2,2,2,32,128]{4,3,2,1,0:T(8,128)(2,1)S(1)} %get-tuple-element.31), channel_id=1, source_target_pairs={{0,1},{2,3},{4,5},{6,7},{8,9},{10,11},{12,13},{14,15},{1,0},{3,2},... | collective-permute-start | bytes 196616 | tf_op jit(solution)/shard_map/ppermute | solution.py:519
  19.4 0.4 %smooth.1.alone_ref = f32[2,2,3,32,128]{4,3,2,1,0:T(8,128)S(1)} custom-call(bf16[2,2,3,32,128]{4,3,2,1,0:T(8,128)(2,1)S(1)} %get-tuple-element.29.rows_ref), custom_call_target="tpu_custom_call" | custom-call | tf_op jit(solution)/shard_map/smooth/pallas_call | solution.py:523
  19.8 1.9 %all-gather = bf16[4,2,3,32,128]{4,3,2,1,0:T(8,128)(2,1)S(1)} all-gather(bf16[2,2,3,32,128]{4,3,2,1,0:T(8,128)(2,1)S(1)} %get-tuple-element.29.rows_ref), channel_id=2, replica_groups=mesh['rx'=2,'space'=16] {'rx'}, dimensions={0}, use_global_device_ids=true | all-gather | bytes 294912 | tf_op jit(solution)/shard_map/all_gather | solution.py:520
  21.8 0.0 collective-permute-done.4.far_in
  21.8 0.6 %collective-permute-done.5.near_in = bf16[2,2,2,32,128]{4,3,2,1,0:T(8,128)(2,1)S(1)} collective-permute-done((bf16[2,2,2,32,128]{4,3,2,1,0:T(8,128)(2,1)S(1)}, bf16[2,2,2,32,128]{4,3,2,1,0:T(8,128)(2,1)S(1)}, u32[]{:S(2)}, u32[]{:S(2)}) %collective-permute-start.5) | collective-permute-done | bytes 65568 | tf_op jit(solution)/shard_map/ppermute | solution.py:519
  22.3 0.9 %block.1 = (bf16[2,2,3,32,128]{4,3,2,1,0:T(8,128)(2,1)}, f32[16,4,8]{2,1,0:T(4,128)S(1)}) custom-call(bf16[2,2,3,32,128]{4,3,2,1,0:T(8,128)(2,1)S(1)} %get-tuple-element.29.rows_ref, f32[2,2,3,32,128]{4,3,2,1,0:T(8,128)S(1)} %smooth.1.alone_ref, bf16[2,2,2,32,128]{4,3,2,1,0:T(8,128)(2,1)S(1)} %collective-permute-done.4.far_in, ...), custom_call_target="tpu_custom_call" | custom-call | tf_op jit(solution)/shard_map/block/pallas_call | solution.py:531
  23.2 10.7 %all_to_all.5 = f32[16,4,8]{2,1,0:T(4,128)S(1)} all-to-all(f32[16,4,8]{2,1,0:T(4,128)S(1)} %get-tuple-element.32), channel_id=1, replica_groups={{15,14,13,12,11,10,9,8,7,6,5,4,3,2,1,0},{31,30,29,28,27,26,25,24,23,22,..., dimensions={0} | all-to-all | bytes 4096 | tf_op jit(solution)/shard_map/all_to_all | solution.py:546
  33.9 0.6 %reduce_sum.9 = f32[4,8]{1,0:T(4,128)} reduce(f32[16,4,8]{2,1,0:T(4,128)S(1)} %all_to_all.5, f32[]{:T(128)} %constant.0.clone.1), dimensions={0}, to_apply=%region_0.0 | reduce | flops 480 | bytes 2180 | tf_op jit(solution)/shard_map/reduce_sum | solution.py:547
Async XLA Ops:
  0.6 4.7 %copy-start.1 = (s32[4]{0:T(128)S(1)}, s32[4]{0:T(128)}, u32[]{:S(2)}) copy-start(s32[4]{0:T(128)} %refs_5_.1) | copy-start | bytes 52
  0.6 4.7 %copy-start.2 = (s32[2]{0:T(128)S(1)}, s32[2]{0:T(128)}, u32[]{:S(2)}) copy-start(s32[2]{0:T(128)} %refs_4_.1) | copy-start | bytes 28
  0.7 4.7 %copy-start.3 = (s32[2]{0:T(128)S(1)}, s32[2]{0:T(128)}, u32[]{:S(2)}) copy-start(s32[2]{0:T(128)} %refs_3_.1) | copy-start | bytes 28
  0.7 4.6 %copy-start = (f32[2,2,3]{2,1,0:T(2,128)S(1)}, f32[2,2,3]{2,1,0:T(2,128)}, u32[]{:S(2)}) copy-start(f32[2,2,3]{2,1,0:T(2,128)} %refs_2_.1) | copy-start | bytes 148
  2.3 7.3 %collective-permute-start.2 = (bf16[13,32,128]{2,1,0:T(8,128)(2,1)S(1)}, bf16[13,32,128]{2,1,0:T(8,128)(2,1)S(1)}, u32[]{:S(2)}, u32[]{:S(2)}) collective-permute-start(bf16[13,32,128]{2,1,0:T(8,128)(2,1)S(1)} %get-tuple-element.25), channel_id=1, source_target_pairs={{0,1},{2,3},{4,5},{6,7},{8,9},{10,11},{12,13},{14,15},{1,0},{3,2},... | collective-permute-start | bytes 319496 | tf_op jit(solution)/shard_map/ppermute | solution.py:488
  5.3 4.3 %collective-permute-start.3 = (bf16[13,32,128]{2,1,0:T(8,128)(2,1)S(1)}, bf16[13,32,128]{2,1,0:T(8,128)(2,1)S(1)}, u32[]{:S(2)}, u32[]{:S(2)}) collective-permute-start(bf16[13,32,128]{2,1,0:T(8,128)(2,1)S(1)} %get-tuple-element.26), channel_id=1, source_target_pairs={{1,2},{3,4},{5,6},{7,8},{9,10},{11,12},{13,14},{17,18},{19,20},{21... | collective-permute-start | bytes 319496 | tf_op jit(solution)/shard_map/ppermute | solution.py:489
  6.5 7.6 %collective-permute-start = (bf16[12,32,128]{2,1,0:T(8,128)(2,1)S(1)}, bf16[12,32,128]{2,1,0:T(8,128)(2,1)S(1)}, u32[]{:S(2)}, u32[]{:S(2)}) collective-permute-start(bf16[12,32,128]{2,1,0:T(8,128)(2,1)S(1)} %get-tuple-element.23), channel_id=1, source_target_pairs={{0,1},{2,3},{4,5},{6,7},{8,9},{10,11},{12,13},{14,15},{1,0},{3,2},... | collective-permute-start | bytes 294920 | tf_op jit(solution)/shard_map/ppermute | solution.py:488
  9.6 4.6 %collective-permute-start.1 = (bf16[12,32,128]{2,1,0:T(8,128)(2,1)S(1)}, bf16[12,32,128]{2,1,0:T(8,128)(2,1)S(1)}, u32[]{:S(2)}, u32[]{:S(2)}) collective-permute-start(bf16[12,32,128]{2,1,0:T(8,128)(2,1)S(1)} %get-tuple-element.24), channel_id=1, source_target_pairs={{1,2},{3,4},{5,6},{7,8},{9,10},{11,12},{13,14},{17,18},{19,20},{21... | collective-permute-start | bytes 294920 | tf_op jit(solution)/shard_map/ppermute | solution.py:489
  15.4 6.4 %collective-permute-start.4 = (bf16[2,2,2,32,128]{4,3,2,1,0:T(8,128)(2,1)S(1)}, bf16[2,2,2,32,128]{4,3,2,1,0:T(8,128)(2,1)S(1)}, u32[]{:S(2)}, u32[]{:S(2)}) collective-permute-start(bf16[2,2,2,32,128]{4,3,2,1,0:T(8,128)(2,1)S(1)} %get-tuple-element.30), channel_id=1, source_target_pairs={{1,2},{3,4},{5,6},{7,8},{9,10},{11,12},{13,14},{17,18},{19,20},{21... | collective-permute-start | bytes 196616 | tf_op jit(solution)/shard_map/ppermute | solution.py:518
  15.5 6.9 %collective-permute-start.5 = (bf16[2,2,2,32,128]{4,3,2,1,0:T(8,128)(2,1)S(1)}, bf16[2,2,2,32,128]{4,3,2,1,0:T(8,128)(2,1)S(1)}, u32[]{:S(2)}, u32[]{:S(2)}) collective-permute-start(bf16[2,2,2,32,128]{4,3,2,1,0:T(8,128)(2,1)S(1)} %get-tuple-element.31), channel_id=1, source_target_pairs={{0,1},{2,3},{4,5},{6,7},{8,9},{10,11},{12,13},{14,15},{1,0},{3,2},... | collective-permute-start | bytes 196616 | tf_op jit(solution)/shard_map/ppermute | solution.py:519

commit v15 on v14

--- a/solution.py
+++ b/solution.py
@@ -209,9 +209,10 @@
         copy.wait()
 
 
-def sweep_kernel(s, count, planes, scalar_ref, own_ref, edge_ref, held_ref, field_ref, near_in, far_in, near_cond, far_cond, *refs):
+def sweep_kernel(s, count, planes, scalar_ref, own_ref, edge_ref, held_ref, field_ref, one_in, other_in, near_cond, far_cond, *refs):
     depth, height, breadth = held_ref.shape
     final = s == count - 1
+    near_in, far_in = (one_in, other_in) if s == 0 else (other_in, one_in)
     if final:
         earlier = refs[:s]
         rows_ref, far_ref, near_ref, one_, two_, got, conds, sent = refs[s:]
@@ -492,7 +493,8 @@
     ends_of = shape((count, 2, REACH) + plane, half)
     earlier = []
     for s in range(count):
-        operands = [scalars, own[s], edges[s], held, field, nears[s], fars[s], nears[0], fars[0]]
+        swaps = (nears[s], fars[s]) if s == 0 else (fars[s], nears[s])
+        operands = [scalars, own[s], edges[s], held, field, *swaps, nears[0], fars[0]]
         scratch = [
             pltpu.VMEM((2, 3, depth + 2) + plane, F32),
             pltpu.VMEM((2, 3, depth + 2) + plane, F32),

time: 34.7 us -> 34.3 us (0.988)
  starting transfers between devices: 10 us -> 8.22 us
  waiting for transfers between devices: 3.87 us -> 4.98 us
    ppermute x1, starting transfers between devices: 3.91 us -> 2.02 us  [shards(): from_near = lax.ppermute(to_near, 'space', near)]
    ppermute x2, waiting for transfers between devices: 3.3 us -> 4.15 us  [shards(): nears.append(lax.ppermute(result[1], 'space', near))]
    ppermute x2, starting transfers between devices: 0.01 us -> 0.58 us  [shards(): fars.append(lax.ppermute(result[0], both, far))]
    ppermute x2, starting transfers between devices: 6.05 us -> 5.55 us  [shards(): nears.append(lax.ppermute(result[1], 'space', near))]
where the time goes in v15:
time: 34.3 us; the launch traced here: 34.1 us
  blocking collectives  12.9 us (38%)
  starting transfers between devices  8.22 us (24%)
  Pallas kernels  6.38 us (19%)
  waiting for transfers between devices  4.98 us (15%)
  other arithmetic  0.76 us (2%)
  between operations  0.73 us (2%)
    all_to_all x1, blocking collectives, shards(): lax.all_to_all(partial_block, 'space', 0, 0, axis_index_groups=backwards)  11 us
    ppermute x2, starting transfers between devices, shards(): nears.append(lax.ppermute(result[1], 'space', near))  5.55 us
    ppermute x2, waiting for transfers between devices, shards(): nears.append(lax.ppermute(result[1], 'space', near))  4.15 us
    pallas_call x2, Pallas kernels, shards(): pl.pallas_call(functools.partial(first_kernel, s), out_shape=tuple(outs),...  2.57 us
    pallas_call x2, Pallas kernels, shards(): pl.pallas_call(functools.partial(sweep_kernel, s, count, peers * depth),...  2.52 us
    ppermute x1, starting transfers between devices, shards(): from_near = lax.ppermute(to_near, 'space', near)  2.02 us
    all_gather x1, blocking collectives, shards(): every = lax.all_gather(rows, 'rx', axis=0)  1.95 us
    pallas_call x1, Pallas kernels, shards(): pl.pallas_call(functools.partial(block_kernel, cells), out_shape=(rows_of...  0.87 us
  transfers between devices with their start and end apart: 6, of which 2 were waited for; matrix products, arithmetic and copies ran while one was open for 1% of the time, Pallas kernels for 8%

profile of v15, /device:TPU:0, one launch (start us, length us, event | category | flops | bytes accessed | tf_op | source)
XLA Modules:
  0.0 34.1 jit_solution(5560665027551550466)
XLA Ops:
  0.6 0.0 copy-start.1
  0.6 0.0 copy-start.2
  0.7 0.0 copy-start.3
  0.7 0.0 copy-start
  0.7 1.6 %first_sweep.2 = (bf16[13,32,128]{2,1,0:T(8,128)(2,1)S(1)}, bf16[13,32,128]{2,1,0:T(8,128)(2,1)S(1)}, f32[2,3,3,32,128]{4,3,2,1,0:T(8,128)S(1)}, f32[2,4,32,128]...) custom-call(f32[2,2,3,3,32,128]{5,4,3,2,1,0:T(8,128)} %planes_ref.1,, ...), custom_call_target="tpu_custom_call" | custom-call | tf_op jit(solution)/shard_map/first_sweep/pallas_call | solution.py:476
  2.3 3.0 %collective-permute-start.2 = (bf16[13,32,128]{2,1,0:T(8,128)(2,1)S(1)}, bf16[13,32,128]{2,1,0:T(8,128)(2,1)S(1)}, u32[]{:S(2)}, u32[]{:S(2)}) collective-permute-start(bf16[13,32,128]{2,1,0:T(8,128)(2,1)S(1)} %get-tuple-element.25), channel_id=1, source_target_pairs={{0,1},{2,3},{4,5},{6,7},{8,9},{10,11},{12,13},{14,15},{1,0},{3,2},... | collective-permute-start | bytes 319496 | tf_op jit(solution)/shard_map/ppermute | solution.py:489
  5.3 0.0 collective-permute-start.3
  5.3 0.0 copy-done
  5.3 0.1 reshape.7
  5.3 0.0 copy-done.1
  5.4 0.0 copy-done.2
  5.4 0.0 copy-done.3
  5.4 0.1 add_convert_fusion
  5.4 0.1 pad_maximum_fusion.refs_0_.scalar_ref
  5.5 1.0 %first_sweep.3 = (bf16[12,32,128]{2,1,0:T(8,128)(2,1)S(1)}, bf16[12,32,128]{2,1,0:T(8,128)(2,1)S(1)}, f32[2,3,3,32,128]{4,3,2,1,0:T(8,128)S(1)}, f32[2,4,32,128]{3,2,1,0:T(8,128)S(1)}) custom-call(f32[1,2,3,3,32,128]{5,4,3,2,1,0:T(8,128)S(1)} %get-tuple-element.18.planes_ref, f32[20]{0:T(128)S(1)} %pad_maximum_fusion.refs_0_.scalar_ref, ...), custom_call_target="tpu_custom_call" | custom-call | tf_op jit(solution)/shard_map/first_sweep/pallas_call | solution.py:476
  6.5 0.6 %collective-permute-start = (bf16[12,32,128]{2,1,0:T(8,128)(2,1)S(1)}, bf16[12,32,128]{2,1,0:T(8,128)(2,1)S(1)}, u32[]{:S(2)}, u32[]{:S(2)}) collective-permute-start(bf16[12,32,128]{2,1,0:T(8,128)(2,1)S(1)} %get-tuple-element.23), channel_id=1, source_target_pairs={{1,2},{3,4},{5,6},{7,8},{9,10},{11,12},{13,14},{17,18},{19,20},{21... | collective-permute-start | bytes 294920 | tf_op jit(solution)/shard_map/ppermute | solution.py:490
  7.1 2.5 %collective-permute-start.1 = (bf16[12,32,128]{2,1,0:T(8,128)(2,1)S(1)}, bf16[12,32,128]{2,1,0:T(8,128)(2,1)S(1)}, u32[]{:S(2)}, u32[]{:S(2)}) collective-permute-start(bf16[12,32,128]{2,1,0:T(8,128)(2,1)S(1)} %get-tuple-element.24), channel_id=1, source_target_pairs={{0,1},{2,3},{4,5},{6,7},{8,9},{10,11},{12,13},{14,15},{1,0},{3,2},... | collective-permute-start | bytes 294920 | tf_op jit(solution)/shard_map/ppermute | solution.py:489
  9.6 0.0 collective-permute-done.2.one_in.near_cond
  9.6 0.0 collective-permute-done.3.other_in.far_cond
  9.6 1.2 %sweeps.2.refs_0_ = bf16[2,3,32,128]{3,2,1,0:T(8,128)(2,1)S(1)} custom-call(f32[20]{0:T(128)S(1)} %pad_maximum_fusion.refs_0_.scalar_ref, f32[2,3,3,32,128]{4,3,2,1,0:T(8,128)S(1)} %get-tuple-element.27.own_ref, f32[2,4,32,128]{3,2,1,0:T(8,128)S(1)} %get-tuple-element.28.edge_ref, f32[3,32,128]{2,1,0:T(8,128)S(1)} %get-tuple-element.19.refs_1_.held_ref, ...), custom_call_target="tpu_custom_call" | custom-call | tf_op jit(solution)/shard_map/sweeps/pallas_call | solution.py:509
  10.9 0.0 collective-permute-done.one_in
  10.9 4.2 %collective-permute-done.1.other_in = bf16[12,32,128]{2,1,0:T(8,128)(2,1)S(1)} collective-permute-done((bf16[12,32,128]{2,1,0:T(8,128)(2,1)S(1)}, bf16[12,32,128]{2,1,0:T(8,128)(2,1)S(1)}, u32[]{:S(2)}, u32[]{:S(2)}) %collective-permute-start.1) | collective-permute-done | bytes 98336 | tf_op jit(solution)/shard_map/ppermute | solution.py:489
  15.1 1.3 %sweeps.3 = (bf16[2,2,3,32,128]{4,3,2,1,0:T(8,128)(2,1)S(1)}, bf16[2,2,2,32,128]{4,3,2,1,0:T(8,128)(2,1)S(1)}, bf16[2,2,2,32,128]{4,3,2,1,0:T(8,128)(2,1)S(1)}) custom-call(f32[20]{0:T(128)S(1)} %pad_maximum_fusion.refs_0_.scalar_ref, f32[2,3,3,32,128]{4,3,2,1,0:T(8,128)S(1)} %get-tuple-element.20.own_ref, f32[2,4,32,128]{3,2,1,0:T(8,128)S(1)} %get-tuple-element.21.edge_ref, ...), custom_call_target="tpu_custom_call" | custom-call | tf_op jit(solution)/shard_map/sweeps/pallas_call | solution.py:509
  16.3 0.1 collective-permute-start.4
  16.4 2.0 %collective-permute-start.5 = (bf16[2,2,2,32,128]{4,3,2,1,0:T(8,128)(2,1)S(1)}, bf16[2,2,2,32,128]{4,3,2,1,0:T(8,128)(2,1)S(1)}, u32[]{:S(2)}, u32[]{:S(2)}) collective-permute-start(bf16[2,2,2,32,128]{4,3,2,1,0:T(8,128)(2,1)S(1)} %get-tuple-element.31), channel_id=1, source_target_pairs={{0,1},{2,3},{4,5},{6,7},{8,9},{10,11},{12,13},{14,15},{1,0},{3,2},... | collective-permute-start | bytes 196616 | tf_op jit(solution)/shard_map/ppermute | solution.py:521
  18.4 0.4 %smooth.1.alone_ref = f32[2,2,3,32,128]{4,3,2,1,0:T(8,128)S(1)} custom-call(bf16[2,2,3,32,128]{4,3,2,1,0:T(8,128)(2,1)S(1)} %get-tuple-element.29.rows_ref), custom_call_target="tpu_custom_call" | custom-call | tf_op jit(solution)/shard_map/smooth/pallas_call | solution.py:525
  18.9 1.9 %all-gather = bf16[4,2,3,32,128]{4,3,2,1,0:T(8,128)(2,1)S(1)} all-gather(bf16[2,2,3,32,128]{4,3,2,1,0:T(8,128)(2,1)S(1)} %get-tuple-element.29.rows_ref), channel_id=2, replica_groups=mesh['rx'=2,'space'=16] {'rx'}, dimensions={0}, use_global_device_ids=true | all-gather | bytes 294912 | tf_op jit(solution)/shard_map/all_gather | solution.py:522
  20.8 0.0 collective-permute-done.4.far_in
  20.8 0.8 %collective-permute-done.5.near_in = bf16[2,2,2,32,128]{4,3,2,1,0:T(8,128)(2,1)S(1)} collective-permute-done((bf16[2,2,2,32,128]{4,3,2,1,0:T(8,128)(2,1)S(1)}, bf16[2,2,2,32,128]{4,3,2,1,0:T(8,128)(2,1)S(1)}, u32[]{:S(2)}, u32[]{:S(2)}) %collective-permute-start.5) | collective-permute-done | bytes 65568 | tf_op jit(solution)/shard_map/ppermute | solution.py:521
  21.6 0.9 %block.1 = (bf16[2,2,3,32,128]{4,3,2,1,0:T(8,128)(2,1)}, f32[16,4,8]{2,1,0:T(4,128)S(1)}) custom-call(bf16[2,2,3,32,128]{4,3,2,1,0:T(8,128)(2,1)S(1)} %get-tuple-element.29.rows_ref, f32[2,2,3,32,128]{4,3,2,1,0:T(8,128)S(1)} %smooth.1.alone_ref, bf16[2,2,2,32,128]{4,3,2,1,0:T(8,128)(2,1)S(1)} %collective-permute-done.4.far_in, ...), custom_call_target="tpu_custom_call" | custom-call | tf_op jit(solution)/shard_map/block/pallas_call | solution.py:533
  22.5 11.0 %all_to_all.5 = f32[16,4,8]{2,1,0:T(4,128)S(1)} all-to-all(f32[16,4,8]{2,1,0:T(4,128)S(1)} %get-tuple-element.32), channel_id=1, replica_groups={{15,14,13,12,11,10,9,8,7,6,5,4,3,2,1,0},{31,30,29,28,27,26,25,24,23,22,..., dimensions={0} | all-to-all | bytes 4096 | tf_op jit(solution)/shard_map/all_to_all | solution.py:548
  33.5 0.6 %reduce_sum.9 = f32[4,8]{1,0:T(4,128)} reduce(f32[16,4,8]{2,1,0:T(4,128)S(1)} %all_to_all.5, f32[]{:T(128)} %constant.0.clone.1), dimensions={0}, to_apply=%region_0.0 | reduce | flops 480 | bytes 2180 | tf_op jit(solution)/shard_map/reduce_sum | solution.py:549
Async XLA Ops:
  0.6 4.7 %copy-start.1 = (s32[4]{0:T(128)S(1)}, s32[4]{0:T(128)}, u32[]{:S(2)}) copy-start(s32[4]{0:T(128)} %refs_5_.1) | copy-start | bytes 52
  0.6 4.7 %copy-start.2 = (s32[2]{0:T(128)S(1)}, s32[2]{0:T(128)}, u32[]{:S(2)}) copy-start(s32[2]{0:T(128)} %refs_4_.1) | copy-start | bytes 28
  0.7 4.7 %copy-start.3 = (s32[2]{0:T(128)S(1)}, s32[2]{0:T(128)}, u32[]{:S(2)}) copy-start(s32[2]{0:T(128)} %refs_3_.1) | copy-start | bytes 28
  0.7 4.6 %copy-start = (f32[2,2,3]{2,1,0:T(2,128)S(1)}, f32[2,2,3]{2,1,0:T(2,128)}, u32[]{:S(2)}) copy-start(f32[2,2,3]{2,1,0:T(2,128)} %refs_2_.1) | copy-start | bytes 148
  2.3 7.4 %collective-permute-start.2 = (bf16[13,32,128]{2,1,0:T(8,128)(2,1)S(1)}, bf16[13,32,128]{2,1,0:T(8,128)(2,1)S(1)}, u32[]{:S(2)}, u32[]{:S(2)}) collective-permute-start(bf16[13,32,128]{2,1,0:T(8,128)(2,1)S(1)} %get-tuple-element.25), channel_id=1, source_target_pairs={{0,1},{2,3},{4,5},{6,7},{8,9},{10,11},{12,13},{14,15},{1,0},{3,2},... | collective-permute-start | bytes 319496 | tf_op jit(solution)/shard_map/ppermute | solution.py:489
  5.3 4.4 %collective-permute-start.3 = (bf16[13,32,128]{2,1,0:T(8,128)(2,1)S(1)}, bf16[13,32,128]{2,1,0:T(8,128)(2,1)S(1)}, u32[]{:S(2)}, u32[]{:S(2)}) collective-permute-start(bf16[13,32,128]{2,1,0:T(8,128)(2,1)S(1)} %get-tuple-element.26), channel_id=1, source_target_pairs={{1,2},{3,4},{5,6},{7,8},{9,10},{11,12},{13,14},{17,18},{19,20},{21... | collective-permute-start | bytes 319496 | tf_op jit(solution)/shard_map/ppermute | solution.py:490
  6.5 4.4 %collective-permute-start = (bf16[12,32,128]{2,1,0:T(8,128)(2,1)S(1)}, bf16[12,32,128]{2,1,0:T(8,128)(2,1)S(1)}, u32[]{:S(2)}, u32[]{:S(2)}) collective-permute-start(bf16[12,32,128]{2,1,0:T(8,128)(2,1)S(1)} %get-tuple-element.23), channel_id=1, source_target_pairs={{1,2},{3,4},{5,6},{7,8},{9,10},{11,12},{13,14},{17,18},{19,20},{21... | collective-permute-start | bytes 294920 | tf_op jit(solution)/shard_map/ppermute | solution.py:490
  7.1 8.0 %collective-permute-start.1 = (bf16[12,32,128]{2,1,0:T(8,128)(2,1)S(1)}, bf16[12,32,128]{2,1,0:T(8,128)(2,1)S(1)}, u32[]{:S(2)}, u32[]{:S(2)}) collective-permute-start(bf16[12,32,128]{2,1,0:T(8,128)(2,1)S(1)} %get-tuple-element.24), channel_id=1, source_target_pairs={{0,1},{2,3},{4,5},{6,7},{8,9},{10,11},{12,13},{14,15},{1,0},{3,2},... | collective-permute-start | bytes 294920 | tf_op jit(solution)/shard_map/ppermute | solution.py:489
  16.3 4.5 %collective-permute-start.4 = (bf16[2,2,2,32,128]{4,3,2,1,0:T(8,128)(2,1)S(1)}, bf16[2,2,2,32,128]{4,3,2,1,0:T(8,128)(2,1)S(1)}, u32[]{:S(2)}, u32[]{:S(2)}) collective-permute-start(bf16[2,2,2,32,128]{4,3,2,1,0:T(8,128)(2,1)S(1)} %get-tuple-element.30), channel_id=1, source_target_pairs={{1,2},{3,4},{5,6},{7,8},{9,10},{11,12},{13,14},{17,18},{19,20},{21... | collective-permute-start | bytes 196616 | tf_op jit(solution)/shard_map/ppermute | solution.py:520
  16.4 5.2 %collective-permute-start.5 = (bf16[2,2,2,32,128]{4,3,2,1,0:T(8,128)(2,1)S(1)}, bf16[2,2,2,32,128]{4,3,2,1,0:T(8,128)(2,1)S(1)}, u32[]{:S(2)}, u32[]{:S(2)}) collective-permute-start(bf16[2,2,2,32,128]{4,3,2,1,0:T(8,128)(2,1)S(1)} %get-tuple-element.31), channel_id=1, source_target_pairs={{0,1},{2,3},{4,5},{6,7},{8,9},{10,11},{12,13},{14,15},{1,0},{3,2},... | collective-permute-start | bytes 196616 | tf_op jit(solution)/shard_map/ppermute | solution.py:521

commit v16 on v15

--- a/solution.py
+++ b/solution.py
@@ -364,9 +364,12 @@
     lax.fori_loop(0, count, one_source, 0)
 
 
-def block_kernel(cells, rows_ref, alone_ref, far_in, near_in, all_ref, smooth_ref, block_ref, got, rounded, sums, sem):
+def block_kernel(cells, rows_ref, alone_ref, far_in, near_in, *refs):
     count, _, depth, height, breadth = rows_ref.shape
-    ranks = all_ref.shape[0]
+    ranks = len(refs) - 5
+    all_refs = (rows_ref,) + refs[: ranks - 1]
+    smooth_ref, block_ref, got, rounded, sums, sem = refs[ranks - 1 :]
+    rank = lax.axis_index("rx")
     steps = Steps(height, breadth)
     many = ranks * count * 2
     index = lax.axis_index("space")
@@ -400,7 +403,7 @@
         mine = [rounded[a // 2, a % 2, p].astype(F32) for a in range(2 * count)]
         for b in range(many):
             r, t = divmod(b // 2, count)
-            other = all_ref[r, t, b % 2, p].astype(F32)
+            other = all_refs[r][t, b % 2, p].astype(F32)
             for a in range(2 * count):
                 prod = mine[a] * other
                 total = prod[:8]
@@ -419,7 +422,8 @@
         table = jnp.dot(coarse, ones, preferred_element_type=F32) + jnp.dot(fine, ones, preferred_element_type=F32)
         line = None
         for b in range(many):
-            add = jnp.where(steps.lane[:8] == b, table[b * 8 : b * 8 + 8], 0.0)
+            place = (rank ^ (b // (2 * count))) * (2 * count) + b % (2 * count)
+            add = jnp.where(steps.lane[:8] == place, table[b * 8 : b * 8 + 8], 0.0)
             line = add if line is None else line + add
         line = jnp.sum(line, axis=0, keepdims=True) * (1.0 / cells)
         for peer in range(block_ref.shape[0]):
@@ -519,7 +523,8 @@
     rows, to_far, to_near = results
     from_far = lax.ppermute(to_far, both, far)
     from_near = lax.ppermute(to_near, "space", near)
-    every = lax.all_gather(rows, "rx", axis=0)
+    assert ranks & (ranks - 1) == 0
+    others = [lax.ppermute(rows, "rx", [(r, r ^ k) for r in range(ranks)]) for k in range(1, ranks)]
 
     many = 2 * count * ranks
     alone = pl.pallas_call(
@@ -533,7 +538,7 @@
     smoothed, partial_block = pl.pallas_call(
         functools.partial(block_kernel, cells),
         out_shape=(rows_of, shape((peers, 2 * count, many), F32)),
-        in_specs=[FULL] * 5,
+        in_specs=[FULL] * (4 + len(others)),
         out_specs=(HBM, FULL),
         scratch_shapes=[
             pltpu.VMEM((2,) + ends_of.shape, half),
@@ -543,7 +548,7 @@
         ],
         compiler_params=KERNEL,
         name="block",
-    )(rows, alone, from_far, from_near, every)
+    )(rows, alone, from_far, from_near, *others)
     backwards = [list(range(peers - 1, -1, -1))]
     pieces = lax.all_to_all(partial_block, "space", 0, 0, axis_index_groups=backwards)
     return (jnp.sum(pieces, axis=0), smoothed)

time: 34.3 us -> 34.8 us (1.015)
  waiting for transfers between devices: 4.98 us -> 7.54 us
  blocking collectives: 12.9 us -> 10.8 us
    ppermute x1, waiting for transfers between devices: 0.81 us -> 3.39 us  [shards(): from_near = lax.ppermute(to_near, 'space', near)]
    all_gather x1 -> x0, blocking collectives: 1.95 us -> none  [shards(): every = lax.all_gather(rows, 'rx', axis=0)]
    ppermute x1, starting transfers between devices: 0.07 us -> 0.5 us  [shards(): from_far = lax.ppermute(to_far, both, far)]
    ppermute x1, starting transfers between devices: 2.02 us -> 1.61 us  [shards(): from_near = lax.ppermute(to_near, 'space', near)]
  transfers between devices with their start and end apart: 6 -> 7, of which waited for: 2 -> 2; matrix products, arithmetic and copies ran while one was open for 1% -> 1% of each run, Pallas kernels for 8% -> 8%
where the time goes in v16:
time: 34.8 us; the launch traced here: 34.6 us
  blocking collectives  10.8 us (31%)
  starting transfers between devices  8.31 us (24%)
  waiting for transfers between devices  7.54 us (22%)
  Pallas kernels  6.38 us (18%)
  other arithmetic  0.76 us (2%)
  between operations  0.74 us (2%)
    all_to_all x1, blocking collectives, shards(): lax.all_to_all(partial_block, 'space', 0, 0, axis_index_groups=backwards)  10.8 us
    ppermute x2, starting transfers between devices, shards(): nears.append(lax.ppermute(result[1], 'space', near))  5.56 us
    ppermute x2, waiting for transfers between devices, shards(): nears.append(lax.ppermute(result[1], 'space', near))  4.15 us
    ppermute x1, waiting for transfers between devices, shards(): from_near = lax.ppermute(to_near, 'space', near)  3.39 us
    pallas_call x2, Pallas kernels, shards(): pl.pallas_call(functools.partial(first_kernel, s), out_shape=tuple(outs),...  2.57 us
    pallas_call x2, Pallas kernels, shards(): pl.pallas_call(functools.partial(sweep_kernel, s, count, peers * depth),...  2.52 us
    ppermute x1, starting transfers between devices, shards(): from_near = lax.ppermute(to_near, 'space', near)  1.61 us
    pallas_call x1, Pallas kernels, shards(): pl.pallas_call(functools.partial(block_kernel, cells), out_shape=(rows_of...  0.88 us
  transfers between devices with their start and end apart: 7, of which 2 were waited for; matrix products, arithmetic and copies ran while one was open for 1% of the time, Pallas kernels for 8%

profile of v16, /device:TPU:0, one launch (start us, length us, event | category | flops | bytes accessed | tf_op | source)
XLA Modules:
  0.0 34.6 jit_solution(2190766504336149595)
XLA Ops:
  0.6 0.0 copy-start.1
  0.6 0.0 copy-start.2
  0.7 0.0 copy-start.3
  0.7 0.0 copy-start
  0.7 1.6 %first_sweep.2 = (bf16[13,32,128]{2,1,0:T(8,128)(2,1)S(1)}, bf16[13,32,128]{2,1,0:T(8,128)(2,1)S(1)}, f32[2,3,3,32,128]{4,3,2,1,0:T(8,128)S(1)}, f32[2,4,32,128]...) custom-call(f32[2,2,3,3,32,128]{5,4,3,2,1,0:T(8,128)} %planes_ref.1,, ...), custom_call_target="tpu_custom_call" | custom-call | tf_op jit(solution)/shard_map/first_sweep/pallas_call | solution.py:480
  2.3 3.0 %collective-permute-start.2 = (bf16[13,32,128]{2,1,0:T(8,128)(2,1)S(1)}, bf16[13,32,128]{2,1,0:T(8,128)(2,1)S(1)}, u32[]{:S(2)}, u32[]{:S(2)}) collective-permute-start(bf16[13,32,128]{2,1,0:T(8,128)(2,1)S(1)} %get-tuple-element.25), channel_id=1, source_target_pairs={{0,1},{2,3},{4,5},{6,7},{8,9},{10,11},{12,13},{14,15},{1,0},{3,2},... | collective-permute-start | bytes 319496 | tf_op jit(solution)/shard_map/ppermute | solution.py:493
  5.3 0.0 collective-permute-start.3
  5.3 0.0 copy-done
  5.3 0.1 reshape.7
  5.3 0.0 copy-done.1
  5.4 0.0 copy-done.2
  5.4 0.0 copy-done.3
  5.4 0.1 add_convert_fusion
  5.4 0.1 pad_maximum_fusion.refs_0_.scalar_ref
  5.5 1.0 %first_sweep.3 = (bf16[12,32,128]{2,1,0:T(8,128)(2,1)S(1)}, bf16[12,32,128]{2,1,0:T(8,128)(2,1)S(1)}, f32[2,3,3,32,128]{4,3,2,1,0:T(8,128)S(1)}, f32[2,4,32,128]{3,2,1,0:T(8,128)S(1)}) custom-call(f32[1,2,3,3,32,128]{5,4,3,2,1,0:T(8,128)S(1)} %get-tuple-element.18.planes_ref, f32[20]{0:T(128)S(1)} %pad_maximum_fusion.refs_0_.scalar_ref, ...), custom_call_target="tpu_custom_call" | custom-call | tf_op jit(solution)/shard_map/first_sweep/pallas_call | solution.py:480
  6.5 0.6 %collective-permute-start = (bf16[12,32,128]{2,1,0:T(8,128)(2,1)S(1)}, bf16[12,32,128]{2,1,0:T(8,128)(2,1)S(1)}, u32[]{:S(2)}, u32[]{:S(2)}) collective-permute-start(bf16[12,32,128]{2,1,0:T(8,128)(2,1)S(1)} %get-tuple-element.23), channel_id=1, source_target_pairs={{1,2},{3,4},{5,6},{7,8},{9,10},{11,12},{13,14},{17,18},{19,20},{21... | collective-permute-start | bytes 294920 | tf_op jit(solution)/shard_map/ppermute | solution.py:494
  7.1 2.6 %collective-permute-start.1 = (bf16[12,32,128]{2,1,0:T(8,128)(2,1)S(1)}, bf16[12,32,128]{2,1,0:T(8,128)(2,1)S(1)}, u32[]{:S(2)}, u32[]{:S(2)}) collective-permute-start(bf16[12,32,128]{2,1,0:T(8,128)(2,1)S(1)} %get-tuple-element.24), channel_id=1, source_target_pairs={{0,1},{2,3},{4,5},{6,7},{8,9},{10,11},{12,13},{14,15},{1,0},{3,2},... | collective-permute-start | bytes 294920 | tf_op jit(solution)/shard_map/ppermute | solution.py:493
  9.6 0.0 collective-permute-done.2.one_in.near_cond
  9.6 0.0 collective-permute-done.3.other_in.far_cond
  9.6 1.2 %sweeps.2.refs_0_ = bf16[2,3,32,128]{3,2,1,0:T(8,128)(2,1)S(1)} custom-call(f32[20]{0:T(128)S(1)} %pad_maximum_fusion.refs_0_.scalar_ref, f32[2,3,3,32,128]{4,3,2,1,0:T(8,128)S(1)} %get-tuple-element.27.own_ref, f32[2,4,32,128]{3,2,1,0:T(8,128)S(1)} %get-tuple-element.28.edge_ref, f32[3,32,128]{2,1,0:T(8,128)S(1)} %get-tuple-element.19.refs_1_.held_ref, ...), custom_call_target="tpu_custom_call" | custom-call | tf_op jit(solution)/shard_map/sweeps/pallas_call | solution.py:513
  10.9 0.0 collective-permute-done.one_in
  10.9 4.1 %collective-permute-done.1.other_in = bf16[12,32,128]{2,1,0:T(8,128)(2,1)S(1)} collective-permute-done((bf16[12,32,128]{2,1,0:T(8,128)(2,1)S(1)}, bf16[12,32,128]{2,1,0:T(8,128)(2,1)S(1)}, u32[]{:S(2)}, u32[]{:S(2)}) %collective-permute-start.1) | collective-permute-done | bytes 98336 | tf_op jit(solution)/shard_map/ppermute | solution.py:493
  15.0 1.3 %sweeps.3 = (bf16[2,2,3,32,128]{4,3,2,1,0:T(8,128)(2,1)S(1)}, bf16[2,2,2,32,128]{4,3,2,1,0:T(8,128)(2,1)S(1)}, bf16[2,2,2,32,128]{4,3,2,1,0:T(8,128)(2,1)S(1)}) custom-call(f32[20]{0:T(128)S(1)} %pad_maximum_fusion.refs_0_.scalar_ref, f32[2,3,3,32,128]{4,3,2,1,0:T(8,128)S(1)} %get-tuple-element.20.own_ref, f32[2,4,32,128]{3,2,1,0:T(8,128)S(1)} %get-tuple-element.21.edge_ref, ...), custom_call_target="tpu_custom_call" | custom-call | tf_op jit(solution)/shard_map/sweeps/pallas_call | solution.py:513
  16.3 0.1 collective-permute-start.6
  16.4 0.5 %collective-permute-start.4 = (bf16[2,2,2,32,128]{4,3,2,1,0:T(8,128)(2,1)S(1)}, bf16[2,2,2,32,128]{4,3,2,1,0:T(8,128)(2,1)S(1)}, u32[]{:S(2)}, u32[]{:S(2)}) collective-permute-start(bf16[2,2,2,32,128]{4,3,2,1,0:T(8,128)(2,1)S(1)} %get-tuple-element.30), channel_id=1, source_target_pairs={{1,2},{3,4},{5,6},{7,8},{9,10},{11,12},{13,14},{17,18},{19,20},{21... | collective-permute-start | bytes 196616 | tf_op jit(solution)/shard_map/ppermute | solution.py:524
  16.9 1.6 %collective-permute-start.5 = (bf16[2,2,2,32,128]{4,3,2,1,0:T(8,128)(2,1)S(1)}, bf16[2,2,2,32,128]{4,3,2,1,0:T(8,128)(2,1)S(1)}, u32[]{:S(2)}, u32[]{:S(2)}) collective-permute-start(bf16[2,2,2,32,128]{4,3,2,1,0:T(8,128)(2,1)S(1)} %get-tuple-element.31), channel_id=1, source_target_pairs={{0,1},{2,3},{4,5},{6,7},{8,9},{10,11},{12,13},{14,15},{1,0},{3,2},... | collective-permute-start | bytes 196616 | tf_op jit(solution)/shard_map/ppermute | solution.py:525
  18.5 0.4 %smooth.1.alone_ref = f32[2,2,3,32,128]{4,3,2,1,0:T(8,128)S(1)} custom-call(bf16[2,2,3,32,128]{4,3,2,1,0:T(8,128)(2,1)S(1)} %get-tuple-element.29.rows_ref), custom_call_target="tpu_custom_call" | custom-call | tf_op jit(solution)/shard_map/smooth/pallas_call | solution.py:530
  18.9 0.0 collective-permute-done.4.far_in
  18.9 3.4 %collective-permute-done.5.near_in = bf16[2,2,2,32,128]{4,3,2,1,0:T(8,128)(2,1)S(1)} collective-permute-done((bf16[2,2,2,32,128]{4,3,2,1,0:T(8,128)(2,1)S(1)}, bf16[2,2,2,32,128]{4,3,2,1,0:T(8,128)(2,1)S(1)}, u32[]{:S(2)}, u32[]{:S(2)}) %collective-permute-start.5) | collective-permute-done | bytes 65568 | tf_op jit(solution)/shard_map/ppermute | solution.py:525
  22.3 0.0 collective-permute-done.6.refs_0_
  22.3 0.9 %block.1 = (bf16[2,2,3,32,128]{4,3,2,1,0:T(8,128)(2,1)}, f32[16,4,8]{2,1,0:T(4,128)S(1)}) custom-call(bf16[2,2,3,32,128]{4,3,2,1,0:T(8,128)(2,1)S(1)} %get-tuple-element.29.rows_ref, f32[2,2,3,32,128]{4,3,2,1,0:T(8,128)S(1)} %smooth.1.alone_ref, bf16[2,2,2,32,128]{4,3,2,1,0:T(8,128)(2,1)S(1)} %collective-permute-done.4.far_in, ...), custom_call_target="tpu_custom_call" | custom-call | tf_op jit(solution)/shard_map/block/pallas_call | solution.py:538
  23.2 10.8 %all_to_all.5 = f32[16,4,8]{2,1,0:T(4,128)S(1)} all-to-all(f32[16,4,8]{2,1,0:T(4,128)S(1)} %get-tuple-element.32), channel_id=1, replica_groups={{15,14,13,12,11,10,9,8,7,6,5,4,3,2,1,0},{31,30,29,28,27,26,25,24,23,22,..., dimensions={0} | all-to-all | bytes 4096 | tf_op jit(solution)/shard_map/all_to_all | solution.py:553
  34.0 0.6 %reduce_sum.9 = f32[4,8]{1,0:T(4,128)} reduce(f32[16,4,8]{2,1,0:T(4,128)S(1)} %all_to_all.5, f32[]{:T(128)} %constant.0.clone.1), dimensions={0}, to_apply=%region_0.0 | reduce | flops 480 | bytes 2180 | tf_op jit(solution)/shard_map/reduce_sum | solution.py:554
Async XLA Ops:
  0.6 4.7 %copy-start.1 = (s32[4]{0:T(128)S(1)}, s32[4]{0:T(128)}, u32[]{:S(2)}) copy-start(s32[4]{0:T(128)} %refs_5_.1) | copy-start | bytes 52
  0.6 4.7 %copy-start.2 = (s32[2]{0:T(128)S(1)}, s32[2]{0:T(128)}, u32[]{:S(2)}) copy-start(s32[2]{0:T(128)} %refs_4_.1) | copy-start | bytes 28
  0.7 4.7 %copy-start.3 = (s32[2]{0:T(128)S(1)}, s32[2]{0:T(128)}, u32[]{:S(2)}) copy-start(s32[2]{0:T(128)} %refs_3_.1) | copy-start | bytes 28
  0.7 4.6 %copy-start = (f32[2,2,3]{2,1,0:T(2,128)S(1)}, f32[2,2,3]{2,1,0:T(2,128)}, u32[]{:S(2)}) copy-start(f32[2,2,3]{2,1,0:T(2,128)} %refs_2_.1) | copy-start | bytes 148
  2.3 7.4 %collective-permute-start.2 = (bf16[13,32,128]{2,1,0:T(8,128)(2,1)S(1)}, bf16[13,32,128]{2,1,0:T(8,128)(2,1)S(1)}, u32[]{:S(2)}, u32[]{:S(2)}) collective-permute-start(bf16[13,32,128]{2,1,0:T(8,128)(2,1)S(1)} %get-tuple-element.25), channel_id=1, source_target_pairs={{0,1},{2,3},{4,5},{6,7},{8,9},{10,11},{12,13},{14,15},{1,0},{3,2},... | collective-permute-start | bytes 319496 | tf_op jit(solution)/shard_map/ppermute | solution.py:493
  5.3 4.4 %collective-permute-start.3 = (bf16[13,32,128]{2,1,0:T(8,128)(2,1)S(1)}, bf16[13,32,128]{2,1,0:T(8,128)(2,1)S(1)}, u32[]{:S(2)}, u32[]{:S(2)}) collective-permute-start(bf16[13,32,128]{2,1,0:T(8,128)(2,1)S(1)} %get-tuple-element.26), channel_id=1, source_target_pairs={{1,2},{3,4},{5,6},{7,8},{9,10},{11,12},{13,14},{17,18},{19,20},{21... | collective-permute-start | bytes 319496 | tf_op jit(solution)/shard_map/ppermute | solution.py:494
  6.5 4.4 %collective-permute-start = (bf16[12,32,128]{2,1,0:T(8,128)(2,1)S(1)}, bf16[12,32,128]{2,1,0:T(8,128)(2,1)S(1)}, u32[]{:S(2)}, u32[]{:S(2)}) collective-permute-start(bf16[12,32,128]{2,1,0:T(8,128)(2,1)S(1)} %get-tuple-element.23), channel_id=1, source_target_pairs={{1,2},{3,4},{5,6},{7,8},{9,10},{11,12},{13,14},{17,18},{19,20},{21... | collective-permute-start | bytes 294920 | tf_op jit(solution)/shard_map/ppermute | solution.py:494
  7.1 8.0 %collective-permute-start.1 = (bf16[12,32,128]{2,1,0:T(8,128)(2,1)S(1)}, bf16[12,32,128]{2,1,0:T(8,128)(2,1)S(1)}, u32[]{:S(2)}, u32[]{:S(2)}) collective-permute-start(bf16[12,32,128]{2,1,0:T(8,128)(2,1)S(1)} %get-tuple-element.24), channel_id=1, source_target_pairs={{0,1},{2,3},{4,5},{6,7},{8,9},{10,11},{12,13},{14,15},{1,0},{3,2},... | collective-permute-start | bytes 294920 | tf_op jit(solution)/shard_map/ppermute | solution.py:493
  16.3 6.0 %collective-permute-start.6 = (bf16[2,2,3,32,128]{4,3,2,1,0:T(8,128)(2,1)S(1)}, bf16[2,2,3,32,128]{4,3,2,1,0:T(8,128)(2,1)S(1)}, u32[]{:S(2)}, u32[]{:S(2)}) collective-permute-start(bf16[2,2,3,32,128]{4,3,2,1,0:T(8,128)(2,1)S(1)} %get-tuple-element.29.rows_ref), channel_id=1, source_target_pairs={{0,16},{16,0},{1,17},{17,1},{2,18},{18,2},{3,19},{19,3},{4,20},{20... | collective-permute-start | bytes 294920 | tf_op jit(solution)/shard_map/ppermute | solution.py:527
  16.4 2.5 %collective-permute-start.4 = (bf16[2,2,2,32,128]{4,3,2,1,0:T(8,128)(2,1)S(1)}, bf16[2,2,2,32,128]{4,3,2,1,0:T(8,128)(2,1)S(1)}, u32[]{:S(2)}, u32[]{:S(2)}) collective-permute-start(bf16[2,2,2,32,128]{4,3,2,1,0:T(8,128)(2,1)S(1)} %get-tuple-element.30), channel_id=1, source_target_pairs={{1,2},{3,4},{5,6},{7,8},{9,10},{11,12},{13,14},{17,18},{19,20},{21... | collective-permute-start | bytes 196616 | tf_op jit(solution)/shard_map/ppermute | solution.py:524
  16.9 5.4 %collective-permute-start.5 = (bf16[2,2,2,32,128]{4,3,2,1,0:T(8,128)(2,1)S(1)}, bf16[2,2,2,32,128]{4,3,2,1,0:T(8,128)(2,1)S(1)}, u32[]{:S(2)}, u32[]{:S(2)}) collective-permute-start(bf16[2,2,2,32,128]{4,3,2,1,0:T(8,128)(2,1)S(1)} %get-tuple-element.31), channel_id=1, source_target_pairs={{0,1},{2,3},{4,5},{6,7},{8,9},{10,11},{12,13},{14,15},{1,0},{3,2},... | collective-permute-start | bytes 196616 | tf_op jit(solution)/shard_map/ppermute | solution.py:525

commit v17 on v15

--- a/solution.py
+++ b/solution.py
@@ -123,7 +123,7 @@
         copies += [pltpu.make_async_copy(a, b, sems.at[k + 1]) for k, (a, b) in enumerate(small)]
         others = [pltpu.make_async_copy(planes_ref.at[pl.ds(1, count - 1)], later_ref, sems.at[len(copies)])]
         others.append(pltpu.make_async_copy(back_ref, field_ref, sems.at[len(copies) + 1]))
-        for copy in copies + others:
+        for copy in copies[1:] + copies[:1] + others:
             copy.start()
         for copy in copies:
             copy.wait()

time: 34.3 us -> 34.3 us (level)
  no operation moved by 1% of the time
where the time goes in v17:
time: 34.3 us; the launch traced here: 34.1 us
  blocking collectives  12.9 us (38%)
  starting transfers between devices  8.23 us (24%)
  Pallas kernels  6.37 us (19%)
  waiting for transfers between devices  4.97 us (14%)
  other arithmetic  0.76 us (2%)
  between operations  0.73 us (2%)
    all_to_all x1, blocking collectives, shards(): lax.all_to_all(partial_block, 'space', 0, 0, axis_index_groups=backwards)  11 us
    ppermute x2, starting transfers between devices, shards(): nears.append(lax.ppermute(result[1], 'space', near))  5.55 us
    ppermute x2, waiting for transfers between devices, shards(): nears.append(lax.ppermute(result[1], 'space', near))  4.15 us
    pallas_call x2, Pallas kernels, shards(): pl.pallas_call(functools.partial(first_kernel, s), out_shape=tuple(outs),...  2.56 us
    pallas_call x2, Pallas kernels, shards(): pl.pallas_call(functools.partial(sweep_kernel, s, count, peers * depth),...  2.52 us
    ppermute x1, starting transfers between devices, shards(): from_near = lax.ppermute(to_near, 'space', near)  2.03 us
    all_gather x1, blocking collectives, shards(): every = lax.all_gather(rows, 'rx', axis=0)  1.95 us
    pallas_call x1, Pallas kernels, shards(): pl.pallas_call(functools.partial(block_kernel, cells), out_shape=(rows_of...  0.87 us
  transfers between devices with their start and end apart: 6, of which 2 were waited for; matrix products, arithmetic and copies ran while one was open for 1% of the time, Pallas kernels for 8%

profile of v17, /device:TPU:0, one launch (start us, length us, event | category | flops | bytes accessed | tf_op | source)
XLA Modules:
  0.0 34.1 jit_solution(16222524734095400)
XLA Ops:
  0.6 0.0 copy-start.1
  0.6 0.0 copy-start.2
  0.7 0.0 copy-start.3
  0.7 0.0 copy-start
  0.7 1.6 %first_sweep.2 = (bf16[13,32,128]{2,1,0:T(8,128)(2,1)S(1)}, bf16[13,32,128]{2,1,0:T(8,128)(2,1)S(1)}, f32[2,3,3,32,128]{4,3,2,1,0:T(8,128)S(1)}, f32[2,4,32,128]...) custom-call(f32[2,2,3,3,32,128]{5,4,3,2,1,0:T(8,128)} %planes_ref.1,, ...), custom_call_target="tpu_custom_call" | custom-call | tf_op jit(solution)/shard_map/first_sweep/pallas_call | solution.py:476
  2.3 3.0 %collective-permute-start.2 = (bf16[13,32,128]{2,1,0:T(8,128)(2,1)S(1)}, bf16[13,32,128]{2,1,0:T(8,128)(2,1)S(1)}, u32[]{:S(2)}, u32[]{:S(2)}) collective-permute-start(bf16[13,32,128]{2,1,0:T(8,128)(2,1)S(1)} %get-tuple-element.25), channel_id=1, source_target_pairs={{0,1},{2,3},{4,5},{6,7},{8,9},{10,11},{12,13},{14,15},{1,0},{3,2},... | collective-permute-start | bytes 319496 | tf_op jit(solution)/shard_map/ppermute | solution.py:489
  5.3 0.0 collective-permute-start.3
  5.3 0.0 copy-done
  5.3 0.1 reshape.7
  5.3 0.0 copy-done.1
  5.3 0.0 copy-done.2
  5.3 0.0 copy-done.3
  5.4 0.1 add_convert_fusion
  5.4 0.1 pad_maximum_fusion.refs_0_.scalar_ref
  5.5 1.0 %first_sweep.3 = (bf16[12,32,128]{2,1,0:T(8,128)(2,1)S(1)}, bf16[12,32,128]{2,1,0:T(8,128)(2,1)S(1)}, f32[2,3,3,32,128]{4,3,2,1,0:T(8,128)S(1)}, f32[2,4,32,128]{3,2,1,0:T(8,128)S(1)}) custom-call(f32[1,2,3,3,32,128]{5,4,3,2,1,0:T(8,128)S(1)} %get-tuple-element.18.planes_ref, f32[20]{0:T(128)S(1)} %pad_maximum_fusion.refs_0_.scalar_ref, ...), custom_call_target="tpu_custom_call" | custom-call | tf_op jit(solution)/shard_map/first_sweep/pallas_call | solution.py:476
  6.5 0.6 %collective-permute-start = (bf16[12,32,128]{2,1,0:T(8,128)(2,1)S(1)}, bf16[12,32,128]{2,1,0:T(8,128)(2,1)S(1)}, u32[]{:S(2)}, u32[]{:S(2)}) collective-permute-start(bf16[12,32,128]{2,1,0:T(8,128)(2,1)S(1)} %get-tuple-element.23), channel_id=1, source_target_pairs={{1,2},{3,4},{5,6},{7,8},{9,10},{11,12},{13,14},{17,18},{19,20},{21... | collective-permute-start | bytes 294920 | tf_op jit(solution)/shard_map/ppermute | solution.py:490
  7.1 2.6 %collective-permute-start.1 = (bf16[12,32,128]{2,1,0:T(8,128)(2,1)S(1)}, bf16[12,32,128]{2,1,0:T(8,128)(2,1)S(1)}, u32[]{:S(2)}, u32[]{:S(2)}) collective-permute-start(bf16[12,32,128]{2,1,0:T(8,128)(2,1)S(1)} %get-tuple-element.24), channel_id=1, source_target_pairs={{0,1},{2,3},{4,5},{6,7},{8,9},{10,11},{12,13},{14,15},{1,0},{3,2},... | collective-permute-start | bytes 294920 | tf_op jit(solution)/shard_map/ppermute | solution.py:489
  9.6 0.0 collective-permute-done.2.one_in.near_cond
  9.6 0.0 collective-permute-done.3.other_in.far_cond
  9.6 1.2 %sweeps.2.refs_0_ = bf16[2,3,32,128]{3,2,1,0:T(8,128)(2,1)S(1)} custom-call(f32[20]{0:T(128)S(1)} %pad_maximum_fusion.refs_0_.scalar_ref, f32[2,3,3,32,128]{4,3,2,1,0:T(8,128)S(1)} %get-tuple-element.27.own_ref, f32[2,4,32,128]{3,2,1,0:T(8,128)S(1)} %get-tuple-element.28.edge_ref, f32[3,32,128]{2,1,0:T(8,128)S(1)} %get-tuple-element.19.refs_1_.held_ref, ...), custom_call_target="tpu_custom_call" | custom-call | tf_op jit(solution)/shard_map/sweeps/pallas_call | solution.py:509
  10.9 0.0 collective-permute-done.one_in
  10.9 4.1 %collective-permute-done.1.other_in = bf16[12,32,128]{2,1,0:T(8,128)(2,1)S(1)} collective-permute-done((bf16[12,32,128]{2,1,0:T(8,128)(2,1)S(1)}, bf16[12,32,128]{2,1,0:T(8,128)(2,1)S(1)}, u32[]{:S(2)}, u32[]{:S(2)}) %collective-permute-start.1) | collective-permute-done | bytes 98336 | tf_op jit(solution)/shard_map/ppermute | solution.py:489
  15.0 1.3 %sweeps.3 = (bf16[2,2,3,32,128]{4,3,2,1,0:T(8,128)(2,1)S(1)}, bf16[2,2,2,32,128]{4,3,2,1,0:T(8,128)(2,1)S(1)}, bf16[2,2,2,32,128]{4,3,2,1,0:T(8,128)(2,1)S(1)}) custom-call(f32[20]{0:T(128)S(1)} %pad_maximum_fusion.refs_0_.scalar_ref, f32[2,3,3,32,128]{4,3,2,1,0:T(8,128)S(1)} %get-tuple-element.20.own_ref, f32[2,4,32,128]{3,2,1,0:T(8,128)S(1)} %get-tuple-element.21.edge_ref, ...), custom_call_target="tpu_custom_call" | custom-call | tf_op jit(solution)/shard_map/sweeps/pallas_call | solution.py:509
  16.3 0.1 collective-permute-start.4
  16.4 2.0 %collective-permute-start.5 = (bf16[2,2,2,32,128]{4,3,2,1,0:T(8,128)(2,1)S(1)}, bf16[2,2,2,32,128]{4,3,2,1,0:T(8,128)(2,1)S(1)}, u32[]{:S(2)}, u32[]{:S(2)}) collective-permute-start(bf16[2,2,2,32,128]{4,3,2,1,0:T(8,128)(2,1)S(1)} %get-tuple-element.31), channel_id=1, source_target_pairs={{0,1},{2,3},{4,5},{6,7},{8,9},{10,11},{12,13},{14,15},{1,0},{3,2},... | collective-permute-start | bytes 196616 | tf_op jit(solution)/shard_map/ppermute | solution.py:521
  18.4 0.4 %smooth.1.alone_ref = f32[2,2,3,32,128]{4,3,2,1,0:T(8,128)S(1)} custom-call(bf16[2,2,3,32,128]{4,3,2,1,0:T(8,128)(2,1)S(1)} %get-tuple-element.29.rows_ref), custom_call_target="tpu_custom_call" | custom-call | tf_op jit(solution)/shard_map/smooth/pallas_call | solution.py:525
  18.9 1.9 %all-gather = bf16[4,2,3,32,128]{4,3,2,1,0:T(8,128)(2,1)S(1)} all-gather(bf16[2,2,3,32,128]{4,3,2,1,0:T(8,128)(2,1)S(1)} %get-tuple-element.29.rows_ref), channel_id=2, replica_groups=mesh['rx'=2,'space'=16] {'rx'}, dimensions={0}, use_global_device_ids=true | all-gather | bytes 294912 | tf_op jit(solution)/shard_map/all_gather | solution.py:522
  20.8 0.0 collective-permute-done.4.far_in
  20.8 0.8 %collective-permute-done.5.near_in = bf16[2,2,2,32,128]{4,3,2,1,0:T(8,128)(2,1)S(1)} collective-permute-done((bf16[2,2,2,32,128]{4,3,2,1,0:T(8,128)(2,1)S(1)}, bf16[2,2,2,32,128]{4,3,2,1,0:T(8,128)(2,1)S(1)}, u32[]{:S(2)}, u32[]{:S(2)}) %collective-permute-start.5) | collective-permute-done | bytes 65568 | tf_op jit(solution)/shard_map/ppermute | solution.py:521
  21.6 0.9 %block.1 = (bf16[2,2,3,32,128]{4,3,2,1,0:T(8,128)(2,1)}, f32[16,4,8]{2,1,0:T(4,128)S(1)}) custom-call(bf16[2,2,3,32,128]{4,3,2,1,0:T(8,128)(2,1)S(1)} %get-tuple-element.29.rows_ref, f32[2,2,3,32,128]{4,3,2,1,0:T(8,128)S(1)} %smooth.1.alone_ref, bf16[2,2,2,32,128]{4,3,2,1,0:T(8,128)(2,1)S(1)} %collective-permute-done.4.far_in, ...), custom_call_target="tpu_custom_call" | custom-call | tf_op jit(solution)/shard_map/block/pallas_call | solution.py:533
  22.5 11.0 %all_to_all.5 = f32[16,4,8]{2,1,0:T(4,128)S(1)} all-to-all(f32[16,4,8]{2,1,0:T(4,128)S(1)} %get-tuple-element.32), channel_id=1, replica_groups={{15,14,13,12,11,10,9,8,7,6,5,4,3,2,1,0},{31,30,29,28,27,26,25,24,23,22,..., dimensions={0} | all-to-all | bytes 4096 | tf_op jit(solution)/shard_map/all_to_all | solution.py:548
  33.5 0.6 %reduce_sum.9 = f32[4,8]{1,0:T(4,128)} reduce(f32[16,4,8]{2,1,0:T(4,128)S(1)} %all_to_all.5, f32[]{:T(128)} %constant.0.clone.1), dimensions={0}, to_apply=%region_0.0 | reduce | flops 480 | bytes 2180 | tf_op jit(solution)/shard_map/reduce_sum | solution.py:549
Async XLA Ops:
  0.6 4.7 %copy-start.1 = (s32[4]{0:T(128)S(1)}, s32[4]{0:T(128)}, u32[]{:S(2)}) copy-start(s32[4]{0:T(128)} %refs_5_.1) | copy-start | bytes 52
  0.6 4.7 %copy-start.2 = (s32[2]{0:T(128)S(1)}, s32[2]{0:T(128)}, u32[]{:S(2)}) copy-start(s32[2]{0:T(128)} %refs_4_.1) | copy-start | bytes 28
  0.7 4.7 %copy-start.3 = (s32[2]{0:T(128)S(1)}, s32[2]{0:T(128)}, u32[]{:S(2)}) copy-start(s32[2]{0:T(128)} %refs_3_.1) | copy-start | bytes 28
  0.7 4.6 %copy-start = (f32[2,2,3]{2,1,0:T(2,128)S(1)}, f32[2,2,3]{2,1,0:T(2,128)}, u32[]{:S(2)}) copy-start(f32[2,2,3]{2,1,0:T(2,128)} %refs_2_.1) | copy-start | bytes 148
  2.3 7.4 %collective-permute-start.2 = (bf16[13,32,128]{2,1,0:T(8,128)(2,1)S(1)}, bf16[13,32,128]{2,1,0:T(8,128)(2,1)S(1)}, u32[]{:S(2)}, u32[]{:S(2)}) collective-permute-start(bf16[13,32,128]{2,1,0:T(8,128)(2,1)S(1)} %get-tuple-element.25), channel_id=1, source_target_pairs={{0,1},{2,3},{4,5},{6,7},{8,9},{10,11},{12,13},{14,15},{1,0},{3,2},... | collective-permute-start | bytes 319496 | tf_op jit(solution)/shard_map/ppermute | solution.py:489
  5.3 4.4 %collective-permute-start.3 = (bf16[13,32,128]{2,1,0:T(8,128)(2,1)S(1)}, bf16[13,32,128]{2,1,0:T(8,128)(2,1)S(1)}, u32[]{:S(2)}, u32[]{:S(2)}) collective-permute-start(bf16[13,32,128]{2,1,0:T(8,128)(2,1)S(1)} %get-tuple-element.26), channel_id=1, source_target_pairs={{1,2},{3,4},{5,6},{7,8},{9,10},{11,12},{13,14},{17,18},{19,20},{21... | collective-permute-start | bytes 319496 | tf_op jit(solution)/shard_map/ppermute | solution.py:490
  6.5 4.4 %collective-permute-start = (bf16[12,32,128]{2,1,0:T(8,128)(2,1)S(1)}, bf16[12,32,128]{2,1,0:T(8,128)(2,1)S(1)}, u32[]{:S(2)}, u32[]{:S(2)}) collective-permute-start(bf16[12,32,128]{2,1,0:T(8,128)(2,1)S(1)} %get-tuple-element.23), channel_id=1, source_target_pairs={{1,2},{3,4},{5,6},{7,8},{9,10},{11,12},{13,14},{17,18},{19,20},{21... | collective-permute-start | bytes 294920 | tf_op jit(solution)/shard_map/ppermute | solution.py:490
  7.1 8.0 %collective-permute-start.1 = (bf16[12,32,128]{2,1,0:T(8,128)(2,1)S(1)}, bf16[12,32,128]{2,1,0:T(8,128)(2,1)S(1)}, u32[]{:S(2)}, u32[]{:S(2)}) collective-permute-start(bf16[12,32,128]{2,1,0:T(8,128)(2,1)S(1)} %get-tuple-element.24), channel_id=1, source_target_pairs={{0,1},{2,3},{4,5},{6,7},{8,9},{10,11},{12,13},{14,15},{1,0},{3,2},... | collective-permute-start | bytes 294920 | tf_op jit(solution)/shard_map/ppermute | solution.py:489
  16.3 4.5 %collective-permute-start.4 = (bf16[2,2,2,32,128]{4,3,2,1,0:T(8,128)(2,1)S(1)}, bf16[2,2,2,32,128]{4,3,2,1,0:T(8,128)(2,1)S(1)}, u32[]{:S(2)}, u32[]{:S(2)}) collective-permute-start(bf16[2,2,2,32,128]{4,3,2,1,0:T(8,128)(2,1)S(1)} %get-tuple-element.30), channel_id=1, source_target_pairs={{1,2},{3,4},{5,6},{7,8},{9,10},{11,12},{13,14},{17,18},{19,20},{21... | collective-permute-start | bytes 196616 | tf_op jit(solution)/shard_map/ppermute | solution.py:520
  16.4 5.2 %collective-permute-start.5 = (bf16[2,2,2,32,128]{4,3,2,1,0:T(8,128)(2,1)S(1)}, bf16[2,2,2,32,128]{4,3,2,1,0:T(8,128)(2,1)S(1)}, u32[]{:S(2)}, u32[]{:S(2)}) collective-permute-start(bf16[2,2,2,32,128]{4,3,2,1,0:T(8,128)(2,1)S(1)} %get-tuple-element.31), channel_id=1, source_target_pairs={{0,1},{2,3},{4,5},{6,7},{8,9},{10,11},{12,13},{14,15},{1,0},{3,2},... | collective-permute-start | bytes 196616 | tf_op jit(solution)/shard_map/ppermute | solution.py:521
